TPU v7x, 32 devices: a whole 2x2x4 slice. The times are simulated.
32 devices in a mesh: grp: 2 (over y), die: 4 (over z), sub: 2 (over x), blk: 2 (over core).
Axes of the slice: x: 2, y: 2, z: 4, core: 2. Of those that a mesh axis runs over, the one named last changes fastest.
Arguments:
- history: float32 [1024, 3, 32, 128], P(('grp', 'die', 'sub', 'blk')), parts along dimension 0, may hold values from -2 to 2
- new_slot: int32 [1024], P(('grp', 'die', 'sub', 'blk')), parts along dimension 0, may hold values from 0 to 511, as said below
- partner: int32 [1024], P(('grp', 'die', 'sub', 'blk')), parts along dimension 0, may hold values from 0 to 511, as said below
- coupling: float32 [1024, 128, 128], P(('grp', 'die', 'sub', 'blk')), parts along dimension 0, as said below
- cap_rate: float32 [1024, 128], P(('grp', 'die', 'sub', 'blk')), parts along dimension 0, may hold values from 0.5 to 5
- device_gain: float32 [1024, 128], P(('grp', 'die', 'sub', 'blk')), parts along dimension 0, may hold values from 0.2 to 2
- wire_gain: float32 [1024, 128], P(('grp', 'die', 'sub', 'blk')), parts along dimension 0, may hold values from 0.2 to 2
- region_gain: float32 [1024, 128], P(('grp', 'die', 'sub', 'blk')), parts along dimension 0, may hold values from 0.2 to 1
- drive: float32 [1024, 32, 128], P(('grp', 'die', 'sub', 'blk')), parts along dimension 0, may hold values from -6 to 6
- region_inverse: float32 [8, 128, 128], P(('grp', 'die'), 'blk'), parts along dimension 0
Outputs:
- updated: float32 [1024, 32, 128], P(('grp', 'die', 'sub', 'blk')), parts along dimension 0
- residual: float32 [1024, 32, 128], P(('grp', 'die', 'sub', 'blk')), parts along dimension 0
There are 2 independent parts, one for each index of `grp`. A program takes and returns all parts, laid end to end along the dimension named above; each array names one. Nothing has to cross between parts.
Inputs may be any that keep to these rules, and one draw needn't show every extreme that they name: `new_slot`: A permutation; a subcircuit moves only between devices that share the sub and blk index. The subcircuits leaving a device fill exactly the slots that its own leaving subcircuits vacate on the receiving side. At most 2 subcircuits of one device go to one other device, and this is reached on every device. Every partner lies on a device with the same sub and blk index. At most 16 subcircuits of one device read from blocks of one owner device, reached on every device. `coupling`: diagonal entries between 1.5 and 3.5.
All inputs are finite; a program needn't handle non-finite values.
Results may differ from a plain program's by a relative error of at most 0.00005.
Values sent between devices are 32-bit elements; how exact they have to be, the bound alone decides.
No kernel may reach another device: no remote copies, remote signals or barrier semaphores. Data moves between devices by JAX's collectives and lax.ppermute only.
A program may use at most 64 MiB of HBM per device.

v0:
```python
import jax
import jax.numpy as jnp
from jax import lax
from jax.sharding import PartitionSpec as P

CAP = 2


def onehot_product(selector, values):
    return jnp.dot(
        selector.astype(jnp.float32),
        values,
        precision=lax.Precision.HIGHEST,
        preferred_element_type=jnp.float32,
    )


def shards(
    history,
    new_slot,
    partner,
    coupling,
    cap_rate,
    device_gain,
    wire_gain,
    region_gain,
    drive,
    region_inverse,
):
    blocks = history.shape[0]
    scen = history.shape[2]
    nodes = history.shape[3]
    ndie = lax.axis_size("die")
    ncol = lax.axis_size("sub") * lax.axis_size("blk")
    column = lax.axis_index("sub") * lax.axis_size("blk") + lax.axis_index("blk")
    first = (lax.axis_index("die") * ncol + column) * blocks
    local = jnp.arange(blocks, dtype=jnp.int32)
    own = first + local
    dest_die = new_slot // (ncol * blocks)
    dest_loc = new_slot % blocks
    moving = new_slot != own
    earlier = (
        (local[:, None] < local[None, :])
        & (dest_die[:, None] == dest_die[None, :])
        & moving[:, None]
        & moving[None, :]
    )
    rank = jnp.sum(earlier.astype(jnp.int32), axis=0)
    target = dest_die * CAP + rank
    outgoing = jnp.arange(ndie * CAP, dtype=jnp.int32)
    pick = (outgoing[:, None] == target[None, :]) & moving[None, :]
    sent_loc = jnp.sum(pick.astype(jnp.int32) * (dest_loc[None, :] + 1), axis=1) - 1
    packed = onehot_product(pick, history.reshape(blocks, -1))
    got, got_loc = (
        lax.all_to_all(packed, "die", split_axis=0, concat_axis=0, tiled=True),
        lax.all_to_all(sent_loc, "die", split_axis=0, concat_axis=0, tiled=True),
    )
    landing = got_loc[None, :] == local[:, None]
    arrived = jnp.any(landing, axis=1)
    placed = onehot_product(landing, got).reshape(history.shape)
    state = jnp.where(arrived[:, None, None, None], placed, history)
    guess = 3.0 * state[:, 0] - 3.0 * state[:, 1] + state[:, 2]
    memory = 4.0 * state[:, 0] - state[:, 1]
    rcap = 2 * max(1, blocks // ndie)
    owner_die = partner // (ncol * blocks)
    owner_loc = partner % blocks
    before = (local[:, None] < local[None, :]) & (owner_die[:, None] == owner_die[None, :])
    order_rank = jnp.sum(before.astype(jnp.int32), axis=0)
    ask = owner_die * rcap + order_rank
    asking = jnp.arange(ndie * rcap, dtype=jnp.int32)[:, None] == ask[None, :]
    ask_loc = jnp.sum(asking.astype(jnp.int32) * (owner_loc[None, :] + 1), axis=1) - 1
    wanted = lax.all_to_all(ask_loc, "die", split_axis=0, concat_axis=0, tiled=True)
    serve = wanted[:, None] == local[None, :]
    rows_out = onehot_product(serve, guess.reshape(blocks, -1))
    back = lax.all_to_all(rows_out, "die", split_axis=0, concat_axis=0, tiled=True)
    neighbour = onehot_product(asking.T, back).reshape(blocks, scen, nodes)
    tnh = jnp.tanh(guess)
    through = jnp.einsum(
        "snk,sik->sni",
        guess,
        coupling,
        precision=lax.Precision.HIGHEST,
        preferred_element_type=jnp.float32,
    )
    diagonal = jnp.diagonal(coupling, axis1=1, axis2=2)
    cap = cap_rate[:, None, :]
    gdev = device_gain[:, None, :]
    wire = wire_gain[:, None, :]
    gain = region_gain[:, None, :]
    pivot = 1.5 * cap + diagonal[:, None, :] + gdev * (1.0 - tnh * tnh) + wire
    residual = (
        0.5 * cap * (3.0 * guess - memory)
        + through
        + gdev * tnh
        + wire * (guess - neighbour)
        - drive
    )
    scaled = residual / pivot
    share = jnp.sum(gain * scaled, axis=0)
    inverse_rows = region_inverse[0]
    height = inverse_rows.shape[0]
    total = lax.psum(share, ("sub", "blk"))
    mine = lax.dynamic_slice_in_dim(total, lax.axis_index("blk") * height, height, 1)
    contribution = jnp.dot(
        mine, inverse_rows, precision=lax.Precision.HIGHEST, preferred_element_type=jnp.float32
    )
    region = lax.psum(contribution, "blk")
    updated = guess + (gain * region[None, :, :] - residual) / pivot
    return (updated, residual)


def solution(mesh):
    in_specs = (
        P(("grp", "die", "sub", "blk"), None, None, None),
        P(("grp", "die", "sub", "blk")),
        P(("grp", "die", "sub", "blk")),
        P(("grp", "die", "sub", "blk"), None, None),
        P(("grp", "die", "sub", "blk"), None),
        P(("grp", "die", "sub", "blk"), None),
        P(("grp", "die", "sub", "blk"), None),
        P(("grp", "die", "sub", "blk"), None),
        P(("grp", "die", "sub", "blk"), None, None),
        P(("grp", "die"), "blk", None),
    )
    out_specs = (
        P(("grp", "die", "sub", "blk"), None, None),
        P(("grp", "die", "sub", "blk"), None, None),
    )
    return jax.shard_map(shards, mesh=mesh, in_specs=in_specs, out_specs=out_specs, check_vma=False)
```

profile of v0, /device:TPU:0, one launch (start us, length us, event | category | flops | bytes accessed | tf_op | source)
XLA Modules:
  0.0 86.6 jit_solution(8156676903323580998)
XLA Ops:
  0.6 0.0 copy-start
  0.6 0.7 fusion.31
  1.3 0.7 add_compare_fusion
  2.0 0.1 convert_reduce_fusion.1
  2.1 0.1 select_reduce_fusion.1
  2.2 0.7 sub.53
  2.9 6.3 %all-to-all-start = ((s32[4,2,1]{1,2,0:T(1,128)}), s32[4,2,1]{1,2,0:T(1,128)S(1)}, u32[]{:S(2)}, u32[]{:S(2)}) async-start(s32[4,2,1]{1,2,0:T(1,128)} %bitcast), calls=%async_computation | async-start | bytes 4096 | tf_op jit(solution)/shard_map/all_to_all | solution.py:56
  9.2 0.0 copy-start.8
  9.2 1.6 %reshape.134 = f32[32,12288,1]{1,0,2:T(8,128)S(1)} reshape(f32[32,3,32,128]{3,2,1,0:T(8,128)} %param.10) | data formatting | bytes 3145728 | tf_op jit(solution)/shard_map/reshape | solution.py:53
  10.8 0.1 compare_and_fusion
  10.9 0.0 copy-done.8
  10.9 0.1 convert_reduce_fusion
  11.0 0.0 copy-start.2
  11.0 1.6 %fusion.24 = f32[4,2,12288]{2,1,0:T(2,128)} fusion(f32[32,12288,1]{1,0,2:T(8,128)S(1)} %reshape.134, pred[4,2,32]{2,0,1:T(4,128)(4,1)S(1)} %compare_and_fusion), kind=kOutput, calls=%fused_computation.38 | convolution fusion | flops 37748736 | bytes 1966336 | tf_op jit(solution)/shard_map/dot_general | solution.py:10
  12.6 2.0 %all-to-all-done = s32[4,2,1]{1,2,0:T(1,128)S(1)} async-done(((s32[4,2,1]{1,2,0:T(1,128)}), s32[4,2,1]{1,2,0:T(1,128)S(1)}, u32[]{:S(2)}, u32[]{:S(2)}) %all-to-all-start) | async-done | bytes 64 | tf_op jit(solution)/shard_map/all_to_all | solution.py:56
  14.7 3.5 %all-to-all-start.1 = ((f32[4,2,12288]{2,1,0:T(2,128)}), f32[4,2,12288]{2,1,0:T(2,128)S(1)}, u32[]{:S(2)}, u32[]{:S(2)}) async-start(f32[4,2,12288]{2,1,0:T(2,128)} %fusion.24), calls=%async_computation.1 | async-start | bytes 786432 | tf_op jit(solution)/shard_map/all_to_all | solution.py:55
  18.1 0.1 select_reduce_fusion
  18.2 0.7 sub.60
  18.9 0.6 broadcast.181
  19.5 0.7 reduce.3
  20.2 0.1 eq.122
  20.3 0.1 fusion.27
  20.4 8.4 %all-to-all-done.1 = f32[4,2,12288]{2,1,0:T(2,128)S(1)} async-done(((f32[4,2,12288]{2,1,0:T(2,128)}), f32[4,2,12288]{2,1,0:T(2,128)S(1)}, u32[]{:S(2)}, u32[]{:S(2)}) %all-to-all-start.1) | async-done | bytes 393248 | tf_op jit(solution)/shard_map/all_to_all | solution.py:55
  28.8 3.2 %all-to-all-start.2 = ((s32[4,16,1]{1,2,0:T(1,128)}), s32[4,16,1]{1,2,0:T(1,128)S(1)}, u32[]{:S(2)}, u32[]{:S(2)}) async-start(s32[4,16,1]{1,2,0:T(1,128)} %bitcast.8), calls=%async_computation.2 | async-start | bytes 4096 | tf_op jit(solution)/shard_map/all_to_all | solution.py:72
  32.1 1.0 %all_to_all.24 = f32[8,12288]{1,0:T(8,128)} reshape(f32[4,2,12288]{2,1,0:T(2,128)S(1)} %all-to-all-done.1) | data formatting | bytes 786432 | tf_op jit(solution)/shard_map/all_to_all | solution.py:55
  33.1 0.0 copy-done.2
  33.1 2.7 %copy_select_fusion = f32[32,3,32,128]{3,0,2,1:T(8,128)S(1)} fusion(f32[32,3,32,128]{3,2,1,0:T(8,128)S(1)} %copy-done.2, f32[3,32,128,8]{2,3,1,0:T(8,128)} %bitcast.61, pred[32]{0:T(512)(128)(4,1)S(1)} %fusion.27, s32[8]{0:T(128)S(1)} %eq.122), kind=kOutput, calls=%fused_computation.1 | convolution fusion | flops 38142208 | bytes 3539008 | tf_op jit(solution)/shard_map/dot_general | solution.py:10
  35.7 0.2 slice_add_fusion
  35.9 0.3 copy.67
  36.2 0.1 reshape.136
  36.3 1.2 %all-to-all-done.2 = s32[4,16,1]{1,2,0:T(1,128)S(1)} async-done(((s32[4,16,1]{1,2,0:T(1,128)}), s32[4,16,1]{1,2,0:T(1,128)S(1)}, u32[]{:S(2)}, u32[]{:S(2)}) %all-to-all-start.2) | async-done | bytes 288 | tf_op jit(solution)/shard_map/all_to_all | solution.py:72
  37.5 1.7 %fusion.13 = f32[4,16,4096]{2,1,0:T(8,128)} fusion(f32[32,4096,1]{1,0,2:T(8,128)S(1)} %reshape.136, s32[4,16]{1,0:T(4,128)S(1)} %bitcast.63), kind=kOutput, calls=%fused_computation.22 | convolution fusion | flops 100665344 | bytes 1573120 | tf_op jit(solution)/shard_map/dot_general | solution.py:10
  39.2 3.9 %all-to-all-start.3 = ((f32[4,16,4096]{2,1,0:T(8,128)}), f32[4,16,4096]{2,1,0:T(8,128)S(1)}, u32[]{:S(2)}, u32[]{:S(2)}) async-start(f32[4,16,4096]{2,1,0:T(8,128)} %fusion.13), calls=%async_computation.3 | async-start | bytes 2097152 | tf_op jit(solution)/shard_map/all_to_all | solution.py:75
  43.1 0.0 copy-start.7
  43.1 6.3 %copy.70 = f32[32,128,128]{0,2,1:T(8,128)} copy(f32[32,128,128]{2,1,0:T(8,128)} %param.13) | data formatting | bytes 4194304 | tf_op args[3]
  49.4 1.8 %gather_fusion = f32[128,32]{1,0:T(8,128)S(1)} fusion(f32[32,128,128]{0,2,1:T(8,128)} %copy.70, s32[128]{0:T(128)S(1)} %or_bitcast_fusion), kind=kCustom, calls=%fused_computation | custom fusion | bytes 33792 | tf_op jit(solution)/shard_map/jit(diagonal)/gather | solution.py:85
  51.2 0.1 copy.71
  51.3 0.0 copy-done.7
  51.3 0.0 copy-start.1
  51.3 0.2 fusion.38
  51.5 1.4 %copy-done.1 = f32[32,128,128]{2,1,0:T(8,128)S(1)} copy-done((f32[32,128,128]{2,1,0:T(8,128)S(1)}, f32[32,128,128]{2,1,0:T(8,128)}, u32[]{:S(2)}) %copy-start.1) | copy-done | bytes 2097176
  52.9 0.0 copy-start.4
  52.9 0.0 copy-start.5
  52.9 0.0 copy-start.6
  52.9 4.2 %fusion.8 = f32[32,32,128]{2,1,0:T(8,128)} fusion(f32[32,128,128]{2,1,0:T(8,128)S(1)} %copy-done.1, f32[32,32,128]{2,0,1:T(8,128)S(1)} %fusion.38), kind=kOutput, calls=%fused_computation.13 | convolution fusion | flops 201326592 | bytes 3145728 | tf_op jit(solution)/shard_map/snk,sik->sni/dot_general | solution.py:78
  57.0 9.6 %all-to-all-done.3 = f32[4,16,4096]{2,1,0:T(8,128)S(1)} async-done(((f32[4,16,4096]{2,1,0:T(8,128)}), f32[4,16,4096]{2,1,0:T(8,128)S(1)}, u32[]{:S(2)}, u32[]{:S(2)}) %all-to-all-start.3) | async-done | bytes 1048608 | tf_op jit(solution)/shard_map/all_to_all | solution.py:75
  66.7 0.0 copy-start.3
  66.7 1.0 %copy-done.3 = f32[4,16,4096]{2,1,0:T(8,128)} copy-done((f32[4,16,4096]{2,1,0:T(8,128)}, f32[4,16,4096]{2,1,0:T(8,128)S(1)}, u32[]{:S(2)}) %copy-start.3) | copy-done | bytes 1048600
  67.6 0.0 copy-done.4
  67.6 0.0 copy-done.5
  67.6 0.0 copy-done.6
  67.6 2.7 %multiply_reduce_fusion = (f32[32,128]{1,0:T(8,128)S(1)}, f32[32,32,128]{2,0,1:T(8,128)S(1)}) fusion(f32[32,128]{1,0:T(8,128)S(1)} %get-tuple-element.12, f32[32,128]{1,0:T(8,128)S(1)} %copy-done.4, f32[32,128]{1,0:T(8,128)S(1)} %copy-done.5, f32[32,128]{1,0:T(8,128)S(1)} %copy-done.6, f32[32,1,32,128]{3,0,2,1:T(8,128)S(1)} %slice_add_fusion, ...), kind=kOutput, calls=%fused_computation.16 | convolution fusion | flops 103282688 | bytes 4292736 | tf_op jit(solution)/shard_map/dot_general | solution.py:10
  70.4 10.1 %psum.14 = f32[32,128]{1,0:T(8,128)S(1)} all-reduce(f32[32,128]{1,0:T(8,128)S(1)} %get-tuple-element.18), channel_id=1, replica_groups=mesh['grp'=2,'die'=4,'sub'=2,'blk'=2] {'sub','blk'}, use_global_device_ids=true, to_apply=%region_6.7 | all-reduce | flops 4096 | bytes 32768 | tf_op jit(solution)/shard_map/psum | solution.py:102
  80.5 0.0 copy-done
  80.5 0.2 fusion.10
  80.8 3.4 %psum.15 = f32[32,128]{1,0:T(8,128)S(1)} all-reduce(f32[32,128]{1,0:T(8,128)S(1)} %fusion.10), channel_id=1, replica_groups=mesh['grp'=2,'die'=4,'sub'=2,'blk'=2] {'blk'}, use_global_device_ids=true, to_apply=%region_7.8 | all-reduce | flops 4096 | bytes 32768 | tf_op jit(solution)/shard_map/psum | solution.py:107
  84.1 1.1 %copy.73 = f32[32,32,128]{2,1,0:T(8,128)} copy(f32[32,32,128]{2,0,1:T(8,128)S(1)} %get-tuple-element.19) | data formatting | bytes 1048576
  85.2 0.3 divide_add_fusion
  85.5 1.1 %copy.72 = f32[32,32,128]{2,1,0:T(8,128)} copy(f32[32,32,128]{2,0,1:T(8,128)S(1)} %divide_add_fusion) | data formatting | bytes 1048576
  (8 shorter events, 0.1 us)
Async XLA Ops:
  0.6 79.9 %copy-start = (f32[1,64,128]{2,1,0:T(8,128)S(1)}, f32[1,64,128]{2,1,0:T(8,128)}, u32[]{:S(2)}) copy-start(f32[1,64,128]{2,1,0:T(8,128)} %param.19) | copy-start | bytes 98308
  2.9 11.8 %all-to-all-start = ((s32[4,2,1]{1,2,0:T(1,128)}), s32[4,2,1]{1,2,0:T(1,128)S(1)}, u32[]{:S(2)}, u32[]{:S(2)}) async-start(s32[4,2,1]{1,2,0:T(1,128)} %bitcast), calls=%async_computation | async-start | bytes 4096 | tf_op jit(solution)/shard_map/all_to_all | solution.py:56
  9.2 1.7 %copy-start.8 = (s32[32]{0:T(128)S(1)}, s32[32]{0:T(128)}, u32[]{:S(2)}) copy-start(s32[32]{0:T(128)} %param.12) | copy-start | bytes 388
  11.0 22.1 %copy-start.2 = (f32[32,3,32,128]{3,2,1,0:T(8,128)S(1)}, f32[32,3,32,128]{3,2,1,0:T(8,128)}, u32[]{:S(2)}) copy-start(f32[32,3,32,128]{3,2,1,0:T(8,128)} %param.10) | copy-start | bytes 4718596
  14.7 14.2 %all-to-all-start.1 = ((f32[4,2,12288]{2,1,0:T(2,128)}), f32[4,2,12288]{2,1,0:T(2,128)S(1)}, u32[]{:S(2)}, u32[]{:S(2)}) async-start(f32[4,2,12288]{2,1,0:T(2,128)} %fusion.24), calls=%async_computation.1 | async-start | bytes 786432 | tf_op jit(solution)/shard_map/all_to_all | solution.py:55
  28.8 8.7 %all-to-all-start.2 = ((s32[4,16,1]{1,2,0:T(1,128)}), s32[4,16,1]{1,2,0:T(1,128)S(1)}, u32[]{:S(2)}, u32[]{:S(2)}) async-start(s32[4,16,1]{1,2,0:T(1,128)} %bitcast.8), calls=%async_computation.2 | async-start | bytes 4096 | tf_op jit(solution)/shard_map/all_to_all | solution.py:72
  39.2 27.5 %all-to-all-start.3 = ((f32[4,16,4096]{2,1,0:T(8,128)}), f32[4,16,4096]{2,1,0:T(8,128)S(1)}, u32[]{:S(2)}, u32[]{:S(2)}) async-start(f32[4,16,4096]{2,1,0:T(8,128)} %fusion.13), calls=%async_computation.3 | async-start | bytes 2097152 | tf_op jit(solution)/shard_map/all_to_all | solution.py:75
  43.1 8.2 %copy-start.7 = (f32[32,128]{1,0:T(8,128)S(1)}, f32[32,128]{1,0:T(8,128)}, u32[]{:S(2)}) copy-start(f32[32,128]{1,0:T(8,128)} %param.14) | copy-start | bytes 49156
  51.3 1.6 %copy-start.1 = (f32[32,128,128]{2,1,0:T(8,128)S(1)}, f32[32,128,128]{2,1,0:T(8,128)}, u32[]{:S(2)}) copy-start(f32[32,128,128]{2,1,0:T(8,128)} %param.13) | copy-start | bytes 6291460
  52.9 14.8 %copy-start.4 = (f32[32,128]{1,0:T(8,128)S(1)}, f32[32,128]{1,0:T(8,128)}, u32[]{:S(2)}) copy-start(f32[32,128]{1,0:T(8,128)} %param.16) | copy-start | bytes 49156
  52.9 14.8 %copy-start.5 = (f32[32,128]{1,0:T(8,128)S(1)}, f32[32,128]{1,0:T(8,128)}, u32[]{:S(2)}) copy-start(f32[32,128]{1,0:T(8,128)} %param.15) | copy-start | bytes 49156
  52.9 14.8 %copy-start.6 = (f32[32,128]{1,0:T(8,128)S(1)}, f32[32,128]{1,0:T(8,128)}, u32[]{:S(2)}) copy-start(f32[32,128]{1,0:T(8,128)} %param.17) | copy-start | bytes 49156
  66.7 1.0 %copy-start.3 = (f32[4,16,4096]{2,1,0:T(8,128)}, f32[4,16,4096]{2,1,0:T(8,128)S(1)}, u32[]{:S(2)}) copy-start(f32[4,16,4096]{2,1,0:T(8,128)S(1)} %all-to-all-done.3) | copy-start | bytes 3145732
where the time goes:
time: 87.3 us; the launch traced here: 86.6 us
  waiting for transfers between devices  21.3 us (24%)
  local copies, waits for them, and re-layouts  17.8 us (20%)
  starting transfers between devices  16.9 us (19%)
  blocking collectives  13.5 us (15%)
  matrix products  13 us (15%)
  other arithmetic  3.28 us (4%)
    unnamed x21, local copies, waits for them, and re-layouts  10.9 us
    psum x1, blocking collectives, shards(): total = lax.psum(share, ('sub', 'blk'))  10.1 us
    all_to_all x1, waiting for transfers between devices, shards(): lax.all_to_all(rows_out, 'die', split_axis=0, concat_axis=0, tiled=True)  9.62 us
    dot_general x4, matrix products, onehot_product(): jnp.dot(selector.astype(jnp.float32), values, precision=lax.Precision.HIG...  8.68 us
    all_to_all x1, waiting for transfers between devices, shards(): lax.all_to_all(packed, 'die', split_axis=0, concat_axis=0, tiled=True)  8.45 us
    all_to_all x1, starting transfers between devices, shards(): lax.all_to_all(sent_loc, 'die', split_axis=0, concat_axis=0, tiled=True)  6.32 us
    dot_general x1, matrix products, shards(): jnp.einsum('snk,sik->sni', guess, coupling, precision=lax.Precision.HIGHE...  4.15 us
    all_to_all x1, starting transfers between devices, shards(): lax.all_to_all(rows_out, 'die', split_axis=0, concat_axis=0, tiled=True)  3.91 us
  transfers between devices with their start and end apart: 4, of which 4 were waited for; matrix products, arithmetic and copies ran while one was open for 25% of the time, Pallas kernels for 0%

commit v1 on v0

v1 whole, which is shorter than its diff:
```python
import functools

import jax
import jax.numpy as jnp
from jax import lax
from jax.experimental import pallas as pl
from jax.experimental.pallas import tpu as pltpu
from jax.sharding import PartitionSpec as P

CAP = 2
META = 128
VMEM = pl.BlockSpec(memory_space=pltpu.VMEM)
SMEM = pl.BlockSpec(memory_space=pltpu.SMEM)
ANY = pl.BlockSpec(memory_space=pl.ANY)
F32 = jnp.float32
I32 = jnp.int32


def divmod_static(value, size):
    if size & (size - 1) == 0:
        return lax.shift_right_logical(value, size.bit_length() - 1), value & (size - 1)
    whole = lax.div(value, size)
    return whole, value - whole * size


def wrap(value, n):
    return jnp.where(value >= n, value - n, value)


def bit_of(index):
    return lax.shift_left(jnp.int32(1), index)


def bits_set(x):
    x = x - (lax.shift_right_logical(x, 1) & 0x55555555)
    x = (x & 0x33333333) + (lax.shift_right_logical(x, 2) & 0x33333333)
    x = (x + lax.shift_right_logical(x, 4)) & 0x0F0F0F0F
    x = x + lax.shift_right_logical(x, 8)
    x = x + lax.shift_right_logical(x, 16)
    return x & 63


def lowest(mask):
    return bits_set((mask & -mask) - 1) & 31


def predict(raw):
    return 3.0 * raw[0] - 3.0 * raw[1] + raw[2]


def slope(raw, guess):
    return 3.0 * guess - (4.0 * raw[0] - raw[1])


def leave_kernel(n, span, here_ref, new_slot_ref, partner_ref, history_ref, meta_ref, *rest):
    outs, (source, count, raw, sems) = rest[: n - 1], rest[n - 1 :]
    blocks = history_ref.shape[0]
    die = here_ref[0]

    def clear(at, carry):
        meta_ref[at] = jnp.where(at > n, -1, 0)
        return carry

    lax.fori_loop(0, 1 + n + n * CAP, clear, 0)
    for at in range(n):
        count[at] = 0
    for at in range(n * CAP):
        source[at] = -1

    def step(at, stays):
        dest, local = divmod_static(new_slot_ref[at], span)
        local = divmod_static(local, blocks)[1]
        leaving = dest != die

        @pl.when(leaving)
        def _():
            rank = count[dest]
            count[dest] = rank + 1
            meta_ref[1 + n + dest * CAP + rank] = local
            turn = wrap(dest - die + n, n) * CAP + rank
            source[turn] = at
            pltpu.make_async_copy(history_ref.at[at], raw.at[turn], sems.at[turn]).start()

        owner, local_read = divmod_static(partner_ref[at], span)
        local_read = divmod_static(local_read, blocks)[1]
        meta_ref[1 + owner] = meta_ref[1 + owner] | bit_of(local_read)
        return stays | jnp.where(leaving, 0, bit_of(local))

    meta_ref[0] = ~lax.fori_loop(0, blocks, step, jnp.int32(0), unroll=True)
    for turn in range(CAP, n * CAP):

        @pl.when(source[turn] >= 0)
        def _(turn=turn):
            pltpu.make_async_copy(history_ref.at[0], raw.at[turn], sems.at[turn]).wait()
            guess = predict(raw.at[turn])
            outs[turn // CAP - 1][turn % CAP, 0] = guess
            outs[turn // CAP - 1][turn % CAP, 1] = slope(raw.at[turn], guess)


def predict_kernel(span, here_ref, new_slot_ref, history_ref, guess_ref, slope_ref):
    blocks = history_ref.shape[0]
    for at in range(blocks):
        dest, local = divmod_static(new_slot_ref[at], span)
        local = divmod_static(local, blocks)[1]

        @pl.when(dest == here_ref[0])
        def _(at=at, local=local):
            raw = history_ref.at[at]
            guess = predict(raw)
            guess_ref[local] = guess
            slope_ref[local] = slope(raw, guess)


def early_kernel(n, depth, here_ref, mine_ref, *rest):
    metas, guess_ref, outs = rest[: n - 1], rest[n - 1], rest[n:]
    die, moved = here_ref[0], mine_ref[0]
    for j in range(1, n):
        want = metas[j - 1][1 + die] & ~moved
        for slot in range(depth):
            outs[j - 1][slot] = guess_ref[lowest(want)]
            want = want & (want - 1)


def late_kernel(n, depth, rcap, here_ref, mine_ref, *rest):
    metas, rest = rest[: n - 1], rest[n - 1 :]
    arrived, rest = rest[: n - 1], rest[n - 1 :]
    old_guess, old_slope, guess_ref, slope_ref = rest[:4]
    outs = rest[4:]
    die, moved = here_ref[0], mine_ref[0]

    def keep(at, carry):
        guess_ref[at] = old_guess[at]
        slope_ref[at] = old_slope[at]
        return carry

    lax.fori_loop(0, guess_ref.shape[0], keep, 0, unroll=8)
    for k in range(1, n):
        for rank in range(CAP):
            place = metas[k - 1][1 + n + die * CAP + rank]

            @pl.when(place >= 0)
            def _(k=k, rank=rank, place=place):
                guess_ref[place] = arrived[k - 1][rank, 0]
                slope_ref[place] = arrived[k - 1][rank, 1]

    for j in range(1, n):
        want = metas[j - 1][1 + die]
        still = want & ~moved
        for slot in range(depth):
            still = still & (still - 1)
        late = want & moved
        for slot in range(depth, rcap):
            @pl.when(still != 0)
            def _(still=still, slot=slot):
                outs[j - 1][slot - depth] = guess_ref[lowest(still)]

            still = still & (still - 1)
        for slot in range(rcap - 1, depth - 1, -1):

            @pl.when(late != 0)
            def _(late=late, slot=slot):
                outs[j - 1][slot - depth] = guess_ref[lowest(late)]

            late = late & (late - 1)


def where_kernel(n, span, rcap, here_ref, partner_ref, mine_ref, *rest):
    metas, index_ref = rest[: n - 1], rest[n - 1]
    blocks = index_ref.shape[0]
    die = here_ref[0]
    table = rest[n]
    for k in range(1, n):
        table[k] = metas[n - k - 1][0]

    def step(at, carry):
        owner, local = divmod_static(partner_ref[at], span)
        local = divmod_static(local, blocks)[1]
        k = wrap(owner - die + n, n)
        want, moved = mine_ref[1 + owner], table[k]
        bit = bit_of(local)
        below = bit - 1
        early = bits_set(want & ~moved & below)
        late = rcap - 1 - bits_set(want & moved & below)
        slot = jnp.where((moved & bit) != 0, late, early)
        index_ref[at] = jnp.where(k == 0, (n - 1) * rcap + local, (k - 1) * rcap + slot)
        return carry

    table[0] = 0
    lax.fori_loop(0, blocks, step, 0)


def local_kernel(
    guess_ref, slope_ref, coupling_ref, cap_ref, gdev_ref, wire_ref, drive_ref, base_ref, inv_ref
):
    nodes = coupling_ref.shape[1]
    rows = lax.broadcasted_iota(I32, (nodes, nodes), 0)
    cols = lax.broadcasted_iota(I32, (nodes, nodes), 1)
    for at in range(guess_ref.shape[0]):
        guess = guess_ref[at]
        coupling = coupling_ref[at]
        cap = cap_ref[at : at + 1, :]
        gdev = gdev_ref[at : at + 1, :]
        wire = wire_ref[at : at + 1, :]
        through = lax.dot_general(
            guess,
            coupling,
            (((1,), (1,)), ((), ())),
            precision=lax.Precision.HIGHEST,
            preferred_element_type=F32,
        )
        diagonal = jnp.sum(jnp.where(rows == cols, coupling, 0.0), axis=0, keepdims=True)
        tnh = jnp.tanh(guess)
        inv_ref[at] = 1.0 / (1.5 * cap + diagonal + gdev * (1.0 - tnh * tnh) + wire)
        base_ref[at] = (
            0.5 * cap * slope_ref[at] + through + gdev * tnh + wire * guess - drive_ref[at]
        )


def residual_kernel(n, depth, rcap, index_ref, base_ref, inv_ref, guess_ref, wire_ref, gain_ref, *rest):
    early, rest = rest[: n - 1], rest[n - 1 :]
    late, rest = rest[: n - 1], rest[n - 1 :]
    residual_ref, share_ref, partial_ref, pool, sems = rest
    blocks = guess_ref.shape[0]
    copies = [pltpu.make_async_copy(guess_ref, pool.at[pl.ds((n - 1) * rcap, blocks)], sems.at[0])]
    for k in range(1, n):
        low = (k - 1) * rcap
        if depth:
            copies.append(
                pltpu.make_async_copy(early[k - 1], pool.at[pl.ds(low, depth)], sems.at[2 * k - 1])
            )
        copies.append(
            pltpu.make_async_copy(
                late[k - 1], pool.at[pl.ds(low + depth, rcap - depth)], sems.at[2 * k]
            )
        )
    for copy in copies:
        copy.start()
    for copy in copies:
        copy.wait()
    share = jnp.zeros(share_ref.shape, F32)
    for at in range(blocks):
        residual = base_ref[at] - wire_ref[at : at + 1, :] * pool[index_ref[at]]
        residual_ref[at] = residual
        scaled = residual * inv_ref[at]
        partial_ref[at] = guess_ref[at] - scaled
        share = share + gain_ref[at : at + 1, :] * scaled
    share_ref[...] = share


def update_kernel(m, nblk, blk_ref, *rest):
    shares, rest = rest[:m], rest[m:]
    inverses, (partial_ref, inv_ref, gain_ref, updated_ref, whole) = rest[:nblk], rest[nblk:]
    height = inverses[0].shape[0]
    for k in range(nblk):
        at = wrap(blk_ref[0] + k, nblk)
        whole[pl.ds(pl.multiple_of(at * height, height), height), :] = inverses[k][...]
    total = shares[0][...]
    for share in shares[1:]:
        total = total + share[...]
    region = jnp.dot(
        total, whole[...], precision=lax.Precision.HIGHEST, preferred_element_type=F32
    )
    for at in range(partial_ref.shape[0]):
        updated_ref[at] = partial_ref[at] + gain_ref[at : at + 1, :] * inv_ref[at] * region


def call(body, outs, ins, in_specs, out_specs, scratch=(), flops=0, limit=16):
    moved = sum(x.size * 4 for x in ins) + sum(x.size * 4 for x in outs)
    return pl.pallas_call(
        body,
        out_shape=outs,
        in_specs=in_specs,
        out_specs=out_specs,
        scratch_shapes=list(scratch),
        compiler_params=pltpu.CompilerParams(vmem_limit_bytes=limit << 20),
        cost_estimate=pl.CostEstimate(flops=flops, bytes_accessed=moved, transcendentals=0),
    )(*ins)


def turn(x, axes, n, k):
    return lax.ppermute(x, axes, [(d, (d + k) % n) for d in range(n)])


def shards(
    history,
    new_slot,
    partner,
    coupling,
    cap_rate,
    device_gain,
    wire_gain,
    region_gain,
    drive,
    region_inverse,
):
    blocks, _, scen, nodes = history.shape
    n = lax.axis_size("die")
    nblk = lax.axis_size("blk")
    ncol = lax.axis_size("sub") * nblk
    rcap = 2 * max(1, blocks // n)
    depth = max(0, rcap - CAP * (n - 1))
    span = ncol * blocks
    die = lax.axis_index("die")
    blk = lax.axis_index("blk")
    column = lax.axis_index("sub") * nblk + blk
    here = jnp.stack([die, (die * ncol + column) * blocks]).astype(I32)
    block = jax.ShapeDtypeStruct((blocks, scen, nodes), F32)

    inverses = [region_inverse[0]]
    inverses += [turn(region_inverse[0], "blk", nblk, nblk - k) for k in range(1, nblk)]

    pair = jax.ShapeDtypeStruct((CAP, 2, scen, nodes), F32)
    meta, *leaving = call(
        functools.partial(leave_kernel, n, span),
        [jax.ShapeDtypeStruct((META,), I32)] + [pair] * (n - 1),
        [here, new_slot, partner, history],
        [SMEM, SMEM, SMEM, ANY],
        [SMEM] + [VMEM] * (n - 1),
        [
            pltpu.SMEM((n * CAP,), I32),
            pltpu.SMEM((n,), I32),
            pltpu.VMEM((n * CAP, 3, scen, nodes), F32),
            pltpu.SemaphoreType.DMA((n * CAP,)),
        ],
    )
    metas = [turn(meta, "die", n, k) for k in range(1, n)]
    arrived = [turn(leaving[k - 1], "die", n, k) for k in range(1, n)]
    old_guess, old_slope = call(
        functools.partial(predict_kernel, span),
        [block, block],
        [here, new_slot, history],
        [SMEM, SMEM, VMEM],
        [VMEM, VMEM],
    )
    if depth:
        packed = call(
            functools.partial(early_kernel, n, depth),
            [jax.ShapeDtypeStruct((depth, scen, nodes), F32)] * (n - 1),
            [here, meta, *metas, old_guess],
            [SMEM] * (n + 1) + [VMEM],
            [VMEM] * (n - 1),
        )
        early = [turn(packed[k - 1], "die", n, n - k) for k in range(1, n)]
    else:
        early = [old_guess] * (n - 1)
    guess, slopes, *packed = call(
        functools.partial(late_kernel, n, depth, rcap),
        [block, block] + [jax.ShapeDtypeStruct((rcap - depth, scen, nodes), F32)] * (n - 1),
        [here, meta, *metas, *arrived, old_guess, old_slope],
        [SMEM] * (n + 1) + [VMEM] * (n + 1),
        [VMEM] * (n + 1),
    )
    late = [turn(packed[k - 1], "die", n, n - k) for k in range(1, n)]
    (index,) = call(
        functools.partial(where_kernel, n, span, rcap),
        [jax.ShapeDtypeStruct((blocks,), I32)],
        [here, partner, meta, *metas],
        [SMEM] * (n + 2),
        [SMEM],
        [pltpu.SMEM((n,), I32)],
    )
    step = 8 if blocks % 8 == 0 else blocks
    wide = pl.BlockSpec((step, scen, nodes), lambda i: (i, 0, 0))
    flat = pl.BlockSpec((step, nodes), lambda i: (i, 0))
    base, inv = pl.pallas_call(
        local_kernel,
        grid=(blocks // step,),
        out_shape=[block, block],
        in_specs=[
            wide,
            wide,
            pl.BlockSpec((step, nodes, nodes), lambda i: (i, 0, 0)),
            flat,
            flat,
            flat,
            wide,
        ],
        out_specs=[wide, wide],
        compiler_params=pltpu.CompilerParams(vmem_limit_bytes=16 << 20),
        cost_estimate=pl.CostEstimate(
            flops=12 * blocks * scen * nodes * nodes, bytes_accessed=5 << 20, transcendentals=0
        ),
    )(guess, slopes, coupling, cap_rate, device_gain, wire_gain, drive)
    residual, share, partial = call(
        functools.partial(residual_kernel, n, depth, rcap),
        [block, jax.ShapeDtypeStruct((scen, nodes), F32), block],
        [index, base, inv, guess, wire_gain, region_gain, *early, *late],
        [SMEM] + [VMEM] * 5 + [ANY] * (2 * n - 2),
        [VMEM] * 3,
        [
            pltpu.VMEM(((n - 1) * rcap + blocks, scen, nodes), F32),
            pltpu.SemaphoreType.DMA((2 * n,)),
        ],
    )
    shares = [share] + [turn(share, ("sub", "blk"), ncol, k) for k in range(1, ncol)]
    (updated,) = call(
        functools.partial(update_kernel, ncol, nblk),
        [block],
        [blk.reshape(1).astype(I32), *shares, *inverses, partial, inv, region_gain],
        [SMEM] + [VMEM] * (ncol + nblk + 3),
        [VMEM],
        [pltpu.VMEM((nodes, nodes), F32)],
        flops=12 * scen * nodes * nodes,
    )
    return (updated, residual)


def solution(mesh):
    every = ("grp", "die", "sub", "blk")
    in_specs = (
        P(every, None, None, None),
        P(every),
        P(every),
        P(every, None, None),
        P(every, None),
        P(every, None),
        P(every, None),
        P(every, None),
        P(every, None, None),
        P(("grp", "die"), "blk", None),
    )
    out_specs = (P(every, None, None), P(every, None, None))
    return jax.shard_map(shards, mesh=mesh, in_specs=in_specs, out_specs=out_specs, check_vma=False)
```

time: 87.3 us -> 55.2 us (0.63)
  the two profiles are of different devices: /device:TPU:0 before, /device:TPU:9 now
where the time goes in v1:
time: 55.2 us; the launch traced here: 54.1 us
  starting transfers between devices  18.9 us (34%)
  waiting for transfers between devices  17.7 us (32%)
  Pallas kernels  13.9 us (25%)
  local copies, waits for them, and re-layouts  2.76 us (5%)
  between operations  0.85 us (2%)
    ppermute x16, starting transfers between devices, turn(): return lax.ppermute(x, axes, [(d, (d + k) % n) for d in range(n)])  18.9 us
    ppermute x16, waiting for transfers between devices, turn(): return lax.ppermute(x, axes, [(d, (d + k) % n) for d in range(n)])  17.7 us
    pallas_call x7, Pallas kernels, call(): pl.pallas_call(body, out_shape=outs, in_specs=in_specs, out_specs=out_spe...  10.2 us
    pallas_call x1, Pallas kernels, shards(): pl.pallas_call(local_kernel, grid=(blocks // step,), out_shape=[block, bl...  3.76 us
    unnamed x24, local copies, waits for them, and re-layouts  2.76 us
  transfers between devices with their start and end apart: 16, of which 4 were waited for; matrix products, arithmetic and copies ran while one was open for 0% of the time, Pallas kernels for 19%

profile of v1, /device:TPU:9, one launch (start us, length us, event | category | flops | bytes accessed | tf_op | source)
XLA Modules:
  0.0 54.1 jit_solution(11691111265271488150)
XLA Ops:
  0.6 0.1 pad_add_fusion.here_ref
  0.7 0.0 copy-start
  0.7 1.4 %copy-done = f32[32,3,32,128]{3,2,1,0:T(8,128)S(1)} copy-done((f32[32,3,32,128]{3,2,1,0:T(8,128)S(1)}, f32[32,3,32,128]{3,2,1,0:T(8,128)}, u32[]{:S(2)}) %copy-start) | copy-done | bytes 1572888
  2.1 0.0 copy-start.9
  2.1 0.7 %copy-done.9 = s32[32]{0:T(128)S(1)} copy-done((s32[32]{0:T(128)S(1)}, s32[32]{0:T(128)}, u32[]{:S(2)}) %copy-start.9) | copy-done | bytes 152
  2.8 0.0 copy-start.10
  2.8 0.7 %copy-done.10 = s32[32]{0:T(128)S(1)} copy-done((s32[32]{0:T(128)S(1)}, s32[32]{0:T(128)}, u32[]{:S(2)}) %copy-start.10) | copy-done | bytes 152
  3.4 0.0 copy-start.1
  3.4 0.0 copy-start.11
  3.4 0.0 copy-start.6
  3.4 0.0 copy-start.3
  3.5 0.0 copy-start.4
  3.5 0.0 copy-start.7
  3.5 0.0 copy-start.8
  3.5 1.8 %shard_map.113 = (s32[128]{0:T(128)S(1)}, f32[2,2,32,128]{3,2,1,0:T(8,128)S(1)}, f32[2,2,32,128]{3,2,1,0:T(8,128)S(1)}, f32[2,2,32,128]{3,2,1,0:T(8,128)S(1)}) custom-call(s32[2]{0:T(128)S(1)} %pad_add_fusion.here_ref, s32[32]{0:T(128)S(1)} %copy-done.9, s32[32]{0:T(128)S(1)} %copy-done.10, f32[32,3,32,128]{3,2,1,0:T(8,128)S(1)} %copy-done), custom_call_target="tpu_custom_call" | custom-call | bytes 1770248 | tf_op jit(solution)/shard_map/pallas_call | solution.py:269
  5.3 1.5 %collective-permute-start.3 = (f32[2,2,32,128]{3,2,1,0:T(8,128)S(1)}, f32[2,2,32,128]{3,2,1,0:T(8,128)S(1)}, u32[]{:S(2)}, u32[]{:S(2)}) collective-permute-start(f32[2,2,32,128]{3,2,1,0:T(8,128)S(1)} %get-tuple-element.22), channel_id=1, source_target_pairs={{0,4},{4,8},{8,12},{12,0},{1,5},{5,9},{9,13},{13,1},{2,6},{6,10},{... | collective-permute-start | bytes 196616 | tf_op jit(solution)/shard_map/ppermute | solution.py:281
  6.8 0.9 %collective-permute-start.4 = (f32[2,2,32,128]{3,2,1,0:T(8,128)S(1)}, f32[2,2,32,128]{3,2,1,0:T(8,128)S(1)}, u32[]{:S(2)}, u32[]{:S(2)}) collective-permute-start(f32[2,2,32,128]{3,2,1,0:T(8,128)S(1)} %get-tuple-element.23), channel_id=1, source_target_pairs={{0,8},{4,12},{8,0},{12,4},{1,9},{5,13},{9,1},{13,5},{2,10},{6,14},... | collective-permute-start | bytes 196616 | tf_op jit(solution)/shard_map/ppermute | solution.py:281
  7.8 1.4 %collective-permute-start.5 = (f32[2,2,32,128]{3,2,1,0:T(8,128)S(1)}, f32[2,2,32,128]{3,2,1,0:T(8,128)S(1)}, u32[]{:S(2)}, u32[]{:S(2)}) collective-permute-start(f32[2,2,32,128]{3,2,1,0:T(8,128)S(1)} %get-tuple-element.24), channel_id=1, source_target_pairs={{0,12},{4,0},{8,4},{12,8},{1,13},{5,1},{9,5},{13,9},{2,14},{6,2},{... | collective-permute-start | bytes 196616 | tf_op jit(solution)/shard_map/ppermute | solution.py:281
  9.2 0.1 collective-permute-start
  9.2 3.2 %collective-permute-start.1 = (s32[128]{0:T(128)S(1)}, s32[128]{0:T(128)S(1)}, u32[]{:S(2)}, u32[]{:S(2)}) collective-permute-start(s32[128]{0:T(128)S(1)} %get-tuple-element.21.mine_ref), channel_id=1, source_target_pairs={{0,8},{4,12},{8,0},{12,4},{1,9},{5,13},{9,1},{13,5},{2,10},{6,14},... | collective-permute-start | bytes 1544 | tf_op jit(solution)/shard_map/ppermute | solution.py:281
  12.5 0.3 collective-permute-done.rest_0_
  12.7 1.8 %collective-permute-start.2 = (s32[128]{0:T(128)S(1)}, s32[128]{0:T(128)S(1)}, u32[]{:S(2)}, u32[]{:S(2)}) collective-permute-start(s32[128]{0:T(128)S(1)} %get-tuple-element.21.mine_ref), channel_id=1, source_target_pairs={{0,12},{4,0},{8,4},{12,8},{1,13},{5,1},{9,5},{13,9},{2,14},{6,2},{... | collective-permute-start | bytes 1544 | tf_op jit(solution)/shard_map/ppermute | solution.py:281
  14.6 0.0 copy-done.1
  14.6 0.9 %shard_map.115 = (f32[32,32,128]{2,1,0:T(8,128)S(1)}, f32[32,32,128]{2,1,0:T(8,128)S(1)}) custom-call(s32[2]{0:T(128)S(1)} %pad_add_fusion.here_ref, s32[32]{0:T(128)S(1)} %copy-done.9, f32[32,3,32,128]{3,2,1,0:T(8,128)S(1)} %copy-done.1), custom_call_target="tpu_custom_call" | custom-call | bytes 2621576 | tf_op jit(solution)/shard_map/pallas_call | solution.py:269
  15.5 0.0 collective-permute-done.1.rest_1_
  15.5 0.0 collective-permute-done.2.rest_2_
  15.5 0.0 collective-permute-done.3.rest_3_
  15.5 0.0 collective-permute-done.4.rest_4_
  15.6 0.0 collective-permute-done.5.rest_5_
  15.6 1.0 %shard_map.116 = (f32[32,32,128]{2,1,0:T(8,128)S(1)}, f32[32,32,128]{2,1,0:T(8,128)S(1)}, f32[6,32,128]{2,1,0:T(8,128)S(1)}, f32[6,32,128]{2,1,0:T(8,128)S(1)}, f32[6,32,128]{2,1,0:T(8,128)S(1)}) custom-call(s32[2]{0:T(128)S(1)} %pad_add_fusion.here_ref, s32[128]{0:T(128)S(1)} %get-tuple-element.21.mine_ref, s32[128]{0:T(128)S(1)} %collective-permute-done.rest_0_, ...), custom_call_target="tpu_custom_call" | custom-call | bytes 2590728 | tf_op jit(solution)/shard_map/pallas_call | solution.py:269
  16.6 0.0 copy-start.5
  16.6 2.1 %collective-permute-start.10 = (f32[6,32,128]{2,1,0:T(8,128)S(1)}, f32[6,32,128]{2,1,0:T(8,128)S(1)}, u32[]{:S(2)}, u32[]{:S(2)}) collective-permute-start(f32[6,32,128]{2,1,0:T(8,128)S(1)} %get-tuple-element.35), channel_id=1, source_target_pairs={{0,8},{4,12},{8,0},{12,4},{1,9},{5,13},{9,1},{13,5},{2,10},{6,14},... | collective-permute-start | bytes 294920 | tf_op jit(solution)/shard_map/ppermute | solution.py:281
  18.7 0.8 %shard_map.118 = (f32[10,32,128]{2,1,0:T(8,128)S(1)}, f32[10,32,128]{2,1,0:T(8,128)S(1)}, f32[10,32,128]{2,1,0:T(8,128)S(1)}) custom-call(s32[2]{0:T(128)S(1)} %pad_add_fusion.here_ref, s32[128]{0:T(128)S(1)} %get-tuple-element.21.mine_ref, s32[128]{0:T(128)S(1)} %collective-permute-done.rest_0_, s32[128]{0:T(128)S(1)} %collective-permute-done.1.rest_1_, ...), custom_call_target="tpu_custom_call" | custom-call | bytes 1017864 | tf_op jit(solution)/shard_map/pallas_call | solution.py:269
  19.4 0.1 collective-permute-start.6
  19.5 1.7 %collective-permute-start.7 = (f32[10,32,128]{2,1,0:T(8,128)S(1)}, f32[10,32,128]{2,1,0:T(8,128)S(1)}, u32[]{:S(2)}, u32[]{:S(2)}) collective-permute-start(f32[10,32,128]{2,1,0:T(8,128)S(1)} %get-tuple-element.32), channel_id=1, source_target_pairs={{0,8},{4,12},{8,0},{12,4},{1,9},{5,13},{9,1},{13,5},{2,10},{6,14},... | collective-permute-start | bytes 491528 | tf_op jit(solution)/shard_map/ppermute | solution.py:281
  21.2 0.9 %collective-permute-start.8 = (f32[10,32,128]{2,1,0:T(8,128)S(1)}, f32[10,32,128]{2,1,0:T(8,128)S(1)}, u32[]{:S(2)}, u32[]{:S(2)}) collective-permute-start(f32[10,32,128]{2,1,0:T(8,128)S(1)} %get-tuple-element.33), channel_id=1, source_target_pairs={{0,4},{4,8},{8,12},{12,0},{1,5},{5,9},{9,13},{13,1},{2,6},{6,10},{... | collective-permute-start | bytes 491528 | tf_op jit(solution)/shard_map/ppermute | solution.py:281
  22.2 0.0 collective-permute-start.11
  22.2 0.0 collective-permute-done.10.rest_4_
  22.2 1.4 %collective-permute-start.9 = (f32[6,32,128]{2,1,0:T(8,128)S(1)}, f32[6,32,128]{2,1,0:T(8,128)S(1)}, u32[]{:S(2)}, u32[]{:S(2)}) collective-permute-start(f32[6,32,128]{2,1,0:T(8,128)S(1)} %get-tuple-element.34), channel_id=1, source_target_pairs={{0,12},{4,0},{8,4},{12,8},{1,13},{5,1},{9,5},{13,9},{2,14},{6,2},{... | collective-permute-start | bytes 294920 | tf_op jit(solution)/shard_map/ppermute | solution.py:281
  23.7 0.0 copy-done.11
  23.7 2.0 %shard_map.114.index_ref = s32[32]{0:T(128)S(1)} custom-call(s32[2]{0:T(128)S(1)} %pad_add_fusion.here_ref, s32[32]{0:T(128)S(1)} %copy-done.11, s32[128]{0:T(128)S(1)} %get-tuple-element.21.mine_ref, s32[128]{0:T(128)S(1)} %collective-permute-done.rest_0_, s32[128]{0:T(128)S(1)} %collective-permute-done.1.rest_1_, s32[128]{0:T(128)S(1)} %collective-permute-done.2.rest_2_), custom_call_target="tpu_custom_call" | custom-call | bytes 2312 | tf_op jit(solution)/shard_map/pallas_call | solution.py:269
  25.7 14.8 %collective-permute-done.11.rest_5_ = f32[6,32,128]{2,1,0:T(8,128)S(1)} collective-permute-done((f32[6,32,128]{2,1,0:T(8,128)S(1)}, f32[6,32,128]{2,1,0:T(8,128)S(1)}, u32[]{:S(2)}, u32[]{:S(2)}) %collective-permute-start.11) | collective-permute-done | bytes 98336 | tf_op jit(solution)/shard_map/ppermute | solution.py:281
  40.5 0.0 copy-done.6
  40.5 1.5 %collective-permute-start.15 = (f32[64,128]{1,0:T(8,128)S(1)}, f32[64,128]{1,0:T(8,128)S(1)}, u32[]{:S(2)}, u32[]{:S(2)}) collective-permute-start(f32[64,128]{1,0:T(8,128)S(1)} %bitcast.4), channel_id=1, source_target_pairs={{0,1},{1,0},{2,3},{3,2},{4,5},{5,4},{6,7},{7,6},{8,9},{9,8},{10,11... | collective-permute-start | bytes 98312 | tf_op jit(solution)/shard_map/ppermute | solution.py:281
  42.0 0.0 copy-done.2
  42.0 0.0 copy-done.3
  42.0 0.0 copy-done.4
  42.0 0.0 copy-done.7
  42.0 0.0 copy-done.8
  42.1 3.8 %shard_map.117 = (f32[32,32,128]{2,1,0:T(8,128)S(1)}, f32[32,32,128]{2,1,0:T(8,128)S(1)}) custom-call(f32[32,32,128]{2,1,0:T(8,128)S(1)} %get-tuple-element.27.guess_ref, f32[32,32,128]{2,1,0:T(8,128)S(1)} %get-tuple-element.28.slope_ref, f32[32,128,128]{2,1,0:T(8,128)S(1)} %copy-done.2, f32[32,128]{1,0:T(8,128)S(1)} %copy-done.7, f32[32,128]{1,0:T(8,128)S(1)} %copy-done.8, ...), custom_call_target="tpu_custom_call" | custom-call | flops 201326592 | bytes 5242880 | tf_op jit(solution)/shard_map/pallas_call | solution.py:365
  45.8 0.0 collective-permute-done.9.rest_3_
  45.8 0.0 collective-permute-done.6.rest_0_
  45.8 0.0 collective-permute-done.7.rest_1_
  45.8 0.0 collective-permute-done.8.rest_2_
  45.9 0.0 copy-done.5
  45.9 2.6 %shard_map.119 = (f32[32,32,128]{2,1,0:T(8,128)}, f32[32,128]{1,0:T(8,128)S(1)}, f32[32,32,128]{2,1,0:T(8,128)S(1)}) custom-call(s32[32]{0:T(128)S(1)} %shard_map.114.index_ref, f32[32,32,128]{2,1,0:T(8,128)S(1)} %get-tuple-element.29.base_ref, f32[32,32,128]{2,1,0:T(8,128)S(1)} %get-tuple-element.30.inv_ref.rest_7_, ...), custom_call_target="tpu_custom_call" | custom-call | bytes 3457152 | tf_op jit(solution)/shard_map/pallas_call | solution.py:269
  48.5 1.2 %collective-permute-start.12 = (f32[32,128]{1,0:T(8,128)S(1)}, f32[32,128]{1,0:T(8,128)S(1)}, u32[]{:S(2)}, u32[]{:S(2)}) collective-permute-start(f32[32,128]{1,0:T(8,128)S(1)} %get-tuple-element.37.rest_0_), channel_id=1, source_target_pairs={{0,1},{1,2},{2,3},{3,0},{4,5},{5,6},{6,7},{7,4},{8,9},{9,10},{10,1... | collective-permute-start | bytes 49160 | tf_op jit(solution)/shard_map/ppermute | solution.py:281
  49.7 0.2 collective-permute-start.13
  49.9 0.6 %collective-permute-start.14 = (f32[32,128]{1,0:T(8,128)S(1)}, f32[32,128]{1,0:T(8,128)S(1)}, u32[]{:S(2)}, u32[]{:S(2)}) collective-permute-start(f32[32,128]{1,0:T(8,128)S(1)} %get-tuple-element.37.rest_0_), channel_id=1, source_target_pairs={{0,3},{1,0},{2,1},{3,2},{4,7},{5,4},{6,5},{7,6},{8,11},{9,8},{10,9... | collective-permute-start | bytes 49160 | tf_op jit(solution)/shard_map/ppermute | solution.py:281
  50.5 0.0 collective-permute-done.15.rest_5_
  50.5 0.0 collective-permute-done.12.rest_1_
  50.6 1.9 %collective-permute-done.13.rest_2_ = f32[32,128]{1,0:T(8,128)S(1)} collective-permute-done((f32[32,128]{1,0:T(8,128)S(1)}, f32[32,128]{1,0:T(8,128)S(1)}, u32[]{:S(2)}, u32[]{:S(2)}) %collective-permute-start.13) | collective-permute-done | bytes 16416 | tf_op jit(solution)/shard_map/ppermute | solution.py:281
  52.4 0.7 %collective-permute-done.14.rest_3_ = f32[32,128]{1,0:T(8,128)S(1)} collective-permute-done((f32[32,128]{1,0:T(8,128)S(1)}, f32[32,128]{1,0:T(8,128)S(1)}, u32[]{:S(2)}, u32[]{:S(2)}) %collective-permute-start.14) | collective-permute-done | bytes 16416 | tf_op jit(solution)/shard_map/ppermute | solution.py:281
  53.1 1.0 %shard_map.120 = f32[32,32,128]{2,1,0:T(8,128)} custom-call(s32[1]{0:T(128)} %bitcast.blk_ref, f32[32,128]{1,0:T(8,128)S(1)} %get-tuple-element.37.rest_0_, f32[32,128]{1,0:T(8,128)S(1)} %collective-permute-done.12.rest_1_, f32[32,128]{1,0:T(8,128)S(1)} %collective-permute-done.13.rest_2_, f32[32,128]{1,0:T(8,128)S(1)} %collective-permute-done.14.rest_3_, ...), custom_call_target="tpu_custom_call" | custom-call | flops 6291456 | bytes 1720324 | tf_op jit(solution)/shard_map/pallas_call | solution.py:269
  (1 shorter events, 0.0 us)
Async XLA Ops:
  0.7 1.4 %copy-start = (f32[32,3,32,128]{3,2,1,0:T(8,128)S(1)}, f32[32,3,32,128]{3,2,1,0:T(8,128)}, u32[]{:S(2)}) copy-start(f32[32,3,32,128]{3,2,1,0:T(8,128)} %history_ref.3) | copy-start | bytes 4718596
  2.1 0.7 %copy-start.9 = (s32[32]{0:T(128)S(1)}, s32[32]{0:T(128)}, u32[]{:S(2)}) copy-start(s32[32]{0:T(128)} %new_slot_ref.3) | copy-start | bytes 388
  2.8 0.7 %copy-start.10 = (s32[32]{0:T(128)S(1)}, s32[32]{0:T(128)}, u32[]{:S(2)}) copy-start(s32[32]{0:T(128)} %partner_ref.3) | copy-start | bytes 388
  3.4 11.1 %copy-start.1 = (f32[32,3,32,128]{3,2,1,0:T(8,128)S(1)}, f32[32,3,32,128]{3,2,1,0:T(8,128)}, u32[]{:S(2)}) copy-start(f32[32,3,32,128]{3,2,1,0:T(8,128)} %history_ref.3) | copy-start | bytes 4718596
  3.4 20.2 %copy-start.11 = (s32[32]{0:T(128)S(1)}, s32[32]{0:T(128)}, u32[]{:S(2)}) copy-start(s32[32]{0:T(128)} %partner_ref.3) | copy-start | bytes 388
  3.4 37.0 %copy-start.6 = (f32[1,64,128]{2,1,0:T(8,128)S(1)}, f32[1,64,128]{2,1,0:T(8,128)}, u32[]{:S(2)}) copy-start(f32[1,64,128]{2,1,0:T(8,128)} %param.19) | copy-start | bytes 98308
  3.4 38.6 %copy-start.2 = (f32[32,128,128]{2,1,0:T(8,128)S(1)}, f32[32,128,128]{2,1,0:T(8,128)}, u32[]{:S(2)}) copy-start(f32[32,128,128]{2,1,0:T(8,128)} %coupling_ref.1) | copy-start | bytes 6291460
  3.4 38.6 %copy-start.3 = (f32[32,32,128]{2,1,0:T(8,128)S(1)}, f32[32,32,128]{2,1,0:T(8,128)}, u32[]{:S(2)}) copy-start(f32[32,32,128]{2,1,0:T(8,128)} %drive_ref.1) | copy-start | bytes 1572868
  3.5 38.6 %copy-start.4 = (f32[32,128]{1,0:T(8,128)S(1)}, f32[32,128]{1,0:T(8,128)}, u32[]{:S(2)}) copy-start(f32[32,128]{1,0:T(8,128)} %wire_ref.3) | copy-start | bytes 49156
  3.5 38.6 %copy-start.7 = (f32[32,128]{1,0:T(8,128)S(1)}, f32[32,128]{1,0:T(8,128)}, u32[]{:S(2)}) copy-start(f32[32,128]{1,0:T(8,128)} %cap_ref.1) | copy-start | bytes 49156
  3.5 38.6 %copy-start.8 = (f32[32,128]{1,0:T(8,128)S(1)}, f32[32,128]{1,0:T(8,128)}, u32[]{:S(2)}) copy-start(f32[32,128]{1,0:T(8,128)} %gdev_ref.1) | copy-start | bytes 49156
  5.3 10.2 %collective-permute-start.3 = (f32[2,2,32,128]{3,2,1,0:T(8,128)S(1)}, f32[2,2,32,128]{3,2,1,0:T(8,128)S(1)}, u32[]{:S(2)}, u32[]{:S(2)}) collective-permute-start(f32[2,2,32,128]{3,2,1,0:T(8,128)S(1)} %get-tuple-element.22), channel_id=1, source_target_pairs={{0,4},{4,8},{8,12},{12,0},{1,5},{5,9},{9,13},{13,1},{2,6},{6,10},{... | collective-permute-start | bytes 196616 | tf_op jit(solution)/shard_map/ppermute | solution.py:281
  6.8 8.7 %collective-permute-start.4 = (f32[2,2,32,128]{3,2,1,0:T(8,128)S(1)}, f32[2,2,32,128]{3,2,1,0:T(8,128)S(1)}, u32[]{:S(2)}, u32[]{:S(2)}) collective-permute-start(f32[2,2,32,128]{3,2,1,0:T(8,128)S(1)} %get-tuple-element.23), channel_id=1, source_target_pairs={{0,8},{4,12},{8,0},{12,4},{1,9},{5,13},{9,1},{13,5},{2,10},{6,14},... | collective-permute-start | bytes 196616 | tf_op jit(solution)/shard_map/ppermute | solution.py:281
  7.8 7.8 %collective-permute-start.5 = (f32[2,2,32,128]{3,2,1,0:T(8,128)S(1)}, f32[2,2,32,128]{3,2,1,0:T(8,128)S(1)}, u32[]{:S(2)}, u32[]{:S(2)}) collective-permute-start(f32[2,2,32,128]{3,2,1,0:T(8,128)S(1)} %get-tuple-element.24), channel_id=1, source_target_pairs={{0,12},{4,0},{8,4},{12,8},{1,13},{5,1},{9,5},{13,9},{2,14},{6,2},{... | collective-permute-start | bytes 196616 | tf_op jit(solution)/shard_map/ppermute | solution.py:281
  9.2 3.6 %collective-permute-start = (s32[128]{0:T(128)S(1)}, s32[128]{0:T(128)S(1)}, u32[]{:S(2)}, u32[]{:S(2)}) collective-permute-start(s32[128]{0:T(128)S(1)} %get-tuple-element.21.mine_ref), channel_id=1, source_target_pairs={{0,4},{4,8},{8,12},{12,0},{1,5},{5,9},{9,13},{13,1},{2,6},{6,10},{... | collective-permute-start | bytes 1544 | tf_op jit(solution)/shard_map/ppermute | solution.py:281
  9.2 6.3 %collective-permute-start.1 = (s32[128]{0:T(128)S(1)}, s32[128]{0:T(128)S(1)}, u32[]{:S(2)}, u32[]{:S(2)}) collective-permute-start(s32[128]{0:T(128)S(1)} %get-tuple-element.21.mine_ref), channel_id=1, source_target_pairs={{0,8},{4,12},{8,0},{12,4},{1,9},{5,13},{9,1},{13,5},{2,10},{6,14},... | collective-permute-start | bytes 1544 | tf_op jit(solution)/shard_map/ppermute | solution.py:281
  12.7 2.8 %collective-permute-start.2 = (s32[128]{0:T(128)S(1)}, s32[128]{0:T(128)S(1)}, u32[]{:S(2)}, u32[]{:S(2)}) collective-permute-start(s32[128]{0:T(128)S(1)} %get-tuple-element.21.mine_ref), channel_id=1, source_target_pairs={{0,12},{4,0},{8,4},{12,8},{1,13},{5,1},{9,5},{13,9},{2,14},{6,2},{... | collective-permute-start | bytes 1544 | tf_op jit(solution)/shard_map/ppermute | solution.py:281
  16.6 29.3 %copy-start.5 = (f32[32,128]{1,0:T(8,128)S(1)}, f32[32,128]{1,0:T(8,128)}, u32[]{:S(2)}) copy-start(f32[32,128]{1,0:T(8,128)} %rest_8_.1) | copy-start | bytes 49156
  16.6 5.7 %collective-permute-start.10 = (f32[6,32,128]{2,1,0:T(8,128)S(1)}, f32[6,32,128]{2,1,0:T(8,128)S(1)}, u32[]{:S(2)}, u32[]{:S(2)}) collective-permute-start(f32[6,32,128]{2,1,0:T(8,128)S(1)} %get-tuple-element.35), channel_id=1, source_target_pairs={{0,8},{4,12},{8,0},{12,4},{1,9},{5,13},{9,1},{13,5},{2,10},{6,14},... | collective-permute-start | bytes 294920 | tf_op jit(solution)/shard_map/ppermute | solution.py:281
  19.4 26.4 %collective-permute-start.6 = (f32[10,32,128]{2,1,0:T(8,128)S(1)}, f32[10,32,128]{2,1,0:T(8,128)S(1)}, u32[]{:S(2)}, u32[]{:S(2)}) collective-permute-start(f32[10,32,128]{2,1,0:T(8,128)S(1)} %get-tuple-element.31), channel_id=1, source_target_pairs={{0,12},{4,0},{8,4},{12,8},{1,13},{5,1},{9,5},{13,9},{2,14},{6,2},{... | collective-permute-start | bytes 491528 | tf_op jit(solution)/shard_map/ppermute | solution.py:281
  19.5 26.3 %collective-permute-start.7 = (f32[10,32,128]{2,1,0:T(8,128)S(1)}, f32[10,32,128]{2,1,0:T(8,128)S(1)}, u32[]{:S(2)}, u32[]{:S(2)}) collective-permute-start(f32[10,32,128]{2,1,0:T(8,128)S(1)} %get-tuple-element.32), channel_id=1, source_target_pairs={{0,8},{4,12},{8,0},{12,4},{1,9},{5,13},{9,1},{13,5},{2,10},{6,14},... | collective-permute-start | bytes 491528 | tf_op jit(solution)/shard_map/ppermute | solution.py:281
  21.2 24.6 %collective-permute-start.8 = (f32[10,32,128]{2,1,0:T(8,128)S(1)}, f32[10,32,128]{2,1,0:T(8,128)S(1)}, u32[]{:S(2)}, u32[]{:S(2)}) collective-permute-start(f32[10,32,128]{2,1,0:T(8,128)S(1)} %get-tuple-element.33), channel_id=1, source_target_pairs={{0,4},{4,8},{8,12},{12,0},{1,5},{5,9},{9,13},{13,1},{2,6},{6,10},{... | collective-permute-start | bytes 491528 | tf_op jit(solution)/shard_map/ppermute | solution.py:281
  22.2 18.3 %collective-permute-start.11 = (f32[6,32,128]{2,1,0:T(8,128)S(1)}, f32[6,32,128]{2,1,0:T(8,128)S(1)}, u32[]{:S(2)}, u32[]{:S(2)}) collective-permute-start(f32[6,32,128]{2,1,0:T(8,128)S(1)} %get-tuple-element.36), channel_id=1, source_target_pairs={{0,4},{4,8},{8,12},{12,0},{1,5},{5,9},{9,13},{13,1},{2,6},{6,10},{... | collective-permute-start | bytes 294920 | tf_op jit(solution)/shard_map/ppermute | solution.py:281
  22.2 23.6 %collective-permute-start.9 = (f32[6,32,128]{2,1,0:T(8,128)S(1)}, f32[6,32,128]{2,1,0:T(8,128)S(1)}, u32[]{:S(2)}, u32[]{:S(2)}) collective-permute-start(f32[6,32,128]{2,1,0:T(8,128)S(1)} %get-tuple-element.34), channel_id=1, source_target_pairs={{0,12},{4,0},{8,4},{12,8},{1,13},{5,1},{9,5},{13,9},{2,14},{6,2},{... | collective-permute-start | bytes 294920 | tf_op jit(solution)/shard_map/ppermute | solution.py:281
  40.5 10.1 %collective-permute-start.15 = (f32[64,128]{1,0:T(8,128)S(1)}, f32[64,128]{1,0:T(8,128)S(1)}, u32[]{:S(2)}, u32[]{:S(2)}) collective-permute-start(f32[64,128]{1,0:T(8,128)S(1)} %bitcast.4), channel_id=1, source_target_pairs={{0,1},{1,0},{2,3},{3,2},{4,5},{5,4},{6,7},{7,6},{8,9},{9,8},{10,11... | collective-permute-start | bytes 98312 | tf_op jit(solution)/shard_map/ppermute | solution.py:281
  48.5 2.1 %collective-permute-start.12 = (f32[32,128]{1,0:T(8,128)S(1)}, f32[32,128]{1,0:T(8,128)S(1)}, u32[]{:S(2)}, u32[]{:S(2)}) collective-permute-start(f32[32,128]{1,0:T(8,128)S(1)} %get-tuple-element.37.rest_0_), channel_id=1, source_target_pairs={{0,1},{1,2},{2,3},{3,0},{4,5},{5,6},{6,7},{7,4},{8,9},{9,10},{10,1... | collective-permute-start | bytes 49160 | tf_op jit(solution)/shard_map/ppermute | solution.py:281
  49.7 2.8 %collective-permute-start.13 = (f32[32,128]{1,0:T(8,128)S(1)}, f32[32,128]{1,0:T(8,128)S(1)}, u32[]{:S(2)}, u32[]{:S(2)}) collective-permute-start(f32[32,128]{1,0:T(8,128)S(1)} %get-tuple-element.37.rest_0_), channel_id=1, source_target_pairs={{0,2},{1,3},{2,0},{3,1},{4,6},{5,7},{6,4},{7,5},{8,10},{9,11},{10,... | collective-permute-start | bytes 49160 | tf_op jit(solution)/shard_map/ppermute | solution.py:281
  49.9 3.2 %collective-permute-start.14 = (f32[32,128]{1,0:T(8,128)S(1)}, f32[32,128]{1,0:T(8,128)S(1)}, u32[]{:S(2)}, u32[]{:S(2)}) collective-permute-start(f32[32,128]{1,0:T(8,128)S(1)} %get-tuple-element.37.rest_0_), channel_id=1, source_target_pairs={{0,3},{1,0},{2,1},{3,2},{4,7},{5,4},{6,5},{7,6},{8,11},{9,8},{10,9... | collective-permute-start | bytes 49160 | tf_op jit(solution)/shard_map/ppermute | solution.py:281

commit v2 on v1

v2 whole, which is shorter than its diff:
```python
import functools

import jax
import jax.numpy as jnp
from jax import lax
from jax.experimental import pallas as pl
from jax.experimental.pallas import tpu as pltpu
from jax.sharding import PartitionSpec as P

CAP = 2
META = 128
AHEAD = 4
EARLY = 64 << 20
LATE = 64 << 20
VMEM = pl.BlockSpec(memory_space=pltpu.VMEM)
SMEM = pl.BlockSpec(memory_space=pltpu.SMEM)
ANY = pl.BlockSpec(memory_space=pl.ANY)
HBM = pl.BlockSpec(memory_space=pltpu.HBM)
F32 = jnp.float32
I32 = jnp.int32


def divmod_static(value, size):
    if size & (size - 1) == 0:
        return lax.shift_right_logical(value, size.bit_length() - 1), value & (size - 1)
    whole = lax.div(value, size)
    return whole, value - whole * size


def bit_of(index):
    return lax.shift_left(jnp.int32(1), index)


def bits_set(x):
    x = x - (lax.shift_right_logical(x, 1) & 0x55555555)
    x = (x & 0x33333333) + (lax.shift_right_logical(x, 2) & 0x33333333)
    x = (x + lax.shift_right_logical(x, 4)) & 0x0F0F0F0F
    x = x + lax.shift_right_logical(x, 8)
    x = x + lax.shift_right_logical(x, 16)
    return x & 63


def lowest(mask):
    return bits_set((mask & -mask) - 1) & 31


def predict(raw):
    return 3.0 * raw[0] - 3.0 * raw[1] + raw[2]


def slope(raw, guess):
    return 3.0 * guess - (4.0 * raw[0] - raw[1])


def meta_kernel(n, span, here_ref, new_slot_ref, partner_ref, meta_ref, slots, reads, count, sems):
    blocks = new_slot_ref.shape[0]
    die = here_ref[0]
    copies = [
        pltpu.make_async_copy(new_slot_ref, slots, sems.at[0]),
        pltpu.make_async_copy(partner_ref, reads, sems.at[1]),
    ]
    for copy in copies:
        copy.start()
    for at in range(1 + n + n * CAP):
        meta_ref[at] = -1 if at > n else 0
    for at in range(n):
        count[at] = 0
    for copy in copies:
        copy.wait()

    stays = jnp.int32(0)
    for at in range(blocks):
        dest, local = divmod_static(slots[at], span)
        bit = bit_of(divmod_static(local, blocks)[1])
        leaving = dest != die

        @pl.when(leaving)
        def _(dest=dest, local=local):
            rank = count[dest]
            count[dest] = rank + 1
            meta_ref[1 + n + dest * CAP + rank] = divmod_static(local, blocks)[1]

        stays = stays | jnp.where(leaving, 0, bit)
        owner, local = divmod_static(reads[at], span)
        owner = 1 + owner
        meta_ref[owner] = meta_ref[owner] | bit_of(divmod_static(local, blocks)[1])
    meta_ref[0] = ~stays


def predict_kernel(_, history_ref, guess_ref, slope_ref):
    for at in range(history_ref.shape[0]):
        raw = history_ref.at[at]
        guess = predict(raw)
        guess_ref[at] = guess
        slope_ref[at] = slope(raw, guess)


def place_kernel(n, ahead, span, here_ref, mine_ref, new_slot_ref, old_guess, old_slope, *rest):
    metas, (guess_ref, slope_ref, *rest) = rest[: n - 1], rest[n - 1 :]
    outs, (source, count) = rest[: n - 1], rest[n - 1 :]
    blocks = old_guess.shape[0]
    die = here_ref[0]
    for at in range(n):
        count[at] = 0
    for at in range(n * CAP):
        source[at] = 0
    for at in range(blocks):
        dest, local = divmod_static(new_slot_ref[at], span)
        local = divmod_static(local, blocks)[1]

        @pl.when(dest == die)
        def _(at=at, local=local):
            guess_ref[local] = old_guess[at]
            slope_ref[local] = old_slope[at]

        @pl.when(dest != die)
        def _(at=at, dest=dest):
            rank = count[dest]
            count[dest] = rank + 1
            source[(dest ^ die) * CAP + rank] = at

    for turn in range(CAP, n * CAP):
        outs[turn // CAP - 1][turn % CAP] = old_guess[source[turn]]
        outs[turn // CAP - 1][CAP + turn % CAP] = old_slope[source[turn]]
    for meta, out, some in zip(metas, outs, ahead):
        want = meta[1 + die] & ~mine_ref[0]
        for slot in range(some):
            out[2 * CAP + slot] = guess_ref[lowest(want)]
            want = want & (want - 1)


def early_kernel(n, depth, ahead, here_ref, mine_ref, *rest):
    m = n - 2
    metas, guess_ref, outs = rest[:m], rest[m], rest[m + 1 :]
    die, moved = here_ref[0], mine_ref[0]
    for meta, out in zip(metas, outs):
        want = meta[1 + die] & ~moved
        for slot in range(ahead):
            want = want & (want - 1)
        for slot in range(depth - ahead):
            out[slot] = guess_ref[lowest(want)]
            want = want & (want - 1)


def late_kernel(n, depth, rcap, here_ref, mine_ref, *rest):
    metas, rest = rest[: n - 1], rest[n - 1 :]
    arrived, rest = rest[: n - 1], rest[n - 1 :]
    old_guess, old_slope, _, guess_ref, slope_ref = rest[:5]
    outs = rest[5:]
    die, moved = here_ref[0], mine_ref[0]

    for at in range(guess_ref.shape[0]):
        guess_ref[at] = old_guess[at]
        slope_ref[at] = old_slope[at]
    for k in range(1, n):
        for rank in range(CAP):
            place = metas[k - 1][1 + n + die * CAP + rank]

            @pl.when(place >= 0)
            def _(k=k, rank=rank, place=place):
                guess_ref[place] = arrived[k - 1][rank]
                slope_ref[place] = arrived[k - 1][CAP + rank]

    for meta, out in zip(metas, outs):
        want = meta[1 + die]
        still = want & ~moved
        late = want & moved
        for slot in range(depth):
            still = still & (still - 1)
        for slot in range(rcap - depth):

            @pl.when(still != 0)
            def _(out=out, still=still, slot=slot):
                out[slot] = guess_ref[lowest(still)]

            still = still & (still - 1)
        for slot in range(rcap - depth - 1, -1, -1):

            @pl.when(late != 0)
            def _(out=out, late=late, slot=slot):
                out[slot] = guess_ref[lowest(late)]

            late = late & (late - 1)


def where_kernel(n, span, depth, rcap, here_ref, partner_ref, mine_ref, _, *rest):
    metas, (index_ref, moves) = rest[: n - 1], rest[n - 1 :]
    blocks = index_ref.shape[0]
    die = here_ref[0]
    own = (n - 1) * depth
    moves[0] = 0
    for k in range(1, n):
        moves[k] = metas[k - 1][0]

    def step(at, carry):
        owner, local = divmod_static(partner_ref[at], span)
        local = divmod_static(local, blocks)[1]
        k = owner ^ die
        want, moved = mine_ref[1 + owner], moves[k]
        bit = bit_of(local)
        below = bit - 1
        stays = bits_set(want & ~moved & below)
        late = rcap - 1 - bits_set(want & moved & below)
        slot = jnp.where((moved & bit) != 0, late, stays)
        early = (k - 1) * depth + slot
        late = own + blocks + (k - 1) * (rcap - depth) + slot - depth
        index_ref[at] = jnp.where(k == 0, own + local, jnp.where(slot < depth, early, late))
        return carry

    lax.fori_loop(0, blocks, step, 0)


def local_kernel(
    guess_ref, slope_ref, coupling_ref, cap_ref, gdev_ref, wire_ref, gain_ref, drive_ref, base_ref, inv_ref, scale_ref
):
    nodes = coupling_ref.shape[1]
    rows = lax.broadcasted_iota(I32, (nodes, nodes), 0)
    cols = lax.broadcasted_iota(I32, (nodes, nodes), 1)
    for at in range(guess_ref.shape[0]):
        guess = guess_ref[at]
        coupling = coupling_ref[at]
        cap = cap_ref[at : at + 1, :]
        gdev = gdev_ref[at : at + 1, :]
        wire = wire_ref[at : at + 1, :]
        through = lax.dot_general(
            guess,
            coupling,
            (((1,), (1,)), ((), ())),
            precision=lax.Precision.HIGHEST,
            preferred_element_type=F32,
        )
        diagonal = jnp.sum(jnp.where(rows == cols, coupling, 0.0), axis=0, keepdims=True)
        tnh = jnp.tanh(guess)
        inv = 1.0 / (1.5 * cap + diagonal + gdev * (1.0 - tnh * tnh) + wire)
        inv_ref[at] = inv
        scale_ref[at] = gain_ref[at : at + 1, :] * inv
        base_ref[at] = (
            0.5 * cap * slope_ref[at] + through + gdev * tnh + wire * guess - drive_ref[at]
        )


def gather_kernel(depth, ahead, index_ref, *rest):
    m = len(ahead)
    first, rest = rest[:m], rest[m:]
    early, (guess_ref, _, near_ref, pool) = rest[: max(m - 1, 0)], rest[max(m - 1, 0) :]
    blocks = guess_ref.shape[0]
    for k in range(m):
        for slot in range(depth):
            block = first[k][2 * CAP + slot] if slot < ahead[k] else early[k - 1][slot - ahead[k]]
            pool[k * depth + slot] = block
    for at in range(blocks):
        pool[m * depth + at] = guess_ref[at]
    for at in range(blocks):
        near_ref[at] = pool[jnp.minimum(index_ref[at], m * depth + blocks - 1)]


def residual_kernel(n, nblk, head, index_ref, blk_ref, near_ref, base_ref, inv_ref, scale_ref, guess_ref, wire_ref, *rest):
    late, rest = rest[: n - 1], rest[n - 1 :]
    inverses, (residual_ref, share_ref, partial_ref, whole_ref, pool) = rest[:nblk], rest[nblk:]
    start = 0
    for ref in late:
        for slot in range(ref.shape[0]):
            pool[start + slot] = ref[slot]
        start += ref.shape[0]
    height = inverses[0].shape[0]
    for k in range(nblk):
        whole_ref[pl.ds(pl.multiple_of((blk_ref[0] ^ k) * height, height), height), :] = inverses[k][...]
    share = jnp.zeros(share_ref.shape, F32)
    for at in range(guess_ref.shape[0]):
        index = index_ref[at]
        other = jnp.where(index >= head, pool[jnp.maximum(index - head, 0)], near_ref[at])
        residual = base_ref[at] - wire_ref[at : at + 1, :] * other
        residual_ref[at] = residual
        partial_ref[at] = guess_ref[at] - residual * inv_ref[at]
        share = share + scale_ref[at] * residual
    share_ref[...] = share


def store_kernel(value_ref, out_ref, sem):
    copy = pltpu.make_async_copy(value_ref, out_ref, sem)
    copy.start()
    copy.wait()


def update_kernel(m, parts, *rest):
    shares, (whole_ref, partial_ref, scale_ref, updated_ref, held, sems) = rest[:m], rest[m:]
    total = shares[0][...]
    for share in shares[1:]:
        total = total + share[...]
    region = jnp.dot(
        total, whole_ref[...], precision=lax.Precision.HIGHEST, preferred_element_type=F32
    )
    step = partial_ref.shape[0] // parts
    copies = []
    for part in range(parts):
        for at in range(part * step, (part + 1) * step):
            held[at] = partial_ref[at] + scale_ref[at] * region
        span = pl.ds(part * step, step)
        copies.append(pltpu.make_async_copy(held.at[span], updated_ref.at[span], sems.at[part]))
        copies[-1].start()
    for copy in copies:
        copy.wait()


def call(body, outs, ins, in_specs, out_specs, scratch=(), flops=0, moved=0, limit=8):
    return pl.pallas_call(
        body,
        out_shape=outs,
        in_specs=in_specs,
        out_specs=out_specs,
        scratch_shapes=list(scratch),
        compiler_params=pltpu.CompilerParams(vmem_limit_bytes=limit << 20),
        cost_estimate=pl.CostEstimate(flops=flops, bytes_accessed=moved, transcendentals=0),
    )(*ins)


def swap(x, axes, n, k):
    return lax.ppermute(x, axes, [(d, d ^ k) for d in range(n)])


def shards(
    history,
    new_slot,
    partner,
    coupling,
    cap_rate,
    device_gain,
    wire_gain,
    region_gain,
    drive,
    region_inverse,
):
    blocks, _, scen, nodes = history.shape
    n = lax.axis_size("die")
    nblk = lax.axis_size("blk")
    ncol = lax.axis_size("sub") * nblk
    for size in (n, nblk, ncol):
        assert size & (size - 1) == 0
    assert blocks <= 32
    rcap = 2 * max(1, blocks // n)
    depth = max(0, rcap - CAP * (n - 1))
    some = min(AHEAD, depth)
    ahead = [depth] + [some] * (n - 2)
    span = ncol * blocks
    die = lax.axis_index("die").astype(I32).reshape(1)
    blk = lax.axis_index("blk").astype(I32).reshape(1)
    def tiles(count):
        return jax.ShapeDtypeStruct((count, scen, nodes), F32)

    block = tiles(blocks)
    square = jax.ShapeDtypeStruct((nodes, nodes), F32)

    (meta,) = call(
        functools.partial(meta_kernel, n, span),
        [jax.ShapeDtypeStruct((META,), I32)],
        [
            die,
            pltpu.with_memory_space_constraint(new_slot, pltpu.HBM),
            pltpu.with_memory_space_constraint(partner, pltpu.HBM),
        ],
        [SMEM, HBM, HBM],
        [SMEM],
        [
            pltpu.SMEM((blocks,), I32),
            pltpu.SMEM((blocks,), I32),
            pltpu.SMEM((n,), I32),
            pltpu.SemaphoreType.DMA((2,)),
        ],
    )
    metas = [swap(meta, "die", n, k) for k in range(1, n)]
    step = 8 if blocks % 8 == 0 else blocks
    wide = pl.BlockSpec((step, scen, nodes), lambda i: (i, 0, 0))
    flat = pl.BlockSpec((step, nodes), lambda i: (i, 0))
    raw_guess, raw_slope = pl.pallas_call(
        predict_kernel,
        grid=(blocks // step,),
        out_shape=[block, block],
        in_specs=[ANY, pl.BlockSpec((step, 3, scen, nodes), lambda i: (i, 0, 0, 0))],
        out_specs=[wide, wide],
        compiler_params=pltpu.CompilerParams(vmem_limit_bytes=8 << 20),
        cost_estimate=pl.CostEstimate(flops=0, bytes_accessed=0, transcendentals=0),
    )(meta, pltpu.with_memory_space_constraint(history, pltpu.HBM))
    old_guess, old_slope, *leaving = call(
        functools.partial(place_kernel, n, ahead, span),
        [block, block] + [tiles(2 * CAP + some) for some in ahead],
        [die, meta, new_slot, raw_guess, raw_slope, *metas],
        [SMEM] * 3 + [VMEM] * 2 + [SMEM] * (n - 1),
        [VMEM] * (n + 1),
        [pltpu.SMEM((n * CAP,), I32), pltpu.SMEM((n,), I32)],
    )
    arrived = [swap(leaving[k - 1], "die", n, k) for k in range(1, n)]
    early, order = [], old_guess
    if depth:
        packed = call(
            functools.partial(early_kernel, n, depth, some),
            [tiles(depth - some)] * (n - 2),
            [die, meta, *metas[1:], old_guess],
            [SMEM] * n + [VMEM],
            [VMEM] * (n - 2),
            moved=EARLY,
        )
        order = packed[0]
        early = [swap(packed[k - 2], "die", n, k) for k in range(2, n)]
    guess, slopes, *packed = call(
        functools.partial(late_kernel, n, depth, rcap),
        [block, block] + [tiles(rcap - depth)] * (n - 1),
        [die, meta, *metas, *arrived, old_guess, old_slope, order],
        [SMEM] * (n + 1) + [VMEM] * (n + 1) + [ANY],
        [VMEM] * (n + 1),
        moved=LATE,
    )
    late = [swap(packed[k - 1], "die", n, k) for k in range(1, n)]
    (index,) = call(
        functools.partial(where_kernel, n, span, depth, rcap),
        [jax.ShapeDtypeStruct((blocks,), I32)],
        [die, partner, meta, guess, *metas],
        [SMEM] * 3 + [ANY] + [SMEM] * (n - 1),
        [SMEM],
        [pltpu.SMEM((n,), I32)],
    )
    base, inv, scale = pl.pallas_call(
        local_kernel,
        grid=(blocks // step,),
        out_shape=[block, block, block],
        in_specs=[
            wide,
            wide,
            pl.BlockSpec((step, nodes, nodes), lambda i: (i, 0, 0)),
            flat,
            flat,
            flat,
            flat,
            wide,
        ],
        out_specs=[wide, wide, wide],
        compiler_params=pltpu.CompilerParams(vmem_limit_bytes=8 << 20),
        cost_estimate=pl.CostEstimate(
            flops=0, bytes_accessed=0, transcendentals=0
        ),
    )(guess, slopes, coupling, cap_rate, device_gain, wire_gain, region_gain, drive)
    head = (n - 1) * depth + blocks
    (near,) = call(
        functools.partial(gather_kernel, depth, ahead if depth else []),
        [block],
        [index, *(arrived + early if depth else []), guess, base],
        [SMEM] + [VMEM] * (2 * n - 2 if depth else 1) + [ANY],
        [VMEM],
        [pltpu.VMEM((head, scen, nodes), F32)],
    )
    inverses = [region_inverse[0]]
    inverses += [swap(region_inverse[0], "blk", nblk, k) for k in range(1, nblk)]
    residual, share, partial, whole = call(
        functools.partial(residual_kernel, n, nblk, head),
        [block, jax.ShapeDtypeStruct((scen, nodes), F32), block, square],
        [index, blk, near, base, inv, scale, guess, wire_gain, *late, *inverses],
        [SMEM] * 2 + [VMEM] * (6 + n - 1 + nblk),
        [VMEM] * 4,
        [pltpu.VMEM((sum(x.shape[0] for x in late), scen, nodes), F32)],
    )
    (stored,) = call(
        store_kernel, [block], [residual], [ANY], [HBM], [pltpu.SemaphoreType.DMA]
    )
    shares = [share] + [swap(share, ("sub", "blk"), ncol, k) for k in range(1, ncol)]
    parts = 4 if blocks % 4 == 0 else 1
    (updated,) = call(
        functools.partial(update_kernel, ncol, parts),
        [block],
        [*shares, whole, partial, scale],
        [VMEM] * (ncol + 3),
        [HBM],
        [pltpu.VMEM((blocks, scen, nodes), F32), pltpu.SemaphoreType.DMA((parts,))],
        flops=12 * scen * nodes * nodes,
    )
    return (updated, stored)


def solution(mesh):
    every = ("grp", "die", "sub", "blk")
    in_specs = (
        P(every, None, None, None),
        P(every),
        P(every),
        P(every, None, None),
        P(every, None),
        P(every, None),
        P(every, None),
        P(every, None),
        P(every, None, None),
        P(("grp", "die"), "blk", None),
    )
    out_specs = (P(every, None, None), P(every, None, None))
    return jax.shard_map(shards, mesh=mesh, in_specs=in_specs, out_specs=out_specs, check_vma=False)
```

time: 55.2 us -> 60.5 us (1.096)
  the two profiles are of different devices: /device:TPU:9 before, /device:TPU:0 now
where the time goes in v2:
time: 60.5 us; the launch traced here: 60 us
  starting transfers between devices  23.7 us (39%)
  Pallas kernels  17.6 us (29%)
  waiting for transfers between devices  12.4 us (20%)
  local copies, waits for them, and re-layouts  5.33 us (9%)
  between operations  0.96 us (2%)
    ppermute x15, starting transfers between devices, swap(): return lax.ppermute(x, axes, [(d, d ^ k) for d in range(n)])  23.7 us
    ppermute x15, waiting for transfers between devices, swap(): return lax.ppermute(x, axes, [(d, d ^ k) for d in range(n)])  12.4 us
    pallas_call x9, Pallas kernels, call(): pl.pallas_call(body, out_shape=outs, in_specs=in_specs, out_specs=out_spe...  11.6 us
    unnamed x46, local copies, waits for them, and re-layouts  5.33 us
    pallas_call x1, Pallas kernels, shards(): pl.pallas_call(local_kernel, grid=(blocks // step,), out_shape=[block, bl...  3.74 us
    pallas_call x1, Pallas kernels, shards(): pl.pallas_call(predict_kernel, grid=(blocks // step,), out_shape=[block,...  2.23 us
  transfers between devices with their start and end apart: 15, of which 4 were waited for; matrix products, arithmetic and copies ran while one was open for 0% of the time, Pallas kernels for 21%

profile of v2, /device:TPU:0, one launch (start us, length us, event | category | flops | bytes accessed | tf_op | source)
XLA Modules:
  0.0 60.0 jit_solution(5662219662274733364)
XLA Ops:
  0.6 1.5 %shard_map.113._.mine_ref = s32[128]{0:T(128)S(1)} custom-call(s32[1]{0:T(128)} %bitcast.here_ref, s32[32]{0:T(128)} %new_slot_ref.3, s32[32]{0:T(128)} %partner_ref.3), custom_call_target="tpu_custom_call" | custom-call | tf_op jit(solution)/shard_map/pallas_call | solution.py:306
  2.2 0.0 copy-start.10
  2.2 0.0 copy-start.9
  2.2 0.0 copy-start
  2.2 0.0 copy-start.1
  2.2 0.0 copy-start.8
  2.2 5.1 %collective-permute-start.2 = (s32[128]{0:T(128)S(1)}, s32[128]{0:T(128)S(1)}, u32[]{:S(2)}, u32[]{:S(2)}) collective-permute-start(s32[128]{0:T(128)S(1)} %shard_map.113._.mine_ref), channel_id=1, source_target_pairs={{0,12},{4,8},{8,4},{12,0},{1,13},{5,9},{9,5},{13,1},{2,14},{6,10},... | collective-permute-start | bytes 1544 | tf_op jit(solution)/shard_map/ppermute | solution.py:318
  7.4 0.0 collective-permute-start.1
  7.4 0.6 %collective-permute-start = (s32[128]{0:T(128)S(1)}, s32[128]{0:T(128)S(1)}, u32[]{:S(2)}, u32[]{:S(2)}) collective-permute-start(s32[128]{0:T(128)S(1)} %shard_map.113._.mine_ref), channel_id=1, source_target_pairs={{0,4},{4,0},{8,12},{12,8},{1,5},{5,1},{9,13},{13,9},{2,6},{6,2},{1... | collective-permute-start | bytes 1544 | tf_op jit(solution)/shard_map/ppermute | solution.py:318
  8.0 2.2 %shard_map.114 = (f32[32,32,128]{2,1,0:T(8,128)S(1)}, f32[32,32,128]{2,1,0:T(8,128)S(1)}) custom-call(s32[128]{0:T(128)S(1)} %shard_map.113._.mine_ref, f32[32,3,32,128]{3,2,1,0:T(8,128)} %history_ref.1), custom_call_target="tpu_custom_call" | custom-call | tf_op jit(solution)/shard_map/pallas_call | solution.py:374
  10.2 0.0 collective-permute-done.2.rest_2_.rest_1_
  10.3 0.0 copy-start.15
  10.3 1.5 %collective-permute-done.1.rest_1_.rest_0_ = s32[128]{0:T(128)S(1)} collective-permute-done((s32[128]{0:T(128)S(1)}, s32[128]{0:T(128)S(1)}, u32[]{:S(2)}, u32[]{:S(2)}) %collective-permute-start.1) | collective-permute-done | bytes 544 | tf_op jit(solution)/shard_map/ppermute | solution.py:318
  11.8 0.0 collective-permute-done.rest_0_
  11.8 0.7 %copy-done.21 = s32[32]{0:T(128)S(1)} copy-done((s32[32]{0:T(128)S(1)}, s32[32]{0:T(128)}, u32[]{:S(2)}) %copy-start.21) | copy-done | bytes 152
  12.5 1.0 %shard_map.115 = (f32[32,32,128]{2,1,0:T(8,128)S(1)}, f32[32,32,128]{2,1,0:T(8,128)S(1)}, f32[14,32,128]{2,1,0:T(8,128)S(1)}, f32[8,32,128]{2,1,0:T(8,128)S(1)}, f32[8,32,128]{2,1,0:T(8,128)S(1)}) custom-call(s32[1]{0:T(128)} %bitcast.here_ref, s32[128]{0:T(128)S(1)} %shard_map.113._.mine_ref, s32[32]{0:T(128)S(1)} %copy-done.21, ...), custom_call_target="tpu_custom_call" | custom-call | tf_op jit(solution)/shard_map/pallas_call | solution.py:306
  13.5 0.1 collective-permute-start.3
  13.6 2.8 %collective-permute-start.4 = (f32[8,32,128]{2,1,0:T(8,128)S(1)}, f32[8,32,128]{2,1,0:T(8,128)S(1)}, u32[]{:S(2)}, u32[]{:S(2)}) collective-permute-start(f32[8,32,128]{2,1,0:T(8,128)S(1)} %get-tuple-element.26), channel_id=1, source_target_pairs={{0,8},{4,12},{8,0},{12,4},{1,9},{5,13},{9,1},{13,5},{2,10},{6,14},... | collective-permute-start | bytes 393224 | tf_op jit(solution)/shard_map/ppermute | solution.py:318
  16.4 1.6 %collective-permute-start.5 = (f32[8,32,128]{2,1,0:T(8,128)S(1)}, f32[8,32,128]{2,1,0:T(8,128)S(1)}, u32[]{:S(2)}, u32[]{:S(2)}) collective-permute-start(f32[8,32,128]{2,1,0:T(8,128)S(1)} %get-tuple-element.27), channel_id=1, source_target_pairs={{0,12},{4,8},{8,4},{12,0},{1,13},{5,9},{9,5},{13,1},{2,14},{6,10},... | collective-permute-start | bytes 393224 | tf_op jit(solution)/shard_map/ppermute | solution.py:318
  18.0 1.3 %shard_map.116 = (f32[6,32,128]{2,1,0:T(8,128)}, f32[6,32,128]{2,1,0:T(8,128)S(1)}) custom-call(s32[1]{0:T(128)} %bitcast.here_ref, s32[128]{0:T(128)S(1)} %shard_map.113._.mine_ref, s32[128]{0:T(128)S(1)} %collective-permute-done.1.rest_1_.rest_0_, s32[128]{0:T(128)S(1)} %collective-permute-done.2.rest_2_.rest_1_, ...), custom_call_target="tpu_custom_call" | custom-call | bytes 67108864 | tf_op jit(solution)/shard_map/pallas_call | solution.py:306
  19.2 2.2 %collective-permute-start.7 = (f32[6,32,128]{2,1,0:T(8,128)S(1)}, f32[6,32,128]{2,1,0:T(8,128)S(1)}, u32[]{:S(2)}, u32[]{:S(2)}) collective-permute-start(f32[6,32,128]{2,1,0:T(8,128)S(1)} %get-tuple-element.32), channel_id=1, source_target_pairs={{0,12},{4,8},{8,4},{12,0},{1,13},{5,9},{9,5},{13,1},{2,14},{6,10},... | collective-permute-start | bytes 294920 | tf_op jit(solution)/shard_map/ppermute | solution.py:318
  21.5 0.0 collective-permute-start.6
  21.5 8.5 %collective-permute-done.4.rest_4_.rest_1_ = f32[8,32,128]{2,1,0:T(8,128)S(1)} collective-permute-done((f32[8,32,128]{2,1,0:T(8,128)S(1)}, f32[8,32,128]{2,1,0:T(8,128)S(1)}, u32[]{:S(2)}, u32[]{:S(2)}) %collective-permute-start.4) | collective-permute-done | bytes 131104 | tf_op jit(solution)/shard_map/ppermute | solution.py:318
  29.9 0.0 collective-permute-done.5.rest_5_.rest_2_
  29.9 0.0 collective-permute-done.3.rest_3_.rest_0_
  29.9 1.7 %shard_map.117 = (f32[32,32,128]{2,1,0:T(8,128)S(1)}, f32[32,32,128]{2,1,0:T(8,128)S(1)}, f32[6,32,128]{2,1,0:T(8,128)}, f32[6,32,128]{2,1,0:T(8,128)}, f32[6,32,128]{2,1,0:T(8,128)}) custom-call(s32[1]{0:T(128)} %bitcast.here_ref, s32[128]{0:T(128)S(1)} %shard_map.113._.mine_ref, s32[128]{0:T(128)S(1)} %collective-permute-done.rest_0_, ...), custom_call_target="tpu_custom_call" | custom-call | bytes 67108864 | tf_op jit(solution)/shard_map/pallas_call | solution.py:306
  31.7 0.0 copy-done.10
  31.7 0.0 copy-done.4
  31.7 0.8 %copy-done.2 = f32[32,32,128]{2,1,0:T(8,128)} copy-done((f32[32,32,128]{2,1,0:T(8,128)}, f32[32,32,128]{2,1,0:T(8,128)S(1)}, u32[]{:S(2)}) %copy-start.2) | copy-done | bytes 524312
  32.5 6.4 %collective-permute-start.8 = (f32[6,32,128]{2,1,0:T(8,128)}, f32[6,32,128]{2,1,0:T(8,128)}, u32[]{:S(2)}, u32[]{:S(2)}) collective-permute-start(f32[6,32,128]{2,1,0:T(8,128)} %get-tuple-element.37), channel_id=1, source_target_pairs={{0,4},{4,0},{8,12},{12,8},{1,5},{5,1},{9,13},{13,9},{2,6},{6,2},{1... | collective-permute-start | bytes 294920 | tf_op jit(solution)/shard_map/ppermute | solution.py:318
  38.8 1.2 %collective-permute-start.9 = (f32[6,32,128]{2,1,0:T(8,128)}, f32[6,32,128]{2,1,0:T(8,128)}, u32[]{:S(2)}, u32[]{:S(2)}) collective-permute-start(f32[6,32,128]{2,1,0:T(8,128)} %get-tuple-element.38), channel_id=1, source_target_pairs={{0,8},{4,12},{8,0},{12,4},{1,9},{5,13},{9,1},{13,5},{2,10},{6,14},... | collective-permute-start | bytes 294920 | tf_op jit(solution)/shard_map/ppermute | solution.py:318
  40.1 1.5 %collective-permute-start.10 = (f32[6,32,128]{2,1,0:T(8,128)}, f32[6,32,128]{2,1,0:T(8,128)}, u32[]{:S(2)}, u32[]{:S(2)}) collective-permute-start(f32[6,32,128]{2,1,0:T(8,128)} %get-tuple-element.39), channel_id=1, source_target_pairs={{0,12},{4,8},{8,4},{12,0},{1,13},{5,9},{9,5},{13,1},{2,14},{6,10},... | collective-permute-start | bytes 294920 | tf_op jit(solution)/shard_map/ppermute | solution.py:318
  41.5 0.0 collective-permute-done.7.rest_4_
  41.5 0.0 copy-done.15
  41.5 0.6 %copy-done.6 = f32[6,32,128]{2,1,0:T(8,128)} copy-done((f32[6,32,128]{2,1,0:T(8,128)}, f32[6,32,128]{2,1,0:T(8,128)S(1)}, u32[]{:S(2)}) %copy-start.6) | copy-done | bytes 98328
  42.1 0.0 copy-done.17
  42.2 0.0 copy-done.19
  42.2 0.1 collective-permute-start.11
  42.3 0.0 copy-start.22
  42.3 0.0 copy-start.3
  42.3 1.0 %copy-done.3 = f32[32,32,128]{2,1,0:T(8,128)S(1)} copy-done((f32[32,32,128]{2,1,0:T(8,128)S(1)}, f32[32,32,128]{2,1,0:T(8,128)}, u32[]{:S(2)}) %copy-start.3) | copy-done | bytes 524312
  43.4 0.7 %copy-done.12 = f32[32,128]{1,0:T(8,128)S(1)} copy-done((f32[32,128]{1,0:T(8,128)S(1)}, f32[32,128]{1,0:T(8,128)}, u32[]{:S(2)}) %copy-start.12) | copy-done | bytes 16408
  44.1 0.7 %copy-done.13 = f32[32,128]{1,0:T(8,128)S(1)} copy-done((f32[32,128]{1,0:T(8,128)S(1)}, f32[32,128]{1,0:T(8,128)}, u32[]{:S(2)}) %copy-start.13) | copy-done | bytes 16408
  44.8 0.7 %copy-done.14 = f32[32,128]{1,0:T(8,128)S(1)} copy-done((f32[32,128]{1,0:T(8,128)S(1)}, f32[32,128]{1,0:T(8,128)}, u32[]{:S(2)}) %copy-start.14) | copy-done | bytes 16408
  45.5 3.7 %shard_map.119 = (f32[32,32,128]{2,1,0:T(8,128)S(1)}, f32[32,32,128]{2,1,0:T(8,128)S(1)}, f32[32,32,128]{2,1,0:T(8,128)S(1)}) custom-call(f32[32,32,128]{2,1,0:T(8,128)S(1)} %get-tuple-element.31._.guess_ref.rest_5_, f32[32,32,128]{2,1,0:T(8,128)S(1)} %copy-done.3, f32[32,128,128]{2,1,0:T(8,128)S(1)} %copy-done, f32[32,128]{1,0:T(8,128)S(1)} %copy-done.12, ...), custom_call_target="tpu_custom_call" | custom-call | tf_op jit(solution)/shard_map/pallas_call | solution.py:421
  49.3 0.0 copy-done.11
  49.3 2.0 %shard_map.118.index_ref = s32[32]{0:T(128)S(1)} custom-call(s32[1]{0:T(128)} %bitcast.here_ref, s32[32]{0:T(128)S(1)} %copy-done.22, s32[128]{0:T(128)S(1)} %copy-done.11, f32[32,32,128]{2,1,0:T(8,128)S(1)} %get-tuple-element.31._.guess_ref.rest_5_, s32[128]{0:T(128)S(1)} %copy-done.20, s32[128]{0:T(128)S(1)} %copy-done.18, s32[128]{0:T(128)S(1)} %copy-done.16), custom_call_target="tpu_custom_call" | custom-call | tf_op jit(solution)/shard_map/pallas_call | solution.py:306
  51.3 0.0 collective-permute-done.6.rest_3_
  51.3 0.0 copy-done.5
  51.3 0.0 copy-done.7
  51.3 1.0 %shard_map.120.near_ref = f32[32,32,128]{2,1,0:T(8,128)S(1)} custom-call(s32[32]{0:T(128)S(1)} %shard_map.118.index_ref, f32[14,32,128]{2,1,0:T(8,128)S(1)} %collective-permute-done.3.rest_3_.rest_0_, f32[8,32,128]{2,1,0:T(8,128)S(1)} %collective-permute-done.4.rest_4_.rest_1_, f32[8,32,128]{2,1,0:T(8,128)S(1)} %copy-done.5, ...), custom_call_target="tpu_custom_call" | custom-call | tf_op jit(solution)/shard_map/pallas_call | solution.py:306
  52.4 0.0 collective-permute-done.11.rest_4_
  52.4 0.0 collective-permute-done.8.rest_0_
  52.4 0.0 collective-permute-done.9.rest_1_
  52.4 0.0 collective-permute-done.10.rest_2_
  52.4 1.2 %shard_map.121 = (f32[32,32,128]{2,1,0:T(8,128)S(1)}, f32[32,128]{1,0:T(8,128)S(1)}, f32[32,32,128]{2,1,0:T(8,128)S(1)}, f32[128,128]{1,0:T(8,128)S(1)}) custom-call(s32[32]{0:T(128)S(1)} %shard_map.118.index_ref, s32[1]{0:T(128)} %bitcast.1.blk_ref, f32[32,32,128]{2,1,0:T(8,128)S(1)} %shard_map.120.near_ref, ...), custom_call_target="tpu_custom_call" | custom-call | tf_op jit(solution)/shard_map/pallas_call | solution.py:306
  53.6 1.6 %collective-permute-start.14 = (f32[32,128]{1,0:T(8,128)S(1)}, f32[32,128]{1,0:T(8,128)S(1)}, u32[]{:S(2)}, u32[]{:S(2)}) collective-permute-start(f32[32,128]{1,0:T(8,128)S(1)} %get-tuple-element.40.rest_0_), channel_id=1, source_target_pairs={{0,3},{1,2},{2,1},{3,0},{4,7},{5,6},{6,5},{7,4},{8,11},{9,10},{10,... | collective-permute-start | bytes 49160 | tf_op jit(solution)/shard_map/ppermute | solution.py:318
  55.3 0.5 collective-permute-start.13
  55.8 0.0 collective-permute-start.12
  55.8 0.8 %shard_map.123 = f32[32,32,128]{2,1,0:T(8,128)} custom-call(f32[32,32,128]{2,1,0:T(8,128)S(1)} %get-tuple-element.43.value_ref), custom_call_target="tpu_custom_call" | custom-call | tf_op jit(solution)/shard_map/pallas_call | solution.py:306
  56.6 0.3 collective-permute-done.14.rest_3_
  56.9 2.1 %collective-permute-done.13.rest_2_ = f32[32,128]{1,0:T(8,128)S(1)} collective-permute-done((f32[32,128]{1,0:T(8,128)S(1)}, f32[32,128]{1,0:T(8,128)S(1)}, u32[]{:S(2)}, u32[]{:S(2)}) %collective-permute-start.13) | collective-permute-done | bytes 16416 | tf_op jit(solution)/shard_map/ppermute | solution.py:318
  59.0 0.0 collective-permute-done.12.rest_1_
  59.0 1.0 %shard_map.122 = f32[32,32,128]{2,1,0:T(8,128)} custom-call(f32[32,128]{1,0:T(8,128)S(1)} %get-tuple-element.40.rest_0_, f32[32,128]{1,0:T(8,128)S(1)} %collective-permute-done.12.rest_1_, f32[32,128]{1,0:T(8,128)S(1)} %collective-permute-done.13.rest_2_, f32[32,128]{1,0:T(8,128)S(1)} %collective-permute-done.14.rest_3_, ...), custom_call_target="tpu_custom_call" | custom-call | flops 6291456 | tf_op jit(solution)/shard_map/pallas_call | solution.py:306
  (23 shorter events, 0.0 us)
Async XLA Ops:
  2.2 29.5 %copy-start.10 = (s32[128]{0:T(128)}, s32[128]{0:T(128)S(1)}, u32[]{:S(2)}) copy-start(s32[128]{0:T(128)S(1)} %shard_map.113._.mine_ref) | copy-start | bytes 1540
  2.2 40.0 %copy-start.9 = (f32[1,64,128]{2,1,0:T(8,128)S(1)}, f32[1,64,128]{2,1,0:T(8,128)}, u32[]{:S(2)}) copy-start(f32[1,64,128]{2,1,0:T(8,128)} %param.19) | copy-start | bytes 98308
  2.2 40.1 %copy-start = (f32[32,128,128]{2,1,0:T(8,128)S(1)}, f32[32,128,128]{2,1,0:T(8,128)}, u32[]{:S(2)}) copy-start(f32[32,128,128]{2,1,0:T(8,128)} %coupling_ref.1) | copy-start | bytes 6291460
  2.2 40.1 %copy-start.1 = (f32[32,32,128]{2,1,0:T(8,128)S(1)}, f32[32,32,128]{2,1,0:T(8,128)}, u32[]{:S(2)}) copy-start(f32[32,32,128]{2,1,0:T(8,128)} %drive_ref.1) | copy-start | bytes 1572868
  2.2 40.1 %copy-start.8 = (f32[32,128]{1,0:T(8,128)S(1)}, f32[32,128]{1,0:T(8,128)}, u32[]{:S(2)}) copy-start(f32[32,128]{1,0:T(8,128)} %wire_ref.3) | copy-start | bytes 49156
  2.2 8.0 %collective-permute-start.2 = (s32[128]{0:T(128)S(1)}, s32[128]{0:T(128)S(1)}, u32[]{:S(2)}, u32[]{:S(2)}) collective-permute-start(s32[128]{0:T(128)S(1)} %shard_map.113._.mine_ref), channel_id=1, source_target_pairs={{0,12},{4,8},{8,4},{12,0},{1,13},{5,9},{9,5},{13,1},{2,14},{6,10},... | collective-permute-start | bytes 1544 | tf_op jit(solution)/shard_map/ppermute | solution.py:318
  7.4 4.4 %collective-permute-start.1 = (s32[128]{0:T(128)S(1)}, s32[128]{0:T(128)S(1)}, u32[]{:S(2)}, u32[]{:S(2)}) collective-permute-start(s32[128]{0:T(128)S(1)} %shard_map.113._.mine_ref), channel_id=1, source_target_pairs={{0,8},{4,12},{8,0},{12,4},{1,9},{5,13},{9,1},{13,5},{2,10},{6,14},... | collective-permute-start | bytes 1544 | tf_op jit(solution)/shard_map/ppermute | solution.py:318
  7.4 4.4 %collective-permute-start = (s32[128]{0:T(128)S(1)}, s32[128]{0:T(128)S(1)}, u32[]{:S(2)}, u32[]{:S(2)}) collective-permute-start(s32[128]{0:T(128)S(1)} %shard_map.113._.mine_ref), channel_id=1, source_target_pairs={{0,4},{4,0},{8,12},{12,8},{1,5},{5,1},{9,13},{13,9},{2,6},{6,2},{1... | collective-permute-start | bytes 1544 | tf_op jit(solution)/shard_map/ppermute | solution.py:318
  10.3 31.3 %copy-start.15 = (s32[128]{0:T(128)}, s32[128]{0:T(128)S(1)}, u32[]{:S(2)}) copy-start(s32[128]{0:T(128)S(1)} %collective-permute-done.2.rest_2_.rest_1_) | copy-start | bytes 1540
  11.8 30.4 %copy-start.17 = (s32[128]{0:T(128)}, s32[128]{0:T(128)S(1)}, u32[]{:S(2)}) copy-start(s32[128]{0:T(128)S(1)} %collective-permute-done.1.rest_1_.rest_0_) | copy-start | bytes 1540
  11.8 30.4 %copy-start.19 = (s32[128]{0:T(128)}, s32[128]{0:T(128)S(1)}, u32[]{:S(2)}) copy-start(s32[128]{0:T(128)S(1)} %collective-permute-done.rest_0_) | copy-start | bytes 1540
  11.8 0.7 %copy-start.21 = (s32[32]{0:T(128)S(1)}, s32[32]{0:T(128)}, u32[]{:S(2)}) copy-start(s32[32]{0:T(128)} %new_slot_ref.3) | copy-start | bytes 388
  13.5 16.4 %collective-permute-start.3 = (f32[14,32,128]{2,1,0:T(8,128)S(1)}, f32[14,32,128]{2,1,0:T(8,128)S(1)}, u32[]{:S(2)}, u32[]{:S(2)}) collective-permute-start(f32[14,32,128]{2,1,0:T(8,128)S(1)} %get-tuple-element.25), channel_id=1, source_target_pairs={{0,4},{4,0},{8,12},{12,8},{1,5},{5,1},{9,13},{13,9},{2,6},{6,2},{1... | collective-permute-start | bytes 688136 | tf_op jit(solution)/shard_map/ppermute | solution.py:318
  13.6 16.4 %collective-permute-start.4 = (f32[8,32,128]{2,1,0:T(8,128)S(1)}, f32[8,32,128]{2,1,0:T(8,128)S(1)}, u32[]{:S(2)}, u32[]{:S(2)}) collective-permute-start(f32[8,32,128]{2,1,0:T(8,128)S(1)} %get-tuple-element.26), channel_id=1, source_target_pairs={{0,8},{4,12},{8,0},{12,4},{1,9},{5,13},{9,1},{13,5},{2,10},{6,14},... | collective-permute-start | bytes 393224 | tf_op jit(solution)/shard_map/ppermute | solution.py:318
  16.4 13.6 %collective-permute-start.5 = (f32[8,32,128]{2,1,0:T(8,128)S(1)}, f32[8,32,128]{2,1,0:T(8,128)S(1)}, u32[]{:S(2)}, u32[]{:S(2)}) collective-permute-start(f32[8,32,128]{2,1,0:T(8,128)S(1)} %get-tuple-element.27), channel_id=1, source_target_pairs={{0,12},{4,8},{8,4},{12,0},{1,13},{5,9},{9,5},{13,1},{2,14},{6,10},... | collective-permute-start | bytes 393224 | tf_op jit(solution)/shard_map/ppermute | solution.py:318
  19.2 22.3 %collective-permute-start.7 = (f32[6,32,128]{2,1,0:T(8,128)S(1)}, f32[6,32,128]{2,1,0:T(8,128)S(1)}, u32[]{:S(2)}, u32[]{:S(2)}) collective-permute-start(f32[6,32,128]{2,1,0:T(8,128)S(1)} %get-tuple-element.32), channel_id=1, source_target_pairs={{0,12},{4,8},{8,4},{12,0},{1,13},{5,9},{9,5},{13,1},{2,14},{6,10},... | collective-permute-start | bytes 294920 | tf_op jit(solution)/shard_map/ppermute | solution.py:318
  21.5 29.8 %collective-permute-start.6 = (f32[6,32,128]{2,1,0:T(8,128)}, f32[6,32,128]{2,1,0:T(8,128)}, u32[]{:S(2)}, u32[]{:S(2)}) collective-permute-start(f32[6,32,128]{2,1,0:T(8,128)} %get-tuple-element.30.rest_8_), channel_id=1, source_target_pairs={{0,8},{4,12},{8,0},{12,4},{1,9},{5,13},{9,1},{13,5},{2,10},{6,14},... | collective-permute-start | bytes 294920 | tf_op jit(solution)/shard_map/ppermute | solution.py:318
  29.9 1.7 %copy-start.4 = (f32[8,32,128]{2,1,0:T(8,128)}, f32[8,32,128]{2,1,0:T(8,128)S(1)}, u32[]{:S(2)}) copy-start(f32[8,32,128]{2,1,0:T(8,128)S(1)} %collective-permute-done.5.rest_5_.rest_2_) | copy-start | bytes 393220
  31.7 0.8 %copy-start.2 = (f32[32,32,128]{2,1,0:T(8,128)}, f32[32,32,128]{2,1,0:T(8,128)S(1)}, u32[]{:S(2)}) copy-start(f32[32,32,128]{2,1,0:T(8,128)S(1)} %get-tuple-element.33.slope_ref) | copy-start | bytes 1572868
  32.5 19.9 %collective-permute-start.8 = (f32[6,32,128]{2,1,0:T(8,128)}, f32[6,32,128]{2,1,0:T(8,128)}, u32[]{:S(2)}, u32[]{:S(2)}) collective-permute-start(f32[6,32,128]{2,1,0:T(8,128)} %get-tuple-element.37), channel_id=1, source_target_pairs={{0,4},{4,0},{8,12},{12,8},{1,5},{5,1},{9,13},{13,9},{2,6},{6,2},{1... | collective-permute-start | bytes 294920 | tf_op jit(solution)/shard_map/ppermute | solution.py:318
  38.8 13.6 %collective-permute-start.9 = (f32[6,32,128]{2,1,0:T(8,128)}, f32[6,32,128]{2,1,0:T(8,128)}, u32[]{:S(2)}, u32[]{:S(2)}) collective-permute-start(f32[6,32,128]{2,1,0:T(8,128)} %get-tuple-element.38), channel_id=1, source_target_pairs={{0,8},{4,12},{8,0},{12,4},{1,9},{5,13},{9,1},{13,5},{2,10},{6,14},... | collective-permute-start | bytes 294920 | tf_op jit(solution)/shard_map/ppermute | solution.py:318
  40.1 12.3 %collective-permute-start.10 = (f32[6,32,128]{2,1,0:T(8,128)}, f32[6,32,128]{2,1,0:T(8,128)}, u32[]{:S(2)}, u32[]{:S(2)}) collective-permute-start(f32[6,32,128]{2,1,0:T(8,128)} %get-tuple-element.39), channel_id=1, source_target_pairs={{0,12},{4,8},{8,4},{12,0},{1,13},{5,9},{9,5},{13,1},{2,14},{6,10},... | collective-permute-start | bytes 294920 | tf_op jit(solution)/shard_map/ppermute | solution.py:318
  41.5 0.6 %copy-start.6 = (f32[6,32,128]{2,1,0:T(8,128)}, f32[6,32,128]{2,1,0:T(8,128)S(1)}, u32[]{:S(2)}) copy-start(f32[6,32,128]{2,1,0:T(8,128)S(1)} %collective-permute-done.7.rest_4_) | copy-start | bytes 294916
  42.2 10.2 %collective-permute-start.11 = (f32[64,128]{1,0:T(8,128)S(1)}, f32[64,128]{1,0:T(8,128)}, u32[]{:S(2)}, u32[]{:S(2)}) collective-permute-start(f32[64,128]{1,0:T(8,128)S(1)} %bitcast.3), channel_id=1, source_target_pairs={{0,1},{1,0},{2,3},{3,2},{4,5},{5,4},{6,7},{7,6},{8,9},{9,8},{10,11... | collective-permute-start | bytes 98312 | tf_op jit(solution)/shard_map/ppermute | solution.py:318
  42.2 7.0 %copy-start.11 = (s32[128]{0:T(128)S(1)}, s32[128]{0:T(128)}, u32[]{:S(2)}) copy-start(s32[128]{0:T(128)} %copy-done.10) | copy-start | bytes 1540
  42.2 7.0 %copy-start.16 = (s32[128]{0:T(128)S(1)}, s32[128]{0:T(128)}, u32[]{:S(2)}) copy-start(s32[128]{0:T(128)} %copy-done.15) | copy-start | bytes 1540
  42.3 7.0 %copy-start.18 = (s32[128]{0:T(128)S(1)}, s32[128]{0:T(128)}, u32[]{:S(2)}) copy-start(s32[128]{0:T(128)} %copy-done.17) | copy-start | bytes 1540
  42.3 7.0 %copy-start.20 = (s32[128]{0:T(128)S(1)}, s32[128]{0:T(128)}, u32[]{:S(2)}) copy-start(s32[128]{0:T(128)} %copy-done.19) | copy-start | bytes 1540
  42.3 7.0 %copy-start.22 = (s32[32]{0:T(128)S(1)}, s32[32]{0:T(128)}, u32[]{:S(2)}) copy-start(s32[32]{0:T(128)} %partner_ref.3) | copy-start | bytes 388
  42.3 1.0 %copy-start.3 = (f32[32,32,128]{2,1,0:T(8,128)S(1)}, f32[32,32,128]{2,1,0:T(8,128)}, u32[]{:S(2)}) copy-start(f32[32,32,128]{2,1,0:T(8,128)} %copy-done.2) | copy-start | bytes 1572868
  43.4 0.7 %copy-start.12 = (f32[32,128]{1,0:T(8,128)S(1)}, f32[32,128]{1,0:T(8,128)}, u32[]{:S(2)}) copy-start(f32[32,128]{1,0:T(8,128)} %cap_ref.1) | copy-start | bytes 49156
  44.1 0.7 %copy-start.13 = (f32[32,128]{1,0:T(8,128)S(1)}, f32[32,128]{1,0:T(8,128)}, u32[]{:S(2)}) copy-start(f32[32,128]{1,0:T(8,128)} %gdev_ref.1) | copy-start | bytes 49156
  44.8 0.7 %copy-start.14 = (f32[32,128]{1,0:T(8,128)S(1)}, f32[32,128]{1,0:T(8,128)}, u32[]{:S(2)}) copy-start(f32[32,128]{1,0:T(8,128)} %gain_ref.1) | copy-start | bytes 49156
  45.5 5.8 %copy-start.5 = (f32[8,32,128]{2,1,0:T(8,128)S(1)}, f32[8,32,128]{2,1,0:T(8,128)}, u32[]{:S(2)}) copy-start(f32[8,32,128]{2,1,0:T(8,128)} %copy-done.4) | copy-start | bytes 393220
  45.5 5.8 %copy-start.7 = (f32[6,32,128]{2,1,0:T(8,128)S(1)}, f32[6,32,128]{2,1,0:T(8,128)}, u32[]{:S(2)}) copy-start(f32[6,32,128]{2,1,0:T(8,128)} %copy-done.6) | copy-start | bytes 294916
  53.6 3.2 %collective-permute-start.14 = (f32[32,128]{1,0:T(8,128)S(1)}, f32[32,128]{1,0:T(8,128)S(1)}, u32[]{:S(2)}, u32[]{:S(2)}) collective-permute-start(f32[32,128]{1,0:T(8,128)S(1)} %get-tuple-element.40.rest_0_), channel_id=1, source_target_pairs={{0,3},{1,2},{2,1},{3,0},{4,7},{5,6},{6,5},{7,4},{8,11},{9,10},{10,... | collective-permute-start | bytes 49160 | tf_op jit(solution)/shard_map/ppermute | solution.py:318
  55.3 3.7 %collective-permute-start.13 = (f32[32,128]{1,0:T(8,128)S(1)}, f32[32,128]{1,0:T(8,128)S(1)}, u32[]{:S(2)}, u32[]{:S(2)}) collective-permute-start(f32[32,128]{1,0:T(8,128)S(1)} %get-tuple-element.40.rest_0_), channel_id=1, source_target_pairs={{0,2},{1,3},{2,0},{3,1},{4,6},{5,7},{6,4},{7,5},{8,10},{9,11},{10,... | collective-permute-start | bytes 49160 | tf_op jit(solution)/shard_map/ppermute | solution.py:318
  55.8 3.2 %collective-permute-start.12 = (f32[32,128]{1,0:T(8,128)S(1)}, f32[32,128]{1,0:T(8,128)S(1)}, u32[]{:S(2)}, u32[]{:S(2)}) collective-permute-start(f32[32,128]{1,0:T(8,128)S(1)} %get-tuple-element.40.rest_0_), channel_id=1, source_target_pairs={{0,1},{1,0},{2,3},{3,2},{4,5},{5,4},{6,7},{7,6},{8,9},{9,8},{10,11... | collective-permute-start | bytes 49160 | tf_op jit(solution)/shard_map/ppermute | solution.py:318

commit v3 on v2

v3 whole, which is shorter than its diff:
```python
import functools

import jax
import jax.numpy as jnp
from jax import lax
from jax.experimental import pallas as pl
from jax.experimental.pallas import tpu as pltpu
from jax.sharding import PartitionSpec as P

CAP = 2
VMEM = pl.BlockSpec(memory_space=pltpu.VMEM)
SMEM = pl.BlockSpec(memory_space=pltpu.SMEM)
ANY = pl.BlockSpec(memory_space=pl.ANY)
HBM = pl.BlockSpec(memory_space=pltpu.HBM)
F32 = jnp.float32
I32 = jnp.int32


def divmod_static(value, size):
    if size & (size - 1) == 0:
        return lax.shift_right_logical(value, size.bit_length() - 1), value & (size - 1)
    whole = lax.div(value, size)
    return whole, value - whole * size


def bit_of(index):
    return lax.shift_left(jnp.int32(1), index)


def bits_set(x):
    x = x - (lax.shift_right_logical(x, 1) & 0x55555555)
    x = (x & 0x33333333) + (lax.shift_right_logical(x, 2) & 0x33333333)
    x = (x + lax.shift_right_logical(x, 4)) & 0x0F0F0F0F
    x = x + lax.shift_right_logical(x, 8)
    x = x + lax.shift_right_logical(x, 16)
    return x & 63


def lowest(mask):
    return bits_set((mask & -mask) - 1) & 31


def halves(mask):
    return [mask & 0xFFFF, lax.shift_right_logical(mask, 16)]


def joined(low, high):
    return low | lax.shift_left(high, 16)


def predict(raw):
    return 3.0 * raw[0] - 3.0 * raw[1] + raw[2]


def slope(raw, guess):
    return 3.0 * guess - (4.0 * raw[0] - raw[1])


def leave_kernel(
    n, span, here_ref, new_slot_ref, partner_ref, history_ref, rows_ref,
    slots, reads, mine_ref, raw_ref, inverse_ref, *rest
):
    outs, (source, place, count, sems) = rest[: n - 1], rest[n - 1 :]
    blocks, _, scen, nodes = history_ref.shape
    die = here_ref[0]
    copies = [
        pltpu.make_async_copy(new_slot_ref, slots, sems.at[0]),
        pltpu.make_async_copy(partner_ref, reads, sems.at[1]),
        pltpu.make_async_copy(history_ref, raw_ref, sems.at[2]),
        pltpu.make_async_copy(rows_ref, inverse_ref, sems.at[3]),
    ]
    for copy in copies:
        copy.start()
    for at in range(n):
        mine_ref[at] = 0
        count[at] = 0
    for at in range(n * CAP):
        source[at] = 0
        place[at] = -1
    copies[0].wait()
    copies[1].wait()

    for at in range(blocks):
        dest, local = divmod_static(slots[at], span)
        local = divmod_static(local, blocks)[1]

        @pl.when(dest != die)
        def _(at=at, dest=dest, local=local):
            rank = count[dest]
            count[dest] = rank + 1
            turn = (dest ^ die) * CAP + rank
            source[turn] = at
            place[turn] = local

        owner, local = divmod_static(reads[at], span)
        mine_ref[owner] = mine_ref[owner] | bit_of(divmod_static(local, blocks)[1])
    copies[2].wait()
    lane = lax.broadcasted_iota(I32, (8, nodes), 1)
    for k in range(1, n):
        out = outs[k - 1]
        for rank in range(CAP):
            raw = raw_ref.at[source[k * CAP + rank]]
            guess = predict(raw)
            out[pl.ds(rank * scen, scen), :] = guess
            out[pl.ds((CAP + rank) * scen, scen), :] = slope(raw, guess)
        row = jnp.zeros((8, nodes), I32)
        values = halves(mine_ref[die ^ k])
        values += [place[k * CAP + rank] for rank in range(CAP)]
        for j, value in enumerate(values):
            row = jnp.where(lane == j, value, row)
        out[pl.ds(2 * CAP * scen, 8), :] = row.astype(F32)
    copies[3].wait()


def place_kernel(span, here_ref, slots, raw_ref, guess_ref, slope_ref):
    blocks = raw_ref.shape[0]
    for at in range(blocks):
        dest, local = divmod_static(slots[at], span)
        local = divmod_static(local, blocks)[1]

        @pl.when(dest == here_ref[0])
        def _(at=at, local=local):
            raw = raw_ref.at[at]
            guess = predict(raw)
            guess_ref[local] = guess
            slope_ref[local] = slope(raw, guess)


def serve_kernel(n, rcap, nblk, blk_ref, *rest):
    arrived, rest = rest[: n - 1], rest[n - 1 :]
    inverses, rest = rest[:nblk], rest[nblk:]
    old_guess, old_slope, guess_ref, slope_ref, whole_ref, *rest = rest
    outs, (ints, meta, sem) = rest[: n - 1], rest[n - 1 :]
    blocks, scen, nodes = guess_ref.shape
    for k in range(1, n):
        ints[k - 1] = arrived[k - 1][pl.ds(2 * CAP * scen, 8), :].astype(I32)
    copy = pltpu.make_async_copy(ints, meta, sem)
    copy.start()
    for at in range(blocks):
        guess_ref[at] = old_guess[at]
        slope_ref[at] = old_slope[at]
    height = inverses[0].shape[0]
    for k in range(nblk):
        at = pl.multiple_of((blk_ref[0] ^ k) * height, height)
        whole_ref[pl.ds(at, height), :] = inverses[k][...]
    copy.wait()
    for k in range(1, n):
        for rank in range(CAP):
            place = meta[k - 1, 0, 2 + rank]

            @pl.when(place >= 0)
            def _(k=k, rank=rank, place=place):
                guess_ref[place] = arrived[k - 1][pl.ds(rank * scen, scen), :]
                slope_ref[place] = arrived[k - 1][pl.ds((CAP + rank) * scen, scen), :]

    for k in range(1, n):
        want = joined(meta[k - 1, 0, 0], meta[k - 1, 0, 1])
        for slot in range(rcap):
            outs[k - 1][slot] = guess_ref[lowest(want)]
            want = want & (want - 1)


def where_kernel(n, span, rcap, here_ref, reads, mine_ref, _, index_ref):
    blocks = index_ref.shape[0]
    die = here_ref[0]

    def step(at, carry):
        owner, local = divmod_static(reads[at], span)
        local = divmod_static(local, blocks)[1]
        k = owner ^ die
        slot = bits_set(mine_ref[owner] & (bit_of(local) - 1))
        index_ref[at] = jnp.where(k == 0, local - blocks, (k - 1) * rcap + slot)
        return carry

    lax.fori_loop(0, blocks, step, 0)


def local_kernel(
    guess_ref, slope_ref, coupling_ref, cap_ref, gdev_ref, wire_ref, gain_ref, drive_ref,
    base_ref, inv_ref, scale_ref, kept_ref
):
    nodes = coupling_ref.shape[1]
    rows = lax.broadcasted_iota(I32, (nodes, nodes), 0)
    cols = lax.broadcasted_iota(I32, (nodes, nodes), 1)
    for at in range(guess_ref.shape[0]):
        guess = guess_ref[at]
        coupling = coupling_ref[at]
        cap = cap_ref[at : at + 1, :]
        gdev = gdev_ref[at : at + 1, :]
        wire = wire_ref[at : at + 1, :]
        through = lax.dot_general(
            guess,
            coupling,
            (((1,), (1,)), ((), ())),
            precision=lax.Precision.HIGHEST,
            preferred_element_type=F32,
        )
        diagonal = jnp.sum(jnp.where(rows == cols, coupling, 0.0), axis=0, keepdims=True)
        tnh = jnp.tanh(guess)
        inv = 1.0 / (1.5 * cap + diagonal + gdev * (1.0 - tnh * tnh) + wire)
        inv_ref[at] = inv
        kept_ref[at : at + 1, :] = wire
        scale_ref[at] = gain_ref[at : at + 1, :] * inv
        base_ref[at] = (
            0.5 * cap * slope_ref[at] + through + gdev * tnh + wire * guess - drive_ref[at]
        )


def residual_kernel(n, index_ref, base_ref, inv_ref, scale_ref, guess_ref, wire_ref, *rest):
    blocks_in, (residual_ref, share_ref, partial_ref, pool) = rest[: n - 1], rest[n - 1 :]
    blocks = guess_ref.shape[0]
    start = 0
    for ref in blocks_in:
        for slot in range(ref.shape[0]):
            pool[start + slot] = ref[slot]
        start += ref.shape[0]
    share = jnp.zeros(share_ref.shape, F32)
    for at in range(blocks):
        index = index_ref[at]
        own = index < 0
        near = guess_ref[jnp.where(own, index + blocks, 0)]
        other = jnp.where(own, near, pool[jnp.maximum(index, 0)])
        residual = base_ref[at] - wire_ref[at : at + 1, :] * other
        residual_ref[at] = residual
        partial_ref[at] = guess_ref[at] - residual * inv_ref[at]
        share = share + scale_ref[at] * residual
    share_ref[...] = share


def store_kernel(value_ref, out_ref, sem):
    copy = pltpu.make_async_copy(value_ref, out_ref, sem)
    copy.start()
    copy.wait()


def update_kernel(m, parts, *rest):
    shares, (whole_ref, partial_ref, scale_ref, updated_ref, held, sems) = rest[:m], rest[m:]
    total = shares[0][...]
    for share in shares[1:]:
        total = total + share[...]
    region = jnp.dot(
        total, whole_ref[...], precision=lax.Precision.HIGHEST, preferred_element_type=F32
    )
    step = partial_ref.shape[0] // parts
    copies = []
    for part in range(parts):
        for at in range(part * step, (part + 1) * step):
            held[at] = partial_ref[at] + scale_ref[at] * region
        span = pl.ds(part * step, step)
        copies.append(pltpu.make_async_copy(held.at[span], updated_ref.at[span], sems.at[part]))
        copies[-1].start()
    for copy in copies:
        copy.wait()


def call(body, outs, ins, in_specs, out_specs, scratch=(), limit=8):
    return pl.pallas_call(
        body,
        out_shape=outs,
        in_specs=in_specs,
        out_specs=out_specs,
        scratch_shapes=list(scratch),
        compiler_params=pltpu.CompilerParams(vmem_limit_bytes=limit << 20),
        cost_estimate=pl.CostEstimate(flops=0, bytes_accessed=0, transcendentals=0),
    )(*ins)


def in_hbm(x):
    return pltpu.with_memory_space_constraint(x, pltpu.HBM)


def swap(x, axes, n, k):
    return lax.ppermute(x, axes, [(d, d ^ k) for d in range(n)])


def shards(
    history,
    new_slot,
    partner,
    coupling,
    cap_rate,
    device_gain,
    wire_gain,
    region_gain,
    drive,
    region_inverse,
):
    blocks, _, scen, nodes = history.shape
    n = lax.axis_size("die")
    nblk = lax.axis_size("blk")
    ncol = lax.axis_size("sub") * nblk
    for size in (n, nblk, ncol):
        assert size & (size - 1) == 0
    assert blocks <= 32
    rcap = 2 * max(1, blocks // n)
    span = ncol * blocks
    die = lax.axis_index("die").astype(I32).reshape(1)
    blk = lax.axis_index("blk").astype(I32).reshape(1)

    def tiles(count):
        return jax.ShapeDtypeStruct((count, scen, nodes), F32)

    def ints(count):
        return jax.ShapeDtypeStruct((count,), I32)

    block = tiles(blocks)
    square = jax.ShapeDtypeStruct((nodes, nodes), F32)
    rows = region_inverse[0]
    message = jax.ShapeDtypeStruct((2 * CAP * scen + 8, nodes), F32)

    slots, reads, mine, raw, rows, *leaving = call(
        functools.partial(leave_kernel, n, span),
        [
            ints(blocks),
            ints(blocks),
            ints(n),
            jax.ShapeDtypeStruct(history.shape, F32),
            jax.ShapeDtypeStruct(rows.shape, F32),
        ]
        + [message] * (n - 1),
        [die, in_hbm(new_slot), in_hbm(partner), in_hbm(history), in_hbm(rows)],
        [SMEM] + [HBM] * 4,
        [SMEM] * 3 + [VMEM] * (n + 1),
        [pltpu.SMEM((n * CAP,), I32)] * 2
        + [pltpu.SMEM((n,), I32), pltpu.SemaphoreType.DMA((4,))],
    )
    arrived = [swap(leaving[k - 1], "die", n, k) for k in range(1, n)]
    inverses = [rows] + [swap(rows, "blk", nblk, k) for k in range(1, nblk)]
    old_guess, old_slope = call(
        functools.partial(place_kernel, span),
        [block, block],
        [die, slots, raw],
        [SMEM, SMEM, VMEM],
        [VMEM, VMEM],
    )
    guess, slopes, whole, *served = call(
        functools.partial(serve_kernel, n, rcap, nblk),
        [block, block, square] + [tiles(rcap)] * (n - 1),
        [blk, *arrived, *inverses, old_guess, old_slope],
        [SMEM] + [VMEM] * (n - 1 + nblk + 2),
        [VMEM] * (n + 2),
        [
            pltpu.VMEM((n - 1, 8, nodes), I32),
            pltpu.SMEM((n - 1, 8, nodes), I32),
            pltpu.SemaphoreType.DMA,
        ],
    )
    others = [swap(served[k - 1], "die", n, k) for k in range(1, n)]
    (index,) = call(
        functools.partial(where_kernel, n, span, rcap),
        [ints(blocks)],
        [die, reads, mine, guess],
        [SMEM] * 3 + [ANY],
        [SMEM],
    )
    step = 8 if blocks % 8 == 0 else blocks
    wide = pl.BlockSpec((step, scen, nodes), lambda i: (i, 0, 0))
    flat = pl.BlockSpec((step, nodes), lambda i: (i, 0))
    base, inv, scale, wire = pl.pallas_call(
        local_kernel,
        grid=(blocks // step,),
        out_shape=[block, block, block, jax.ShapeDtypeStruct((blocks, nodes), F32)],
        in_specs=[
            wide,
            wide,
            pl.BlockSpec((step, nodes, nodes), lambda i: (i, 0, 0)),
            flat,
            flat,
            flat,
            flat,
            wide,
        ],
        out_specs=[wide, wide, wide, flat],
        compiler_params=pltpu.CompilerParams(vmem_limit_bytes=8 << 20),
        cost_estimate=pl.CostEstimate(flops=0, bytes_accessed=0, transcendentals=0),
    )(
        guess,
        slopes,
        in_hbm(coupling),
        in_hbm(cap_rate),
        in_hbm(device_gain),
        in_hbm(wire_gain),
        in_hbm(region_gain),
        in_hbm(drive),
    )
    residual, share, partial = call(
        functools.partial(residual_kernel, n),
        [block, jax.ShapeDtypeStruct((scen, nodes), F32), block],
        [index, base, inv, scale, guess, wire, *others],
        [SMEM] + [VMEM] * (5 + n - 1),
        [VMEM] * 3,
        [pltpu.VMEM(((n - 1) * rcap, scen, nodes), F32)],
    )
    (stored,) = call(
        store_kernel, [block], [residual], [ANY], [HBM], [pltpu.SemaphoreType.DMA]
    )
    shares = [share] + [swap(share, ("sub", "blk"), ncol, k) for k in range(1, ncol)]
    parts = 4 if blocks % 4 == 0 else 1
    (updated,) = call(
        functools.partial(update_kernel, ncol, parts),
        [block],
        [*shares, whole, partial, scale],
        [VMEM] * (ncol + 3),
        [HBM],
        [pltpu.VMEM((blocks, scen, nodes), F32), pltpu.SemaphoreType.DMA((parts,))],
    )
    return (updated, stored)


def solution(mesh):
    every = ("grp", "die", "sub", "blk")
    in_specs = (
        P(every, None, None, None),
        P(every),
        P(every),
        P(every, None, None),
        P(every, None),
        P(every, None),
        P(every, None),
        P(every, None),
        P(every, None, None),
        P(("grp", "die"), "blk", None),
    )
    out_specs = (P(every, None, None), P(every, None, None))
    return jax.shard_map(shards, mesh=mesh, in_specs=in_specs, out_specs=out_specs, check_vma=False)
```

time: 60.5 us -> 44.9 us (0.74)
  the two profiles are of different devices: /device:TPU:0 before, /device:TPU:9 now
where the time goes in v3:
time: 44.9 us; the launch traced here: 44.3 us
  waiting for transfers between devices  18.4 us (41%)
  Pallas kernels  13.6 us (30%)
  starting transfers between devices  11.6 us (26%)
  between operations  0.73 us (2%)
    ppermute x10, waiting for transfers between devices, swap(): return lax.ppermute(x, axes, [(d, d ^ k) for d in range(n)])  18.4 us
    ppermute x10, starting transfers between devices, swap(): return lax.ppermute(x, axes, [(d, d ^ k) for d in range(n)])  11.6 us
    pallas_call x7, Pallas kernels, call(): pl.pallas_call(body, out_shape=outs, in_specs=in_specs, out_specs=out_spe...  8.36 us
    pallas_call x1, Pallas kernels, shards(): pl.pallas_call(local_kernel, grid=(blocks // step,), out_shape=[block, bl...  5.19 us
  transfers between devices with their start and end apart: 10, of which 6 were waited for; matrix products, arithmetic and copies ran while one was open for 0% of the time, Pallas kernels for 19%

profile of v3, /device:TPU:9, one launch (start us, length us, event | category | flops | bytes accessed | tf_op | source)
XLA Modules:
  0.0 44.3 jit_solution(5909678392092896407)
XLA Ops:
  0.6 2.1 %shard_map.113 = (s32[32]{0:T(128)S(1)}, s32[32]{0:T(128)S(1)}, s32[4]{0:T(128)S(1)}, f32[32,3,32,128]{3,2,1,0:T(8,128)S(1)}, f32[64,128]{1,0:T(8,128)S(1)}, /*i...) custom-call(s32[1]{0:T(128)} %bitcast.here_ref, s32[32]{0:T(128)} %new_slot_ref.1, ...), custom_call_target="tpu_custom_call" | custom-call | tf_op jit(solution)/shard_map/pallas_call | solution.py:257
  2.7 0.1 collective-permute-start
  2.8 2.5 %collective-permute-start.1 = (f32[136,128]{1,0:T(8,128)S(1)}, f32[136,128]{1,0:T(8,128)S(1)}, u32[]{:S(2)}, u32[]{:S(2)}) collective-permute-start(f32[136,128]{1,0:T(8,128)S(1)} %get-tuple-element.28), channel_id=1, source_target_pairs={{0,8},{4,12},{8,0},{12,4},{1,9},{5,13},{9,1},{13,5},{2,10},{6,14},... | collective-permute-start | bytes 208904 | tf_op jit(solution)/shard_map/ppermute | solution.py:273
  5.3 0.2 collective-permute-start.2
  5.5 1.5 %collective-permute-start.3 = (f32[64,128]{1,0:T(8,128)S(1)}, f32[64,128]{1,0:T(8,128)S(1)}, u32[]{:S(2)}, u32[]{:S(2)}) collective-permute-start(f32[64,128]{1,0:T(8,128)S(1)} %get-tuple-element.30.rest_3_), channel_id=1, source_target_pairs={{0,1},{1,0},{2,3},{3,2},{4,5},{5,4},{6,7},{7,6},{8,9},{9,8},{10,11... | collective-permute-start | bytes 98312 | tf_op jit(solution)/shard_map/ppermute | solution.py:273
  7.0 0.9 %shard_map.114 = (f32[32,32,128]{2,1,0:T(8,128)S(1)}, f32[32,32,128]{2,1,0:T(8,128)S(1)}) custom-call(s32[1]{0:T(128)} %bitcast.here_ref, s32[32]{0:T(128)S(1)} %get-tuple-element.31.slots, f32[32,3,32,128]{3,2,1,0:T(8,128)S(1)} %get-tuple-element.32.raw_ref), custom_call_target="tpu_custom_call" | custom-call | tf_op jit(solution)/shard_map/pallas_call | solution.py:257
  7.9 0.0 collective-permute-done.3.rest_4_
  7.9 0.0 collective-permute-done.rest_0_
  7.9 0.1 collective-permute-done.1.rest_1_
  8.1 2.7 %collective-permute-done.2.rest_2_ = f32[136,128]{1,0:T(8,128)S(1)} collective-permute-done((f32[136,128]{1,0:T(8,128)S(1)}, f32[136,128]{1,0:T(8,128)S(1)}, u32[]{:S(2)}, u32[]{:S(2)}) %collective-permute-start.2) | collective-permute-done | bytes 69664 | tf_op jit(solution)/shard_map/ppermute | solution.py:273
  10.8 1.1 %shard_map.115 = (f32[32,32,128]{2,1,0:T(8,128)S(1)}, f32[32,32,128]{2,1,0:T(8,128)S(1)}, f32[128,128]{1,0:T(8,128)S(1)}, f32[16,32,128]{2,1,0:T(8,128)S(1)}, f3...) custom-call(s32[1]{0:T(128)} %bitcast.2.blk_ref, f32[136,128]{1,0:T(8,128)S(1)} %collective-permute-done.rest_0_, ...), custom_call_target="tpu_custom_call" | custom-call | tf_op jit(solution)/shard_map/pallas_call | solution.py:257
  11.9 0.8 %collective-permute-start.4 = (f32[16,32,128]{2,1,0:T(8,128)S(1)}, f32[16,32,128]{2,1,0:T(8,128)S(1)}, u32[]{:S(2)}, u32[]{:S(2)}) collective-permute-start(f32[16,32,128]{2,1,0:T(8,128)S(1)} %get-tuple-element.41), channel_id=1, source_target_pairs={{0,4},{4,0},{8,12},{12,8},{1,5},{5,1},{9,13},{13,9},{2,6},{6,2},{1... | collective-permute-start | bytes 786440 | tf_op jit(solution)/shard_map/ppermute | solution.py:273
  12.7 2.1 %collective-permute-start.5 = (f32[16,32,128]{2,1,0:T(8,128)S(1)}, f32[16,32,128]{2,1,0:T(8,128)S(1)}, u32[]{:S(2)}, u32[]{:S(2)}) collective-permute-start(f32[16,32,128]{2,1,0:T(8,128)S(1)} %get-tuple-element.42), channel_id=1, source_target_pairs={{0,8},{4,12},{8,0},{12,4},{1,9},{5,13},{9,1},{13,5},{2,10},{6,14},... | collective-permute-start | bytes 786440 | tf_op jit(solution)/shard_map/ppermute | solution.py:273
  14.8 0.0 collective-permute-start.6
  14.8 1.7 %shard_map.116.index_ref = s32[32]{0:T(128)S(1)} custom-call(s32[1]{0:T(128)} %bitcast.here_ref, s32[32]{0:T(128)S(1)} %get-tuple-element.25.reads, s32[4]{0:T(128)S(1)} %get-tuple-element.26.mine_ref, f32[32,32,128]{2,1,0:T(8,128)S(1)} %get-tuple-element.35._.guess_ref), custom_call_target="tpu_custom_call" | custom-call | tf_op jit(solution)/shard_map/pallas_call | solution.py:257
  16.5 5.2 %shard_map.117 = (f32[32,32,128]{2,1,0:T(8,128)S(1)}, f32[32,32,128]{2,1,0:T(8,128)S(1)}, f32[32,32,128]{2,1,0:T(8,128)S(1)}, f32[32,128]{1,0:T(8,128)S(1)}) custom-call(f32[32,32,128]{2,1,0:T(8,128)S(1)} %get-tuple-element.35._.guess_ref, f32[32,32,128]{2,1,0:T(8,128)S(1)} %get-tuple-element.36.slope_ref, f32[32,128,128]{2,1,0:T(8,128)} %coupling_ref.1, ...), custom_call_target="tpu_custom_call" | custom-call | tf_op jit(solution)/shard_map/pallas_call | solution.py:359
  21.7 0.0 collective-permute-done.4.rest_0_
  21.7 3.2 %collective-permute-done.5.rest_1_ = f32[16,32,128]{2,1,0:T(8,128)S(1)} collective-permute-done((f32[16,32,128]{2,1,0:T(8,128)S(1)}, f32[16,32,128]{2,1,0:T(8,128)S(1)}, u32[]{:S(2)}, u32[]{:S(2)}) %collective-permute-start.5) | collective-permute-done | bytes 262176 | tf_op jit(solution)/shard_map/ppermute | solution.py:273
  24.9 11.1 %collective-permute-done.6.rest_2_ = f32[16,32,128]{2,1,0:T(8,128)S(1)} collective-permute-done((f32[16,32,128]{2,1,0:T(8,128)S(1)}, f32[16,32,128]{2,1,0:T(8,128)S(1)}, u32[]{:S(2)}, u32[]{:S(2)}) %collective-permute-start.6) | collective-permute-done | bytes 262176 | tf_op jit(solution)/shard_map/ppermute | solution.py:273
  36.0 0.8 %shard_map.118 = (f32[32,32,128]{2,1,0:T(8,128)S(1)}, f32[32,128]{1,0:T(8,128)S(1)}, f32[32,32,128]{2,1,0:T(8,128)S(1)}) custom-call(s32[32]{0:T(128)S(1)} %shard_map.116.index_ref, f32[32,32,128]{2,1,0:T(8,128)S(1)} %get-tuple-element.37.base_ref, f32[32,32,128]{2,1,0:T(8,128)S(1)} %get-tuple-element.38.inv_ref, ...), custom_call_target="tpu_custom_call" | custom-call | tf_op jit(solution)/shard_map/pallas_call | solution.py:257
  36.8 3.9 %collective-permute-start.9 = (f32[32,128]{1,0:T(8,128)S(1)}, f32[32,128]{1,0:T(8,128)S(1)}, u32[]{:S(2)}, u32[]{:S(2)}) collective-permute-start(f32[32,128]{1,0:T(8,128)S(1)} %get-tuple-element.44.rest_0_), channel_id=1, source_target_pairs={{0,3},{1,2},{2,1},{3,0},{4,7},{5,6},{6,5},{7,4},{8,11},{9,10},{10,... | collective-permute-start | bytes 49160 | tf_op jit(solution)/shard_map/ppermute | solution.py:273
  40.7 0.3 collective-permute-start.8
  40.9 0.2 collective-permute-start.7
  41.1 0.8 %shard_map.120 = f32[32,32,128]{2,1,0:T(8,128)} custom-call(f32[32,32,128]{2,1,0:T(8,128)S(1)} %get-tuple-element.47.value_ref), custom_call_target="tpu_custom_call" | custom-call | tf_op jit(solution)/shard_map/pallas_call | solution.py:257
  42.0 0.5 %collective-permute-done.9.rest_3_ = f32[32,128]{1,0:T(8,128)S(1)} collective-permute-done((f32[32,128]{1,0:T(8,128)S(1)}, f32[32,128]{1,0:T(8,128)S(1)}, u32[]{:S(2)}, u32[]{:S(2)}) %collective-permute-start.9) | collective-permute-done | bytes 16416 | tf_op jit(solution)/shard_map/ppermute | solution.py:273
  42.5 0.8 %collective-permute-done.8.rest_2_ = f32[32,128]{1,0:T(8,128)S(1)} collective-permute-done((f32[32,128]{1,0:T(8,128)S(1)}, f32[32,128]{1,0:T(8,128)S(1)}, u32[]{:S(2)}, u32[]{:S(2)}) %collective-permute-start.8) | collective-permute-done | bytes 16416 | tf_op jit(solution)/shard_map/ppermute | solution.py:273
  43.3 0.0 collective-permute-done.7.rest_1_
  43.3 1.0 %shard_map.119 = f32[32,32,128]{2,1,0:T(8,128)} custom-call(f32[32,128]{1,0:T(8,128)S(1)} %get-tuple-element.44.rest_0_, f32[32,128]{1,0:T(8,128)S(1)} %collective-permute-done.7.rest_1_, f32[32,128]{1,0:T(8,128)S(1)} %collective-permute-done.8.rest_2_, f32[32,128]{1,0:T(8,128)S(1)} %collective-permute-done.9.rest_3_, ...), custom_call_target="tpu_custom_call" | custom-call | tf_op jit(solution)/shard_map/pallas_call | solution.py:257
Async XLA Ops:
  2.7 5.2 %collective-permute-start = (f32[136,128]{1,0:T(8,128)S(1)}, f32[136,128]{1,0:T(8,128)S(1)}, u32[]{:S(2)}, u32[]{:S(2)}) collective-permute-start(f32[136,128]{1,0:T(8,128)S(1)} %get-tuple-element.27), channel_id=1, source_target_pairs={{0,4},{4,0},{8,12},{12,8},{1,5},{5,1},{9,13},{13,9},{2,6},{6,2},{1... | collective-permute-start | bytes 208904 | tf_op jit(solution)/shard_map/ppermute | solution.py:273
  2.8 5.2 %collective-permute-start.1 = (f32[136,128]{1,0:T(8,128)S(1)}, f32[136,128]{1,0:T(8,128)S(1)}, u32[]{:S(2)}, u32[]{:S(2)}) collective-permute-start(f32[136,128]{1,0:T(8,128)S(1)} %get-tuple-element.28), channel_id=1, source_target_pairs={{0,8},{4,12},{8,0},{12,4},{1,9},{5,13},{9,1},{13,5},{2,10},{6,14},... | collective-permute-start | bytes 208904 | tf_op jit(solution)/shard_map/ppermute | solution.py:273
  5.3 5.5 %collective-permute-start.2 = (f32[136,128]{1,0:T(8,128)S(1)}, f32[136,128]{1,0:T(8,128)S(1)}, u32[]{:S(2)}, u32[]{:S(2)}) collective-permute-start(f32[136,128]{1,0:T(8,128)S(1)} %get-tuple-element.29), channel_id=1, source_target_pairs={{0,12},{4,8},{8,4},{12,0},{1,13},{5,9},{9,5},{13,1},{2,14},{6,10},... | collective-permute-start | bytes 208904 | tf_op jit(solution)/shard_map/ppermute | solution.py:273
  5.5 2.5 %collective-permute-start.3 = (f32[64,128]{1,0:T(8,128)S(1)}, f32[64,128]{1,0:T(8,128)S(1)}, u32[]{:S(2)}, u32[]{:S(2)}) collective-permute-start(f32[64,128]{1,0:T(8,128)S(1)} %get-tuple-element.30.rest_3_), channel_id=1, source_target_pairs={{0,1},{1,0},{2,3},{3,2},{4,5},{5,4},{6,7},{7,6},{8,9},{9,8},{10,11... | collective-permute-start | bytes 98312 | tf_op jit(solution)/shard_map/ppermute | solution.py:273
  11.9 9.9 %collective-permute-start.4 = (f32[16,32,128]{2,1,0:T(8,128)S(1)}, f32[16,32,128]{2,1,0:T(8,128)S(1)}, u32[]{:S(2)}, u32[]{:S(2)}) collective-permute-start(f32[16,32,128]{2,1,0:T(8,128)S(1)} %get-tuple-element.41), channel_id=1, source_target_pairs={{0,4},{4,0},{8,12},{12,8},{1,5},{5,1},{9,13},{13,9},{2,6},{6,2},{1... | collective-permute-start | bytes 786440 | tf_op jit(solution)/shard_map/ppermute | solution.py:273
  12.7 12.2 %collective-permute-start.5 = (f32[16,32,128]{2,1,0:T(8,128)S(1)}, f32[16,32,128]{2,1,0:T(8,128)S(1)}, u32[]{:S(2)}, u32[]{:S(2)}) collective-permute-start(f32[16,32,128]{2,1,0:T(8,128)S(1)} %get-tuple-element.42), channel_id=1, source_target_pairs={{0,8},{4,12},{8,0},{12,4},{1,9},{5,13},{9,1},{13,5},{2,10},{6,14},... | collective-permute-start | bytes 786440 | tf_op jit(solution)/shard_map/ppermute | solution.py:273
  14.8 21.2 %collective-permute-start.6 = (f32[16,32,128]{2,1,0:T(8,128)S(1)}, f32[16,32,128]{2,1,0:T(8,128)S(1)}, u32[]{:S(2)}, u32[]{:S(2)}) collective-permute-start(f32[16,32,128]{2,1,0:T(8,128)S(1)} %get-tuple-element.43), channel_id=1, source_target_pairs={{0,12},{4,8},{8,4},{12,0},{1,13},{5,9},{9,5},{13,1},{2,14},{6,10},... | collective-permute-start | bytes 786440 | tf_op jit(solution)/shard_map/ppermute | solution.py:273
  36.8 5.7 %collective-permute-start.9 = (f32[32,128]{1,0:T(8,128)S(1)}, f32[32,128]{1,0:T(8,128)S(1)}, u32[]{:S(2)}, u32[]{:S(2)}) collective-permute-start(f32[32,128]{1,0:T(8,128)S(1)} %get-tuple-element.44.rest_0_), channel_id=1, source_target_pairs={{0,3},{1,2},{2,1},{3,0},{4,7},{5,6},{6,5},{7,4},{8,11},{9,10},{10,... | collective-permute-start | bytes 49160 | tf_op jit(solution)/shard_map/ppermute | solution.py:273
  40.7 2.6 %collective-permute-start.8 = (f32[32,128]{1,0:T(8,128)S(1)}, f32[32,128]{1,0:T(8,128)S(1)}, u32[]{:S(2)}, u32[]{:S(2)}) collective-permute-start(f32[32,128]{1,0:T(8,128)S(1)} %get-tuple-element.44.rest_0_), channel_id=1, source_target_pairs={{0,2},{1,3},{2,0},{3,1},{4,6},{5,7},{6,4},{7,5},{8,10},{9,11},{10,... | collective-permute-start | bytes 49160 | tf_op jit(solution)/shard_map/ppermute | solution.py:273
  40.9 2.3 %collective-permute-start.7 = (f32[32,128]{1,0:T(8,128)S(1)}, f32[32,128]{1,0:T(8,128)S(1)}, u32[]{:S(2)}, u32[]{:S(2)}) collective-permute-start(f32[32,128]{1,0:T(8,128)S(1)} %get-tuple-element.44.rest_0_), channel_id=1, source_target_pairs={{0,1},{1,0},{2,3},{3,2},{4,5},{5,4},{6,7},{7,6},{8,9},{9,8},{10,11... | collective-permute-start | bytes 49160 | tf_op jit(solution)/shard_map/ppermute | solution.py:273

commit v4 on v3

--- a/solution.py
+++ b/solution.py
@@ -72,7 +72,6 @@
     for copy in copies:
         copy.start()
     for at in range(n):
-        mine_ref[at] = 0
         count[at] = 0
     for at in range(n * CAP):
         source[at] = 0
@@ -80,6 +79,9 @@
     copies[0].wait()
     copies[1].wait()
 
+    wants = [jnp.int32(0)] * n
+    for at in range(n):
+        mine_ref[at] = 0
     for at in range(blocks):
         dest, local = divmod_static(slots[at], span)
         local = divmod_static(local, blocks)[1]
@@ -93,7 +95,14 @@
             place[turn] = local
 
         owner, local = divmod_static(reads[at], span)
-        mine_ref[owner] = mine_ref[owner] | bit_of(divmod_static(local, blocks)[1])
+        bit = bit_of(divmod_static(local, blocks)[1])
+        for other in range(n if n <= 8 else 0):
+            wants[other] = wants[other] | jnp.where(owner == other, bit, 0)
+        if n > 8:
+            mine_ref[owner] = mine_ref[owner] | bit
+    if n <= 8:
+        for at in range(n):
+            mine_ref[at] = wants[at]
     copies[2].wait()
     lane = lax.broadcasted_iota(I32, (8, nodes), 1)
     for k in range(1, n):
@@ -126,7 +135,8 @@
             slope_ref[local] = slope(raw, guess)
 
 
-def serve_kernel(n, rcap, nblk, blk_ref, *rest):
+def serve_kernel(rounds, rcap, nblk, blk_ref, *rest):
+    n = len(rounds) + 1
     arrived, rest = rest[: n - 1], rest[n - 1 :]
     inverses, rest = rest[:nblk], rest[nblk:]
     old_guess, old_slope, guess_ref, slope_ref, whole_ref, *rest = rest
@@ -153,23 +163,26 @@
                 guess_ref[place] = arrived[k - 1][pl.ds(rank * scen, scen), :]
                 slope_ref[place] = arrived[k - 1][pl.ds((CAP + rank) * scen, scen), :]
 
-    for k in range(1, n):
+    for k, out in zip(rounds, outs):
         want = joined(meta[k - 1, 0, 0], meta[k - 1, 0, 1])
         for slot in range(rcap):
-            outs[k - 1][slot] = guess_ref[lowest(want)]
+            out[slot] = guess_ref[lowest(want)]
             want = want & (want - 1)
 
 
-def where_kernel(n, span, rcap, here_ref, reads, mine_ref, _, index_ref):
+def where_kernel(rounds, span, rcap, here_ref, reads, mine_ref, _, index_ref, starts):
     blocks = index_ref.shape[0]
     die = here_ref[0]
+    starts[0] = 0
+    for at, k in enumerate(rounds):
+        starts[k] = at * rcap
 
     def step(at, carry):
         owner, local = divmod_static(reads[at], span)
         local = divmod_static(local, blocks)[1]
         k = owner ^ die
         slot = bits_set(mine_ref[owner] & (bit_of(local) - 1))
-        index_ref[at] = jnp.where(k == 0, local - blocks, (k - 1) * rcap + slot)
+        index_ref[at] = jnp.where(k == 0, local - blocks, starts[k] + slot)
         return carry
 
     lax.fori_loop(0, blocks, step, 0)
@@ -333,8 +346,9 @@
         [SMEM, SMEM, VMEM],
         [VMEM, VMEM],
     )
+    rounds = [*range(2, n), 1]
     guess, slopes, whole, *served = call(
-        functools.partial(serve_kernel, n, rcap, nblk),
+        functools.partial(serve_kernel, rounds, rcap, nblk),
         [block, block, square] + [tiles(rcap)] * (n - 1),
         [blk, *arrived, *inverses, old_guess, old_slope],
         [SMEM] + [VMEM] * (n - 1 + nblk + 2),
@@ -345,13 +359,14 @@
             pltpu.SemaphoreType.DMA,
         ],
     )
-    others = [swap(served[k - 1], "die", n, k) for k in range(1, n)]
+    others = [swap(x, "die", n, k) for x, k in zip(served, rounds)]
     (index,) = call(
-        functools.partial(where_kernel, n, span, rcap),
+        functools.partial(where_kernel, rounds, span, rcap),
         [ints(blocks)],
         [die, reads, mine, guess],
         [SMEM] * 3 + [ANY],
         [SMEM],
+        [pltpu.SMEM((n,), I32)],
     )
     step = 8 if blocks % 8 == 0 else blocks
     wide = pl.BlockSpec((step, scen, nodes), lambda i: (i, 0, 0))

time: 44.9 us -> 44.2 us (0.984); the launches traced: 44.3 us -> 44 us
  starting transfers between devices: 11.6 us -> 10.4 us
  waiting for transfers between devices: 18.4 us -> 19.3 us
    ppermute x10, starting transfers between devices: 11.6 us -> 10.4 us  [swap(): return lax.ppermute(x, axes, [(d, d ^ k) for d in range(n)])]
    ppermute x10, waiting for transfers between devices: 18.4 us -> 19.3 us  [swap(): return lax.ppermute(x, axes, [(d, d ^ k) for d in range(n)])]
  transfers between devices with their start and end apart: 10 -> 10, of which waited for: 6 -> 6; matrix products, arithmetic and copies ran while one was open for 0% -> 0% of each run, Pallas kernels for 19% -> 20%
where the time goes in v4:
time: 44.2 us; the launch traced here: 44 us
  waiting for transfers between devices  19.3 us (44%)
  Pallas kernels  13.6 us (31%)
  starting transfers between devices  10.4 us (24%)
  between operations  0.72 us (2%)
    ppermute x10, waiting for transfers between devices, swap(): return lax.ppermute(x, axes, [(d, d ^ k) for d in range(n)])  19.3 us
    ppermute x10, starting transfers between devices, swap(): return lax.ppermute(x, axes, [(d, d ^ k) for d in range(n)])  10.4 us
    pallas_call x7, Pallas kernels, call(): pl.pallas_call(body, out_shape=outs, in_specs=in_specs, out_specs=out_spe...  8.36 us
    pallas_call x1, Pallas kernels, shards(): pl.pallas_call(local_kernel, grid=(blocks // step,), out_shape=[block, bl...  5.19 us
  transfers between devices with their start and end apart: 10, of which 6 were waited for; matrix products, arithmetic and copies ran while one was open for 0% of the time, Pallas kernels for 20%

profile of v4, /device:TPU:9, one launch (start us, length us, event | category | flops | bytes accessed | tf_op | source)
XLA Modules:
  0.0 44.0 jit_solution(9162469187285657711)
XLA Ops:
  0.6 2.1 %shard_map.113 = (s32[32]{0:T(128)S(1)}, s32[32]{0:T(128)S(1)}, s32[4]{0:T(128)S(1)}, f32[32,3,32,128]{3,2,1,0:T(8,128)S(1)}, f32[64,128]{1,0:T(8,128)S(1)}, /*i...) custom-call(s32[1]{0:T(128)} %bitcast.here_ref, s32[32]{0:T(128)} %new_slot_ref.1, ...), custom_call_target="tpu_custom_call" | custom-call | tf_op jit(solution)/shard_map/pallas_call | solution.py:270
  2.7 0.1 collective-permute-start
  2.8 2.5 %collective-permute-start.1 = (f32[136,128]{1,0:T(8,128)S(1)}, f32[136,128]{1,0:T(8,128)S(1)}, u32[]{:S(2)}, u32[]{:S(2)}) collective-permute-start(f32[136,128]{1,0:T(8,128)S(1)} %get-tuple-element.28), channel_id=1, source_target_pairs={{0,8},{4,12},{8,0},{12,4},{1,9},{5,13},{9,1},{13,5},{2,10},{6,14},... | collective-permute-start | bytes 208904 | tf_op jit(solution)/shard_map/ppermute | solution.py:286
  5.3 0.2 collective-permute-start.2
  5.5 1.5 %collective-permute-start.3 = (f32[64,128]{1,0:T(8,128)S(1)}, f32[64,128]{1,0:T(8,128)S(1)}, u32[]{:S(2)}, u32[]{:S(2)}) collective-permute-start(f32[64,128]{1,0:T(8,128)S(1)} %get-tuple-element.30.rest_3_), channel_id=1, source_target_pairs={{0,1},{1,0},{2,3},{3,2},{4,5},{5,4},{6,7},{7,6},{8,9},{9,8},{10,11... | collective-permute-start | bytes 98312 | tf_op jit(solution)/shard_map/ppermute | solution.py:286
  7.0 0.9 %shard_map.114 = (f32[32,32,128]{2,1,0:T(8,128)S(1)}, f32[32,32,128]{2,1,0:T(8,128)S(1)}) custom-call(s32[1]{0:T(128)} %bitcast.here_ref, s32[32]{0:T(128)S(1)} %get-tuple-element.31.slots, f32[32,3,32,128]{3,2,1,0:T(8,128)S(1)} %get-tuple-element.32.raw_ref), custom_call_target="tpu_custom_call" | custom-call | tf_op jit(solution)/shard_map/pallas_call | solution.py:270
  7.9 0.0 collective-permute-done.3.rest_4_
  7.9 0.0 collective-permute-done.rest_0_
  7.9 0.1 collective-permute-done.1.rest_1_
  8.1 2.7 %collective-permute-done.2.rest_2_ = f32[136,128]{1,0:T(8,128)S(1)} collective-permute-done((f32[136,128]{1,0:T(8,128)S(1)}, f32[136,128]{1,0:T(8,128)S(1)}, u32[]{:S(2)}, u32[]{:S(2)}) %collective-permute-start.2) | collective-permute-done | bytes 69664 | tf_op jit(solution)/shard_map/ppermute | solution.py:286
  10.8 1.1 %shard_map.115 = (f32[32,32,128]{2,1,0:T(8,128)S(1)}, f32[32,32,128]{2,1,0:T(8,128)S(1)}, f32[128,128]{1,0:T(8,128)S(1)}, f32[16,32,128]{2,1,0:T(8,128)S(1)}, f3...) custom-call(s32[1]{0:T(128)} %bitcast.2.blk_ref, f32[136,128]{1,0:T(8,128)S(1)} %collective-permute-done.rest_0_, ...), custom_call_target="tpu_custom_call" | custom-call | tf_op jit(solution)/shard_map/pallas_call | solution.py:270
  11.9 0.6 %collective-permute-start.4 = (f32[16,32,128]{2,1,0:T(8,128)S(1)}, f32[16,32,128]{2,1,0:T(8,128)S(1)}, u32[]{:S(2)}, u32[]{:S(2)}) collective-permute-start(f32[16,32,128]{2,1,0:T(8,128)S(1)} %get-tuple-element.41), channel_id=1, source_target_pairs={{0,8},{4,12},{8,0},{12,4},{1,9},{5,13},{9,1},{13,5},{2,10},{6,14},... | collective-permute-start | bytes 786440 | tf_op jit(solution)/shard_map/ppermute | solution.py:286
  12.4 1.5 %collective-permute-start.5 = (f32[16,32,128]{2,1,0:T(8,128)S(1)}, f32[16,32,128]{2,1,0:T(8,128)S(1)}, u32[]{:S(2)}, u32[]{:S(2)}) collective-permute-start(f32[16,32,128]{2,1,0:T(8,128)S(1)} %get-tuple-element.42), channel_id=1, source_target_pairs={{0,12},{4,8},{8,4},{12,0},{1,13},{5,9},{9,5},{13,1},{2,14},{6,10},... | collective-permute-start | bytes 786440 | tf_op jit(solution)/shard_map/ppermute | solution.py:286
  13.9 1.6 %collective-permute-start.6 = (f32[16,32,128]{2,1,0:T(8,128)S(1)}, f32[16,32,128]{2,1,0:T(8,128)S(1)}, u32[]{:S(2)}, u32[]{:S(2)}) collective-permute-start(f32[16,32,128]{2,1,0:T(8,128)S(1)} %get-tuple-element.43), channel_id=1, source_target_pairs={{0,4},{4,0},{8,12},{12,8},{1,5},{5,1},{9,13},{13,9},{2,6},{6,2},{1... | collective-permute-start | bytes 786440 | tf_op jit(solution)/shard_map/ppermute | solution.py:286
  15.5 1.7 %shard_map.116.index_ref = s32[32]{0:T(128)S(1)} custom-call(s32[1]{0:T(128)} %bitcast.here_ref, s32[32]{0:T(128)S(1)} %get-tuple-element.25.reads, s32[4]{0:T(128)S(1)} %get-tuple-element.26.mine_ref, f32[32,32,128]{2,1,0:T(8,128)S(1)} %get-tuple-element.35._.guess_ref), custom_call_target="tpu_custom_call" | custom-call | tf_op jit(solution)/shard_map/pallas_call | solution.py:270
  17.2 5.2 %shard_map.117 = (f32[32,32,128]{2,1,0:T(8,128)S(1)}, f32[32,32,128]{2,1,0:T(8,128)S(1)}, f32[32,32,128]{2,1,0:T(8,128)S(1)}, f32[32,128]{1,0:T(8,128)S(1)}) custom-call(f32[32,32,128]{2,1,0:T(8,128)S(1)} %get-tuple-element.35._.guess_ref, f32[32,32,128]{2,1,0:T(8,128)S(1)} %get-tuple-element.36.slope_ref, f32[32,128,128]{2,1,0:T(8,128)} %coupling_ref.1, ...), custom_call_target="tpu_custom_call" | custom-call | tf_op jit(solution)/shard_map/pallas_call | solution.py:374
  22.4 3.5 %collective-permute-done.4.rest_0_ = f32[16,32,128]{2,1,0:T(8,128)S(1)} collective-permute-done((f32[16,32,128]{2,1,0:T(8,128)S(1)}, f32[16,32,128]{2,1,0:T(8,128)S(1)}, u32[]{:S(2)}, u32[]{:S(2)}) %collective-permute-start.4) | collective-permute-done | bytes 262176 | tf_op jit(solution)/shard_map/ppermute | solution.py:286
  25.9 11.2 %collective-permute-done.5.rest_1_ = f32[16,32,128]{2,1,0:T(8,128)S(1)} collective-permute-done((f32[16,32,128]{2,1,0:T(8,128)S(1)}, f32[16,32,128]{2,1,0:T(8,128)S(1)}, u32[]{:S(2)}, u32[]{:S(2)}) %collective-permute-start.5) | collective-permute-done | bytes 262176 | tf_op jit(solution)/shard_map/ppermute | solution.py:286
  37.1 0.0 collective-permute-done.6.rest_2_
  37.1 0.8 %shard_map.118 = (f32[32,32,128]{2,1,0:T(8,128)S(1)}, f32[32,128]{1,0:T(8,128)S(1)}, f32[32,32,128]{2,1,0:T(8,128)S(1)}) custom-call(s32[32]{0:T(128)S(1)} %shard_map.116.index_ref, f32[32,32,128]{2,1,0:T(8,128)S(1)} %get-tuple-element.37.base_ref, f32[32,32,128]{2,1,0:T(8,128)S(1)} %get-tuple-element.38.inv_ref, ...), custom_call_target="tpu_custom_call" | custom-call | tf_op jit(solution)/shard_map/pallas_call | solution.py:270
  37.8 2.1 %collective-permute-start.9 = (f32[32,128]{1,0:T(8,128)S(1)}, f32[32,128]{1,0:T(8,128)S(1)}, u32[]{:S(2)}, u32[]{:S(2)}) collective-permute-start(f32[32,128]{1,0:T(8,128)S(1)} %get-tuple-element.44.rest_0_), channel_id=1, source_target_pairs={{0,3},{1,2},{2,1},{3,0},{4,7},{5,6},{6,5},{7,4},{8,11},{9,10},{10,... | collective-permute-start | bytes 49160 | tf_op jit(solution)/shard_map/ppermute | solution.py:286
  40.0 0.3 collective-permute-start.8
  40.2 0.2 collective-permute-start.7
  40.5 0.8 %shard_map.120 = f32[32,32,128]{2,1,0:T(8,128)} custom-call(f32[32,32,128]{2,1,0:T(8,128)S(1)} %get-tuple-element.47.value_ref), custom_call_target="tpu_custom_call" | custom-call | tf_op jit(solution)/shard_map/pallas_call | solution.py:270
  41.3 0.5 %collective-permute-done.9.rest_3_ = f32[32,128]{1,0:T(8,128)S(1)} collective-permute-done((f32[32,128]{1,0:T(8,128)S(1)}, f32[32,128]{1,0:T(8,128)S(1)}, u32[]{:S(2)}, u32[]{:S(2)}) %collective-permute-start.9) | collective-permute-done | bytes 16416 | tf_op jit(solution)/shard_map/ppermute | solution.py:286
  41.8 1.2 %collective-permute-done.8.rest_2_ = f32[32,128]{1,0:T(8,128)S(1)} collective-permute-done((f32[32,128]{1,0:T(8,128)S(1)}, f32[32,128]{1,0:T(8,128)S(1)}, u32[]{:S(2)}, u32[]{:S(2)}) %collective-permute-start.8) | collective-permute-done | bytes 16416 | tf_op jit(solution)/shard_map/ppermute | solution.py:286
  43.0 0.0 collective-permute-done.7.rest_1_
  43.0 1.0 %shard_map.119 = f32[32,32,128]{2,1,0:T(8,128)} custom-call(f32[32,128]{1,0:T(8,128)S(1)} %get-tuple-element.44.rest_0_, f32[32,128]{1,0:T(8,128)S(1)} %collective-permute-done.7.rest_1_, f32[32,128]{1,0:T(8,128)S(1)} %collective-permute-done.8.rest_2_, f32[32,128]{1,0:T(8,128)S(1)} %collective-permute-done.9.rest_3_, ...), custom_call_target="tpu_custom_call" | custom-call | tf_op jit(solution)/shard_map/pallas_call | solution.py:270
Async XLA Ops:
  2.7 5.2 %collective-permute-start = (f32[136,128]{1,0:T(8,128)S(1)}, f32[136,128]{1,0:T(8,128)S(1)}, u32[]{:S(2)}, u32[]{:S(2)}) collective-permute-start(f32[136,128]{1,0:T(8,128)S(1)} %get-tuple-element.27), channel_id=1, source_target_pairs={{0,4},{4,0},{8,12},{12,8},{1,5},{5,1},{9,13},{13,9},{2,6},{6,2},{1... | collective-permute-start | bytes 208904 | tf_op jit(solution)/shard_map/ppermute | solution.py:286
  2.8 5.2 %collective-permute-start.1 = (f32[136,128]{1,0:T(8,128)S(1)}, f32[136,128]{1,0:T(8,128)S(1)}, u32[]{:S(2)}, u32[]{:S(2)}) collective-permute-start(f32[136,128]{1,0:T(8,128)S(1)} %get-tuple-element.28), channel_id=1, source_target_pairs={{0,8},{4,12},{8,0},{12,4},{1,9},{5,13},{9,1},{13,5},{2,10},{6,14},... | collective-permute-start | bytes 208904 | tf_op jit(solution)/shard_map/ppermute | solution.py:286
  5.3 5.5 %collective-permute-start.2 = (f32[136,128]{1,0:T(8,128)S(1)}, f32[136,128]{1,0:T(8,128)S(1)}, u32[]{:S(2)}, u32[]{:S(2)}) collective-permute-start(f32[136,128]{1,0:T(8,128)S(1)} %get-tuple-element.29), channel_id=1, source_target_pairs={{0,12},{4,8},{8,4},{12,0},{1,13},{5,9},{9,5},{13,1},{2,14},{6,10},... | collective-permute-start | bytes 208904 | tf_op jit(solution)/shard_map/ppermute | solution.py:286
  5.5 2.5 %collective-permute-start.3 = (f32[64,128]{1,0:T(8,128)S(1)}, f32[64,128]{1,0:T(8,128)S(1)}, u32[]{:S(2)}, u32[]{:S(2)}) collective-permute-start(f32[64,128]{1,0:T(8,128)S(1)} %get-tuple-element.30.rest_3_), channel_id=1, source_target_pairs={{0,1},{1,0},{2,3},{3,2},{4,5},{5,4},{6,7},{7,6},{8,9},{9,8},{10,11... | collective-permute-start | bytes 98312 | tf_op jit(solution)/shard_map/ppermute | solution.py:286
  11.9 14.0 %collective-permute-start.4 = (f32[16,32,128]{2,1,0:T(8,128)S(1)}, f32[16,32,128]{2,1,0:T(8,128)S(1)}, u32[]{:S(2)}, u32[]{:S(2)}) collective-permute-start(f32[16,32,128]{2,1,0:T(8,128)S(1)} %get-tuple-element.41), channel_id=1, source_target_pairs={{0,8},{4,12},{8,0},{12,4},{1,9},{5,13},{9,1},{13,5},{2,10},{6,14},... | collective-permute-start | bytes 786440 | tf_op jit(solution)/shard_map/ppermute | solution.py:286
  12.4 24.6 %collective-permute-start.5 = (f32[16,32,128]{2,1,0:T(8,128)S(1)}, f32[16,32,128]{2,1,0:T(8,128)S(1)}, u32[]{:S(2)}, u32[]{:S(2)}) collective-permute-start(f32[16,32,128]{2,1,0:T(8,128)S(1)} %get-tuple-element.42), channel_id=1, source_target_pairs={{0,12},{4,8},{8,4},{12,0},{1,13},{5,9},{9,5},{13,1},{2,14},{6,10},... | collective-permute-start | bytes 786440 | tf_op jit(solution)/shard_map/ppermute | solution.py:286
  13.9 23.2 %collective-permute-start.6 = (f32[16,32,128]{2,1,0:T(8,128)S(1)}, f32[16,32,128]{2,1,0:T(8,128)S(1)}, u32[]{:S(2)}, u32[]{:S(2)}) collective-permute-start(f32[16,32,128]{2,1,0:T(8,128)S(1)} %get-tuple-element.43), channel_id=1, source_target_pairs={{0,4},{4,0},{8,12},{12,8},{1,5},{5,1},{9,13},{13,9},{2,6},{6,2},{1... | collective-permute-start | bytes 786440 | tf_op jit(solution)/shard_map/ppermute | solution.py:286
  37.8 3.9 %collective-permute-start.9 = (f32[32,128]{1,0:T(8,128)S(1)}, f32[32,128]{1,0:T(8,128)S(1)}, u32[]{:S(2)}, u32[]{:S(2)}) collective-permute-start(f32[32,128]{1,0:T(8,128)S(1)} %get-tuple-element.44.rest_0_), channel_id=1, source_target_pairs={{0,3},{1,2},{2,1},{3,0},{4,7},{5,6},{6,5},{7,4},{8,11},{9,10},{10,... | collective-permute-start | bytes 49160 | tf_op jit(solution)/shard_map/ppermute | solution.py:286
  40.0 3.0 %collective-permute-start.8 = (f32[32,128]{1,0:T(8,128)S(1)}, f32[32,128]{1,0:T(8,128)S(1)}, u32[]{:S(2)}, u32[]{:S(2)}) collective-permute-start(f32[32,128]{1,0:T(8,128)S(1)} %get-tuple-element.44.rest_0_), channel_id=1, source_target_pairs={{0,2},{1,3},{2,0},{3,1},{4,6},{5,7},{6,4},{7,5},{8,10},{9,11},{10,... | collective-permute-start | bytes 49160 | tf_op jit(solution)/shard_map/ppermute | solution.py:286
  40.2 2.8 %collective-permute-start.7 = (f32[32,128]{1,0:T(8,128)S(1)}, f32[32,128]{1,0:T(8,128)S(1)}, u32[]{:S(2)}, u32[]{:S(2)}) collective-permute-start(f32[32,128]{1,0:T(8,128)S(1)} %get-tuple-element.44.rest_0_), channel_id=1, source_target_pairs={{0,1},{1,0},{2,3},{3,2},{4,5},{5,4},{6,7},{7,6},{8,9},{9,8},{10,11... | collective-permute-start | bytes 49160 | tf_op jit(solution)/shard_map/ppermute | solution.py:286

commit v5 on v4

--- a/solution.py
+++ b/solution.py
@@ -37,7 +37,7 @@
 
 
 def lowest(mask):
-    return bits_set((mask & -mask) - 1) & 31
+    return (31 - lax.clz(mask & -mask)) & 31
 
 
 def halves(mask):
@@ -57,18 +57,25 @@
 
 
 def leave_kernel(
-    n, span, here_ref, new_slot_ref, partner_ref, history_ref, rows_ref,
+    rounds, span, here_ref, new_slot_ref, partner_ref, history_ref, rows_ref,
     slots, reads, mine_ref, raw_ref, inverse_ref, *rest
 ):
+    n = len(rounds) + 1
     outs, (source, place, count, sems) = rest[: n - 1], rest[n - 1 :]
     blocks, _, scen, nodes = history_ref.shape
+    pieces = 4 if blocks % 4 == 0 else 1
+    piece = blocks // pieces
     die = here_ref[0]
     copies = [
         pltpu.make_async_copy(new_slot_ref, slots, sems.at[0]),
         pltpu.make_async_copy(partner_ref, reads, sems.at[1]),
-        pltpu.make_async_copy(history_ref, raw_ref, sems.at[2]),
-        pltpu.make_async_copy(rows_ref, inverse_ref, sems.at[3]),
+        pltpu.make_async_copy(rows_ref, inverse_ref, sems.at[2]),
     ]
+    for at in range(pieces):
+        some = pl.ds(at * piece, piece)
+        copies.append(
+            pltpu.make_async_copy(history_ref.at[some], raw_ref.at[some], sems.at[3 + at])
+        )
     for copy in copies:
         copy.start()
     for at in range(n):
@@ -103,10 +110,10 @@
     if n <= 8:
         for at in range(n):
             mine_ref[at] = wants[at]
-    copies[2].wait()
+    for copy in copies[2:]:
+        copy.wait()
     lane = lax.broadcasted_iota(I32, (8, nodes), 1)
-    for k in range(1, n):
-        out = outs[k - 1]
+    for k, out in zip(rounds, outs):
         for rank in range(CAP):
             raw = raw_ref.at[source[k * CAP + rank]]
             guess = predict(raw)
@@ -118,7 +125,6 @@
         for j, value in enumerate(values):
             row = jnp.where(lane == j, value, row)
         out[pl.ds(2 * CAP * scen, 8), :] = row.astype(F32)
-    copies[3].wait()
 
 
 def place_kernel(span, here_ref, slots, raw_ref, guess_ref, slope_ref):
@@ -135,15 +141,14 @@
             slope_ref[local] = slope(raw, guess)
 
 
-def serve_kernel(rounds, rcap, nblk, blk_ref, *rest):
-    n = len(rounds) + 1
+def serve_kernel(n, rcap, nblk, blk_ref, *rest):
     arrived, rest = rest[: n - 1], rest[n - 1 :]
     inverses, rest = rest[:nblk], rest[nblk:]
     old_guess, old_slope, guess_ref, slope_ref, whole_ref, *rest = rest
     outs, (ints, meta, sem) = rest[: n - 1], rest[n - 1 :]
     blocks, scen, nodes = guess_ref.shape
-    for k in range(1, n):
-        ints[k - 1] = arrived[k - 1][pl.ds(2 * CAP * scen, 8), :].astype(I32)
+    for k in range(n - 1):
+        ints[k] = arrived[k][pl.ds(2 * CAP * scen, 8), :].astype(I32)
     copy = pltpu.make_async_copy(ints, meta, sem)
     copy.start()
     for at in range(blocks):
@@ -154,17 +159,17 @@
         at = pl.multiple_of((blk_ref[0] ^ k) * height, height)
         whole_ref[pl.ds(at, height), :] = inverses[k][...]
     copy.wait()
-    for k in range(1, n):
+    for k in range(n - 1):
         for rank in range(CAP):
-            place = meta[k - 1, 0, 2 + rank]
+            place = meta[k, 0, 2 + rank]
 
             @pl.when(place >= 0)
             def _(k=k, rank=rank, place=place):
-                guess_ref[place] = arrived[k - 1][pl.ds(rank * scen, scen), :]
-                slope_ref[place] = arrived[k - 1][pl.ds((CAP + rank) * scen, scen), :]
-
-    for k, out in zip(rounds, outs):
-        want = joined(meta[k - 1, 0, 0], meta[k - 1, 0, 1])
+                guess_ref[place] = arrived[k][pl.ds(rank * scen, scen), :]
+                slope_ref[place] = arrived[k][pl.ds((CAP + rank) * scen, scen), :]
+
+    for k, out in enumerate(outs):
+        want = joined(meta[k, 0, 0], meta[k, 0, 1])
         for slot in range(rcap):
             out[slot] = guess_ref[lowest(want)]
             want = want & (want - 1)
@@ -321,8 +326,9 @@
     rows = region_inverse[0]
     message = jax.ShapeDtypeStruct((2 * CAP * scen + 8, nodes), F32)
 
+    rounds = [*range(2, n), 1]
     slots, reads, mine, raw, rows, *leaving = call(
-        functools.partial(leave_kernel, n, span),
+        functools.partial(leave_kernel, rounds, span),
         [
             ints(blocks),
             ints(blocks),
@@ -335,9 +341,9 @@
         [SMEM] + [HBM] * 4,
         [SMEM] * 3 + [VMEM] * (n + 1),
         [pltpu.SMEM((n * CAP,), I32)] * 2
-        + [pltpu.SMEM((n,), I32), pltpu.SemaphoreType.DMA((4,))],
-    )
-    arrived = [swap(leaving[k - 1], "die", n, k) for k in range(1, n)]
+        + [pltpu.SMEM((n,), I32), pltpu.SemaphoreType.DMA((7,))],
+    )
+    arrived = [swap(x, "die", n, k) for x, k in zip(leaving, rounds)]
     inverses = [rows] + [swap(rows, "blk", nblk, k) for k in range(1, nblk)]
     old_guess, old_slope = call(
         functools.partial(place_kernel, span),
@@ -346,9 +352,8 @@
         [SMEM, SMEM, VMEM],
         [VMEM, VMEM],
     )
-    rounds = [*range(2, n), 1]
     guess, slopes, whole, *served = call(
-        functools.partial(serve_kernel, rounds, rcap, nblk),
+        functools.partial(serve_kernel, n, rcap, nblk),
         [block, block, square] + [tiles(rcap)] * (n - 1),
         [blk, *arrived, *inverses, old_guess, old_slope],
         [SMEM] + [VMEM] * (n - 1 + nblk + 2),

time: 44.2 us -> 44.5 us (level)
  starting transfers between devices: 10.4 us -> 11.1 us
    ppermute x10, starting transfers between devices: 10.4 us -> 11.1 us  [swap(): return lax.ppermute(x, axes, [(d, d ^ k) for d in range(n)])]
  transfers between devices with their start and end apart: 10 -> 10, of which waited for: 6 -> 6; matrix products, arithmetic and copies ran while one was open for 0% -> 0% of each run, Pallas kernels for 20% -> 19%
where the time goes in v5:
time: 44.5 us; the launch traced here: 44.3 us
  waiting for transfers between devices  19.2 us (43%)
  Pallas kernels  13.4 us (30%)
  starting transfers between devices  11.1 us (25%)
  between operations  0.7 us (2%)
    ppermute x10, waiting for transfers between devices, swap(): return lax.ppermute(x, axes, [(d, d ^ k) for d in range(n)])  19.2 us
    ppermute x10, starting transfers between devices, swap(): return lax.ppermute(x, axes, [(d, d ^ k) for d in range(n)])  11.1 us
    pallas_call x7, Pallas kernels, call(): pl.pallas_call(body, out_shape=outs, in_specs=in_specs, out_specs=out_spe...  8.16 us
    pallas_call x1, Pallas kernels, shards(): pl.pallas_call(local_kernel, grid=(blocks // step,), out_shape=[block, bl...  5.19 us
  transfers between devices with their start and end apart: 10, of which 6 were waited for; matrix products, arithmetic and copies ran while one was open for 0% of the time, Pallas kernels for 19%

profile of v5, /device:TPU:9, one launch (start us, length us, event | category | flops | bytes accessed | tf_op | source)
XLA Modules:
  0.0 44.3 jit_solution(10980748459536255266)
XLA Ops:
  0.6 2.1 %shard_map.113 = (s32[32]{0:T(128)S(1)}, s32[32]{0:T(128)S(1)}, s32[4]{0:T(128)S(1)}, f32[32,3,32,128]{3,2,1,0:T(8,128)S(1)}, f32[64,128]{1,0:T(8,128)S(1)}, /*i...) custom-call(s32[1]{0:T(128)} %bitcast.here_ref, s32[32]{0:T(128)} %new_slot_ref.1, ...), custom_call_target="tpu_custom_call" | custom-call | tf_op jit(solution)/shard_map/pallas_call | solution.py:275
  2.7 2.4 %collective-permute-start = (f32[136,128]{1,0:T(8,128)S(1)}, f32[136,128]{1,0:T(8,128)S(1)}, u32[]{:S(2)}, u32[]{:S(2)}) collective-permute-start(f32[136,128]{1,0:T(8,128)S(1)} %get-tuple-element.27), channel_id=1, source_target_pairs={{0,8},{4,12},{8,0},{12,4},{1,9},{5,13},{9,1},{13,5},{2,10},{6,14},... | collective-permute-start | bytes 208904 | tf_op jit(solution)/shard_map/ppermute | solution.py:291
  5.1 0.0 collective-permute-start.1
  5.1 1.3 %collective-permute-start.2 = (f32[136,128]{1,0:T(8,128)S(1)}, f32[136,128]{1,0:T(8,128)S(1)}, u32[]{:S(2)}, u32[]{:S(2)}) collective-permute-start(f32[136,128]{1,0:T(8,128)S(1)} %get-tuple-element.29), channel_id=1, source_target_pairs={{0,4},{4,0},{8,12},{12,8},{1,5},{5,1},{9,13},{13,9},{2,6},{6,2},{1... | collective-permute-start | bytes 208904 | tf_op jit(solution)/shard_map/ppermute | solution.py:291
  6.3 1.5 %collective-permute-start.3 = (f32[64,128]{1,0:T(8,128)S(1)}, f32[64,128]{1,0:T(8,128)S(1)}, u32[]{:S(2)}, u32[]{:S(2)}) collective-permute-start(f32[64,128]{1,0:T(8,128)S(1)} %get-tuple-element.30.rest_3_), channel_id=1, source_target_pairs={{0,1},{1,0},{2,3},{3,2},{4,5},{5,4},{6,7},{7,6},{8,9},{9,8},{10,11... | collective-permute-start | bytes 98312 | tf_op jit(solution)/shard_map/ppermute | solution.py:291
  7.8 0.9 %shard_map.114 = (f32[32,32,128]{2,1,0:T(8,128)S(1)}, f32[32,32,128]{2,1,0:T(8,128)S(1)}) custom-call(s32[1]{0:T(128)} %bitcast.here_ref, s32[32]{0:T(128)S(1)} %get-tuple-element.31.slots, f32[32,3,32,128]{3,2,1,0:T(8,128)S(1)} %get-tuple-element.32.raw_ref), custom_call_target="tpu_custom_call" | custom-call | tf_op jit(solution)/shard_map/pallas_call | solution.py:275
  8.8 0.0 collective-permute-done.3.rest_4_
  8.8 0.3 collective-permute-done.rest_0_
  9.1 2.1 %collective-permute-done.1.rest_1_ = f32[136,128]{1,0:T(8,128)S(1)} collective-permute-done((f32[136,128]{1,0:T(8,128)S(1)}, f32[136,128]{1,0:T(8,128)S(1)}, u32[]{:S(2)}, u32[]{:S(2)}) %collective-permute-start.1) | collective-permute-done | bytes 69664 | tf_op jit(solution)/shard_map/ppermute | solution.py:291
  11.2 0.0 collective-permute-done.2.rest_2_
  11.2 0.9 %shard_map.115 = (f32[32,32,128]{2,1,0:T(8,128)S(1)}, f32[32,32,128]{2,1,0:T(8,128)S(1)}, f32[128,128]{1,0:T(8,128)S(1)}, f32[16,32,128]{2,1,0:T(8,128)S(1)}, f3...) custom-call(s32[1]{0:T(128)} %bitcast.2.blk_ref, f32[136,128]{1,0:T(8,128)S(1)} %collective-permute-done.rest_0_, ...), custom_call_target="tpu_custom_call" | custom-call | tf_op jit(solution)/shard_map/pallas_call | solution.py:275
  12.1 1.9 %collective-permute-start.4 = (f32[16,32,128]{2,1,0:T(8,128)S(1)}, f32[16,32,128]{2,1,0:T(8,128)S(1)}, u32[]{:S(2)}, u32[]{:S(2)}) collective-permute-start(f32[16,32,128]{2,1,0:T(8,128)S(1)} %get-tuple-element.41), channel_id=1, source_target_pairs={{0,8},{4,12},{8,0},{12,4},{1,9},{5,13},{9,1},{13,5},{2,10},{6,14},... | collective-permute-start | bytes 786440 | tf_op jit(solution)/shard_map/ppermute | solution.py:291
  14.0 0.4 collective-permute-start.5
  14.4 1.3 %collective-permute-start.6 = (f32[16,32,128]{2,1,0:T(8,128)S(1)}, f32[16,32,128]{2,1,0:T(8,128)S(1)}, u32[]{:S(2)}, u32[]{:S(2)}) collective-permute-start(f32[16,32,128]{2,1,0:T(8,128)S(1)} %get-tuple-element.43), channel_id=1, source_target_pairs={{0,4},{4,0},{8,12},{12,8},{1,5},{5,1},{9,13},{13,9},{2,6},{6,2},{1... | collective-permute-start | bytes 786440 | tf_op jit(solution)/shard_map/ppermute | solution.py:291
  15.7 1.7 %shard_map.116.index_ref = s32[32]{0:T(128)S(1)} custom-call(s32[1]{0:T(128)} %bitcast.here_ref, s32[32]{0:T(128)S(1)} %get-tuple-element.25.reads, s32[4]{0:T(128)S(1)} %get-tuple-element.26.mine_ref, f32[32,32,128]{2,1,0:T(8,128)S(1)} %get-tuple-element.35._.guess_ref), custom_call_target="tpu_custom_call" | custom-call | tf_op jit(solution)/shard_map/pallas_call | solution.py:275
  17.4 5.2 %shard_map.117 = (f32[32,32,128]{2,1,0:T(8,128)S(1)}, f32[32,32,128]{2,1,0:T(8,128)S(1)}, f32[32,32,128]{2,1,0:T(8,128)S(1)}, f32[32,128]{1,0:T(8,128)S(1)}) custom-call(f32[32,32,128]{2,1,0:T(8,128)S(1)} %get-tuple-element.35._.guess_ref, f32[32,32,128]{2,1,0:T(8,128)S(1)} %get-tuple-element.36.slope_ref, f32[32,128,128]{2,1,0:T(8,128)} %coupling_ref.1, ...), custom_call_target="tpu_custom_call" | custom-call | tf_op jit(solution)/shard_map/pallas_call | solution.py:379
  22.6 7.4 %collective-permute-done.4.rest_0_ = f32[16,32,128]{2,1,0:T(8,128)S(1)} collective-permute-done((f32[16,32,128]{2,1,0:T(8,128)S(1)}, f32[16,32,128]{2,1,0:T(8,128)S(1)}, u32[]{:S(2)}, u32[]{:S(2)}) %collective-permute-start.4) | collective-permute-done | bytes 262176 | tf_op jit(solution)/shard_map/ppermute | solution.py:291
  30.0 7.8 %collective-permute-done.5.rest_1_ = f32[16,32,128]{2,1,0:T(8,128)S(1)} collective-permute-done((f32[16,32,128]{2,1,0:T(8,128)S(1)}, f32[16,32,128]{2,1,0:T(8,128)S(1)}, u32[]{:S(2)}, u32[]{:S(2)}) %collective-permute-start.5) | collective-permute-done | bytes 262176 | tf_op jit(solution)/shard_map/ppermute | solution.py:291
  37.8 0.0 collective-permute-done.6.rest_2_
  37.8 0.8 %shard_map.118 = (f32[32,32,128]{2,1,0:T(8,128)S(1)}, f32[32,128]{1,0:T(8,128)S(1)}, f32[32,32,128]{2,1,0:T(8,128)S(1)}) custom-call(s32[32]{0:T(128)S(1)} %shard_map.116.index_ref, f32[32,32,128]{2,1,0:T(8,128)S(1)} %get-tuple-element.37.base_ref, f32[32,32,128]{2,1,0:T(8,128)S(1)} %get-tuple-element.38.inv_ref, ...), custom_call_target="tpu_custom_call" | custom-call | tf_op jit(solution)/shard_map/pallas_call | solution.py:275
  38.6 1.8 %collective-permute-start.9 = (f32[32,128]{1,0:T(8,128)S(1)}, f32[32,128]{1,0:T(8,128)S(1)}, u32[]{:S(2)}, u32[]{:S(2)}) collective-permute-start(f32[32,128]{1,0:T(8,128)S(1)} %get-tuple-element.44.rest_0_), channel_id=1, source_target_pairs={{0,3},{1,2},{2,1},{3,0},{4,7},{5,6},{6,5},{7,4},{8,11},{9,10},{10,... | collective-permute-start | bytes 49160 | tf_op jit(solution)/shard_map/ppermute | solution.py:291
  40.4 0.3 collective-permute-start.8
  40.7 0.2 collective-permute-start.7
  40.9 0.8 %shard_map.120 = f32[32,32,128]{2,1,0:T(8,128)} custom-call(f32[32,32,128]{2,1,0:T(8,128)S(1)} %get-tuple-element.47.value_ref), custom_call_target="tpu_custom_call" | custom-call | tf_op jit(solution)/shard_map/pallas_call | solution.py:275
  41.7 0.5 %collective-permute-done.9.rest_3_ = f32[32,128]{1,0:T(8,128)S(1)} collective-permute-done((f32[32,128]{1,0:T(8,128)S(1)}, f32[32,128]{1,0:T(8,128)S(1)}, u32[]{:S(2)}, u32[]{:S(2)}) %collective-permute-start.9) | collective-permute-done | bytes 16416 | tf_op jit(solution)/shard_map/ppermute | solution.py:291
  42.2 1.1 %collective-permute-done.8.rest_2_ = f32[32,128]{1,0:T(8,128)S(1)} collective-permute-done((f32[32,128]{1,0:T(8,128)S(1)}, f32[32,128]{1,0:T(8,128)S(1)}, u32[]{:S(2)}, u32[]{:S(2)}) %collective-permute-start.8) | collective-permute-done | bytes 16416 | tf_op jit(solution)/shard_map/ppermute | solution.py:291
  43.3 0.0 collective-permute-done.7.rest_1_
  43.3 1.0 %shard_map.119 = f32[32,32,128]{2,1,0:T(8,128)} custom-call(f32[32,128]{1,0:T(8,128)S(1)} %get-tuple-element.44.rest_0_, f32[32,128]{1,0:T(8,128)S(1)} %collective-permute-done.7.rest_1_, f32[32,128]{1,0:T(8,128)S(1)} %collective-permute-done.8.rest_2_, f32[32,128]{1,0:T(8,128)S(1)} %collective-permute-done.9.rest_3_, ...), custom_call_target="tpu_custom_call" | custom-call | tf_op jit(solution)/shard_map/pallas_call | solution.py:275
Async XLA Ops:
  2.7 6.4 %collective-permute-start = (f32[136,128]{1,0:T(8,128)S(1)}, f32[136,128]{1,0:T(8,128)S(1)}, u32[]{:S(2)}, u32[]{:S(2)}) collective-permute-start(f32[136,128]{1,0:T(8,128)S(1)} %get-tuple-element.27), channel_id=1, source_target_pairs={{0,8},{4,12},{8,0},{12,4},{1,9},{5,13},{9,1},{13,5},{2,10},{6,14},... | collective-permute-start | bytes 208904 | tf_op jit(solution)/shard_map/ppermute | solution.py:291
  5.1 6.1 %collective-permute-start.1 = (f32[136,128]{1,0:T(8,128)S(1)}, f32[136,128]{1,0:T(8,128)S(1)}, u32[]{:S(2)}, u32[]{:S(2)}) collective-permute-start(f32[136,128]{1,0:T(8,128)S(1)} %get-tuple-element.28), channel_id=1, source_target_pairs={{0,12},{4,8},{8,4},{12,0},{1,13},{5,9},{9,5},{13,1},{2,14},{6,10},... | collective-permute-start | bytes 208904 | tf_op jit(solution)/shard_map/ppermute | solution.py:291
  5.1 6.1 %collective-permute-start.2 = (f32[136,128]{1,0:T(8,128)S(1)}, f32[136,128]{1,0:T(8,128)S(1)}, u32[]{:S(2)}, u32[]{:S(2)}) collective-permute-start(f32[136,128]{1,0:T(8,128)S(1)} %get-tuple-element.29), channel_id=1, source_target_pairs={{0,4},{4,0},{8,12},{12,8},{1,5},{5,1},{9,13},{13,9},{2,6},{6,2},{1... | collective-permute-start | bytes 208904 | tf_op jit(solution)/shard_map/ppermute | solution.py:291
  6.3 2.4 %collective-permute-start.3 = (f32[64,128]{1,0:T(8,128)S(1)}, f32[64,128]{1,0:T(8,128)S(1)}, u32[]{:S(2)}, u32[]{:S(2)}) collective-permute-start(f32[64,128]{1,0:T(8,128)S(1)} %get-tuple-element.30.rest_3_), channel_id=1, source_target_pairs={{0,1},{1,0},{2,3},{3,2},{4,5},{5,4},{6,7},{7,6},{8,9},{9,8},{10,11... | collective-permute-start | bytes 98312 | tf_op jit(solution)/shard_map/ppermute | solution.py:291
  12.1 17.9 %collective-permute-start.4 = (f32[16,32,128]{2,1,0:T(8,128)S(1)}, f32[16,32,128]{2,1,0:T(8,128)S(1)}, u32[]{:S(2)}, u32[]{:S(2)}) collective-permute-start(f32[16,32,128]{2,1,0:T(8,128)S(1)} %get-tuple-element.41), channel_id=1, source_target_pairs={{0,8},{4,12},{8,0},{12,4},{1,9},{5,13},{9,1},{13,5},{2,10},{6,14},... | collective-permute-start | bytes 786440 | tf_op jit(solution)/shard_map/ppermute | solution.py:291
  14.0 23.8 %collective-permute-start.5 = (f32[16,32,128]{2,1,0:T(8,128)S(1)}, f32[16,32,128]{2,1,0:T(8,128)S(1)}, u32[]{:S(2)}, u32[]{:S(2)}) collective-permute-start(f32[16,32,128]{2,1,0:T(8,128)S(1)} %get-tuple-element.42), channel_id=1, source_target_pairs={{0,12},{4,8},{8,4},{12,0},{1,13},{5,9},{9,5},{13,1},{2,14},{6,10},... | collective-permute-start | bytes 786440 | tf_op jit(solution)/shard_map/ppermute | solution.py:291
  14.4 23.4 %collective-permute-start.6 = (f32[16,32,128]{2,1,0:T(8,128)S(1)}, f32[16,32,128]{2,1,0:T(8,128)S(1)}, u32[]{:S(2)}, u32[]{:S(2)}) collective-permute-start(f32[16,32,128]{2,1,0:T(8,128)S(1)} %get-tuple-element.43), channel_id=1, source_target_pairs={{0,4},{4,0},{8,12},{12,8},{1,5},{5,1},{9,13},{13,9},{2,6},{6,2},{1... | collective-permute-start | bytes 786440 | tf_op jit(solution)/shard_map/ppermute | solution.py:291
  38.6 3.6 %collective-permute-start.9 = (f32[32,128]{1,0:T(8,128)S(1)}, f32[32,128]{1,0:T(8,128)S(1)}, u32[]{:S(2)}, u32[]{:S(2)}) collective-permute-start(f32[32,128]{1,0:T(8,128)S(1)} %get-tuple-element.44.rest_0_), channel_id=1, source_target_pairs={{0,3},{1,2},{2,1},{3,0},{4,7},{5,6},{6,5},{7,4},{8,11},{9,10},{10,... | collective-permute-start | bytes 49160 | tf_op jit(solution)/shard_map/ppermute | solution.py:291
  40.4 2.9 %collective-permute-start.8 = (f32[32,128]{1,0:T(8,128)S(1)}, f32[32,128]{1,0:T(8,128)S(1)}, u32[]{:S(2)}, u32[]{:S(2)}) collective-permute-start(f32[32,128]{1,0:T(8,128)S(1)} %get-tuple-element.44.rest_0_), channel_id=1, source_target_pairs={{0,2},{1,3},{2,0},{3,1},{4,6},{5,7},{6,4},{7,5},{8,10},{9,11},{10,... | collective-permute-start | bytes 49160 | tf_op jit(solution)/shard_map/ppermute | solution.py:291
  40.7 2.6 %collective-permute-start.7 = (f32[32,128]{1,0:T(8,128)S(1)}, f32[32,128]{1,0:T(8,128)S(1)}, u32[]{:S(2)}, u32[]{:S(2)}) collective-permute-start(f32[32,128]{1,0:T(8,128)S(1)} %get-tuple-element.44.rest_0_), channel_id=1, source_target_pairs={{0,1},{1,0},{2,3},{3,2},{4,5},{5,4},{6,7},{7,6},{8,9},{9,8},{10,11... | collective-permute-start | bytes 49160 | tf_op jit(solution)/shard_map/ppermute | solution.py:291

commit v6 on v5

--- a/solution.py
+++ b/solution.py
@@ -56,16 +56,31 @@
     return 3.0 * guess - (4.0 * raw[0] - raw[1])
 
 
+def read_masks(n, span, blocks, reads, mine):
+    wants = [jnp.int32(0)] * n
+    for at in range(n):
+        mine[at] = 0
+    for at in range(blocks):
+        owner, local = divmod_static(reads[at], span)
+        bit = bit_of(divmod_static(local, blocks)[1])
+        if n > 8:
+            mine[owner] = mine[owner] | bit
+        else:
+            wants = [want | jnp.where(owner == o, bit, 0) for o, want in enumerate(wants)]
+    if n <= 8:
+        for at in range(n):
+            mine[at] = wants[at]
+
+
 def leave_kernel(
-    rounds, span, here_ref, new_slot_ref, partner_ref, history_ref, rows_ref,
-    slots, reads, mine_ref, raw_ref, inverse_ref, *rest
+    rounds, span, new_slot_ref, partner_ref, history_ref, rows_ref, raw_ref, inverse_ref, *rest
 ):
     n = len(rounds) + 1
-    outs, (source, place, count, sems) = rest[: n - 1], rest[n - 1 :]
+    outs, (slots, reads, mine, source, place, count, sems) = rest[: n - 1], rest[n - 1 :]
     blocks, _, scen, nodes = history_ref.shape
     pieces = 4 if blocks % 4 == 0 else 1
     piece = blocks // pieces
-    die = here_ref[0]
+    die = lax.axis_index("die")
     copies = [
         pltpu.make_async_copy(new_slot_ref, slots, sems.at[0]),
         pltpu.make_async_copy(partner_ref, reads, sems.at[1]),
@@ -86,9 +101,6 @@
     copies[0].wait()
     copies[1].wait()
 
-    wants = [jnp.int32(0)] * n
-    for at in range(n):
-        mine_ref[at] = 0
     for at in range(blocks):
         dest, local = divmod_static(slots[at], span)
         local = divmod_static(local, blocks)[1]
@@ -101,15 +113,7 @@
             source[turn] = at
             place[turn] = local
 
-        owner, local = divmod_static(reads[at], span)
-        bit = bit_of(divmod_static(local, blocks)[1])
-        for other in range(n if n <= 8 else 0):
-            wants[other] = wants[other] | jnp.where(owner == other, bit, 0)
-        if n > 8:
-            mine_ref[owner] = mine_ref[owner] | bit
-    if n <= 8:
-        for at in range(n):
-            mine_ref[at] = wants[at]
+    read_masks(n, span, blocks, reads, mine)
     for copy in copies[2:]:
         copy.wait()
     lane = lax.broadcasted_iota(I32, (8, nodes), 1)
@@ -120,20 +124,24 @@
             out[pl.ds(rank * scen, scen), :] = guess
             out[pl.ds((CAP + rank) * scen, scen), :] = slope(raw, guess)
         row = jnp.zeros((8, nodes), I32)
-        values = halves(mine_ref[die ^ k])
+        values = halves(mine[die ^ k])
         values += [place[k * CAP + rank] for rank in range(CAP)]
         for j, value in enumerate(values):
             row = jnp.where(lane == j, value, row)
         out[pl.ds(2 * CAP * scen, 8), :] = row.astype(F32)
 
 
-def place_kernel(span, here_ref, slots, raw_ref, guess_ref, slope_ref):
+def place_kernel(span, new_slot_ref, raw_ref, guess_ref, slope_ref, slots, sem):
     blocks = raw_ref.shape[0]
+    die = lax.axis_index("die")
+    copy = pltpu.make_async_copy(new_slot_ref, slots, sem)
+    copy.start()
+    copy.wait()
     for at in range(blocks):
         dest, local = divmod_static(slots[at], span)
         local = divmod_static(local, blocks)[1]
 
-        @pl.when(dest == here_ref[0])
+        @pl.when(dest == die)
         def _(at=at, local=local):
             raw = raw_ref.at[at]
             guess = predict(raw)
@@ -141,11 +149,18 @@
             slope_ref[local] = slope(raw, guess)
 
 
-def serve_kernel(n, rcap, nblk, blk_ref, *rest):
+def pack(meta, guess_ref, out):
+    want = joined(meta[0], meta[1])
+    for slot in range(out.shape[0]):
+        out[slot] = guess_ref[lowest(want)]
+        want = want & (want - 1)
+
+
+def serve_kernel(n, nblk, *rest):
     arrived, rest = rest[: n - 1], rest[n - 1 :]
     inverses, rest = rest[:nblk], rest[nblk:]
     old_guess, old_slope, guess_ref, slope_ref, whole_ref, *rest = rest
-    outs, (ints, meta, sem) = rest[: n - 1], rest[n - 1 :]
+    outs, (ints, meta, sem) = rest[: n - 2], rest[n - 2 :]
     blocks, scen, nodes = guess_ref.shape
     for k in range(n - 1):
         ints[k] = arrived[k][pl.ds(2 * CAP * scen, 8), :].astype(I32)
@@ -156,7 +171,7 @@
         slope_ref[at] = old_slope[at]
     height = inverses[0].shape[0]
     for k in range(nblk):
-        at = pl.multiple_of((blk_ref[0] ^ k) * height, height)
+        at = pl.multiple_of((lax.axis_index("blk") ^ k) * height, height)
         whole_ref[pl.ds(at, height), :] = inverses[k][...]
     copy.wait()
     for k in range(n - 1):
@@ -169,24 +184,34 @@
                 slope_ref[place] = arrived[k][pl.ds((CAP + rank) * scen, scen), :]
 
     for k, out in enumerate(outs):
-        want = joined(meta[k, 0, 0], meta[k, 0, 1])
-        for slot in range(rcap):
-            out[slot] = guess_ref[lowest(want)]
-            want = want & (want - 1)
-
-
-def where_kernel(rounds, span, rcap, here_ref, reads, mine_ref, _, index_ref, starts):
+        pack([meta[k, 0, 0], meta[k, 0, 1]], guess_ref, out)
+
+
+def nearest_kernel(arrived, guess_ref, _, out, ints, meta, sem):
+    ints[...] = arrived[pl.ds(arrived.shape[0] - 8, 8), :].astype(I32)
+    copy = pltpu.make_async_copy(ints, meta, sem)
+    copy.start()
+    copy.wait()
+    pack([meta[0, 0], meta[0, 1]], guess_ref, out)
+
+
+def where_kernel(rounds, span, rcap, partner_ref, _, index_ref, reads, mine, starts, sem):
+    n = len(rounds) + 1
     blocks = index_ref.shape[0]
-    die = here_ref[0]
+    die = lax.axis_index("die")
+    copy = pltpu.make_async_copy(partner_ref, reads, sem)
+    copy.start()
     starts[0] = 0
     for at, k in enumerate(rounds):
         starts[k] = at * rcap
+    copy.wait()
+    read_masks(n, span, blocks, reads, mine)
 
     def step(at, carry):
         owner, local = divmod_static(reads[at], span)
         local = divmod_static(local, blocks)[1]
         k = owner ^ die
-        slot = bits_set(mine_ref[owner] & (bit_of(local) - 1))
+        slot = bits_set(mine[owner] & (bit_of(local) - 1))
         index_ref[at] = jnp.where(k == 0, local - blocks, starts[k] + slot)
         return carry
 
@@ -312,14 +337,12 @@
     assert blocks <= 32
     rcap = 2 * max(1, blocks // n)
     span = ncol * blocks
-    die = lax.axis_index("die").astype(I32).reshape(1)
-    blk = lax.axis_index("blk").astype(I32).reshape(1)
 
     def tiles(count):
         return jax.ShapeDtypeStruct((count, scen, nodes), F32)
 
-    def ints(count):
-        return jax.ShapeDtypeStruct((count,), I32)
+    def scalars(count):
+        return pltpu.SMEM((count,), I32)
 
     block = tiles(blocks)
     square = jax.ShapeDtypeStruct((nodes, nodes), F32)
@@ -327,37 +350,35 @@
     message = jax.ShapeDtypeStruct((2 * CAP * scen + 8, nodes), F32)
 
     rounds = [*range(2, n), 1]
-    slots, reads, mine, raw, rows, *leaving = call(
+    new_slot, partner = in_hbm(new_slot), in_hbm(partner)
+    raw, rows, *leaving = call(
         functools.partial(leave_kernel, rounds, span),
-        [
-            ints(blocks),
-            ints(blocks),
-            ints(n),
-            jax.ShapeDtypeStruct(history.shape, F32),
-            jax.ShapeDtypeStruct(rows.shape, F32),
-        ]
+        [jax.ShapeDtypeStruct(history.shape, F32), jax.ShapeDtypeStruct(rows.shape, F32)]
         + [message] * (n - 1),
-        [die, in_hbm(new_slot), in_hbm(partner), in_hbm(history), in_hbm(rows)],
-        [SMEM] + [HBM] * 4,
-        [SMEM] * 3 + [VMEM] * (n + 1),
-        [pltpu.SMEM((n * CAP,), I32)] * 2
-        + [pltpu.SMEM((n,), I32), pltpu.SemaphoreType.DMA((7,))],
+        [new_slot, partner, in_hbm(history), in_hbm(rows)],
+        [HBM] * 4,
+        [VMEM] * (n + 1),
+        [scalars(blocks)] * 2
+        + [scalars(n)]
+        + [scalars(n * CAP)] * 2
+        + [scalars(n), pltpu.SemaphoreType.DMA((7,))],
     )
     arrived = [swap(x, "die", n, k) for x, k in zip(leaving, rounds)]
     inverses = [rows] + [swap(rows, "blk", nblk, k) for k in range(1, nblk)]
     old_guess, old_slope = call(
         functools.partial(place_kernel, span),
         [block, block],
-        [die, slots, raw],
-        [SMEM, SMEM, VMEM],
+        [new_slot, raw],
+        [HBM, VMEM],
         [VMEM, VMEM],
+        [scalars(blocks), pltpu.SemaphoreType.DMA],
     )
     guess, slopes, whole, *served = call(
-        functools.partial(serve_kernel, n, rcap, nblk),
-        [block, block, square] + [tiles(rcap)] * (n - 1),
-        [blk, *arrived, *inverses, old_guess, old_slope],
-        [SMEM] + [VMEM] * (n - 1 + nblk + 2),
-        [VMEM] * (n + 2),
+        functools.partial(serve_kernel, n, nblk),
+        [block, block, square] + [tiles(rcap)] * (n - 2),
+        [*arrived, *inverses, old_guess, old_slope],
+        [VMEM] * (n - 1 + nblk + 2),
+        [VMEM] * (n + 1),
         [
             pltpu.VMEM((n - 1, 8, nodes), I32),
             pltpu.SMEM((n - 1, 8, nodes), I32),
@@ -367,11 +388,11 @@
     others = [swap(x, "die", n, k) for x, k in zip(served, rounds)]
     (index,) = call(
         functools.partial(where_kernel, rounds, span, rcap),
-        [ints(blocks)],
-        [die, reads, mine, guess],
-        [SMEM] * 3 + [ANY],
+        [jax.ShapeDtypeStruct((blocks,), I32)],
+        [partner, guess],
+        [HBM, ANY],
         [SMEM],
-        [pltpu.SMEM((n,), I32)],
+        [scalars(blocks), scalars(n), scalars(n), pltpu.SemaphoreType.DMA],
     )
     step = 8 if blocks % 8 == 0 else blocks
     wide = pl.BlockSpec((step, scen, nodes), lambda i: (i, 0, 0))
@@ -403,6 +424,15 @@
         in_hbm(region_gain),
         in_hbm(drive),
     )
+    (near,) = call(
+        nearest_kernel,
+        [tiles(rcap)],
+        [arrived[-1], guess, base],
+        [VMEM, VMEM, ANY],
+        [VMEM],
+        [pltpu.VMEM((8, nodes), I32), pltpu.SMEM((8, nodes), I32), pltpu.SemaphoreType.DMA],
+    )
+    others.append(swap(near, "die", n, rounds[-1]))
     residual, share, partial = call(
         functools.partial(residual_kernel, n),
         [block, jax.ShapeDtypeStruct((scen, nodes), F32), block],

time: 44.5 us -> 46.5 us (1.045)
  the two profiles are of different devices: /device:TPU:9 before, /device:TPU:0 now
where the time goes in v6:
time: 46.5 us; the launch traced here: 46.3 us
  waiting for transfers between devices  20.3 us (44%)
  Pallas kernels  13.8 us (30%)
  starting transfers between devices  11.5 us (25%)
  between operations  0.7 us (2%)
    ppermute x10, waiting for transfers between devices, swap(): return lax.ppermute(x, axes, [(d, d ^ k) for d in range(n)])  20.3 us
    ppermute x10, starting transfers between devices, swap(): return lax.ppermute(x, axes, [(d, d ^ k) for d in range(n)])  11.5 us
    pallas_call x8, Pallas kernels, call(): pl.pallas_call(body, out_shape=outs, in_specs=in_specs, out_specs=out_spe...  8.6 us
    pallas_call x1, Pallas kernels, shards(): pl.pallas_call(local_kernel, grid=(blocks // step,), out_shape=[block, bl...  5.17 us
  transfers between devices with their start and end apart: 10, of which 8 were waited for; matrix products, arithmetic and copies ran while one was open for 0% of the time, Pallas kernels for 21%

profile of v6, /device:TPU:0, one launch (start us, length us, event | category | flops | bytes accessed | tf_op | source)
XLA Modules:
  0.0 46.3 jit_solution(12055266727192411244)
XLA Ops:
  0.6 1.5 %shard_map.113 = (f32[32,3,32,128]{3,2,1,0:T(8,128)S(1)}, f32[64,128]{1,0:T(8,128)S(1)}, f32[136,128]{1,0:T(8,128)S(1)}, f32[136,128]{1,0:T(8,128)S(1)}, f32[136,128]{1,0:T(8,128)S(1)}) custom-call(s32[32]{0:T(128)} %new_slot_ref.3, s32[32]{0:T(128)} %partner_ref.3, f32[32,3,32,128]{3,2,1,0:T(8,128)} %history_ref.1, f32[64,128]{1,0:T(8,128)} %bitcast.1), custom_call_target="tpu_custom_call" | custom-call | tf_op jit(solution)/shard_map/pallas_call | solution.py:300
  2.1 4.1 %collective-permute-start = (f32[136,128]{1,0:T(8,128)S(1)}, f32[136,128]{1,0:T(8,128)S(1)}, u32[]{:S(2)}, u32[]{:S(2)}) collective-permute-start(f32[136,128]{1,0:T(8,128)S(1)} %get-tuple-element.21), channel_id=1, source_target_pairs={{0,8},{4,12},{8,0},{12,4},{1,9},{5,13},{9,1},{13,5},{2,10},{6,14},... | collective-permute-start | bytes 208904 | tf_op jit(solution)/shard_map/ppermute | solution.py:316
  6.2 1.3 %collective-permute-start.1 = (f32[136,128]{1,0:T(8,128)S(1)}, f32[136,128]{1,0:T(8,128)S(1)}, u32[]{:S(2)}, u32[]{:S(2)}) collective-permute-start(f32[136,128]{1,0:T(8,128)S(1)} %get-tuple-element.22), channel_id=1, source_target_pairs={{0,12},{4,8},{8,4},{12,0},{1,13},{5,9},{9,5},{13,1},{2,14},{6,10},... | collective-permute-start | bytes 208904 | tf_op jit(solution)/shard_map/ppermute | solution.py:316
  7.6 0.2 collective-permute-start.2
  7.8 0.0 collective-permute-start.3
  7.8 1.1 %shard_map.114 = (f32[32,32,128]{2,1,0:T(8,128)S(1)}, f32[32,32,128]{2,1,0:T(8,128)S(1)}) custom-call(s32[32]{0:T(128)} %new_slot_ref.3, f32[32,3,32,128]{3,2,1,0:T(8,128)S(1)} %get-tuple-element.25.raw_ref), custom_call_target="tpu_custom_call" | custom-call | tf_op jit(solution)/shard_map/pallas_call | solution.py:300
  8.9 0.1 collective-permute-done.3.rest_4_
  9.0 1.1 %collective-permute-done.rest_0_ = f32[136,128]{1,0:T(8,128)S(1)} collective-permute-done((f32[136,128]{1,0:T(8,128)S(1)}, f32[136,128]{1,0:T(8,128)S(1)}, u32[]{:S(2)}, u32[]{:S(2)}) %collective-permute-start) | collective-permute-done | bytes 69664 | tf_op jit(solution)/shard_map/ppermute | solution.py:316
  10.1 2.5 %collective-permute-done.1.rest_1_ = f32[136,128]{1,0:T(8,128)S(1)} collective-permute-done((f32[136,128]{1,0:T(8,128)S(1)}, f32[136,128]{1,0:T(8,128)S(1)}, u32[]{:S(2)}, u32[]{:S(2)}) %collective-permute-start.1) | collective-permute-done | bytes 69664 | tf_op jit(solution)/shard_map/ppermute | solution.py:316
  12.6 0.1 collective-permute-done.2.rest_2_.arrived
  12.6 0.9 %shard_map.115 = (f32[32,32,128]{2,1,0:T(8,128)S(1)}, f32[32,32,128]{2,1,0:T(8,128)S(1)}, f32[128,128]{1,0:T(8,128)S(1)}, f32[16,32,128]{2,1,0:T(8,128)S(1)}, f32[16,32,128]{2,1,0:T(8,128)S(1)}) custom-call(f32[136,128]{1,0:T(8,128)S(1)} %collective-permute-done.rest_0_, f32[136,128]{1,0:T(8,128)S(1)} %collective-permute-done.1.rest_1_, ...), custom_call_target="tpu_custom_call" | custom-call | tf_op jit(solution)/shard_map/pallas_call | solution.py:300
  13.5 3.0 %collective-permute-start.4 = (f32[16,32,128]{2,1,0:T(8,128)S(1)}, f32[16,32,128]{2,1,0:T(8,128)S(1)}, u32[]{:S(2)}, u32[]{:S(2)}) collective-permute-start(f32[16,32,128]{2,1,0:T(8,128)S(1)} %get-tuple-element.34), channel_id=1, source_target_pairs={{0,8},{4,12},{8,0},{12,4},{1,9},{5,13},{9,1},{13,5},{2,10},{6,14},... | collective-permute-start | bytes 786440 | tf_op jit(solution)/shard_map/ppermute | solution.py:316
  16.5 0.4 collective-permute-start.5
  17.0 5.2 %shard_map.117 = (f32[32,32,128]{2,1,0:T(8,128)S(1)}, f32[32,32,128]{2,1,0:T(8,128)S(1)}, f32[32,32,128]{2,1,0:T(8,128)S(1)}, f32[32,128]{1,0:T(8,128)S(1)}) custom-call(f32[32,32,128]{2,1,0:T(8,128)S(1)} %get-tuple-element.28._.guess_ref, f32[32,32,128]{2,1,0:T(8,128)S(1)} %get-tuple-element.29.slope_ref, f32[32,128,128]{2,1,0:T(8,128)} %coupling_ref.1, ...), custom_call_target="tpu_custom_call" | custom-call | tf_op jit(solution)/shard_map/pallas_call | solution.py:400
  22.1 0.7 %shard_map.118 = f32[16,32,128]{2,1,0:T(8,128)S(1)} custom-call(f32[136,128]{1,0:T(8,128)S(1)} %collective-permute-done.2.rest_2_.arrived, f32[32,32,128]{2,1,0:T(8,128)S(1)} %get-tuple-element.28._.guess_ref, f32[32,32,128]{2,1,0:T(8,128)S(1)} %get-tuple-element.30._.base_ref), custom_call_target="tpu_custom_call" | custom-call | tf_op jit(solution)/shard_map/pallas_call | solution.py:300
  22.8 0.5 collective-permute-start.6
  23.3 1.9 %shard_map.116.index_ref = s32[32]{0:T(128)S(1)} custom-call(s32[32]{0:T(128)} %partner_ref.3, f32[32,32,128]{2,1,0:T(8,128)S(1)} %get-tuple-element.28._.guess_ref), custom_call_target="tpu_custom_call" | custom-call | tf_op jit(solution)/shard_map/pallas_call | solution.py:300
  25.2 9.1 %collective-permute-done.4.rest_0_ = f32[16,32,128]{2,1,0:T(8,128)S(1)} collective-permute-done((f32[16,32,128]{2,1,0:T(8,128)S(1)}, f32[16,32,128]{2,1,0:T(8,128)S(1)}, u32[]{:S(2)}, u32[]{:S(2)}) %collective-permute-start.4) | collective-permute-done | bytes 262176 | tf_op jit(solution)/shard_map/ppermute | solution.py:316
  34.3 0.0 collective-permute-done.5.rest_1_
  34.3 5.3 %collective-permute-done.6.rest_2_ = f32[16,32,128]{2,1,0:T(8,128)S(1)} collective-permute-done((f32[16,32,128]{2,1,0:T(8,128)S(1)}, f32[16,32,128]{2,1,0:T(8,128)S(1)}, u32[]{:S(2)}, u32[]{:S(2)}) %collective-permute-start.6) | collective-permute-done | bytes 262176 | tf_op jit(solution)/shard_map/ppermute | solution.py:316
  39.6 0.8 %shard_map.119 = (f32[32,32,128]{2,1,0:T(8,128)S(1)}, f32[32,128]{1,0:T(8,128)S(1)}, f32[32,32,128]{2,1,0:T(8,128)S(1)}) custom-call(s32[32]{0:T(128)S(1)} %shard_map.116.index_ref, f32[32,32,128]{2,1,0:T(8,128)S(1)} %get-tuple-element.30._.base_ref, f32[32,32,128]{2,1,0:T(8,128)S(1)} %get-tuple-element.31.inv_ref, ...), custom_call_target="tpu_custom_call" | custom-call | tf_op jit(solution)/shard_map/pallas_call | solution.py:300
  40.4 1.2 %collective-permute-start.9 = (f32[32,128]{1,0:T(8,128)S(1)}, f32[32,128]{1,0:T(8,128)S(1)}, u32[]{:S(2)}, u32[]{:S(2)}) collective-permute-start(f32[32,128]{1,0:T(8,128)S(1)} %get-tuple-element.36.rest_0_), channel_id=1, source_target_pairs={{0,3},{1,2},{2,1},{3,0},{4,7},{5,6},{6,5},{7,4},{8,11},{9,10},{10,... | collective-permute-start | bytes 49160 | tf_op jit(solution)/shard_map/ppermute | solution.py:316
  41.6 0.5 %collective-permute-start.8 = (f32[32,128]{1,0:T(8,128)S(1)}, f32[32,128]{1,0:T(8,128)S(1)}, u32[]{:S(2)}, u32[]{:S(2)}) collective-permute-start(f32[32,128]{1,0:T(8,128)S(1)} %get-tuple-element.36.rest_0_), channel_id=1, source_target_pairs={{0,2},{1,3},{2,0},{3,1},{4,6},{5,7},{6,4},{7,5},{8,10},{9,11},{10,... | collective-permute-start | bytes 49160 | tf_op jit(solution)/shard_map/ppermute | solution.py:316
  42.1 0.2 collective-permute-start.7
  42.3 0.8 %shard_map.121 = f32[32,32,128]{2,1,0:T(8,128)} custom-call(f32[32,32,128]{2,1,0:T(8,128)S(1)} %get-tuple-element.39.value_ref), custom_call_target="tpu_custom_call" | custom-call | tf_op jit(solution)/shard_map/pallas_call | solution.py:300
  43.1 0.5 %collective-permute-done.9.rest_3_ = f32[32,128]{1,0:T(8,128)S(1)} collective-permute-done((f32[32,128]{1,0:T(8,128)S(1)}, f32[32,128]{1,0:T(8,128)S(1)}, u32[]{:S(2)}, u32[]{:S(2)}) %collective-permute-start.9) | collective-permute-done | bytes 16416 | tf_op jit(solution)/shard_map/ppermute | solution.py:316
  43.6 1.7 %collective-permute-done.8.rest_2_ = f32[32,128]{1,0:T(8,128)S(1)} collective-permute-done((f32[32,128]{1,0:T(8,128)S(1)}, f32[32,128]{1,0:T(8,128)S(1)}, u32[]{:S(2)}, u32[]{:S(2)}) %collective-permute-start.8) | collective-permute-done | bytes 16416 | tf_op jit(solution)/shard_map/ppermute | solution.py:316
  45.3 0.0 collective-permute-done.7.rest_1_
  45.3 1.0 %shard_map.120 = f32[32,32,128]{2,1,0:T(8,128)} custom-call(f32[32,128]{1,0:T(8,128)S(1)} %get-tuple-element.36.rest_0_, f32[32,128]{1,0:T(8,128)S(1)} %collective-permute-done.7.rest_1_, f32[32,128]{1,0:T(8,128)S(1)} %collective-permute-done.8.rest_2_, f32[32,128]{1,0:T(8,128)S(1)} %collective-permute-done.9.rest_3_, ...), custom_call_target="tpu_custom_call" | custom-call | tf_op jit(solution)/shard_map/pallas_call | solution.py:300
Async XLA Ops:
  2.1 8.0 %collective-permute-start = (f32[136,128]{1,0:T(8,128)S(1)}, f32[136,128]{1,0:T(8,128)S(1)}, u32[]{:S(2)}, u32[]{:S(2)}) collective-permute-start(f32[136,128]{1,0:T(8,128)S(1)} %get-tuple-element.21), channel_id=1, source_target_pairs={{0,8},{4,12},{8,0},{12,4},{1,9},{5,13},{9,1},{13,5},{2,10},{6,14},... | collective-permute-start | bytes 208904 | tf_op jit(solution)/shard_map/ppermute | solution.py:316
  6.2 6.3 %collective-permute-start.1 = (f32[136,128]{1,0:T(8,128)S(1)}, f32[136,128]{1,0:T(8,128)S(1)}, u32[]{:S(2)}, u32[]{:S(2)}) collective-permute-start(f32[136,128]{1,0:T(8,128)S(1)} %get-tuple-element.22), channel_id=1, source_target_pairs={{0,12},{4,8},{8,4},{12,0},{1,13},{5,9},{9,5},{13,1},{2,14},{6,10},... | collective-permute-start | bytes 208904 | tf_op jit(solution)/shard_map/ppermute | solution.py:316
  7.6 5.1 %collective-permute-start.2 = (f32[136,128]{1,0:T(8,128)S(1)}, f32[136,128]{1,0:T(8,128)S(1)}, u32[]{:S(2)}, u32[]{:S(2)}) collective-permute-start(f32[136,128]{1,0:T(8,128)S(1)} %get-tuple-element.23), channel_id=1, source_target_pairs={{0,4},{4,0},{8,12},{12,8},{1,5},{5,1},{9,13},{13,9},{2,6},{6,2},{1... | collective-permute-start | bytes 208904 | tf_op jit(solution)/shard_map/ppermute | solution.py:316
  7.8 1.2 %collective-permute-start.3 = (f32[64,128]{1,0:T(8,128)S(1)}, f32[64,128]{1,0:T(8,128)S(1)}, u32[]{:S(2)}, u32[]{:S(2)}) collective-permute-start(f32[64,128]{1,0:T(8,128)S(1)} %get-tuple-element.24.rest_3_), channel_id=1, source_target_pairs={{0,1},{1,0},{2,3},{3,2},{4,5},{5,4},{6,7},{7,6},{8,9},{9,8},{10,11... | collective-permute-start | bytes 98312 | tf_op jit(solution)/shard_map/ppermute | solution.py:316
  13.5 20.8 %collective-permute-start.4 = (f32[16,32,128]{2,1,0:T(8,128)S(1)}, f32[16,32,128]{2,1,0:T(8,128)S(1)}, u32[]{:S(2)}, u32[]{:S(2)}) collective-permute-start(f32[16,32,128]{2,1,0:T(8,128)S(1)} %get-tuple-element.34), channel_id=1, source_target_pairs={{0,8},{4,12},{8,0},{12,4},{1,9},{5,13},{9,1},{13,5},{2,10},{6,14},... | collective-permute-start | bytes 786440 | tf_op jit(solution)/shard_map/ppermute | solution.py:316
  16.5 17.8 %collective-permute-start.5 = (f32[16,32,128]{2,1,0:T(8,128)S(1)}, f32[16,32,128]{2,1,0:T(8,128)S(1)}, u32[]{:S(2)}, u32[]{:S(2)}) collective-permute-start(f32[16,32,128]{2,1,0:T(8,128)S(1)} %get-tuple-element.35), channel_id=1, source_target_pairs={{0,12},{4,8},{8,4},{12,0},{1,13},{5,9},{9,5},{13,1},{2,14},{6,10},... | collective-permute-start | bytes 786440 | tf_op jit(solution)/shard_map/ppermute | solution.py:316
  22.8 16.8 %collective-permute-start.6 = (f32[16,32,128]{2,1,0:T(8,128)S(1)}, f32[16,32,128]{2,1,0:T(8,128)S(1)}, u32[]{:S(2)}, u32[]{:S(2)}) collective-permute-start(f32[16,32,128]{2,1,0:T(8,128)S(1)} %shard_map.118), channel_id=1, source_target_pairs={{0,4},{4,0},{8,12},{12,8},{1,5},{5,1},{9,13},{13,9},{2,6},{6,2},{1... | collective-permute-start | bytes 786440 | tf_op jit(solution)/shard_map/ppermute | solution.py:316
  40.4 3.2 %collective-permute-start.9 = (f32[32,128]{1,0:T(8,128)S(1)}, f32[32,128]{1,0:T(8,128)S(1)}, u32[]{:S(2)}, u32[]{:S(2)}) collective-permute-start(f32[32,128]{1,0:T(8,128)S(1)} %get-tuple-element.36.rest_0_), channel_id=1, source_target_pairs={{0,3},{1,2},{2,1},{3,0},{4,7},{5,6},{6,5},{7,4},{8,11},{9,10},{10,... | collective-permute-start | bytes 49160 | tf_op jit(solution)/shard_map/ppermute | solution.py:316
  41.6 3.7 %collective-permute-start.8 = (f32[32,128]{1,0:T(8,128)S(1)}, f32[32,128]{1,0:T(8,128)S(1)}, u32[]{:S(2)}, u32[]{:S(2)}) collective-permute-start(f32[32,128]{1,0:T(8,128)S(1)} %get-tuple-element.36.rest_0_), channel_id=1, source_target_pairs={{0,2},{1,3},{2,0},{3,1},{4,6},{5,7},{6,4},{7,5},{8,10},{9,11},{10,... | collective-permute-start | bytes 49160 | tf_op jit(solution)/shard_map/ppermute | solution.py:316
  42.1 3.2 %collective-permute-start.7 = (f32[32,128]{1,0:T(8,128)S(1)}, f32[32,128]{1,0:T(8,128)S(1)}, u32[]{:S(2)}, u32[]{:S(2)}) collective-permute-start(f32[32,128]{1,0:T(8,128)S(1)} %get-tuple-element.36.rest_0_), channel_id=1, source_target_pairs={{0,1},{1,0},{2,3},{3,2},{4,5},{5,4},{6,7},{7,6},{8,9},{9,8},{10,11... | collective-permute-start | bytes 49160 | tf_op jit(solution)/shard_map/ppermute | solution.py:316

commit v7 on v6

--- a/solution.py
+++ b/solution.py
@@ -38,6 +38,11 @@
 
 def lowest(mask):
     return (31 - lax.clz(mask & -mask)) & 31
+
+
+def cut(x):
+    high = x.astype(jnp.bfloat16)
+    return high, (x - high.astype(F32)).astype(jnp.bfloat16)
 
 
 def halves(mask):
@@ -160,7 +165,7 @@
     arrived, rest = rest[: n - 1], rest[n - 1 :]
     inverses, rest = rest[:nblk], rest[nblk:]
     old_guess, old_slope, guess_ref, slope_ref, whole_ref, *rest = rest
-    outs, (ints, meta, sem) = rest[: n - 2], rest[n - 2 :]
+    outs, (ints, meta, sem) = rest[: n - 1], rest[n - 1 :]
     blocks, scen, nodes = guess_ref.shape
     for k in range(n - 1):
         ints[k] = arrived[k][pl.ds(2 * CAP * scen, 8), :].astype(I32)
@@ -172,7 +177,9 @@
     height = inverses[0].shape[0]
     for k in range(nblk):
         at = pl.multiple_of((lax.axis_index("blk") ^ k) * height, height)
-        whole_ref[pl.ds(at, height), :] = inverses[k][...]
+        high, low = cut(inverses[k][...])
+        whole_ref[pl.ds(at, height), :] = high
+        whole_ref[pl.ds(nodes + at, height), :] = low
     copy.wait()
     for k in range(n - 1):
         for rank in range(CAP):
@@ -185,14 +192,6 @@
 
     for k, out in enumerate(outs):
         pack([meta[k, 0, 0], meta[k, 0, 1]], guess_ref, out)
-
-
-def nearest_kernel(arrived, guess_ref, _, out, ints, meta, sem):
-    ints[...] = arrived[pl.ds(arrived.shape[0] - 8, 8), :].astype(I32)
-    copy = pltpu.make_async_copy(ints, meta, sem)
-    copy.start()
-    copy.wait()
-    pack([meta[0, 0], meta[0, 1]], guess_ref, out)
 
 
 def where_kernel(rounds, span, rcap, partner_ref, _, index_ref, reads, mine, starts, sem):
@@ -249,8 +248,8 @@
         )
 
 
-def residual_kernel(n, index_ref, base_ref, inv_ref, scale_ref, guess_ref, wire_ref, *rest):
-    blocks_in, (residual_ref, share_ref, partial_ref, pool) = rest[: n - 1], rest[n - 1 :]
+def share_kernel(n, index_ref, base_ref, scale_ref, guess_ref, wire_ref, *rest):
+    blocks_in, (share_ref, near_ref, pool) = rest[: n - 1], rest[n - 1 :]
     blocks = guess_ref.shape[0]
     start = 0
     for ref in blocks_in:
@@ -262,18 +261,25 @@
         index = index_ref[at]
         own = index < 0
         near = guess_ref[jnp.where(own, index + blocks, 0)]
-        other = jnp.where(own, near, pool[jnp.maximum(index, 0)])
-        residual = base_ref[at] - wire_ref[at : at + 1, :] * other
-        residual_ref[at] = residual
-        partial_ref[at] = guess_ref[at] - residual * inv_ref[at]
-        share = share + scale_ref[at] * residual
+        near = jnp.where(own, near, pool[jnp.maximum(index, 0)])
+        near_ref[at] = near
+        share = share + scale_ref[at] * (base_ref[at] - wire_ref[at : at + 1, :] * near)
     share_ref[...] = share
 
 
-def store_kernel(value_ref, out_ref, sem):
-    copy = pltpu.make_async_copy(value_ref, out_ref, sem)
-    copy.start()
-    copy.wait()
+def residual_kernel(parts, near_ref, base_ref, inv_ref, guess_ref, wire_ref, partial_ref, out_ref, held, sems):
+    step = guess_ref.shape[0] // parts
+    copies = []
+    for part in range(parts):
+        for at in range(part * step, (part + 1) * step):
+            residual = base_ref[at] - wire_ref[at : at + 1, :] * near_ref[at]
+            held[at] = residual
+            partial_ref[at] = guess_ref[at] - residual * inv_ref[at]
+        some = pl.ds(part * step, step)
+        copies.append(pltpu.make_async_copy(held.at[some], out_ref.at[some], sems.at[part]))
+        copies[-1].start()
+    for copy in copies:
+        copy.wait()
 
 
 def update_kernel(m, parts, *rest):
@@ -281,9 +287,11 @@
     total = shares[0][...]
     for share in shares[1:]:
         total = total + share[...]
-    region = jnp.dot(
-        total, whole_ref[...], precision=lax.Precision.HIGHEST, preferred_element_type=F32
-    )
+    nodes = total.shape[1]
+    high, low = cut(total)
+    region = jnp.dot(high, whole_ref[:nodes, :], preferred_element_type=F32)
+    region += jnp.dot(low, whole_ref[:nodes, :], preferred_element_type=F32)
+    region += jnp.dot(high, whole_ref[nodes:, :], preferred_element_type=F32)
     step = partial_ref.shape[0] // parts
     copies = []
     for part in range(parts):
@@ -345,7 +353,7 @@
         return pltpu.SMEM((count,), I32)
 
     block = tiles(blocks)
-    square = jax.ShapeDtypeStruct((nodes, nodes), F32)
+    square = jax.ShapeDtypeStruct((2 * nodes, nodes), jnp.bfloat16)
     rows = region_inverse[0]
     message = jax.ShapeDtypeStruct((2 * CAP * scen + 8, nodes), F32)
 
@@ -375,10 +383,10 @@
     )
     guess, slopes, whole, *served = call(
         functools.partial(serve_kernel, n, nblk),
-        [block, block, square] + [tiles(rcap)] * (n - 2),
+        [block, block, square] + [tiles(rcap)] * (n - 1),
         [*arrived, *inverses, old_guess, old_slope],
         [VMEM] * (n - 1 + nblk + 2),
-        [VMEM] * (n + 1),
+        [VMEM] * (n + 2),
         [
             pltpu.VMEM((n - 1, 8, nodes), I32),
             pltpu.SMEM((n - 1, 8, nodes), I32),
@@ -424,28 +432,24 @@
         in_hbm(region_gain),
         in_hbm(drive),
     )
-    (near,) = call(
-        nearest_kernel,
-        [tiles(rcap)],
-        [arrived[-1], guess, base],
-        [VMEM, VMEM, ANY],
-        [VMEM],
-        [pltpu.VMEM((8, nodes), I32), pltpu.SMEM((8, nodes), I32), pltpu.SemaphoreType.DMA],
-    )
-    others.append(swap(near, "die", n, rounds[-1]))
-    residual, share, partial = call(
-        functools.partial(residual_kernel, n),
-        [block, jax.ShapeDtypeStruct((scen, nodes), F32), block],
-        [index, base, inv, scale, guess, wire, *others],
-        [SMEM] + [VMEM] * (5 + n - 1),
-        [VMEM] * 3,
+    share, near = call(
+        functools.partial(share_kernel, n),
+        [jax.ShapeDtypeStruct((scen, nodes), F32), block],
+        [index, base, scale, guess, wire, *others],
+        [SMEM] + [VMEM] * (4 + n - 1),
+        [VMEM] * 2,
         [pltpu.VMEM(((n - 1) * rcap, scen, nodes), F32)],
     )
-    (stored,) = call(
-        store_kernel, [block], [residual], [ANY], [HBM], [pltpu.SemaphoreType.DMA]
+    parts = 4 if blocks % 4 == 0 else 1
+    partial, residual = call(
+        functools.partial(residual_kernel, parts),
+        [block, block],
+        [near, base, inv, guess, wire],
+        [VMEM] * 5,
+        [VMEM, HBM],
+        [pltpu.VMEM((blocks, scen, nodes), F32), pltpu.SemaphoreType.DMA((parts,))],
     )
     shares = [share] + [swap(share, ("sub", "blk"), ncol, k) for k in range(1, ncol)]
-    parts = 4 if blocks % 4 == 0 else 1
     (updated,) = call(
         functools.partial(update_kernel, ncol, parts),
         [block],
@@ -454,7 +458,7 @@
         [HBM],
         [pltpu.VMEM((blocks, scen, nodes), F32), pltpu.SemaphoreType.DMA((parts,))],
     )
-    return (updated, stored)
+    return (updated, residual)
 
 
 def solution(mesh):

time: 46.5 us -> 43.9 us (0.944)
  the two profiles are of different devices: /device:TPU:0 before, /device:TPU:9 now
where the time goes in v7:
time: 43.9 us; the launch traced here: 43.7 us
  waiting for transfers between devices  18.8 us (43%)
  Pallas kernels  13.1 us (30%)
  starting transfers between devices  11.1 us (25%)
  between operations  0.7 us (2%)
    ppermute x10, waiting for transfers between devices, swap(): return lax.ppermute(x, axes, [(d, d ^ k) for d in range(n)])  18.8 us
    ppermute x10, starting transfers between devices, swap(): return lax.ppermute(x, axes, [(d, d ^ k) for d in range(n)])  11.1 us
    pallas_call x7, Pallas kernels, call(): pl.pallas_call(body, out_shape=outs, in_specs=in_specs, out_specs=out_spe...  7.96 us
    pallas_call x1, Pallas kernels, shards(): pl.pallas_call(local_kernel, grid=(blocks // step,), out_shape=[block, bl...  5.19 us
  transfers between devices with their start and end apart: 10, of which 6 were waited for; matrix products, arithmetic and copies ran while one was open for 0% of the time, Pallas kernels for 21%

profile of v7, /device:TPU:9, one launch (start us, length us, event | category | flops | bytes accessed | tf_op | source)
XLA Modules:
  0.0 43.7 jit_solution(11915468985619037908)
XLA Ops:
  0.6 1.5 %shard_map.113 = (f32[32,3,32,128]{3,2,1,0:T(8,128)S(1)}, f32[64,128]{1,0:T(8,128)S(1)}, f32[136,128]{1,0:T(8,128)S(1)}, f32[136,128]{1,0:T(8,128)S(1)}, f32[136,128]{1,0:T(8,128)S(1)}) custom-call(s32[32]{0:T(128)} %new_slot_ref.3, s32[32]{0:T(128)} %partner_ref.3, f32[32,3,32,128]{3,2,1,0:T(8,128)} %history_ref.1, f32[64,128]{1,0:T(8,128)} %bitcast.1), custom_call_target="tpu_custom_call" | custom-call | tf_op jit(solution)/shard_map/pallas_call | solution.py:308
  2.1 2.4 %collective-permute-start = (f32[136,128]{1,0:T(8,128)S(1)}, f32[136,128]{1,0:T(8,128)S(1)}, u32[]{:S(2)}, u32[]{:S(2)}) collective-permute-start(f32[136,128]{1,0:T(8,128)S(1)} %get-tuple-element.23), channel_id=1, source_target_pairs={{0,8},{4,12},{8,0},{12,4},{1,9},{5,13},{9,1},{13,5},{2,10},{6,14},... | collective-permute-start | bytes 208904 | tf_op jit(solution)/shard_map/ppermute | solution.py:324
  4.5 0.0 collective-permute-start.1
  4.5 1.3 %collective-permute-start.2 = (f32[136,128]{1,0:T(8,128)S(1)}, f32[136,128]{1,0:T(8,128)S(1)}, u32[]{:S(2)}, u32[]{:S(2)}) collective-permute-start(f32[136,128]{1,0:T(8,128)S(1)} %get-tuple-element.25), channel_id=1, source_target_pairs={{0,4},{4,0},{8,12},{12,8},{1,5},{5,1},{9,13},{13,9},{2,6},{6,2},{1... | collective-permute-start | bytes 208904 | tf_op jit(solution)/shard_map/ppermute | solution.py:324
  5.7 1.5 %collective-permute-start.3 = (f32[64,128]{1,0:T(8,128)S(1)}, f32[64,128]{1,0:T(8,128)S(1)}, u32[]{:S(2)}, u32[]{:S(2)}) collective-permute-start(f32[64,128]{1,0:T(8,128)S(1)} %get-tuple-element.26.rest_3_), channel_id=1, source_target_pairs={{0,1},{1,0},{2,3},{3,2},{4,5},{5,4},{6,7},{7,6},{8,9},{9,8},{10,11... | collective-permute-start | bytes 98312 | tf_op jit(solution)/shard_map/ppermute | solution.py:324
  7.2 1.1 %shard_map.114 = (f32[32,32,128]{2,1,0:T(8,128)S(1)}, f32[32,32,128]{2,1,0:T(8,128)S(1)}) custom-call(s32[32]{0:T(128)} %new_slot_ref.3, f32[32,3,32,128]{3,2,1,0:T(8,128)S(1)} %get-tuple-element.27.raw_ref), custom_call_target="tpu_custom_call" | custom-call | tf_op jit(solution)/shard_map/pallas_call | solution.py:308
  8.3 0.0 collective-permute-done.3.rest_4_
  8.3 0.2 collective-permute-done.rest_0_
  8.5 2.1 %collective-permute-done.1.rest_1_ = f32[136,128]{1,0:T(8,128)S(1)} collective-permute-done((f32[136,128]{1,0:T(8,128)S(1)}, f32[136,128]{1,0:T(8,128)S(1)}, u32[]{:S(2)}, u32[]{:S(2)}) %collective-permute-start.1) | collective-permute-done | bytes 69664 | tf_op jit(solution)/shard_map/ppermute | solution.py:324
  10.6 0.0 collective-permute-done.2.rest_2_
  10.6 0.9 %shard_map.115 = (f32[32,32,128]{2,1,0:T(8,128)S(1)}, f32[32,32,128]{2,1,0:T(8,128)S(1)}, bf16[256,128]{1,0:T(8,128)(2,1)S(1)}, f32[16,32,128]{2,1,0:T(8,128)S(1...) custom-call(f32[136,128]{1,0:T(8,128)S(1)} %collective-permute-done.rest_0_, ...), custom_call_target="tpu_custom_call" | custom-call | tf_op jit(solution)/shard_map/pallas_call | solution.py:308
  11.5 1.9 %collective-permute-start.4 = (f32[16,32,128]{2,1,0:T(8,128)S(1)}, f32[16,32,128]{2,1,0:T(8,128)S(1)}, u32[]{:S(2)}, u32[]{:S(2)}) collective-permute-start(f32[16,32,128]{2,1,0:T(8,128)S(1)} %get-tuple-element.35), channel_id=1, source_target_pairs={{0,8},{4,12},{8,0},{12,4},{1,9},{5,13},{9,1},{13,5},{2,10},{6,14},... | collective-permute-start | bytes 786440 | tf_op jit(solution)/shard_map/ppermute | solution.py:324
  13.4 0.4 collective-permute-start.5
  13.8 1.3 %collective-permute-start.6 = (f32[16,32,128]{2,1,0:T(8,128)S(1)}, f32[16,32,128]{2,1,0:T(8,128)S(1)}, u32[]{:S(2)}, u32[]{:S(2)}) collective-permute-start(f32[16,32,128]{2,1,0:T(8,128)S(1)} %get-tuple-element.37), channel_id=1, source_target_pairs={{0,4},{4,0},{8,12},{12,8},{1,5},{5,1},{9,13},{13,9},{2,6},{6,2},{1... | collective-permute-start | bytes 786440 | tf_op jit(solution)/shard_map/ppermute | solution.py:324
  15.1 1.9 %shard_map.116.index_ref = s32[32]{0:T(128)S(1)} custom-call(s32[32]{0:T(128)} %partner_ref.3, f32[32,32,128]{2,1,0:T(8,128)S(1)} %get-tuple-element.30._.guess_ref), custom_call_target="tpu_custom_call" | custom-call | tf_op jit(solution)/shard_map/pallas_call | solution.py:308
  17.1 5.2 %shard_map.117 = (f32[32,32,128]{2,1,0:T(8,128)S(1)}, f32[32,32,128]{2,1,0:T(8,128)S(1)}, f32[32,32,128]{2,1,0:T(8,128)S(1)}, f32[32,128]{1,0:T(8,128)S(1)}) custom-call(f32[32,32,128]{2,1,0:T(8,128)S(1)} %get-tuple-element.30._.guess_ref, f32[32,32,128]{2,1,0:T(8,128)S(1)} %get-tuple-element.31.slope_ref, f32[32,128,128]{2,1,0:T(8,128)} %coupling_ref.1, ...), custom_call_target="tpu_custom_call" | custom-call | tf_op jit(solution)/shard_map/pallas_call | solution.py:408
  22.3 7.1 %collective-permute-done.4.rest_0_ = f32[16,32,128]{2,1,0:T(8,128)S(1)} collective-permute-done((f32[16,32,128]{2,1,0:T(8,128)S(1)}, f32[16,32,128]{2,1,0:T(8,128)S(1)}, u32[]{:S(2)}, u32[]{:S(2)}) %collective-permute-start.4) | collective-permute-done | bytes 262176 | tf_op jit(solution)/shard_map/ppermute | solution.py:324
  29.4 7.8 %collective-permute-done.5.rest_1_ = f32[16,32,128]{2,1,0:T(8,128)S(1)} collective-permute-done((f32[16,32,128]{2,1,0:T(8,128)S(1)}, f32[16,32,128]{2,1,0:T(8,128)S(1)}, u32[]{:S(2)}, u32[]{:S(2)}) %collective-permute-start.5) | collective-permute-done | bytes 262176 | tf_op jit(solution)/shard_map/ppermute | solution.py:324
  37.2 0.0 collective-permute-done.6.rest_2_
  37.2 0.7 %shard_map.118 = (f32[32,128]{1,0:T(8,128)S(1)}, f32[32,32,128]{2,1,0:T(8,128)S(1)}) custom-call(s32[32]{0:T(128)S(1)} %shard_map.116.index_ref, f32[32,32,128]{2,1,0:T(8,128)S(1)} %get-tuple-element.32.base_ref, f32[32,32,128]{2,1,0:T(8,128)S(1)} %get-tuple-element.33.scale_ref.rest_6_, f32[32,32,128]{2,1,0:T(8,128)S(1)} %get-tuple-element.30._.guess_ref, ...), custom_call_target="tpu_custom_call" | custom-call | tf_op jit(solution)/shard_map/pallas_call | solution.py:308
  38.0 1.9 %collective-permute-start.9 = (f32[32,128]{1,0:T(8,128)S(1)}, f32[32,128]{1,0:T(8,128)S(1)}, u32[]{:S(2)}, u32[]{:S(2)}) collective-permute-start(f32[32,128]{1,0:T(8,128)S(1)} %get-tuple-element.38.rest_0_), channel_id=1, source_target_pairs={{0,3},{1,2},{2,1},{3,0},{4,7},{5,6},{6,5},{7,4},{8,11},{9,10},{10,... | collective-permute-start | bytes 49160 | tf_op jit(solution)/shard_map/ppermute | solution.py:324
  39.8 0.3 collective-permute-start.8
  40.1 0.2 collective-permute-start.7
  40.3 0.8 %shard_map.119 = (f32[32,32,128]{2,1,0:T(8,128)S(1)}, f32[32,32,128]{2,1,0:T(8,128)}) custom-call(f32[32,32,128]{2,1,0:T(8,128)S(1)} %get-tuple-element.40.near_ref, f32[32,32,128]{2,1,0:T(8,128)S(1)} %get-tuple-element.32.base_ref, f32[32,32,128]{2,1,0:T(8,128)S(1)} %get-tuple-element.41.inv_ref, f32[32,32,128]{2,1,0:T(8,128)S(1)} %get-tuple-element.30._.guess_ref, ...), custom_call_target="tpu_custom_call" | custom-call | tf_op jit(solution)/shard_map/pallas_call | solution.py:308
  41.1 0.5 %collective-permute-done.9.rest_3_ = f32[32,128]{1,0:T(8,128)S(1)} collective-permute-done((f32[32,128]{1,0:T(8,128)S(1)}, f32[32,128]{1,0:T(8,128)S(1)}, u32[]{:S(2)}, u32[]{:S(2)}) %collective-permute-start.9) | collective-permute-done | bytes 16416 | tf_op jit(solution)/shard_map/ppermute | solution.py:324
  41.6 1.1 %collective-permute-done.8.rest_2_ = f32[32,128]{1,0:T(8,128)S(1)} collective-permute-done((f32[32,128]{1,0:T(8,128)S(1)}, f32[32,128]{1,0:T(8,128)S(1)}, u32[]{:S(2)}, u32[]{:S(2)}) %collective-permute-start.8) | collective-permute-done | bytes 16416 | tf_op jit(solution)/shard_map/ppermute | solution.py:324
  42.7 0.0 collective-permute-done.7.rest_1_
  42.7 1.0 %shard_map.120 = f32[32,32,128]{2,1,0:T(8,128)} custom-call(f32[32,128]{1,0:T(8,128)S(1)} %get-tuple-element.38.rest_0_, f32[32,128]{1,0:T(8,128)S(1)} %collective-permute-done.7.rest_1_, f32[32,128]{1,0:T(8,128)S(1)} %collective-permute-done.8.rest_2_, f32[32,128]{1,0:T(8,128)S(1)} %collective-permute-done.9.rest_3_, ...), custom_call_target="tpu_custom_call" | custom-call | tf_op jit(solution)/shard_map/pallas_call | solution.py:308
Async XLA Ops:
  2.1 6.4 %collective-permute-start = (f32[136,128]{1,0:T(8,128)S(1)}, f32[136,128]{1,0:T(8,128)S(1)}, u32[]{:S(2)}, u32[]{:S(2)}) collective-permute-start(f32[136,128]{1,0:T(8,128)S(1)} %get-tuple-element.23), channel_id=1, source_target_pairs={{0,8},{4,12},{8,0},{12,4},{1,9},{5,13},{9,1},{13,5},{2,10},{6,14},... | collective-permute-start | bytes 208904 | tf_op jit(solution)/shard_map/ppermute | solution.py:324
  4.5 6.1 %collective-permute-start.1 = (f32[136,128]{1,0:T(8,128)S(1)}, f32[136,128]{1,0:T(8,128)S(1)}, u32[]{:S(2)}, u32[]{:S(2)}) collective-permute-start(f32[136,128]{1,0:T(8,128)S(1)} %get-tuple-element.24), channel_id=1, source_target_pairs={{0,12},{4,8},{8,4},{12,0},{1,13},{5,9},{9,5},{13,1},{2,14},{6,10},... | collective-permute-start | bytes 208904 | tf_op jit(solution)/shard_map/ppermute | solution.py:324
  4.5 6.1 %collective-permute-start.2 = (f32[136,128]{1,0:T(8,128)S(1)}, f32[136,128]{1,0:T(8,128)S(1)}, u32[]{:S(2)}, u32[]{:S(2)}) collective-permute-start(f32[136,128]{1,0:T(8,128)S(1)} %get-tuple-element.25), channel_id=1, source_target_pairs={{0,4},{4,0},{8,12},{12,8},{1,5},{5,1},{9,13},{13,9},{2,6},{6,2},{1... | collective-permute-start | bytes 208904 | tf_op jit(solution)/shard_map/ppermute | solution.py:324
  5.7 2.6 %collective-permute-start.3 = (f32[64,128]{1,0:T(8,128)S(1)}, f32[64,128]{1,0:T(8,128)S(1)}, u32[]{:S(2)}, u32[]{:S(2)}) collective-permute-start(f32[64,128]{1,0:T(8,128)S(1)} %get-tuple-element.26.rest_3_), channel_id=1, source_target_pairs={{0,1},{1,0},{2,3},{3,2},{4,5},{5,4},{6,7},{7,6},{8,9},{9,8},{10,11... | collective-permute-start | bytes 98312 | tf_op jit(solution)/shard_map/ppermute | solution.py:324
  11.5 17.9 %collective-permute-start.4 = (f32[16,32,128]{2,1,0:T(8,128)S(1)}, f32[16,32,128]{2,1,0:T(8,128)S(1)}, u32[]{:S(2)}, u32[]{:S(2)}) collective-permute-start(f32[16,32,128]{2,1,0:T(8,128)S(1)} %get-tuple-element.35), channel_id=1, source_target_pairs={{0,8},{4,12},{8,0},{12,4},{1,9},{5,13},{9,1},{13,5},{2,10},{6,14},... | collective-permute-start | bytes 786440 | tf_op jit(solution)/shard_map/ppermute | solution.py:324
  13.4 23.8 %collective-permute-start.5 = (f32[16,32,128]{2,1,0:T(8,128)S(1)}, f32[16,32,128]{2,1,0:T(8,128)S(1)}, u32[]{:S(2)}, u32[]{:S(2)}) collective-permute-start(f32[16,32,128]{2,1,0:T(8,128)S(1)} %get-tuple-element.36), channel_id=1, source_target_pairs={{0,12},{4,8},{8,4},{12,0},{1,13},{5,9},{9,5},{13,1},{2,14},{6,10},... | collective-permute-start | bytes 786440 | tf_op jit(solution)/shard_map/ppermute | solution.py:324
  13.8 23.4 %collective-permute-start.6 = (f32[16,32,128]{2,1,0:T(8,128)S(1)}, f32[16,32,128]{2,1,0:T(8,128)S(1)}, u32[]{:S(2)}, u32[]{:S(2)}) collective-permute-start(f32[16,32,128]{2,1,0:T(8,128)S(1)} %get-tuple-element.37), channel_id=1, source_target_pairs={{0,4},{4,0},{8,12},{12,8},{1,5},{5,1},{9,13},{13,9},{2,6},{6,2},{1... | collective-permute-start | bytes 786440 | tf_op jit(solution)/shard_map/ppermute | solution.py:324
  38.0 3.6 %collective-permute-start.9 = (f32[32,128]{1,0:T(8,128)S(1)}, f32[32,128]{1,0:T(8,128)S(1)}, u32[]{:S(2)}, u32[]{:S(2)}) collective-permute-start(f32[32,128]{1,0:T(8,128)S(1)} %get-tuple-element.38.rest_0_), channel_id=1, source_target_pairs={{0,3},{1,2},{2,1},{3,0},{4,7},{5,6},{6,5},{7,4},{8,11},{9,10},{10,... | collective-permute-start | bytes 49160 | tf_op jit(solution)/shard_map/ppermute | solution.py:324
  39.8 2.9 %collective-permute-start.8 = (f32[32,128]{1,0:T(8,128)S(1)}, f32[32,128]{1,0:T(8,128)S(1)}, u32[]{:S(2)}, u32[]{:S(2)}) collective-permute-start(f32[32,128]{1,0:T(8,128)S(1)} %get-tuple-element.38.rest_0_), channel_id=1, source_target_pairs={{0,2},{1,3},{2,0},{3,1},{4,6},{5,7},{6,4},{7,5},{8,10},{9,11},{10,... | collective-permute-start | bytes 49160 | tf_op jit(solution)/shard_map/ppermute | solution.py:324
  40.1 2.6 %collective-permute-start.7 = (f32[32,128]{1,0:T(8,128)S(1)}, f32[32,128]{1,0:T(8,128)S(1)}, u32[]{:S(2)}, u32[]{:S(2)}) collective-permute-start(f32[32,128]{1,0:T(8,128)S(1)} %get-tuple-element.38.rest_0_), channel_id=1, source_target_pairs={{0,1},{1,0},{2,3},{3,2},{4,5},{5,4},{6,7},{7,6},{8,9},{9,8},{10,11... | collective-permute-start | bytes 49160 | tf_op jit(solution)/shard_map/ppermute | solution.py:324

commit v8 on v7

--- a/solution.py
+++ b/solution.py
@@ -37,12 +37,7 @@
 
 
 def lowest(mask):
-    return (31 - lax.clz(mask & -mask)) & 31
-
-
-def cut(x):
-    high = x.astype(jnp.bfloat16)
-    return high, (x - high.astype(F32)).astype(jnp.bfloat16)
+    return jnp.maximum(31 - lax.clz(mask & -mask), 0)
 
 
 def halves(mask):
@@ -121,7 +116,7 @@
     read_masks(n, span, blocks, reads, mine)
     for copy in copies[2:]:
         copy.wait()
-    lane = lax.broadcasted_iota(I32, (8, nodes), 1)
+    line = lax.broadcasted_iota(I32, (8, nodes), 0)
     for k, out in zip(rounds, outs):
         for rank in range(CAP):
             raw = raw_ref.at[source[k * CAP + rank]]
@@ -132,7 +127,7 @@
         values = halves(mine[die ^ k])
         values += [place[k * CAP + rank] for rank in range(CAP)]
         for j, value in enumerate(values):
-            row = jnp.where(lane == j, value, row)
+            row = jnp.where(line == j, value, row)
         out[pl.ds(2 * CAP * scen, 8), :] = row.astype(F32)
 
 
@@ -154,47 +149,41 @@
             slope_ref[local] = slope(raw, guess)
 
 
-def pack(meta, guess_ref, out):
-    want = joined(meta[0], meta[1])
-    for slot in range(out.shape[0]):
-        out[slot] = guess_ref[lowest(want)]
-        want = want & (want - 1)
-
-
-def serve_kernel(n, nblk, *rest):
+def serve_kernel(picks, nblk, *rest):
+    n = len(picks) + 1
     arrived, rest = rest[: n - 1], rest[n - 1 :]
     inverses, rest = rest[:nblk], rest[nblk:]
     old_guess, old_slope, guess_ref, slope_ref, whole_ref, *rest = rest
-    outs, (ints, meta, sem) = rest[: n - 1], rest[n - 1 :]
+    outs = rest
     blocks, scen, nodes = guess_ref.shape
-    for k in range(n - 1):
-        ints[k] = arrived[k][pl.ds(2 * CAP * scen, 8), :].astype(I32)
-    copy = pltpu.make_async_copy(ints, meta, sem)
-    copy.start()
+
+    def told(k, j):
+        return arrived[k][2 * CAP * scen + j, 0].astype(I32)
+
     for at in range(blocks):
         guess_ref[at] = old_guess[at]
         slope_ref[at] = old_slope[at]
     height = inverses[0].shape[0]
     for k in range(nblk):
         at = pl.multiple_of((lax.axis_index("blk") ^ k) * height, height)
-        high, low = cut(inverses[k][...])
-        whole_ref[pl.ds(at, height), :] = high
-        whole_ref[pl.ds(nodes + at, height), :] = low
-    copy.wait()
+        whole_ref[pl.ds(at, height), :] = inverses[k][...]
     for k in range(n - 1):
         for rank in range(CAP):
-            place = meta[k, 0, 2 + rank]
+            place = told(k, 2 + rank)
 
             @pl.when(place >= 0)
             def _(k=k, rank=rank, place=place):
                 guess_ref[place] = arrived[k][pl.ds(rank * scen, scen), :]
                 slope_ref[place] = arrived[k][pl.ds((CAP + rank) * scen, scen), :]
 
-    for k, out in enumerate(outs):
-        pack([meta[k, 0, 0], meta[k, 0, 1]], guess_ref, out)
-
-
-def where_kernel(rounds, span, rcap, partner_ref, _, index_ref, reads, mine, starts, sem):
+    for k, out in zip(picks, outs):
+        want = joined(told(k, 0), told(k, 1))
+        for slot in range(out.shape[0]):
+            out[slot] = guess_ref[lowest(want)]
+            want = want & (want - 1)
+
+
+def where_kernel(rounds, span, rcap, last, partner_ref, _, index_ref, late_ref, reads, mine, starts, sem):
     n = len(rounds) + 1
     blocks = index_ref.shape[0]
     die = lax.axis_index("die")
@@ -206,15 +195,18 @@
     copy.wait()
     read_masks(n, span, blocks, reads, mine)
 
-    def step(at, carry):
+    def step(at, count):
         owner, local = divmod_static(reads[at], span)
         local = divmod_static(local, blocks)[1]
         k = owner ^ die
         slot = bits_set(mine[owner] & (bit_of(local) - 1))
         index_ref[at] = jnp.where(k == 0, local - blocks, starts[k] + slot)
-        return carry
-
-    lax.fori_loop(0, blocks, step, 0)
+        late_ref[1 + count] = at
+        return count + jnp.where(k == rounds[last], 1, 0)
+
+    for at in range(1 + blocks):
+        late_ref[at] = 0
+    late_ref[0] = lax.fori_loop(0, blocks, step, jnp.int32(0))
 
 
 def local_kernel(
@@ -248,36 +240,52 @@
         )
 
 
-def share_kernel(n, index_ref, base_ref, scale_ref, guess_ref, wire_ref, *rest):
-    blocks_in, (share_ref, near_ref, pool) = rest[: n - 1], rest[n - 1 :]
+def gather_kernel(rcap, last, index_ref, base_ref, scale_ref, guess_ref, wire_ref, *rest):
+    blocks_in, (near_ref, share_ref, pool) = rest[:-3], rest[-3:]
     blocks = guess_ref.shape[0]
-    start = 0
-    for ref in blocks_in:
-        for slot in range(ref.shape[0]):
-            pool[start + slot] = ref[slot]
-        start += ref.shape[0]
+    for at, ref in enumerate(blocks_in):
+        for slot in range(rcap):
+            pool[(at + (at >= last)) * rcap + slot] = ref[slot]
     share = jnp.zeros(share_ref.shape, F32)
     for at in range(blocks):
         index = index_ref[at]
         own = index < 0
         near = guess_ref[jnp.where(own, index + blocks, 0)]
         near = jnp.where(own, near, pool[jnp.maximum(index, 0)])
+        missing = (index >= last * rcap) & (index < (last + 1) * rcap)
+        near = jnp.where(missing, 0.0, near)
         near_ref[at] = near
         share = share + scale_ref[at] * (base_ref[at] - wire_ref[at : at + 1, :] * near)
     share_ref[...] = share
 
 
-def residual_kernel(parts, near_ref, base_ref, inv_ref, guess_ref, wire_ref, partial_ref, out_ref, held, sems):
+def share_kernel(rcap, last, index_ref, late_ref, scale_ref, wire_ref, part_ref, block_ref, share_ref):
+    share = part_ref[...]
+    for slot in range(min(rcap, wire_ref.shape[0])):
+        at = late_ref[1 + slot]
+        there = slot < late_ref[0]
+        block = block_ref[jnp.where(there, index_ref[at] - last * rcap, 0)]
+        share = share - jnp.where(there, scale_ref[at] * wire_ref[pl.ds(at, 1), :] * block, 0.0)
+    share_ref[...] = share
+
+
+def residual_kernel(
+    rcap, last, parts, index_ref, near_ref, block_ref, base_ref, inv_ref, guess_ref, wire_ref,
+    partial_ref, out_ref, held, sems
+):
     step = guess_ref.shape[0] // parts
     copies = []
     for part in range(parts):
         for at in range(part * step, (part + 1) * step):
-            residual = base_ref[at] - wire_ref[at : at + 1, :] * near_ref[at]
+            slot = index_ref[at] - last * rcap
+            missing = (slot >= 0) & (slot < rcap)
+            near = jnp.where(missing, block_ref[jnp.where(missing, slot, 0)], near_ref[at])
+            residual = base_ref[at] - wire_ref[at : at + 1, :] * near
             held[at] = residual
             partial_ref[at] = guess_ref[at] - residual * inv_ref[at]
         some = pl.ds(part * step, step)
         copies.append(pltpu.make_async_copy(held.at[some], out_ref.at[some], sems.at[part]))
-        copies[-1].start()
+        copies[-1].start(priority=part % 2)
     for copy in copies:
         copy.wait()
 
@@ -287,11 +295,9 @@
     total = shares[0][...]
     for share in shares[1:]:
         total = total + share[...]
-    nodes = total.shape[1]
-    high, low = cut(total)
-    region = jnp.dot(high, whole_ref[:nodes, :], preferred_element_type=F32)
-    region += jnp.dot(low, whole_ref[:nodes, :], preferred_element_type=F32)
-    region += jnp.dot(high, whole_ref[nodes:, :], preferred_element_type=F32)
+    region = jnp.dot(
+        total, whole_ref[...], precision=lax.Precision.HIGHEST, preferred_element_type=F32
+    )
     step = partial_ref.shape[0] // parts
     copies = []
     for part in range(parts):
@@ -299,7 +305,7 @@
             held[at] = partial_ref[at] + scale_ref[at] * region
         span = pl.ds(part * step, step)
         copies.append(pltpu.make_async_copy(held.at[span], updated_ref.at[span], sems.at[part]))
-        copies[-1].start()
+        copies[-1].start(priority=part % 2)
     for copy in copies:
         copy.wait()
 
@@ -353,11 +359,12 @@
         return pltpu.SMEM((count,), I32)
 
     block = tiles(blocks)
-    square = jax.ShapeDtypeStruct((2 * nodes, nodes), jnp.bfloat16)
+    square = jax.ShapeDtypeStruct((nodes, nodes), F32)
     rows = region_inverse[0]
     message = jax.ShapeDtypeStruct((2 * CAP * scen + 8, nodes), F32)
 
     rounds = [*range(2, n), 1]
+    replies = [*range(n - 1, 2, -1), 1, 2] if n > 2 else [1]
     new_slot, partner = in_hbm(new_slot), in_hbm(partner)
     raw, rows, *leaving = call(
         functools.partial(leave_kernel, rounds, span),
@@ -382,24 +389,20 @@
         [scalars(blocks), pltpu.SemaphoreType.DMA],
     )
     guess, slopes, whole, *served = call(
-        functools.partial(serve_kernel, n, nblk),
+        functools.partial(serve_kernel, [rounds.index(k) for k in replies], nblk),
         [block, block, square] + [tiles(rcap)] * (n - 1),
         [*arrived, *inverses, old_guess, old_slope],
         [VMEM] * (n - 1 + nblk + 2),
         [VMEM] * (n + 2),
-        [
-            pltpu.VMEM((n - 1, 8, nodes), I32),
-            pltpu.SMEM((n - 1, 8, nodes), I32),
-            pltpu.SemaphoreType.DMA,
-        ],
-    )
-    others = [swap(x, "die", n, k) for x, k in zip(served, rounds)]
-    (index,) = call(
-        functools.partial(where_kernel, rounds, span, rcap),
-        [jax.ShapeDtypeStruct((blocks,), I32)],
+    )
+    others = [swap(x, "die", n, k) for x, k in zip(served, replies)]
+    last = n - 2
+    index, late = call(
+        functools.partial(where_kernel, replies, span, rcap, last),
+        [scalars(blocks), scalars(1 + blocks)],
         [partner, guess],
         [HBM, ANY],
-        [SMEM],
+        [SMEM, SMEM],
         [scalars(blocks), scalars(n), scalars(n), pltpu.SemaphoreType.DMA],
     )
     step = 8 if blocks % 8 == 0 else blocks
@@ -432,20 +435,31 @@
         in_hbm(region_gain),
         in_hbm(drive),
     )
-    share, near = call(
-        functools.partial(share_kernel, n),
-        [jax.ShapeDtypeStruct((scen, nodes), F32), block],
-        [index, base, scale, guess, wire, *others],
-        [SMEM] + [VMEM] * (4 + n - 1),
+    index = pltpu.with_memory_space_constraint(index, pltpu.SMEM)
+    late = pltpu.with_memory_space_constraint(late, pltpu.SMEM)
+    flat_share = jax.ShapeDtypeStruct((scen, nodes), F32)
+    first = others[:last] + others[last + 1 :]
+    near, part = call(
+        functools.partial(gather_kernel, rcap, last),
+        [block, flat_share],
+        [index, base, scale, guess, wire, *first],
+        [SMEM] + [VMEM] * (4 + len(first)),
         [VMEM] * 2,
         [pltpu.VMEM(((n - 1) * rcap, scen, nodes), F32)],
     )
-    parts = 4 if blocks % 4 == 0 else 1
+    (share,) = call(
+        functools.partial(share_kernel, rcap, last),
+        [flat_share],
+        [index, late, scale, wire, part, others[last]],
+        [SMEM] * 2 + [VMEM] * 4,
+        [VMEM],
+    )
+    parts = 8 if blocks % 8 == 0 else 1
     partial, residual = call(
-        functools.partial(residual_kernel, parts),
+        functools.partial(residual_kernel, rcap, last, parts),
         [block, block],
-        [near, base, inv, guess, wire],
-        [VMEM] * 5,
+        [index, near, others[last], base, inv, guess, wire],
+        [SMEM] + [VMEM] * 6,
         [VMEM, HBM],
         [pltpu.VMEM((blocks, scen, nodes), F32), pltpu.SemaphoreType.DMA((parts,))],
     )

time: 43.9 us -> 45.2 us (1.030)
  the two profiles are of different devices: /device:TPU:9 before, /device:TPU:0 now
where the time goes in v8:
time: 45.2 us; the launch traced here: 44.9 us
  waiting for transfers between devices  20.4 us (45%)
  starting transfers between devices  12.1 us (27%)
  Pallas kernels  11.8 us (26%)
  between operations  0.7 us (2%)
    ppermute x10, waiting for transfers between devices, swap(): return lax.ppermute(x, axes, [(d, d ^ k) for d in range(n)])  20.4 us
    ppermute x10, starting transfers between devices, swap(): return lax.ppermute(x, axes, [(d, d ^ k) for d in range(n)])  12.1 us
    pallas_call x8, Pallas kernels, call(): pl.pallas_call(body, out_shape=outs, in_specs=in_specs, out_specs=out_spe...  6.59 us
    pallas_call x1, Pallas kernels, shards(): pl.pallas_call(local_kernel, grid=(blocks // step,), out_shape=[block, bl...  5.19 us
  transfers between devices with their start and end apart: 10, of which 9 were waited for; matrix products, arithmetic and copies ran while one was open for 0% of the time, Pallas kernels for 19%

profile of v8, /device:TPU:0, one launch (start us, length us, event | category | flops | bytes accessed | tf_op | source)
XLA Modules:
  0.0 44.9 jit_solution(12047330228069964653)
XLA Ops:
  0.6 1.5 %shard_map.113 = (f32[32,3,32,128]{3,2,1,0:T(8,128)S(1)}, f32[64,128]{1,0:T(8,128)S(1)}, f32[136,128]{1,0:T(8,128)S(1)}, f32[136,128]{1,0:T(8,128)S(1)}, f32[136,128]{1,0:T(8,128)S(1)}) custom-call(s32[32]{0:T(128)} %new_slot_ref.3, s32[32]{0:T(128)} %partner_ref.3, f32[32,3,32,128]{3,2,1,0:T(8,128)} %history_ref.1, f32[64,128]{1,0:T(8,128)} %bitcast.1), custom_call_target="tpu_custom_call" | custom-call | tf_op jit(solution)/shard_map/pallas_call | solution.py:314
  2.1 4.1 %collective-permute-start = (f32[136,128]{1,0:T(8,128)S(1)}, f32[136,128]{1,0:T(8,128)S(1)}, u32[]{:S(2)}, u32[]{:S(2)}) collective-permute-start(f32[136,128]{1,0:T(8,128)S(1)} %get-tuple-element.25), channel_id=1, source_target_pairs={{0,8},{4,12},{8,0},{12,4},{1,9},{5,13},{9,1},{13,5},{2,10},{6,14},... | collective-permute-start | bytes 208904 | tf_op jit(solution)/shard_map/ppermute | solution.py:330
  6.2 1.3 %collective-permute-start.1 = (f32[136,128]{1,0:T(8,128)S(1)}, f32[136,128]{1,0:T(8,128)S(1)}, u32[]{:S(2)}, u32[]{:S(2)}) collective-permute-start(f32[136,128]{1,0:T(8,128)S(1)} %get-tuple-element.26), channel_id=1, source_target_pairs={{0,12},{4,8},{8,4},{12,0},{1,13},{5,9},{9,5},{13,1},{2,14},{6,10},... | collective-permute-start | bytes 208904 | tf_op jit(solution)/shard_map/ppermute | solution.py:330
  7.6 0.2 collective-permute-start.2
  7.8 0.0 collective-permute-start.3
  7.8 1.1 %shard_map.114 = (f32[32,32,128]{2,1,0:T(8,128)S(1)}, f32[32,32,128]{2,1,0:T(8,128)S(1)}) custom-call(s32[32]{0:T(128)} %new_slot_ref.3, f32[32,3,32,128]{3,2,1,0:T(8,128)S(1)} %get-tuple-element.29.raw_ref), custom_call_target="tpu_custom_call" | custom-call | tf_op jit(solution)/shard_map/pallas_call | solution.py:314
  8.9 0.1 collective-permute-done.3.rest_4_
  9.0 1.1 %collective-permute-done.rest_0_ = f32[136,128]{1,0:T(8,128)S(1)} collective-permute-done((f32[136,128]{1,0:T(8,128)S(1)}, f32[136,128]{1,0:T(8,128)S(1)}, u32[]{:S(2)}, u32[]{:S(2)}) %collective-permute-start) | collective-permute-done | bytes 69664 | tf_op jit(solution)/shard_map/ppermute | solution.py:330
  10.1 2.5 %collective-permute-done.1.rest_1_ = f32[136,128]{1,0:T(8,128)S(1)} collective-permute-done((f32[136,128]{1,0:T(8,128)S(1)}, f32[136,128]{1,0:T(8,128)S(1)}, u32[]{:S(2)}, u32[]{:S(2)}) %collective-permute-start.1) | collective-permute-done | bytes 69664 | tf_op jit(solution)/shard_map/ppermute | solution.py:330
  12.6 0.1 collective-permute-done.2.rest_2_
  12.6 0.5 %shard_map.115 = (f32[32,32,128]{2,1,0:T(8,128)S(1)}, f32[32,32,128]{2,1,0:T(8,128)S(1)}, f32[128,128]{1,0:T(8,128)S(1)}, f32[16,32,128]{2,1,0:T(8,128)S(1)}, f3...) custom-call(f32[136,128]{1,0:T(8,128)S(1)} %collective-permute-done.rest_0_, ...), custom_call_target="tpu_custom_call" | custom-call | tf_op jit(solution)/shard_map/pallas_call | solution.py:314
  13.1 3.3 %collective-permute-start.4 = (f32[16,32,128]{2,1,0:T(8,128)S(1)}, f32[16,32,128]{2,1,0:T(8,128)S(1)}, u32[]{:S(2)}, u32[]{:S(2)}) collective-permute-start(f32[16,32,128]{2,1,0:T(8,128)S(1)} %get-tuple-element.39), channel_id=1, source_target_pairs={{0,12},{4,8},{8,4},{12,0},{1,13},{5,9},{9,5},{13,1},{2,14},{6,10},... | collective-permute-start | bytes 786440 | tf_op jit(solution)/shard_map/ppermute | solution.py:330
  16.4 0.3 collective-permute-start.5
  16.7 0.9 %collective-permute-start.6 = (f32[16,32,128]{2,1,0:T(8,128)S(1)}, f32[16,32,128]{2,1,0:T(8,128)S(1)}, u32[]{:S(2)}, u32[]{:S(2)}) collective-permute-start(f32[16,32,128]{2,1,0:T(8,128)S(1)} %get-tuple-element.42), channel_id=1, source_target_pairs={{0,8},{4,12},{8,0},{12,4},{1,9},{5,13},{9,1},{13,5},{2,10},{6,14},... | collective-permute-start | bytes 786440 | tf_op jit(solution)/shard_map/ppermute | solution.py:330
  17.6 1.4 %shard_map.116 = (s32[32]{0:T(128)S(4)}, s32[33]{0:T(128)S(4)}) custom-call(s32[32]{0:T(128)} %partner_ref.3, f32[32,32,128]{2,1,0:T(8,128)S(1)} %get-tuple-element.32._.guess_ref), custom_call_target="tpu_custom_call" | custom-call | tf_op jit(solution)/shard_map/pallas_call | solution.py:314
  19.0 5.2 %shard_map.117 = (f32[32,32,128]{2,1,0:T(8,128)S(1)}, f32[32,32,128]{2,1,0:T(8,128)S(1)}, f32[32,32,128]{2,1,0:T(8,128)S(1)}, f32[32,128]{1,0:T(8,128)S(1)}) custom-call(f32[32,32,128]{2,1,0:T(8,128)S(1)} %get-tuple-element.32._.guess_ref, f32[32,32,128]{2,1,0:T(8,128)S(1)} %get-tuple-element.35.slope_ref, f32[32,128,128]{2,1,0:T(8,128)} %coupling_ref.1, ...), custom_call_target="tpu_custom_call" | custom-call | tf_op jit(solution)/shard_map/pallas_call | solution.py:411
  24.2 0.1 collective-permute-done.4.rest_0_
  24.3 4.5 %collective-permute-done.5.rest_1_ = f32[16,32,128]{2,1,0:T(8,128)S(1)} collective-permute-done((f32[16,32,128]{2,1,0:T(8,128)S(1)}, f32[16,32,128]{2,1,0:T(8,128)S(1)}, u32[]{:S(2)}, u32[]{:S(2)}) %collective-permute-start.5) | collective-permute-done | bytes 262176 | tf_op jit(solution)/shard_map/ppermute | solution.py:330
  28.8 0.2 shard_map.118
  29.0 9.9 %collective-permute-done.6.block_ref = f32[16,32,128]{2,1,0:T(8,128)S(1)} collective-permute-done((f32[16,32,128]{2,1,0:T(8,128)S(1)}, f32[16,32,128]{2,1,0:T(8,128)S(1)}, u32[]{:S(2)}, u32[]{:S(2)}) %collective-permute-start.6) | collective-permute-done | bytes 262176 | tf_op jit(solution)/shard_map/ppermute | solution.py:330
  38.9 0.1 shard_map.119.rest_0_
  38.9 1.2 %collective-permute-start.9 = (f32[32,128]{1,0:T(8,128)S(1)}, f32[32,128]{1,0:T(8,128)S(1)}, u32[]{:S(2)}, u32[]{:S(2)}) collective-permute-start(f32[32,128]{1,0:T(8,128)S(1)} %shard_map.119.rest_0_), channel_id=1, source_target_pairs={{0,3},{1,2},{2,1},{3,0},{4,7},{5,6},{6,5},{7,4},{8,11},{9,10},{10,... | collective-permute-start | bytes 49160 | tf_op jit(solution)/shard_map/ppermute | solution.py:330
  40.2 0.5 %collective-permute-start.8 = (f32[32,128]{1,0:T(8,128)S(1)}, f32[32,128]{1,0:T(8,128)S(1)}, u32[]{:S(2)}, u32[]{:S(2)}) collective-permute-start(f32[32,128]{1,0:T(8,128)S(1)} %shard_map.119.rest_0_), channel_id=1, source_target_pairs={{0,2},{1,3},{2,0},{3,1},{4,6},{5,7},{6,4},{7,5},{8,10},{9,11},{10,... | collective-permute-start | bytes 49160 | tf_op jit(solution)/shard_map/ppermute | solution.py:330
  40.7 0.2 collective-permute-start.7
  40.9 0.9 %shard_map.120 = (f32[32,32,128]{2,1,0:T(8,128)S(1)}, f32[32,32,128]{2,1,0:T(8,128)}) custom-call(s32[32]{0:T(128)S(4)} %get-tuple-element.33.index_ref, f32[32,32,128]{2,1,0:T(8,128)S(1)} %get-tuple-element.44.near_ref, f32[16,32,128]{2,1,0:T(8,128)S(1)} %collective-permute-done.6.block_ref, f32[32,32,128]{2,1,0:T(8,128)S(1)} %get-tuple-element.38.base_ref, ...), custom_call_target="tpu_custom_call" | custom-call | tf_op jit(solution)/shard_map/pallas_call | solution.py:314
  41.8 0.4 collective-permute-done.9.rest_3_
  42.2 1.7 %collective-permute-done.8.rest_2_ = f32[32,128]{1,0:T(8,128)S(1)} collective-permute-done((f32[32,128]{1,0:T(8,128)S(1)}, f32[32,128]{1,0:T(8,128)S(1)}, u32[]{:S(2)}, u32[]{:S(2)}) %collective-permute-start.8) | collective-permute-done | bytes 16416 | tf_op jit(solution)/shard_map/ppermute | solution.py:330
  43.9 0.0 collective-permute-done.7.rest_1_
  43.9 1.0 %shard_map.121 = f32[32,32,128]{2,1,0:T(8,128)} custom-call(f32[32,128]{1,0:T(8,128)S(1)} %shard_map.119.rest_0_, f32[32,128]{1,0:T(8,128)S(1)} %collective-permute-done.7.rest_1_, f32[32,128]{1,0:T(8,128)S(1)} %collective-permute-done.8.rest_2_, f32[32,128]{1,0:T(8,128)S(1)} %collective-permute-done.9.rest_3_, f32[128,128]{1,0:T(8,128)S(1)} %get-tuple-element.43.rest_4_, ...), custom_call_target="tpu_custom_call" | custom-call | tf_op jit(solution)/shard_map/pallas_call | solution.py:314
Async XLA Ops:
  2.1 8.0 %collective-permute-start = (f32[136,128]{1,0:T(8,128)S(1)}, f32[136,128]{1,0:T(8,128)S(1)}, u32[]{:S(2)}, u32[]{:S(2)}) collective-permute-start(f32[136,128]{1,0:T(8,128)S(1)} %get-tuple-element.25), channel_id=1, source_target_pairs={{0,8},{4,12},{8,0},{12,4},{1,9},{5,13},{9,1},{13,5},{2,10},{6,14},... | collective-permute-start | bytes 208904 | tf_op jit(solution)/shard_map/ppermute | solution.py:330
  6.2 6.3 %collective-permute-start.1 = (f32[136,128]{1,0:T(8,128)S(1)}, f32[136,128]{1,0:T(8,128)S(1)}, u32[]{:S(2)}, u32[]{:S(2)}) collective-permute-start(f32[136,128]{1,0:T(8,128)S(1)} %get-tuple-element.26), channel_id=1, source_target_pairs={{0,12},{4,8},{8,4},{12,0},{1,13},{5,9},{9,5},{13,1},{2,14},{6,10},... | collective-permute-start | bytes 208904 | tf_op jit(solution)/shard_map/ppermute | solution.py:330
  7.6 5.1 %collective-permute-start.2 = (f32[136,128]{1,0:T(8,128)S(1)}, f32[136,128]{1,0:T(8,128)S(1)}, u32[]{:S(2)}, u32[]{:S(2)}) collective-permute-start(f32[136,128]{1,0:T(8,128)S(1)} %get-tuple-element.27), channel_id=1, source_target_pairs={{0,4},{4,0},{8,12},{12,8},{1,5},{5,1},{9,13},{13,9},{2,6},{6,2},{1... | collective-permute-start | bytes 208904 | tf_op jit(solution)/shard_map/ppermute | solution.py:330
  7.8 1.2 %collective-permute-start.3 = (f32[64,128]{1,0:T(8,128)S(1)}, f32[64,128]{1,0:T(8,128)S(1)}, u32[]{:S(2)}, u32[]{:S(2)}) collective-permute-start(f32[64,128]{1,0:T(8,128)S(1)} %get-tuple-element.28.rest_3_), channel_id=1, source_target_pairs={{0,1},{1,0},{2,3},{3,2},{4,5},{5,4},{6,7},{7,6},{8,9},{9,8},{10,11... | collective-permute-start | bytes 98312 | tf_op jit(solution)/shard_map/ppermute | solution.py:330
  13.1 11.1 %collective-permute-start.4 = (f32[16,32,128]{2,1,0:T(8,128)S(1)}, f32[16,32,128]{2,1,0:T(8,128)S(1)}, u32[]{:S(2)}, u32[]{:S(2)}) collective-permute-start(f32[16,32,128]{2,1,0:T(8,128)S(1)} %get-tuple-element.39), channel_id=1, source_target_pairs={{0,12},{4,8},{8,4},{12,0},{1,13},{5,9},{9,5},{13,1},{2,14},{6,10},... | collective-permute-start | bytes 786440 | tf_op jit(solution)/shard_map/ppermute | solution.py:330
  16.4 12.4 %collective-permute-start.5 = (f32[16,32,128]{2,1,0:T(8,128)S(1)}, f32[16,32,128]{2,1,0:T(8,128)S(1)}, u32[]{:S(2)}, u32[]{:S(2)}) collective-permute-start(f32[16,32,128]{2,1,0:T(8,128)S(1)} %get-tuple-element.40), channel_id=1, source_target_pairs={{0,4},{4,0},{8,12},{12,8},{1,5},{5,1},{9,13},{13,9},{2,6},{6,2},{1... | collective-permute-start | bytes 786440 | tf_op jit(solution)/shard_map/ppermute | solution.py:330
  16.7 22.2 %collective-permute-start.6 = (f32[16,32,128]{2,1,0:T(8,128)S(1)}, f32[16,32,128]{2,1,0:T(8,128)S(1)}, u32[]{:S(2)}, u32[]{:S(2)}) collective-permute-start(f32[16,32,128]{2,1,0:T(8,128)S(1)} %get-tuple-element.42), channel_id=1, source_target_pairs={{0,8},{4,12},{8,0},{12,4},{1,9},{5,13},{9,1},{13,5},{2,10},{6,14},... | collective-permute-start | bytes 786440 | tf_op jit(solution)/shard_map/ppermute | solution.py:330
  38.9 3.2 %collective-permute-start.9 = (f32[32,128]{1,0:T(8,128)S(1)}, f32[32,128]{1,0:T(8,128)S(1)}, u32[]{:S(2)}, u32[]{:S(2)}) collective-permute-start(f32[32,128]{1,0:T(8,128)S(1)} %shard_map.119.rest_0_), channel_id=1, source_target_pairs={{0,3},{1,2},{2,1},{3,0},{4,7},{5,6},{6,5},{7,4},{8,11},{9,10},{10,... | collective-permute-start | bytes 49160 | tf_op jit(solution)/shard_map/ppermute | solution.py:330
  40.2 3.7 %collective-permute-start.8 = (f32[32,128]{1,0:T(8,128)S(1)}, f32[32,128]{1,0:T(8,128)S(1)}, u32[]{:S(2)}, u32[]{:S(2)}) collective-permute-start(f32[32,128]{1,0:T(8,128)S(1)} %shard_map.119.rest_0_), channel_id=1, source_target_pairs={{0,2},{1,3},{2,0},{3,1},{4,6},{5,7},{6,4},{7,5},{8,10},{9,11},{10,... | collective-permute-start | bytes 49160 | tf_op jit(solution)/shard_map/ppermute | solution.py:330
  40.7 3.2 %collective-permute-start.7 = (f32[32,128]{1,0:T(8,128)S(1)}, f32[32,128]{1,0:T(8,128)S(1)}, u32[]{:S(2)}, u32[]{:S(2)}) collective-permute-start(f32[32,128]{1,0:T(8,128)S(1)} %shard_map.119.rest_0_), channel_id=1, source_target_pairs={{0,1},{1,0},{2,3},{3,2},{4,5},{5,4},{6,7},{7,6},{8,9},{9,8},{10,11... | collective-permute-start | bytes 49160 | tf_op jit(solution)/shard_map/ppermute | solution.py:330

commit v9 on v8

--- a/solution.py
+++ b/solution.py
@@ -149,8 +149,7 @@
             slope_ref[local] = slope(raw, guess)
 
 
-def serve_kernel(picks, nblk, *rest):
-    n = len(picks) + 1
+def serve_kernel(n, nblk, *rest):
     arrived, rest = rest[: n - 1], rest[n - 1 :]
     inverses, rest = rest[:nblk], rest[nblk:]
     old_guess, old_slope, guess_ref, slope_ref, whole_ref, *rest = rest
@@ -176,7 +175,7 @@
                 guess_ref[place] = arrived[k][pl.ds(rank * scen, scen), :]
                 slope_ref[place] = arrived[k][pl.ds((CAP + rank) * scen, scen), :]
 
-    for k, out in zip(picks, outs):
+    for k, out in enumerate(outs):
         want = joined(told(k, 0), told(k, 1))
         for slot in range(out.shape[0]):
             out[slot] = guess_ref[lowest(want)]
@@ -364,7 +363,6 @@
     message = jax.ShapeDtypeStruct((2 * CAP * scen + 8, nodes), F32)
 
     rounds = [*range(2, n), 1]
-    replies = [*range(n - 1, 2, -1), 1, 2] if n > 2 else [1]
     new_slot, partner = in_hbm(new_slot), in_hbm(partner)
     raw, rows, *leaving = call(
         functools.partial(leave_kernel, rounds, span),
@@ -389,16 +387,16 @@
         [scalars(blocks), pltpu.SemaphoreType.DMA],
     )
     guess, slopes, whole, *served = call(
-        functools.partial(serve_kernel, [rounds.index(k) for k in replies], nblk),
+        functools.partial(serve_kernel, n, nblk),
         [block, block, square] + [tiles(rcap)] * (n - 1),
         [*arrived, *inverses, old_guess, old_slope],
         [VMEM] * (n - 1 + nblk + 2),
         [VMEM] * (n + 2),
     )
-    others = [swap(x, "die", n, k) for x, k in zip(served, replies)]
+    others = [swap(x, "die", n, k) for x, k in zip(served, rounds)]
     last = n - 2
     index, late = call(
-        functools.partial(where_kernel, replies, span, rcap, last),
+        functools.partial(where_kernel, rounds, span, rcap, last),
         [scalars(blocks), scalars(1 + blocks)],
         [partner, guess],
         [HBM, ANY],

time: 45.2 us -> 43.1 us (0.954)
  the two profiles are of different devices: /device:TPU:0 before, /device:TPU:9 now
where the time goes in v9:
time: 43.1 us; the launch traced here: 42.9 us
  waiting for transfers between devices  19.3 us (45%)
  Pallas kernels  11.8 us (27%)
  starting transfers between devices  11.1 us (26%)
  between operations  0.71 us (2%)
    ppermute x10, waiting for transfers between devices, swap(): return lax.ppermute(x, axes, [(d, d ^ k) for d in range(n)])  19.3 us
    ppermute x10, starting transfers between devices, swap(): return lax.ppermute(x, axes, [(d, d ^ k) for d in range(n)])  11.1 us
    pallas_call x8, Pallas kernels, call(): pl.pallas_call(body, out_shape=outs, in_specs=in_specs, out_specs=out_spe...  6.61 us
    pallas_call x1, Pallas kernels, shards(): pl.pallas_call(local_kernel, grid=(blocks // step,), out_shape=[block, bl...  5.19 us
  transfers between devices with their start and end apart: 10, of which 6 were waited for; matrix products, arithmetic and copies ran while one was open for 0% of the time, Pallas kernels for 20%

profile of v9, /device:TPU:9, one launch (start us, length us, event | category | flops | bytes accessed | tf_op | source)
XLA Modules:
  0.0 42.9 jit_solution(11835338399605846366)
XLA Ops:
  0.6 1.5 %shard_map.113 = (f32[32,3,32,128]{3,2,1,0:T(8,128)S(1)}, f32[64,128]{1,0:T(8,128)S(1)}, f32[136,128]{1,0:T(8,128)S(1)}, f32[136,128]{1,0:T(8,128)S(1)}, f32[136,128]{1,0:T(8,128)S(1)}) custom-call(s32[32]{0:T(128)} %new_slot_ref.3, s32[32]{0:T(128)} %partner_ref.3, f32[32,3,32,128]{3,2,1,0:T(8,128)} %history_ref.1, f32[64,128]{1,0:T(8,128)} %bitcast.1), custom_call_target="tpu_custom_call" | custom-call | tf_op jit(solution)/shard_map/pallas_call | solution.py:313
  2.1 2.4 %collective-permute-start = (f32[136,128]{1,0:T(8,128)S(1)}, f32[136,128]{1,0:T(8,128)S(1)}, u32[]{:S(2)}, u32[]{:S(2)}) collective-permute-start(f32[136,128]{1,0:T(8,128)S(1)} %get-tuple-element.25), channel_id=1, source_target_pairs={{0,8},{4,12},{8,0},{12,4},{1,9},{5,13},{9,1},{13,5},{2,10},{6,14},... | collective-permute-start | bytes 208904 | tf_op jit(solution)/shard_map/ppermute | solution.py:329
  4.5 0.0 collective-permute-start.1
  4.5 1.3 %collective-permute-start.2 = (f32[136,128]{1,0:T(8,128)S(1)}, f32[136,128]{1,0:T(8,128)S(1)}, u32[]{:S(2)}, u32[]{:S(2)}) collective-permute-start(f32[136,128]{1,0:T(8,128)S(1)} %get-tuple-element.27), channel_id=1, source_target_pairs={{0,4},{4,0},{8,12},{12,8},{1,5},{5,1},{9,13},{13,9},{2,6},{6,2},{1... | collective-permute-start | bytes 208904 | tf_op jit(solution)/shard_map/ppermute | solution.py:329
  5.7 1.5 %collective-permute-start.3 = (f32[64,128]{1,0:T(8,128)S(1)}, f32[64,128]{1,0:T(8,128)S(1)}, u32[]{:S(2)}, u32[]{:S(2)}) collective-permute-start(f32[64,128]{1,0:T(8,128)S(1)} %get-tuple-element.28.rest_3_), channel_id=1, source_target_pairs={{0,1},{1,0},{2,3},{3,2},{4,5},{5,4},{6,7},{7,6},{8,9},{9,8},{10,11... | collective-permute-start | bytes 98312 | tf_op jit(solution)/shard_map/ppermute | solution.py:329
  7.2 1.1 %shard_map.114 = (f32[32,32,128]{2,1,0:T(8,128)S(1)}, f32[32,32,128]{2,1,0:T(8,128)S(1)}) custom-call(s32[32]{0:T(128)} %new_slot_ref.3, f32[32,3,32,128]{3,2,1,0:T(8,128)S(1)} %get-tuple-element.29.raw_ref), custom_call_target="tpu_custom_call" | custom-call | tf_op jit(solution)/shard_map/pallas_call | solution.py:313
  8.3 0.0 collective-permute-done.3.rest_4_
  8.3 0.2 collective-permute-done.rest_0_
  8.5 2.1 %collective-permute-done.1.rest_1_ = f32[136,128]{1,0:T(8,128)S(1)} collective-permute-done((f32[136,128]{1,0:T(8,128)S(1)}, f32[136,128]{1,0:T(8,128)S(1)}, u32[]{:S(2)}, u32[]{:S(2)}) %collective-permute-start.1) | collective-permute-done | bytes 69664 | tf_op jit(solution)/shard_map/ppermute | solution.py:329
  10.6 0.0 collective-permute-done.2.rest_2_
  10.6 0.5 %shard_map.115 = (f32[32,32,128]{2,1,0:T(8,128)S(1)}, f32[32,32,128]{2,1,0:T(8,128)S(1)}, f32[128,128]{1,0:T(8,128)S(1)}, f32[16,32,128]{2,1,0:T(8,128)S(1)}, f3...) custom-call(f32[136,128]{1,0:T(8,128)S(1)} %collective-permute-done.rest_0_, ...), custom_call_target="tpu_custom_call" | custom-call | tf_op jit(solution)/shard_map/pallas_call | solution.py:313
  11.1 1.9 %collective-permute-start.4 = (f32[16,32,128]{2,1,0:T(8,128)S(1)}, f32[16,32,128]{2,1,0:T(8,128)S(1)}, u32[]{:S(2)}, u32[]{:S(2)}) collective-permute-start(f32[16,32,128]{2,1,0:T(8,128)S(1)} %get-tuple-element.39), channel_id=1, source_target_pairs={{0,8},{4,12},{8,0},{12,4},{1,9},{5,13},{9,1},{13,5},{2,10},{6,14},... | collective-permute-start | bytes 786440 | tf_op jit(solution)/shard_map/ppermute | solution.py:329
  13.0 0.4 %collective-permute-start.5 = (f32[16,32,128]{2,1,0:T(8,128)S(1)}, f32[16,32,128]{2,1,0:T(8,128)S(1)}, u32[]{:S(2)}, u32[]{:S(2)}) collective-permute-start(f32[16,32,128]{2,1,0:T(8,128)S(1)} %get-tuple-element.40), channel_id=1, source_target_pairs={{0,12},{4,8},{8,4},{12,0},{1,13},{5,9},{9,5},{13,1},{2,14},{6,10},... | collective-permute-start | bytes 786440 | tf_op jit(solution)/shard_map/ppermute | solution.py:329
  13.4 1.3 %collective-permute-start.6 = (f32[16,32,128]{2,1,0:T(8,128)S(1)}, f32[16,32,128]{2,1,0:T(8,128)S(1)}, u32[]{:S(2)}, u32[]{:S(2)}) collective-permute-start(f32[16,32,128]{2,1,0:T(8,128)S(1)} %get-tuple-element.42), channel_id=1, source_target_pairs={{0,4},{4,0},{8,12},{12,8},{1,5},{5,1},{9,13},{13,9},{2,6},{6,2},{1... | collective-permute-start | bytes 786440 | tf_op jit(solution)/shard_map/ppermute | solution.py:329
  14.7 1.4 %shard_map.116 = (s32[32]{0:T(128)S(4)}, s32[33]{0:T(128)S(4)}) custom-call(s32[32]{0:T(128)} %partner_ref.3, f32[32,32,128]{2,1,0:T(8,128)S(1)} %get-tuple-element.32._.guess_ref), custom_call_target="tpu_custom_call" | custom-call | tf_op jit(solution)/shard_map/pallas_call | solution.py:313
  16.1 5.2 %shard_map.117 = (f32[32,32,128]{2,1,0:T(8,128)S(1)}, f32[32,32,128]{2,1,0:T(8,128)S(1)}, f32[32,32,128]{2,1,0:T(8,128)S(1)}, f32[32,128]{1,0:T(8,128)S(1)}) custom-call(f32[32,32,128]{2,1,0:T(8,128)S(1)} %get-tuple-element.32._.guess_ref, f32[32,32,128]{2,1,0:T(8,128)S(1)} %get-tuple-element.35.slope_ref, f32[32,128,128]{2,1,0:T(8,128)} %coupling_ref.1, ...), custom_call_target="tpu_custom_call" | custom-call | tf_op jit(solution)/shard_map/pallas_call | solution.py:409
  21.3 7.7 %collective-permute-done.4.rest_0_ = f32[16,32,128]{2,1,0:T(8,128)S(1)} collective-permute-done((f32[16,32,128]{2,1,0:T(8,128)S(1)}, f32[16,32,128]{2,1,0:T(8,128)S(1)}, u32[]{:S(2)}, u32[]{:S(2)}) %collective-permute-start.4) | collective-permute-done | bytes 262176 | tf_op jit(solution)/shard_map/ppermute | solution.py:329
  29.0 7.8 %collective-permute-done.5.rest_1_ = f32[16,32,128]{2,1,0:T(8,128)S(1)} collective-permute-done((f32[16,32,128]{2,1,0:T(8,128)S(1)}, f32[16,32,128]{2,1,0:T(8,128)S(1)}, u32[]{:S(2)}, u32[]{:S(2)}) %collective-permute-start.5) | collective-permute-done | bytes 262176 | tf_op jit(solution)/shard_map/ppermute | solution.py:329
  36.8 0.2 shard_map.118
  37.0 0.0 collective-permute-done.6.block_ref
  37.0 0.1 shard_map.119.rest_0_
  37.1 1.9 %collective-permute-start.9 = (f32[32,128]{1,0:T(8,128)S(1)}, f32[32,128]{1,0:T(8,128)S(1)}, u32[]{:S(2)}, u32[]{:S(2)}) collective-permute-start(f32[32,128]{1,0:T(8,128)S(1)} %shard_map.119.rest_0_), channel_id=1, source_target_pairs={{0,3},{1,2},{2,1},{3,0},{4,7},{5,6},{6,5},{7,4},{8,11},{9,10},{10,... | collective-permute-start | bytes 49160 | tf_op jit(solution)/shard_map/ppermute | solution.py:329
  39.0 0.3 collective-permute-start.8
  39.2 0.2 collective-permute-start.7
  39.4 0.9 %shard_map.120 = (f32[32,32,128]{2,1,0:T(8,128)S(1)}, f32[32,32,128]{2,1,0:T(8,128)}) custom-call(s32[32]{0:T(128)S(4)} %get-tuple-element.33.index_ref, f32[32,32,128]{2,1,0:T(8,128)S(1)} %get-tuple-element.44.near_ref, f32[16,32,128]{2,1,0:T(8,128)S(1)} %collective-permute-done.6.block_ref, f32[32,32,128]{2,1,0:T(8,128)S(1)} %get-tuple-element.38.base_ref, ...), custom_call_target="tpu_custom_call" | custom-call | tf_op jit(solution)/shard_map/pallas_call | solution.py:313
  40.3 0.4 %collective-permute-done.9.rest_3_ = f32[32,128]{1,0:T(8,128)S(1)} collective-permute-done((f32[32,128]{1,0:T(8,128)S(1)}, f32[32,128]{1,0:T(8,128)S(1)}, u32[]{:S(2)}, u32[]{:S(2)}) %collective-permute-start.9) | collective-permute-done | bytes 16416 | tf_op jit(solution)/shard_map/ppermute | solution.py:329
  40.8 1.1 %collective-permute-done.8.rest_2_ = f32[32,128]{1,0:T(8,128)S(1)} collective-permute-done((f32[32,128]{1,0:T(8,128)S(1)}, f32[32,128]{1,0:T(8,128)S(1)}, u32[]{:S(2)}, u32[]{:S(2)}) %collective-permute-start.8) | collective-permute-done | bytes 16416 | tf_op jit(solution)/shard_map/ppermute | solution.py:329
  41.8 0.0 collective-permute-done.7.rest_1_
  41.8 1.0 %shard_map.121 = f32[32,32,128]{2,1,0:T(8,128)} custom-call(f32[32,128]{1,0:T(8,128)S(1)} %shard_map.119.rest_0_, f32[32,128]{1,0:T(8,128)S(1)} %collective-permute-done.7.rest_1_, f32[32,128]{1,0:T(8,128)S(1)} %collective-permute-done.8.rest_2_, f32[32,128]{1,0:T(8,128)S(1)} %collective-permute-done.9.rest_3_, f32[128,128]{1,0:T(8,128)S(1)} %get-tuple-element.43.rest_4_, ...), custom_call_target="tpu_custom_call" | custom-call | tf_op jit(solution)/shard_map/pallas_call | solution.py:313
Async XLA Ops:
  2.1 6.4 %collective-permute-start = (f32[136,128]{1,0:T(8,128)S(1)}, f32[136,128]{1,0:T(8,128)S(1)}, u32[]{:S(2)}, u32[]{:S(2)}) collective-permute-start(f32[136,128]{1,0:T(8,128)S(1)} %get-tuple-element.25), channel_id=1, source_target_pairs={{0,8},{4,12},{8,0},{12,4},{1,9},{5,13},{9,1},{13,5},{2,10},{6,14},... | collective-permute-start | bytes 208904 | tf_op jit(solution)/shard_map/ppermute | solution.py:329
  4.5 6.1 %collective-permute-start.1 = (f32[136,128]{1,0:T(8,128)S(1)}, f32[136,128]{1,0:T(8,128)S(1)}, u32[]{:S(2)}, u32[]{:S(2)}) collective-permute-start(f32[136,128]{1,0:T(8,128)S(1)} %get-tuple-element.26), channel_id=1, source_target_pairs={{0,12},{4,8},{8,4},{12,0},{1,13},{5,9},{9,5},{13,1},{2,14},{6,10},... | collective-permute-start | bytes 208904 | tf_op jit(solution)/shard_map/ppermute | solution.py:329
  4.5 6.1 %collective-permute-start.2 = (f32[136,128]{1,0:T(8,128)S(1)}, f32[136,128]{1,0:T(8,128)S(1)}, u32[]{:S(2)}, u32[]{:S(2)}) collective-permute-start(f32[136,128]{1,0:T(8,128)S(1)} %get-tuple-element.27), channel_id=1, source_target_pairs={{0,4},{4,0},{8,12},{12,8},{1,5},{5,1},{9,13},{13,9},{2,6},{6,2},{1... | collective-permute-start | bytes 208904 | tf_op jit(solution)/shard_map/ppermute | solution.py:329
  5.7 2.6 %collective-permute-start.3 = (f32[64,128]{1,0:T(8,128)S(1)}, f32[64,128]{1,0:T(8,128)S(1)}, u32[]{:S(2)}, u32[]{:S(2)}) collective-permute-start(f32[64,128]{1,0:T(8,128)S(1)} %get-tuple-element.28.rest_3_), channel_id=1, source_target_pairs={{0,1},{1,0},{2,3},{3,2},{4,5},{5,4},{6,7},{7,6},{8,9},{9,8},{10,11... | collective-permute-start | bytes 98312 | tf_op jit(solution)/shard_map/ppermute | solution.py:329
  11.1 17.9 %collective-permute-start.4 = (f32[16,32,128]{2,1,0:T(8,128)S(1)}, f32[16,32,128]{2,1,0:T(8,128)S(1)}, u32[]{:S(2)}, u32[]{:S(2)}) collective-permute-start(f32[16,32,128]{2,1,0:T(8,128)S(1)} %get-tuple-element.39), channel_id=1, source_target_pairs={{0,8},{4,12},{8,0},{12,4},{1,9},{5,13},{9,1},{13,5},{2,10},{6,14},... | collective-permute-start | bytes 786440 | tf_op jit(solution)/shard_map/ppermute | solution.py:329
  13.0 23.8 %collective-permute-start.5 = (f32[16,32,128]{2,1,0:T(8,128)S(1)}, f32[16,32,128]{2,1,0:T(8,128)S(1)}, u32[]{:S(2)}, u32[]{:S(2)}) collective-permute-start(f32[16,32,128]{2,1,0:T(8,128)S(1)} %get-tuple-element.40), channel_id=1, source_target_pairs={{0,12},{4,8},{8,4},{12,0},{1,13},{5,9},{9,5},{13,1},{2,14},{6,10},... | collective-permute-start | bytes 786440 | tf_op jit(solution)/shard_map/ppermute | solution.py:329
  13.4 23.6 %collective-permute-start.6 = (f32[16,32,128]{2,1,0:T(8,128)S(1)}, f32[16,32,128]{2,1,0:T(8,128)S(1)}, u32[]{:S(2)}, u32[]{:S(2)}) collective-permute-start(f32[16,32,128]{2,1,0:T(8,128)S(1)} %get-tuple-element.42), channel_id=1, source_target_pairs={{0,4},{4,0},{8,12},{12,8},{1,5},{5,1},{9,13},{13,9},{2,6},{6,2},{1... | collective-permute-start | bytes 786440 | tf_op jit(solution)/shard_map/ppermute | solution.py:329
  37.1 3.6 %collective-permute-start.9 = (f32[32,128]{1,0:T(8,128)S(1)}, f32[32,128]{1,0:T(8,128)S(1)}, u32[]{:S(2)}, u32[]{:S(2)}) collective-permute-start(f32[32,128]{1,0:T(8,128)S(1)} %shard_map.119.rest_0_), channel_id=1, source_target_pairs={{0,3},{1,2},{2,1},{3,0},{4,7},{5,6},{6,5},{7,4},{8,11},{9,10},{10,... | collective-permute-start | bytes 49160 | tf_op jit(solution)/shard_map/ppermute | solution.py:329
  39.0 2.9 %collective-permute-start.8 = (f32[32,128]{1,0:T(8,128)S(1)}, f32[32,128]{1,0:T(8,128)S(1)}, u32[]{:S(2)}, u32[]{:S(2)}) collective-permute-start(f32[32,128]{1,0:T(8,128)S(1)} %shard_map.119.rest_0_), channel_id=1, source_target_pairs={{0,2},{1,3},{2,0},{3,1},{4,6},{5,7},{6,4},{7,5},{8,10},{9,11},{10,... | collective-permute-start | bytes 49160 | tf_op jit(solution)/shard_map/ppermute | solution.py:329
  39.2 2.6 %collective-permute-start.7 = (f32[32,128]{1,0:T(8,128)S(1)}, f32[32,128]{1,0:T(8,128)S(1)}, u32[]{:S(2)}, u32[]{:S(2)}) collective-permute-start(f32[32,128]{1,0:T(8,128)S(1)} %shard_map.119.rest_0_), channel_id=1, source_target_pairs={{0,1},{1,0},{2,3},{3,2},{4,5},{5,4},{6,7},{7,6},{8,9},{9,8},{10,11... | collective-permute-start | bytes 49160 | tf_op jit(solution)/shard_map/ppermute | solution.py:329

commit v10 on v9

--- a/solution.py
+++ b/solution.py
@@ -76,7 +76,7 @@
     rounds, span, new_slot_ref, partner_ref, history_ref, rows_ref, raw_ref, inverse_ref, *rest
 ):
     n = len(rounds) + 1
-    outs, (slots, reads, mine, source, place, count, sems) = rest[: n - 1], rest[n - 1 :]
+    outs, (slots, reads, sems) = rest[: n - 1], rest[n - 1 :]
     blocks, _, scen, nodes = history_ref.shape
     pieces = 4 if blocks % 4 == 0 else 1
     piece = blocks // pieces
@@ -93,42 +93,44 @@
         )
     for copy in copies:
         copy.start()
-    for at in range(n):
-        count[at] = 0
-    for at in range(n * CAP):
-        source[at] = 0
-        place[at] = -1
+    height = max(8, n)
+    turn = lax.broadcasted_iota(I32, (height, blocks), 0)
+    lane = lax.broadcasted_iota(I32, (height, blocks), 1)
+    line = lax.broadcasted_iota(I32, (8, nodes), 0)
     copies[0].wait()
     copies[1].wait()
 
-    for at in range(blocks):
-        dest, local = divmod_static(slots[at], span)
-        local = divmod_static(local, blocks)[1]
-
-        @pl.when(dest != die)
-        def _(at=at, dest=dest, local=local):
-            rank = count[dest]
-            count[dest] = rank + 1
-            turn = (dest ^ die) * CAP + rank
-            source[turn] = at
-            place[turn] = local
-
-    read_masks(n, span, blocks, reads, mine)
+    dest, local = divmod_static(jnp.broadcast_to(slots[...], (height, blocks)), span)
+    local = divmod_static(local, blocks)[1]
+    goes = turn == (dest ^ die)
+    key = (lane * blocks + local).astype(F32)
+    none = float(blocks * blocks)
+    least = jnp.min(jnp.where(goes, key, none), axis=1, keepdims=True).astype(I32)
+    most = jnp.max(jnp.where(goes, key, -1.0), axis=1, keepdims=True).astype(I32)
+    keys = [jnp.where(least < blocks * blocks, least, -1), jnp.where(most > least, most, -1)]
+    owner, local = divmod_static(jnp.broadcast_to(reads[...], (height, blocks)), span)
+    bits = bit_of(divmod_static(local, blocks)[1])
+    bits = jnp.where(turn == (owner ^ die), bits, 0)
+    bits = jnp.concatenate([bits, jnp.zeros((height, nodes - blocks), I32)], axis=1)
+    shift = 1
+    while shift < blocks:
+        bits = bits | pltpu.roll(bits, nodes - shift, 1)
+        shift *= 2
+    values = halves(bits) + [jnp.where(key < 0, -1, key & (blocks - 1)) for key in keys]
+    values = [jnp.broadcast_to(value, (height, nodes)) for value in values]
+    for k, out in zip(rounds, outs):
+        told = jnp.zeros((8, nodes), I32)
+        for j, value in enumerate(values):
+            told = jnp.where(line == j, value[k : k + 1, :], told)
+        out[pl.ds(2 * CAP * scen, 8), :] = told.astype(F32)
     for copy in copies[2:]:
         copy.wait()
-    line = lax.broadcasted_iota(I32, (8, nodes), 0)
     for k, out in zip(rounds, outs):
-        for rank in range(CAP):
-            raw = raw_ref.at[source[k * CAP + rank]]
+        for rank, key in enumerate(keys):
+            raw = raw_ref.at[lax.shift_right_logical(jnp.maximum(key[k, 0], 0), blocks.bit_length() - 1)]
             guess = predict(raw)
             out[pl.ds(rank * scen, scen), :] = guess
             out[pl.ds((CAP + rank) * scen, scen), :] = slope(raw, guess)
-        row = jnp.zeros((8, nodes), I32)
-        values = halves(mine[die ^ k])
-        values += [place[k * CAP + rank] for rank in range(CAP)]
-        for j, value in enumerate(values):
-            row = jnp.where(line == j, value, row)
-        out[pl.ds(2 * CAP * scen, 8), :] = row.astype(F32)
 
 
 def place_kernel(span, new_slot_ref, raw_ref, guess_ref, slope_ref, slots, sem):
@@ -347,7 +349,7 @@
     ncol = lax.axis_size("sub") * nblk
     for size in (n, nblk, ncol):
         assert size & (size - 1) == 0
-    assert blocks <= 32
+    assert CAP == 2 and blocks <= 32 and blocks & (blocks - 1) == 0
     rcap = 2 * max(1, blocks // n)
     span = ncol * blocks
 
@@ -363,25 +365,26 @@
     message = jax.ShapeDtypeStruct((2 * CAP * scen + 8, nodes), F32)
 
     rounds = [*range(2, n), 1]
-    new_slot, partner = in_hbm(new_slot), in_hbm(partner)
     raw, rows, *leaving = call(
         functools.partial(leave_kernel, rounds, span),
         [jax.ShapeDtypeStruct(history.shape, F32), jax.ShapeDtypeStruct(rows.shape, F32)]
         + [message] * (n - 1),
-        [new_slot, partner, in_hbm(history), in_hbm(rows)],
+        [
+            in_hbm(new_slot.reshape(1, blocks)),
+            in_hbm(partner.reshape(1, blocks)),
+            in_hbm(history),
+            in_hbm(rows),
+        ],
         [HBM] * 4,
         [VMEM] * (n + 1),
-        [scalars(blocks)] * 2
-        + [scalars(n)]
-        + [scalars(n * CAP)] * 2
-        + [scalars(n), pltpu.SemaphoreType.DMA((7,))],
+        [pltpu.VMEM((1, blocks), I32)] * 2 + [pltpu.SemaphoreType.DMA((7,))],
     )
     arrived = [swap(x, "die", n, k) for x, k in zip(leaving, rounds)]
     inverses = [rows] + [swap(rows, "blk", nblk, k) for k in range(1, nblk)]
     old_guess, old_slope = call(
         functools.partial(place_kernel, span),
         [block, block],
-        [new_slot, raw],
+        [in_hbm(new_slot), raw],
         [HBM, VMEM],
         [VMEM, VMEM],
         [scalars(blocks), pltpu.SemaphoreType.DMA],
@@ -398,7 +401,7 @@
     index, late = call(
         functools.partial(where_kernel, rounds, span, rcap, last),
         [scalars(blocks), scalars(1 + blocks)],
-        [partner, guess],
+        [in_hbm(partner), guess],
         [HBM, ANY],
         [SMEM, SMEM],
         [scalars(blocks), scalars(n), scalars(n), pltpu.SemaphoreType.DMA],

time: 43.1 us -> 43.2 us (level)
  no operation moved by 1% of the time
where the time goes in v10:
time: 43.2 us; the launch traced here: 42.9 us
  waiting for transfers between devices  19.3 us (45%)
  Pallas kernels  11.9 us (28%)
  starting transfers between devices  11.1 us (26%)
  between operations  0.71 us (2%)
    ppermute x10, waiting for transfers between devices, swap(): return lax.ppermute(x, axes, [(d, d ^ k) for d in range(n)])  19.3 us
    ppermute x10, starting transfers between devices, swap(): return lax.ppermute(x, axes, [(d, d ^ k) for d in range(n)])  11.1 us
    pallas_call x8, Pallas kernels, call(): pl.pallas_call(body, out_shape=outs, in_specs=in_specs, out_specs=out_spe...  6.66 us
    pallas_call x1, Pallas kernels, shards(): pl.pallas_call(local_kernel, grid=(blocks // step,), out_shape=[block, bl...  5.19 us
  transfers between devices with their start and end apart: 10, of which 6 were waited for; matrix products, arithmetic and copies ran while one was open for 0% of the time, Pallas kernels for 20%

profile of v10, /device:TPU:9, one launch (start us, length us, event | category | flops | bytes accessed | tf_op | source)
XLA Modules:
  0.0 42.9 jit_solution(11579352536456257776)
XLA Ops:
  0.6 1.5 %shard_map.113 = (f32[32,3,32,128]{3,2,1,0:T(8,128)S(1)}, f32[64,128]{1,0:T(8,128)S(1)}, f32[136,128]{1,0:T(8,128)S(1)}, f32[136,128]{1,0:T(8,128)S(1)}, f32[136,128]{1,0:T(8,128)S(1)}) custom-call(s32[1,32]{1,0:T(1,128)} %bitcast.4, s32[1,32]{1,0:T(1,128)} %bitcast.5, f32[32,3,32,128]{3,2,1,0:T(8,128)} %history_ref.1, f32[64,128]{1,0:T(8,128)} %bitcast.3), custom_call_target="tpu_custom_call" | custom-call | tf_op jit(solution)/shard_map/pallas_call | solution.py:315
  2.2 2.4 %collective-permute-start = (f32[136,128]{1,0:T(8,128)S(1)}, f32[136,128]{1,0:T(8,128)S(1)}, u32[]{:S(2)}, u32[]{:S(2)}) collective-permute-start(f32[136,128]{1,0:T(8,128)S(1)} %get-tuple-element.25), channel_id=1, source_target_pairs={{0,8},{4,12},{8,0},{12,4},{1,9},{5,13},{9,1},{13,5},{2,10},{6,14},... | collective-permute-start | bytes 208904 | tf_op jit(solution)/shard_map/ppermute | solution.py:331
  4.5 0.0 collective-permute-start.1
  4.5 1.3 %collective-permute-start.2 = (f32[136,128]{1,0:T(8,128)S(1)}, f32[136,128]{1,0:T(8,128)S(1)}, u32[]{:S(2)}, u32[]{:S(2)}) collective-permute-start(f32[136,128]{1,0:T(8,128)S(1)} %get-tuple-element.27), channel_id=1, source_target_pairs={{0,4},{4,0},{8,12},{12,8},{1,5},{5,1},{9,13},{13,9},{2,6},{6,2},{1... | collective-permute-start | bytes 208904 | tf_op jit(solution)/shard_map/ppermute | solution.py:331
  5.8 1.5 %collective-permute-start.3 = (f32[64,128]{1,0:T(8,128)S(1)}, f32[64,128]{1,0:T(8,128)S(1)}, u32[]{:S(2)}, u32[]{:S(2)}) collective-permute-start(f32[64,128]{1,0:T(8,128)S(1)} %get-tuple-element.28.rest_3_), channel_id=1, source_target_pairs={{0,1},{1,0},{2,3},{3,2},{4,5},{5,4},{6,7},{7,6},{8,9},{9,8},{10,11... | collective-permute-start | bytes 98312 | tf_op jit(solution)/shard_map/ppermute | solution.py:331
  7.3 1.1 %shard_map.114 = (f32[32,32,128]{2,1,0:T(8,128)S(1)}, f32[32,32,128]{2,1,0:T(8,128)S(1)}) custom-call(s32[32]{0:T(128)} %new_slot_ref.1, f32[32,3,32,128]{3,2,1,0:T(8,128)S(1)} %get-tuple-element.29.raw_ref), custom_call_target="tpu_custom_call" | custom-call | tf_op jit(solution)/shard_map/pallas_call | solution.py:315
  8.4 0.0 collective-permute-done.3.rest_4_
  8.4 0.2 collective-permute-done.rest_0_
  8.6 2.1 %collective-permute-done.1.rest_1_ = f32[136,128]{1,0:T(8,128)S(1)} collective-permute-done((f32[136,128]{1,0:T(8,128)S(1)}, f32[136,128]{1,0:T(8,128)S(1)}, u32[]{:S(2)}, u32[]{:S(2)}) %collective-permute-start.1) | collective-permute-done | bytes 69664 | tf_op jit(solution)/shard_map/ppermute | solution.py:331
  10.6 0.0 collective-permute-done.2.rest_2_
  10.6 0.5 %shard_map.115 = (f32[32,32,128]{2,1,0:T(8,128)S(1)}, f32[32,32,128]{2,1,0:T(8,128)S(1)}, f32[128,128]{1,0:T(8,128)S(1)}, f32[16,32,128]{2,1,0:T(8,128)S(1)}, f3...) custom-call(f32[136,128]{1,0:T(8,128)S(1)} %collective-permute-done.rest_0_, ...), custom_call_target="tpu_custom_call" | custom-call | tf_op jit(solution)/shard_map/pallas_call | solution.py:315
  11.2 1.9 %collective-permute-start.4 = (f32[16,32,128]{2,1,0:T(8,128)S(1)}, f32[16,32,128]{2,1,0:T(8,128)S(1)}, u32[]{:S(2)}, u32[]{:S(2)}) collective-permute-start(f32[16,32,128]{2,1,0:T(8,128)S(1)} %get-tuple-element.39), channel_id=1, source_target_pairs={{0,8},{4,12},{8,0},{12,4},{1,9},{5,13},{9,1},{13,5},{2,10},{6,14},... | collective-permute-start | bytes 786440 | tf_op jit(solution)/shard_map/ppermute | solution.py:331
  13.0 0.4 %collective-permute-start.5 = (f32[16,32,128]{2,1,0:T(8,128)S(1)}, f32[16,32,128]{2,1,0:T(8,128)S(1)}, u32[]{:S(2)}, u32[]{:S(2)}) collective-permute-start(f32[16,32,128]{2,1,0:T(8,128)S(1)} %get-tuple-element.40), channel_id=1, source_target_pairs={{0,12},{4,8},{8,4},{12,0},{1,13},{5,9},{9,5},{13,1},{2,14},{6,10},... | collective-permute-start | bytes 786440 | tf_op jit(solution)/shard_map/ppermute | solution.py:331
  13.5 1.3 %collective-permute-start.6 = (f32[16,32,128]{2,1,0:T(8,128)S(1)}, f32[16,32,128]{2,1,0:T(8,128)S(1)}, u32[]{:S(2)}, u32[]{:S(2)}) collective-permute-start(f32[16,32,128]{2,1,0:T(8,128)S(1)} %get-tuple-element.42), channel_id=1, source_target_pairs={{0,4},{4,0},{8,12},{12,8},{1,5},{5,1},{9,13},{13,9},{2,6},{6,2},{1... | collective-permute-start | bytes 786440 | tf_op jit(solution)/shard_map/ppermute | solution.py:331
  14.8 1.4 %shard_map.116 = (s32[32]{0:T(128)S(4)}, s32[33]{0:T(128)S(4)}) custom-call(s32[32]{0:T(128)} %partner_ref.1, f32[32,32,128]{2,1,0:T(8,128)S(1)} %get-tuple-element.32._.guess_ref), custom_call_target="tpu_custom_call" | custom-call | tf_op jit(solution)/shard_map/pallas_call | solution.py:315
  16.2 5.2 %shard_map.117 = (f32[32,32,128]{2,1,0:T(8,128)S(1)}, f32[32,32,128]{2,1,0:T(8,128)S(1)}, f32[32,32,128]{2,1,0:T(8,128)S(1)}, f32[32,128]{1,0:T(8,128)S(1)}) custom-call(f32[32,32,128]{2,1,0:T(8,128)S(1)} %get-tuple-element.32._.guess_ref, f32[32,32,128]{2,1,0:T(8,128)S(1)} %get-tuple-element.35.slope_ref, f32[32,128,128]{2,1,0:T(8,128)} %coupling_ref.1, ...), custom_call_target="tpu_custom_call" | custom-call | tf_op jit(solution)/shard_map/pallas_call | solution.py:412
  21.4 7.7 %collective-permute-done.4.rest_0_ = f32[16,32,128]{2,1,0:T(8,128)S(1)} collective-permute-done((f32[16,32,128]{2,1,0:T(8,128)S(1)}, f32[16,32,128]{2,1,0:T(8,128)S(1)}, u32[]{:S(2)}, u32[]{:S(2)}) %collective-permute-start.4) | collective-permute-done | bytes 262176 | tf_op jit(solution)/shard_map/ppermute | solution.py:331
  29.0 7.8 %collective-permute-done.5.rest_1_ = f32[16,32,128]{2,1,0:T(8,128)S(1)} collective-permute-done((f32[16,32,128]{2,1,0:T(8,128)S(1)}, f32[16,32,128]{2,1,0:T(8,128)S(1)}, u32[]{:S(2)}, u32[]{:S(2)}) %collective-permute-start.5) | collective-permute-done | bytes 262176 | tf_op jit(solution)/shard_map/ppermute | solution.py:331
  36.9 0.2 shard_map.118
  37.1 0.0 collective-permute-done.6.block_ref
  37.1 0.1 shard_map.119.rest_0_
  37.2 1.9 %collective-permute-start.9 = (f32[32,128]{1,0:T(8,128)S(1)}, f32[32,128]{1,0:T(8,128)S(1)}, u32[]{:S(2)}, u32[]{:S(2)}) collective-permute-start(f32[32,128]{1,0:T(8,128)S(1)} %shard_map.119.rest_0_), channel_id=1, source_target_pairs={{0,3},{1,2},{2,1},{3,0},{4,7},{5,6},{6,5},{7,4},{8,11},{9,10},{10,... | collective-permute-start | bytes 49160 | tf_op jit(solution)/shard_map/ppermute | solution.py:331
  39.0 0.3 collective-permute-start.8
  39.3 0.2 collective-permute-start.7
  39.5 0.9 %shard_map.120 = (f32[32,32,128]{2,1,0:T(8,128)S(1)}, f32[32,32,128]{2,1,0:T(8,128)}) custom-call(s32[32]{0:T(128)S(4)} %get-tuple-element.33.index_ref, f32[32,32,128]{2,1,0:T(8,128)S(1)} %get-tuple-element.44.near_ref, f32[16,32,128]{2,1,0:T(8,128)S(1)} %collective-permute-done.6.block_ref, f32[32,32,128]{2,1,0:T(8,128)S(1)} %get-tuple-element.38.base_ref, ...), custom_call_target="tpu_custom_call" | custom-call | tf_op jit(solution)/shard_map/pallas_call | solution.py:315
  40.4 0.4 collective-permute-done.9.rest_3_
  40.8 1.1 %collective-permute-done.8.rest_2_ = f32[32,128]{1,0:T(8,128)S(1)} collective-permute-done((f32[32,128]{1,0:T(8,128)S(1)}, f32[32,128]{1,0:T(8,128)S(1)}, u32[]{:S(2)}, u32[]{:S(2)}) %collective-permute-start.8) | collective-permute-done | bytes 16416 | tf_op jit(solution)/shard_map/ppermute | solution.py:331
  41.9 0.0 collective-permute-done.7.rest_1_
  41.9 1.0 %shard_map.121 = f32[32,32,128]{2,1,0:T(8,128)} custom-call(f32[32,128]{1,0:T(8,128)S(1)} %shard_map.119.rest_0_, f32[32,128]{1,0:T(8,128)S(1)} %collective-permute-done.7.rest_1_, f32[32,128]{1,0:T(8,128)S(1)} %collective-permute-done.8.rest_2_, f32[32,128]{1,0:T(8,128)S(1)} %collective-permute-done.9.rest_3_, f32[128,128]{1,0:T(8,128)S(1)} %get-tuple-element.43.rest_4_, ...), custom_call_target="tpu_custom_call" | custom-call | tf_op jit(solution)/shard_map/pallas_call | solution.py:315
Async XLA Ops:
  2.2 6.4 %collective-permute-start = (f32[136,128]{1,0:T(8,128)S(1)}, f32[136,128]{1,0:T(8,128)S(1)}, u32[]{:S(2)}, u32[]{:S(2)}) collective-permute-start(f32[136,128]{1,0:T(8,128)S(1)} %get-tuple-element.25), channel_id=1, source_target_pairs={{0,8},{4,12},{8,0},{12,4},{1,9},{5,13},{9,1},{13,5},{2,10},{6,14},... | collective-permute-start | bytes 208904 | tf_op jit(solution)/shard_map/ppermute | solution.py:331
  4.5 6.1 %collective-permute-start.1 = (f32[136,128]{1,0:T(8,128)S(1)}, f32[136,128]{1,0:T(8,128)S(1)}, u32[]{:S(2)}, u32[]{:S(2)}) collective-permute-start(f32[136,128]{1,0:T(8,128)S(1)} %get-tuple-element.26), channel_id=1, source_target_pairs={{0,12},{4,8},{8,4},{12,0},{1,13},{5,9},{9,5},{13,1},{2,14},{6,10},... | collective-permute-start | bytes 208904 | tf_op jit(solution)/shard_map/ppermute | solution.py:331
  4.5 6.1 %collective-permute-start.2 = (f32[136,128]{1,0:T(8,128)S(1)}, f32[136,128]{1,0:T(8,128)S(1)}, u32[]{:S(2)}, u32[]{:S(2)}) collective-permute-start(f32[136,128]{1,0:T(8,128)S(1)} %get-tuple-element.27), channel_id=1, source_target_pairs={{0,4},{4,0},{8,12},{12,8},{1,5},{5,1},{9,13},{13,9},{2,6},{6,2},{1... | collective-permute-start | bytes 208904 | tf_op jit(solution)/shard_map/ppermute | solution.py:331
  5.8 2.6 %collective-permute-start.3 = (f32[64,128]{1,0:T(8,128)S(1)}, f32[64,128]{1,0:T(8,128)S(1)}, u32[]{:S(2)}, u32[]{:S(2)}) collective-permute-start(f32[64,128]{1,0:T(8,128)S(1)} %get-tuple-element.28.rest_3_), channel_id=1, source_target_pairs={{0,1},{1,0},{2,3},{3,2},{4,5},{5,4},{6,7},{7,6},{8,9},{9,8},{10,11... | collective-permute-start | bytes 98312 | tf_op jit(solution)/shard_map/ppermute | solution.py:331
  11.2 17.9 %collective-permute-start.4 = (f32[16,32,128]{2,1,0:T(8,128)S(1)}, f32[16,32,128]{2,1,0:T(8,128)S(1)}, u32[]{:S(2)}, u32[]{:S(2)}) collective-permute-start(f32[16,32,128]{2,1,0:T(8,128)S(1)} %get-tuple-element.39), channel_id=1, source_target_pairs={{0,8},{4,12},{8,0},{12,4},{1,9},{5,13},{9,1},{13,5},{2,10},{6,14},... | collective-permute-start | bytes 786440 | tf_op jit(solution)/shard_map/ppermute | solution.py:331
  13.0 23.8 %collective-permute-start.5 = (f32[16,32,128]{2,1,0:T(8,128)S(1)}, f32[16,32,128]{2,1,0:T(8,128)S(1)}, u32[]{:S(2)}, u32[]{:S(2)}) collective-permute-start(f32[16,32,128]{2,1,0:T(8,128)S(1)} %get-tuple-element.40), channel_id=1, source_target_pairs={{0,12},{4,8},{8,4},{12,0},{1,13},{5,9},{9,5},{13,1},{2,14},{6,10},... | collective-permute-start | bytes 786440 | tf_op jit(solution)/shard_map/ppermute | solution.py:331
  13.5 23.6 %collective-permute-start.6 = (f32[16,32,128]{2,1,0:T(8,128)S(1)}, f32[16,32,128]{2,1,0:T(8,128)S(1)}, u32[]{:S(2)}, u32[]{:S(2)}) collective-permute-start(f32[16,32,128]{2,1,0:T(8,128)S(1)} %get-tuple-element.42), channel_id=1, source_target_pairs={{0,4},{4,0},{8,12},{12,8},{1,5},{5,1},{9,13},{13,9},{2,6},{6,2},{1... | collective-permute-start | bytes 786440 | tf_op jit(solution)/shard_map/ppermute | solution.py:331
  37.2 3.6 %collective-permute-start.9 = (f32[32,128]{1,0:T(8,128)S(1)}, f32[32,128]{1,0:T(8,128)S(1)}, u32[]{:S(2)}, u32[]{:S(2)}) collective-permute-start(f32[32,128]{1,0:T(8,128)S(1)} %shard_map.119.rest_0_), channel_id=1, source_target_pairs={{0,3},{1,2},{2,1},{3,0},{4,7},{5,6},{6,5},{7,4},{8,11},{9,10},{10,... | collective-permute-start | bytes 49160 | tf_op jit(solution)/shard_map/ppermute | solution.py:331
  39.0 2.9 %collective-permute-start.8 = (f32[32,128]{1,0:T(8,128)S(1)}, f32[32,128]{1,0:T(8,128)S(1)}, u32[]{:S(2)}, u32[]{:S(2)}) collective-permute-start(f32[32,128]{1,0:T(8,128)S(1)} %shard_map.119.rest_0_), channel_id=1, source_target_pairs={{0,2},{1,3},{2,0},{3,1},{4,6},{5,7},{6,4},{7,5},{8,10},{9,11},{10,... | collective-permute-start | bytes 49160 | tf_op jit(solution)/shard_map/ppermute | solution.py:331
  39.3 2.6 %collective-permute-start.7 = (f32[32,128]{1,0:T(8,128)S(1)}, f32[32,128]{1,0:T(8,128)S(1)}, u32[]{:S(2)}, u32[]{:S(2)}) collective-permute-start(f32[32,128]{1,0:T(8,128)S(1)} %shard_map.119.rest_0_), channel_id=1, source_target_pairs={{0,1},{1,0},{2,3},{3,2},{4,5},{5,4},{6,7},{7,6},{8,9},{9,8},{10,11... | collective-permute-start | bytes 49160 | tf_op jit(solution)/shard_map/ppermute | solution.py:331

commit v11 on v10

--- a/solution.py
+++ b/solution.py
@@ -108,9 +108,10 @@
     least = jnp.min(jnp.where(goes, key, none), axis=1, keepdims=True).astype(I32)
     most = jnp.max(jnp.where(goes, key, -1.0), axis=1, keepdims=True).astype(I32)
     keys = [jnp.where(least < blocks * blocks, least, -1), jnp.where(most > least, most, -1)]
+    stays = jnp.where(dest == die, bit_of(local), 0)
     owner, local = divmod_static(jnp.broadcast_to(reads[...], (height, blocks)), span)
     bits = bit_of(divmod_static(local, blocks)[1])
-    bits = jnp.where(turn == (owner ^ die), bits, 0)
+    bits = jnp.where(turn == 0, stays, jnp.where(turn == (owner ^ die), bits, 0))
     bits = jnp.concatenate([bits, jnp.zeros((height, nodes - blocks), I32)], axis=1)
     shift = 1
     while shift < blocks:
@@ -118,10 +119,13 @@
         shift *= 2
     values = halves(bits) + [jnp.where(key < 0, -1, key & (blocks - 1)) for key in keys]
     values = [jnp.broadcast_to(value, (height, nodes)) for value in values]
+    taken = halves(~bits)
     for k, out in zip(rounds, outs):
         told = jnp.zeros((8, nodes), I32)
         for j, value in enumerate(values):
             told = jnp.where(line == j, value[k : k + 1, :], told)
+        for j, value in enumerate(taken):
+            told = jnp.where(line == len(values) + j, value[0:1, :], told)
         out[pl.ds(2 * CAP * scen, 8), :] = told.astype(F32)
     for copy in copies[2:]:
         copy.wait()
@@ -151,16 +155,30 @@
             slope_ref[local] = slope(raw, guess)
 
 
-def serve_kernel(n, nblk, *rest):
+def told(message, j):
+    return message[message.shape[0] - 8 + j, 0].astype(I32)
+
+
+def read_by(message):
+    return joined(told(message, 0), told(message, 1))
+
+
+def taken_slots(message):
+    return joined(told(message, 2 + CAP), told(message, 3 + CAP))
+
+
+def early_kernel(message, own_message, guess_ref, out):
+    still = read_by(message) & ~taken_slots(own_message)
+    for slot in range(out.shape[0]):
+        out[slot] = guess_ref[lowest(still)]
+        still = still & (still - 1)
+
+
+def serve_kernel(n, nblk, pieces, depth, rcap, _, own_message, *rest):
     arrived, rest = rest[: n - 1], rest[n - 1 :]
     inverses, rest = rest[:nblk], rest[nblk:]
-    old_guess, old_slope, guess_ref, slope_ref, whole_ref, *rest = rest
-    outs = rest
+    old_guess, old_slope, guess_ref, slope_ref, whole_ref, *outs = rest
     blocks, scen, nodes = guess_ref.shape
-
-    def told(k, j):
-        return arrived[k][2 * CAP * scen + j, 0].astype(I32)
-
     for at in range(blocks):
         guess_ref[at] = old_guess[at]
         slope_ref[at] = old_slope[at]
@@ -168,23 +186,45 @@
     for k in range(nblk):
         at = pl.multiple_of((lax.axis_index("blk") ^ k) * height, height)
         whole_ref[pl.ds(at, height), :] = inverses[k][...]
-    for k in range(n - 1):
+    for message in arrived:
         for rank in range(CAP):
-            place = told(k, 2 + rank)
+            place = told(message, 2 + rank)
 
             @pl.when(place >= 0)
-            def _(k=k, rank=rank, place=place):
-                guess_ref[place] = arrived[k][pl.ds(rank * scen, scen), :]
-                slope_ref[place] = arrived[k][pl.ds((CAP + rank) * scen, scen), :]
-
-    for k, out in enumerate(outs):
-        want = joined(told(k, 0), told(k, 1))
-        for slot in range(out.shape[0]):
-            out[slot] = guess_ref[lowest(want)]
-            want = want & (want - 1)
-
-
-def where_kernel(rounds, span, rcap, last, partner_ref, _, index_ref, late_ref, reads, mine, starts, sem):
+            def _(message=message, rank=rank, place=place):
+                guess_ref[place] = message[pl.ds(rank * scen, scen), :]
+                slope_ref[place] = message[pl.ds((CAP + rank) * scen, scen), :]
+
+    taken = taken_slots(own_message)
+    want = read_by(arrived[0])
+    still, come = want & ~taken, want & taken
+    for slot in range(depth):
+        still = still & (still - 1)
+    out = outs[0]
+    for slot in range(rcap - depth):
+
+        @pl.when(still != 0)
+        def _(still=still, slot=slot):
+            out[slot] = guess_ref[lowest(still)]
+
+        still = still & (still - 1)
+    for slot in range(rcap - depth - 1, -1, -1):
+
+        @pl.when(come != 0)
+        def _(come=come, slot=slot):
+            out[slot] = guess_ref[lowest(come)]
+
+        come = come & (come - 1)
+    outs = outs[1:]
+    for k in range(1, n - 1):
+        want = read_by(arrived[k])
+        for out in outs[(k - 1) * pieces : k * pieces]:
+            for slot in range(out.shape[0]):
+                out[slot] = guess_ref[lowest(want)]
+                want = want & (want - 1)
+
+
+def where_kernel(rounds, span, rcap, partner_ref, message, _, index_ref, reads, mine, starts, sem):
     n = len(rounds) + 1
     blocks = index_ref.shape[0]
     die = lax.axis_index("die")
@@ -195,19 +235,22 @@
         starts[k] = at * rcap
     copy.wait()
     read_masks(n, span, blocks, reads, mine)
-
-    def step(at, count):
+    taken = taken_slots(message)
+
+    def step(at, carry):
         owner, local = divmod_static(reads[at], span)
         local = divmod_static(local, blocks)[1]
         k = owner ^ die
-        slot = bits_set(mine[owner] & (bit_of(local) - 1))
+        bit = bit_of(local)
+        want = mine[owner]
+        come = jnp.where(k == rounds[0], taken, 0)
+        low = bits_set(want & ~come & (bit - 1))
+        high = rcap - 1 - bits_set(want & come & (bit - 1))
+        slot = jnp.where((come & bit) != 0, high, low)
         index_ref[at] = jnp.where(k == 0, local - blocks, starts[k] + slot)
-        late_ref[1 + count] = at
-        return count + jnp.where(k == rounds[last], 1, 0)
-
-    for at in range(1 + blocks):
-        late_ref[at] = 0
-    late_ref[0] = lax.fori_loop(0, blocks, step, jnp.int32(0))
+        return carry
+
+    lax.fori_loop(0, blocks, step, 0)
 
 
 def local_kernel(
@@ -241,47 +284,40 @@
         )
 
 
-def gather_kernel(rcap, last, index_ref, base_ref, scale_ref, guess_ref, wire_ref, *rest):
-    blocks_in, (near_ref, share_ref, pool) = rest[:-3], rest[-3:]
+def gather_kernel(depth, index_ref, early_ref, guess_ref, _, first_ref):
     blocks = guess_ref.shape[0]
-    for at, ref in enumerate(blocks_in):
-        for slot in range(rcap):
-            pool[(at + (at >= last)) * rcap + slot] = ref[slot]
+    for at in range(blocks):
+        index = index_ref[at]
+        near = guess_ref[jnp.where(index < 0, index + blocks, 0)]
+        early = early_ref[jnp.clip(index, 0, max(depth, 1) - 1)]
+        first_ref[at] = jnp.where(index < 0, near, early)
+
+
+def share_kernel(depth, index_ref, first_ref, base_ref, scale_ref, wire_ref, *rest):
+    blocks_in, (share_ref, near_ref, pool) = rest[:-3], rest[-3:]
+    blocks = first_ref.shape[0]
+    start = 0
+    for ref in blocks_in:
+        for slot in range(ref.shape[0]):
+            pool[start + slot] = ref[slot]
+        start += ref.shape[0]
     share = jnp.zeros(share_ref.shape, F32)
     for at in range(blocks):
-        index = index_ref[at]
-        own = index < 0
-        near = guess_ref[jnp.where(own, index + blocks, 0)]
-        near = jnp.where(own, near, pool[jnp.maximum(index, 0)])
-        missing = (index >= last * rcap) & (index < (last + 1) * rcap)
-        near = jnp.where(missing, 0.0, near)
+        index = index_ref[at] - depth
+        near = jnp.where(index < 0, first_ref[at], pool[jnp.maximum(index, 0)])
         near_ref[at] = near
         share = share + scale_ref[at] * (base_ref[at] - wire_ref[at : at + 1, :] * near)
     share_ref[...] = share
 
 
-def share_kernel(rcap, last, index_ref, late_ref, scale_ref, wire_ref, part_ref, block_ref, share_ref):
-    share = part_ref[...]
-    for slot in range(min(rcap, wire_ref.shape[0])):
-        at = late_ref[1 + slot]
-        there = slot < late_ref[0]
-        block = block_ref[jnp.where(there, index_ref[at] - last * rcap, 0)]
-        share = share - jnp.where(there, scale_ref[at] * wire_ref[pl.ds(at, 1), :] * block, 0.0)
-    share_ref[...] = share
-
-
 def residual_kernel(
-    rcap, last, parts, index_ref, near_ref, block_ref, base_ref, inv_ref, guess_ref, wire_ref,
-    partial_ref, out_ref, held, sems
+    parts, near_ref, base_ref, inv_ref, guess_ref, wire_ref, partial_ref, out_ref, held, sems
 ):
     step = guess_ref.shape[0] // parts
     copies = []
     for part in range(parts):
         for at in range(part * step, (part + 1) * step):
-            slot = index_ref[at] - last * rcap
-            missing = (slot >= 0) & (slot < rcap)
-            near = jnp.where(missing, block_ref[jnp.where(missing, slot, 0)], near_ref[at])
-            residual = base_ref[at] - wire_ref[at : at + 1, :] * near
+            residual = base_ref[at] - wire_ref[at : at + 1, :] * near_ref[at]
             held[at] = residual
             partial_ref[at] = guess_ref[at] - residual * inv_ref[at]
         some = pl.ds(part * step, step)
@@ -389,21 +425,33 @@
         [VMEM, VMEM],
         [scalars(blocks), pltpu.SemaphoreType.DMA],
     )
+    depth = max(0, rcap - CAP * (n - 1))
+    pieces = 2 if depth else 1
+    sent, early = [], old_guess
+    if depth:
+        (early,) = call(
+            early_kernel,
+            [tiles(depth)],
+            [arrived[0], leaving[0], old_guess],
+            [VMEM] * 3,
+            [VMEM],
+        )
+        sent.append((early, rounds[0]))
     guess, slopes, whole, *served = call(
-        functools.partial(serve_kernel, n, nblk),
-        [block, block, square] + [tiles(rcap)] * (n - 1),
-        [*arrived, *inverses, old_guess, old_slope],
-        [VMEM] * (n - 1 + nblk + 2),
-        [VMEM] * (n + 2),
-    )
-    others = [swap(x, "die", n, k) for x, k in zip(served, rounds)]
-    last = n - 2
-    index, late = call(
-        functools.partial(where_kernel, rounds, span, rcap, last),
-        [scalars(blocks), scalars(1 + blocks)],
-        [in_hbm(partner), guess],
-        [HBM, ANY],
-        [SMEM, SMEM],
+        functools.partial(serve_kernel, n, nblk, pieces, depth, rcap),
+        [block, block, square, tiles(rcap - depth)] + [tiles(rcap // pieces)] * (pieces * (n - 2)),
+        [early, leaving[0], *arrived, *inverses, old_guess, old_slope],
+        [ANY] + [VMEM] * (n + nblk + 2),
+        [VMEM] * (4 + pieces * (n - 2)),
+    )
+    sent += zip(served, [rounds[0]] + [k for k in rounds[1:] for _ in range(pieces)])
+    others = [swap(x, "die", n, k) for x, k in sent]
+    (index,) = call(
+        functools.partial(where_kernel, rounds, span, rcap),
+        [scalars(blocks)],
+        [in_hbm(partner), arrived[0], guess],
+        [HBM, VMEM, ANY],
+        [SMEM],
         [scalars(blocks), scalars(n), scalars(n), pltpu.SemaphoreType.DMA],
     )
     step = 8 if blocks % 8 == 0 else blocks
@@ -437,30 +485,28 @@
         in_hbm(drive),
     )
     index = pltpu.with_memory_space_constraint(index, pltpu.SMEM)
-    late = pltpu.with_memory_space_constraint(late, pltpu.SMEM)
-    flat_share = jax.ShapeDtypeStruct((scen, nodes), F32)
-    first = others[:last] + others[last + 1 :]
-    near, part = call(
-        functools.partial(gather_kernel, rcap, last),
-        [block, flat_share],
-        [index, base, scale, guess, wire, *first],
-        [SMEM] + [VMEM] * (4 + len(first)),
+    early, others = (others[0], others[1:]) if depth else (guess, others)
+    (first,) = call(
+        functools.partial(gather_kernel, depth),
+        [block],
+        [index, early, guess, base],
+        [SMEM, VMEM, VMEM, ANY],
+        [VMEM],
+    )
+    share, near = call(
+        functools.partial(share_kernel, depth),
+        [jax.ShapeDtypeStruct((scen, nodes), F32), block],
+        [index, first, base, scale, wire, *others],
+        [SMEM] + [VMEM] * (4 + len(others)),
         [VMEM] * 2,
-        [pltpu.VMEM(((n - 1) * rcap, scen, nodes), F32)],
-    )
-    (share,) = call(
-        functools.partial(share_kernel, rcap, last),
-        [flat_share],
-        [index, late, scale, wire, part, others[last]],
-        [SMEM] * 2 + [VMEM] * 4,
-        [VMEM],
+        [pltpu.VMEM(((n - 1) * rcap - depth, scen, nodes), F32)],
     )
     parts = 8 if blocks % 8 == 0 else 1
     partial, residual = call(
-        functools.partial(residual_kernel, rcap, last, parts),
+        functools.partial(residual_kernel, parts),
         [block, block],
-        [index, near, others[last], base, inv, guess, wire],
-        [SMEM] + [VMEM] * 6,
+        [near, base, inv, guess, wire],
+        [VMEM] * 5,
         [VMEM, HBM],
         [pltpu.VMEM((blocks, scen, nodes), F32), pltpu.SemaphoreType.DMA((parts,))],
     )

time: 43.2 us -> 43.9 us (1.016)
  the two profiles are of different devices: /device:TPU:9 before, /device:TPU:0 now
where the time goes in v11:
time: 43.9 us; the launch traced here: 43.7 us
  starting transfers between devices  19.9 us (45%)
  Pallas kernels  12.2 us (28%)
  waiting for transfers between devices  10.9 us (25%)
  between operations  0.72 us (2%)
    ppermute x13, starting transfers between devices, swap(): return lax.ppermute(x, axes, [(d, d ^ k) for d in range(n)])  19.9 us
    ppermute x13, waiting for transfers between devices, swap(): return lax.ppermute(x, axes, [(d, d ^ k) for d in range(n)])  10.9 us
    pallas_call x9, Pallas kernels, call(): pl.pallas_call(body, out_shape=outs, in_specs=in_specs, out_specs=out_spe...  7 us
    pallas_call x1, Pallas kernels, shards(): pl.pallas_call(local_kernel, grid=(blocks // step,), out_shape=[block, bl...  5.16 us
  transfers between devices with their start and end apart: 13, of which 6 were waited for; matrix products, arithmetic and copies ran while one was open for 0% of the time, Pallas kernels for 21%

profile of v11, /device:TPU:0, one launch (start us, length us, event | category | flops | bytes accessed | tf_op | source)
XLA Modules:
  0.0 43.7 jit_solution(10286399501623599333)
XLA Ops:
  0.6 1.5 %shard_map.113 = (f32[32,3,32,128]{3,2,1,0:T(8,128)S(1)}, f32[64,128]{1,0:T(8,128)S(1)}, f32[136,128]{1,0:T(8,128)S(1)}, f32[136,128]{1,0:T(8,128)S(1)}, f32[136,128]{1,0:T(8,128)S(1)}) custom-call(s32[1,32]{1,0:T(1,128)} %bitcast.4, s32[1,32]{1,0:T(1,128)} %bitcast.5, f32[32,3,32,128]{3,2,1,0:T(8,128)} %history_ref.1, f32[64,128]{1,0:T(8,128)} %bitcast.3), custom_call_target="tpu_custom_call" | custom-call | tf_op jit(solution)/shard_map/pallas_call | solution.py:351
  2.2 4.1 %collective-permute-start = (f32[136,128]{1,0:T(8,128)S(1)}, f32[136,128]{1,0:T(8,128)S(1)}, u32[]{:S(2)}, u32[]{:S(2)}) collective-permute-start(f32[136,128]{1,0:T(8,128)S(1)} %get-tuple-element.25.own_message), channel_id=1, source_target_pairs={{0,8},{4,12},{8,0},{12,4},{1,9},{5,13},{9,1},{13,5},{2,10},{6,14},... | collective-permute-start | bytes 208904 | tf_op jit(solution)/shard_map/ppermute | solution.py:367
  6.3 1.1 %shard_map.114 = (f32[32,32,128]{2,1,0:T(8,128)S(1)}, f32[32,32,128]{2,1,0:T(8,128)S(1)}) custom-call(s32[32]{0:T(128)} %new_slot_ref.1, f32[32,3,32,128]{3,2,1,0:T(8,128)S(1)} %get-tuple-element.26.raw_ref), custom_call_target="tpu_custom_call" | custom-call | tf_op jit(solution)/shard_map/pallas_call | solution.py:351
  7.3 2.7 %collective-permute-done.message.rest_0_ = f32[136,128]{1,0:T(8,128)S(1)} collective-permute-done((f32[136,128]{1,0:T(8,128)S(1)}, f32[136,128]{1,0:T(8,128)S(1)}, u32[]{:S(2)}, u32[]{:S(2)}) %collective-permute-start) | collective-permute-done | bytes 69664 | tf_op jit(solution)/shard_map/ppermute | solution.py:367
  10.1 0.1 shard_map.115._
  10.1 1.5 %collective-permute-start.4 = (f32[10,32,128]{2,1,0:T(8,128)S(1)}, f32[10,32,128]{2,1,0:T(8,128)S(1)}, u32[]{:S(2)}, u32[]{:S(2)}) collective-permute-start(f32[10,32,128]{2,1,0:T(8,128)S(1)} %shard_map.115._), channel_id=1, source_target_pairs={{0,8},{4,12},{8,0},{12,4},{1,9},{5,13},{9,1},{13,5},{2,10},{6,14},... | collective-permute-start | bytes 491528 | tf_op jit(solution)/shard_map/ppermute | solution.py:367
  11.6 2.1 %collective-permute-start.1 = (f32[136,128]{1,0:T(8,128)S(1)}, f32[136,128]{1,0:T(8,128)S(1)}, u32[]{:S(2)}, u32[]{:S(2)}) collective-permute-start(f32[136,128]{1,0:T(8,128)S(1)} %get-tuple-element.28), channel_id=1, source_target_pairs={{0,12},{4,8},{8,4},{12,0},{1,13},{5,9},{9,5},{13,1},{2,14},{6,10},... | collective-permute-start | bytes 208904 | tf_op jit(solution)/shard_map/ppermute | solution.py:367
  13.7 0.5 %collective-permute-start.2 = (f32[136,128]{1,0:T(8,128)S(1)}, f32[136,128]{1,0:T(8,128)S(1)}, u32[]{:S(2)}, u32[]{:S(2)}) collective-permute-start(f32[136,128]{1,0:T(8,128)S(1)} %get-tuple-element.29), channel_id=1, source_target_pairs={{0,4},{4,0},{8,12},{12,8},{1,5},{5,1},{9,13},{13,9},{2,6},{6,2},{1... | collective-permute-start | bytes 208904 | tf_op jit(solution)/shard_map/ppermute | solution.py:367
  14.2 0.0 collective-permute-start.3
  14.2 1.2 %collective-permute-done.3.rest_4_ = f32[64,128]{1,0:T(8,128)S(1)} collective-permute-done((f32[64,128]{1,0:T(8,128)S(1)}, f32[64,128]{1,0:T(8,128)S(1)}, u32[]{:S(2)}, u32[]{:S(2)}) %collective-permute-start.3) | collective-permute-done | bytes 32800 | tf_op jit(solution)/shard_map/ppermute | solution.py:367
  15.4 4.6 %collective-permute-done.1.rest_1_ = f32[136,128]{1,0:T(8,128)S(1)} collective-permute-done((f32[136,128]{1,0:T(8,128)S(1)}, f32[136,128]{1,0:T(8,128)S(1)}, u32[]{:S(2)}, u32[]{:S(2)}) %collective-permute-start.1) | collective-permute-done | bytes 69664 | tf_op jit(solution)/shard_map/ppermute | solution.py:367
  20.0 0.0 collective-permute-done.2.rest_2_
  20.0 0.6 %shard_map.116 = (f32[32,32,128]{2,1,0:T(8,128)S(1)}, f32[32,32,128]{2,1,0:T(8,128)S(1)}, f32[128,128]{1,0:T(8,128)S(1)}, f32[6,32,128]{2,1,0:T(8,128)S(1)}, f32...) custom-call(f32[10,32,128]{2,1,0:T(8,128)S(1)} %shard_map.115._, ...), custom_call_target="tpu_custom_call" | custom-call | tf_op jit(solution)/shard_map/pallas_call | solution.py:351
  20.6 4.0 %collective-permute-start.6 = (f32[8,32,128]{2,1,0:T(8,128)S(1)}, f32[8,32,128]{2,1,0:T(8,128)S(1)}, u32[]{:S(2)}, u32[]{:S(2)}) collective-permute-start(f32[8,32,128]{2,1,0:T(8,128)S(1)} %get-tuple-element.38), channel_id=1, source_target_pairs={{0,12},{4,8},{8,4},{12,0},{1,13},{5,9},{9,5},{13,1},{2,14},{6,10},... | collective-permute-start | bytes 393224 | tf_op jit(solution)/shard_map/ppermute | solution.py:367
  24.6 0.1 collective-permute-start.7
  24.7 2.3 %collective-permute-start.8 = (f32[8,32,128]{2,1,0:T(8,128)S(1)}, f32[8,32,128]{2,1,0:T(8,128)S(1)}, u32[]{:S(2)}, u32[]{:S(2)}) collective-permute-start(f32[8,32,128]{2,1,0:T(8,128)S(1)} %get-tuple-element.40), channel_id=1, source_target_pairs={{0,4},{4,0},{8,12},{12,8},{1,5},{5,1},{9,13},{13,9},{2,6},{6,2},{1... | collective-permute-start | bytes 393224 | tf_op jit(solution)/shard_map/ppermute | solution.py:367
  26.9 0.0 collective-permute-start.9
  27.0 0.0 collective-permute-done.4.early_ref
  27.0 3.4 %collective-permute-start.5 = (f32[6,32,128]{2,1,0:T(8,128)S(1)}, f32[6,32,128]{2,1,0:T(8,128)S(1)}, u32[]{:S(2)}, u32[]{:S(2)}) collective-permute-start(f32[6,32,128]{2,1,0:T(8,128)S(1)} %get-tuple-element.37), channel_id=1, source_target_pairs={{0,8},{4,12},{8,0},{12,4},{1,9},{5,13},{9,1},{13,5},{2,10},{6,14},... | collective-permute-start | bytes 294920 | tf_op jit(solution)/shard_map/ppermute | solution.py:367
  30.4 5.2 %shard_map.118 = (f32[32,32,128]{2,1,0:T(8,128)S(1)}, f32[32,32,128]{2,1,0:T(8,128)S(1)}, f32[32,32,128]{2,1,0:T(8,128)S(1)}, f32[32,128]{1,0:T(8,128)S(1)}) custom-call(f32[32,32,128]{2,1,0:T(8,128)S(1)} %get-tuple-element.32._.guess_ref, f32[32,32,128]{2,1,0:T(8,128)S(1)} %get-tuple-element.33.slope_ref, f32[32,128,128]{2,1,0:T(8,128)} %coupling_ref.1, ...), custom_call_target="tpu_custom_call" | custom-call | tf_op jit(solution)/shard_map/pallas_call | solution.py:460
  35.5 1.5 %shard_map.117.index_ref = s32[32]{0:T(128)S(4)} custom-call(s32[32]{0:T(128)} %partner_ref.1, f32[136,128]{1,0:T(8,128)S(1)} %collective-permute-done.message.rest_0_, f32[32,32,128]{2,1,0:T(8,128)S(1)} %get-tuple-element.32._.guess_ref), custom_call_target="tpu_custom_call" | custom-call | tf_op jit(solution)/shard_map/pallas_call | solution.py:351
  37.1 0.1 shard_map.119.first_ref
  37.2 0.5 %collective-permute-done.5.rest_0_ = f32[6,32,128]{2,1,0:T(8,128)S(1)} collective-permute-done((f32[6,32,128]{2,1,0:T(8,128)S(1)}, f32[6,32,128]{2,1,0:T(8,128)S(1)}, u32[]{:S(2)}, u32[]{:S(2)}) %collective-permute-start.5) | collective-permute-done | bytes 98336 | tf_op jit(solution)/shard_map/ppermute | solution.py:367
  37.8 0.0 collective-permute-done.6.rest_1_
  37.8 0.0 collective-permute-done.7.rest_2_
  37.8 0.0 collective-permute-done.8.rest_3_
  37.8 0.0 collective-permute-done.9.rest_4_
  37.8 0.2 shard_map.120
  37.9 1.0 %collective-permute-start.12 = (f32[32,128]{1,0:T(8,128)S(1)}, f32[32,128]{1,0:T(8,128)S(1)}, u32[]{:S(2)}, u32[]{:S(2)}) collective-permute-start(f32[32,128]{1,0:T(8,128)S(1)} %get-tuple-element.42.rest_0_), channel_id=1, source_target_pairs={{0,3},{1,2},{2,1},{3,0},{4,7},{5,6},{6,5},{7,4},{8,11},{9,10},{10,... | collective-permute-start | bytes 49160 | tf_op jit(solution)/shard_map/ppermute | solution.py:367
  38.9 0.7 %collective-permute-start.11 = (f32[32,128]{1,0:T(8,128)S(1)}, f32[32,128]{1,0:T(8,128)S(1)}, u32[]{:S(2)}, u32[]{:S(2)}) collective-permute-start(f32[32,128]{1,0:T(8,128)S(1)} %get-tuple-element.42.rest_0_), channel_id=1, source_target_pairs={{0,2},{1,3},{2,0},{3,1},{4,6},{5,7},{6,4},{7,5},{8,10},{9,11},{10,... | collective-permute-start | bytes 49160 | tf_op jit(solution)/shard_map/ppermute | solution.py:367
  39.6 0.3 collective-permute-start.10
  39.9 0.9 %shard_map.121 = (f32[32,32,128]{2,1,0:T(8,128)S(1)}, f32[32,32,128]{2,1,0:T(8,128)}) custom-call(f32[32,32,128]{2,1,0:T(8,128)S(1)} %get-tuple-element.44.near_ref, f32[32,32,128]{2,1,0:T(8,128)S(1)} %get-tuple-element.34._.base_ref, f32[32,32,128]{2,1,0:T(8,128)S(1)} %get-tuple-element.45.inv_ref, f32[32,32,128]{2,1,0:T(8,128)S(1)} %get-tuple-element.32._.guess_ref, ...), custom_call_target="tpu_custom_call" | custom-call | tf_op jit(solution)/shard_map/pallas_call | solution.py:351
  40.7 0.6 %collective-permute-done.12.rest_3_ = f32[32,128]{1,0:T(8,128)S(1)} collective-permute-done((f32[32,128]{1,0:T(8,128)S(1)}, f32[32,128]{1,0:T(8,128)S(1)}, u32[]{:S(2)}, u32[]{:S(2)}) %collective-permute-start.12) | collective-permute-done | bytes 16416 | tf_op jit(solution)/shard_map/ppermute | solution.py:367
  41.3 1.3 %collective-permute-done.11.rest_2_ = f32[32,128]{1,0:T(8,128)S(1)} collective-permute-done((f32[32,128]{1,0:T(8,128)S(1)}, f32[32,128]{1,0:T(8,128)S(1)}, u32[]{:S(2)}, u32[]{:S(2)}) %collective-permute-start.11) | collective-permute-done | bytes 16416 | tf_op jit(solution)/shard_map/ppermute | solution.py:367
  42.6 0.0 collective-permute-done.10.rest_1_
  42.6 1.0 %shard_map.122 = f32[32,32,128]{2,1,0:T(8,128)} custom-call(f32[32,128]{1,0:T(8,128)S(1)} %get-tuple-element.42.rest_0_, f32[32,128]{1,0:T(8,128)S(1)} %collective-permute-done.10.rest_1_, f32[32,128]{1,0:T(8,128)S(1)} %collective-permute-done.11.rest_2_, f32[32,128]{1,0:T(8,128)S(1)} %collective-permute-done.12.rest_3_, ...), custom_call_target="tpu_custom_call" | custom-call | tf_op jit(solution)/shard_map/pallas_call | solution.py:351
Async XLA Ops:
  2.2 7.9 %collective-permute-start = (f32[136,128]{1,0:T(8,128)S(1)}, f32[136,128]{1,0:T(8,128)S(1)}, u32[]{:S(2)}, u32[]{:S(2)}) collective-permute-start(f32[136,128]{1,0:T(8,128)S(1)} %get-tuple-element.25.own_message), channel_id=1, source_target_pairs={{0,8},{4,12},{8,0},{12,4},{1,9},{5,13},{9,1},{13,5},{2,10},{6,14},... | collective-permute-start | bytes 208904 | tf_op jit(solution)/shard_map/ppermute | solution.py:367
  10.1 16.9 %collective-permute-start.4 = (f32[10,32,128]{2,1,0:T(8,128)S(1)}, f32[10,32,128]{2,1,0:T(8,128)S(1)}, u32[]{:S(2)}, u32[]{:S(2)}) collective-permute-start(f32[10,32,128]{2,1,0:T(8,128)S(1)} %shard_map.115._), channel_id=1, source_target_pairs={{0,8},{4,12},{8,0},{12,4},{1,9},{5,13},{9,1},{13,5},{2,10},{6,14},... | collective-permute-start | bytes 491528 | tf_op jit(solution)/shard_map/ppermute | solution.py:367
  11.6 8.4 %collective-permute-start.1 = (f32[136,128]{1,0:T(8,128)S(1)}, f32[136,128]{1,0:T(8,128)S(1)}, u32[]{:S(2)}, u32[]{:S(2)}) collective-permute-start(f32[136,128]{1,0:T(8,128)S(1)} %get-tuple-element.28), channel_id=1, source_target_pairs={{0,12},{4,8},{8,4},{12,0},{1,13},{5,9},{9,5},{13,1},{2,14},{6,10},... | collective-permute-start | bytes 208904 | tf_op jit(solution)/shard_map/ppermute | solution.py:367
  13.7 6.3 %collective-permute-start.2 = (f32[136,128]{1,0:T(8,128)S(1)}, f32[136,128]{1,0:T(8,128)S(1)}, u32[]{:S(2)}, u32[]{:S(2)}) collective-permute-start(f32[136,128]{1,0:T(8,128)S(1)} %get-tuple-element.29), channel_id=1, source_target_pairs={{0,4},{4,0},{8,12},{12,8},{1,5},{5,1},{9,13},{13,9},{2,6},{6,2},{1... | collective-permute-start | bytes 208904 | tf_op jit(solution)/shard_map/ppermute | solution.py:367
  14.2 1.2 %collective-permute-start.3 = (f32[64,128]{1,0:T(8,128)S(1)}, f32[64,128]{1,0:T(8,128)S(1)}, u32[]{:S(2)}, u32[]{:S(2)}) collective-permute-start(f32[64,128]{1,0:T(8,128)S(1)} %get-tuple-element.30.rest_3_), channel_id=1, source_target_pairs={{0,1},{1,0},{2,3},{3,2},{4,5},{5,4},{6,7},{7,6},{8,9},{9,8},{10,11... | collective-permute-start | bytes 98312 | tf_op jit(solution)/shard_map/ppermute | solution.py:367
  20.6 17.2 %collective-permute-start.6 = (f32[8,32,128]{2,1,0:T(8,128)S(1)}, f32[8,32,128]{2,1,0:T(8,128)S(1)}, u32[]{:S(2)}, u32[]{:S(2)}) collective-permute-start(f32[8,32,128]{2,1,0:T(8,128)S(1)} %get-tuple-element.38), channel_id=1, source_target_pairs={{0,12},{4,8},{8,4},{12,0},{1,13},{5,9},{9,5},{13,1},{2,14},{6,10},... | collective-permute-start | bytes 393224 | tf_op jit(solution)/shard_map/ppermute | solution.py:367
  24.6 13.1 %collective-permute-start.7 = (f32[8,32,128]{2,1,0:T(8,128)S(1)}, f32[8,32,128]{2,1,0:T(8,128)S(1)}, u32[]{:S(2)}, u32[]{:S(2)}) collective-permute-start(f32[8,32,128]{2,1,0:T(8,128)S(1)} %get-tuple-element.39), channel_id=1, source_target_pairs={{0,12},{4,8},{8,4},{12,0},{1,13},{5,9},{9,5},{13,1},{2,14},{6,10},... | collective-permute-start | bytes 393224 | tf_op jit(solution)/shard_map/ppermute | solution.py:367
  24.7 13.1 %collective-permute-start.8 = (f32[8,32,128]{2,1,0:T(8,128)S(1)}, f32[8,32,128]{2,1,0:T(8,128)S(1)}, u32[]{:S(2)}, u32[]{:S(2)}) collective-permute-start(f32[8,32,128]{2,1,0:T(8,128)S(1)} %get-tuple-element.40), channel_id=1, source_target_pairs={{0,4},{4,0},{8,12},{12,8},{1,5},{5,1},{9,13},{13,9},{2,6},{6,2},{1... | collective-permute-start | bytes 393224 | tf_op jit(solution)/shard_map/ppermute | solution.py:367
  26.9 10.8 %collective-permute-start.9 = (f32[8,32,128]{2,1,0:T(8,128)S(1)}, f32[8,32,128]{2,1,0:T(8,128)S(1)}, u32[]{:S(2)}, u32[]{:S(2)}) collective-permute-start(f32[8,32,128]{2,1,0:T(8,128)S(1)} %get-tuple-element.41), channel_id=1, source_target_pairs={{0,4},{4,0},{8,12},{12,8},{1,5},{5,1},{9,13},{13,9},{2,6},{6,2},{1... | collective-permute-start | bytes 393224 | tf_op jit(solution)/shard_map/ppermute | solution.py:367
  27.0 10.8 %collective-permute-start.5 = (f32[6,32,128]{2,1,0:T(8,128)S(1)}, f32[6,32,128]{2,1,0:T(8,128)S(1)}, u32[]{:S(2)}, u32[]{:S(2)}) collective-permute-start(f32[6,32,128]{2,1,0:T(8,128)S(1)} %get-tuple-element.37), channel_id=1, source_target_pairs={{0,8},{4,12},{8,0},{12,4},{1,9},{5,13},{9,1},{13,5},{2,10},{6,14},... | collective-permute-start | bytes 294920 | tf_op jit(solution)/shard_map/ppermute | solution.py:367
  37.9 3.4 %collective-permute-start.12 = (f32[32,128]{1,0:T(8,128)S(1)}, f32[32,128]{1,0:T(8,128)S(1)}, u32[]{:S(2)}, u32[]{:S(2)}) collective-permute-start(f32[32,128]{1,0:T(8,128)S(1)} %get-tuple-element.42.rest_0_), channel_id=1, source_target_pairs={{0,3},{1,2},{2,1},{3,0},{4,7},{5,6},{6,5},{7,4},{8,11},{9,10},{10,... | collective-permute-start | bytes 49160 | tf_op jit(solution)/shard_map/ppermute | solution.py:367
  38.9 3.7 %collective-permute-start.11 = (f32[32,128]{1,0:T(8,128)S(1)}, f32[32,128]{1,0:T(8,128)S(1)}, u32[]{:S(2)}, u32[]{:S(2)}) collective-permute-start(f32[32,128]{1,0:T(8,128)S(1)} %get-tuple-element.42.rest_0_), channel_id=1, source_target_pairs={{0,2},{1,3},{2,0},{3,1},{4,6},{5,7},{6,4},{7,5},{8,10},{9,11},{10,... | collective-permute-start | bytes 49160 | tf_op jit(solution)/shard_map/ppermute | solution.py:367
  39.6 3.1 %collective-permute-start.10 = (f32[32,128]{1,0:T(8,128)S(1)}, f32[32,128]{1,0:T(8,128)S(1)}, u32[]{:S(2)}, u32[]{:S(2)}) collective-permute-start(f32[32,128]{1,0:T(8,128)S(1)} %get-tuple-element.42.rest_0_), channel_id=1, source_target_pairs={{0,1},{1,0},{2,3},{3,2},{4,5},{5,4},{6,7},{7,6},{8,9},{9,8},{10,11... | collective-permute-start | bytes 49160 | tf_op jit(solution)/shard_map/ppermute | solution.py:367

commit v12 on v10

--- a/solution.py
+++ b/solution.py
@@ -78,7 +78,7 @@
     n = len(rounds) + 1
     outs, (slots, reads, sems) = rest[: n - 1], rest[n - 1 :]
     blocks, _, scen, nodes = history_ref.shape
-    pieces = 4 if blocks % 4 == 0 else 1
+    pieces = 8 if blocks % 8 == 0 else 1
     piece = blocks // pieces
     die = lax.axis_index("die")
     copies = [
@@ -91,8 +91,8 @@
         copies.append(
             pltpu.make_async_copy(history_ref.at[some], raw_ref.at[some], sems.at[3 + at])
         )
-    for copy in copies:
-        copy.start()
+    for at, copy in enumerate(copies):
+        copy.start(priority=at % 2)
     height = max(8, n)
     turn = lax.broadcasted_iota(I32, (height, blocks), 0)
     lane = lax.broadcasted_iota(I32, (height, blocks), 1)
@@ -151,37 +151,43 @@
             slope_ref[local] = slope(raw, guess)
 
 
-def serve_kernel(n, nblk, *rest):
+def told(message, j):
+    return message[message.shape[0] - 8 + j, 0].astype(I32)
+
+
+def settle(arrived, first, out):
+    scen = out.shape[1]
+    for message in arrived:
+        for rank in range(CAP):
+            place = told(message, 2 + rank)
+
+            @pl.when(place >= 0)
+            def _(message=message, rank=rank, place=place):
+                out[place] = message[pl.ds((first + rank) * scen, scen), :]
+
+
+def serve_kernel(n, *rest):
+    arrived, (old_guess, guess_ref, *outs) = rest[: n - 1], rest[n - 1 :]
+    for at in range(guess_ref.shape[0]):
+        guess_ref[at] = old_guess[at]
+    settle(arrived, 0, guess_ref)
+    for message, out in zip(arrived, outs):
+        want = joined(told(message, 0), told(message, 1))
+        for slot in range(out.shape[0]):
+            out[slot] = guess_ref[lowest(want)]
+            want = want & (want - 1)
+
+
+def merge_kernel(n, nblk, *rest):
     arrived, rest = rest[: n - 1], rest[n - 1 :]
-    inverses, rest = rest[:nblk], rest[nblk:]
-    old_guess, old_slope, guess_ref, slope_ref, whole_ref, *rest = rest
-    outs = rest
-    blocks, scen, nodes = guess_ref.shape
-
-    def told(k, j):
-        return arrived[k][2 * CAP * scen + j, 0].astype(I32)
-
-    for at in range(blocks):
-        guess_ref[at] = old_guess[at]
-        slope_ref[at] = old_slope[at]
+    inverses, (old_slope, _, slope_ref, whole_ref) = rest[:nblk], rest[nblk:]
     height = inverses[0].shape[0]
     for k in range(nblk):
         at = pl.multiple_of((lax.axis_index("blk") ^ k) * height, height)
         whole_ref[pl.ds(at, height), :] = inverses[k][...]
-    for k in range(n - 1):
-        for rank in range(CAP):
-            place = told(k, 2 + rank)
-
-            @pl.when(place >= 0)
-            def _(k=k, rank=rank, place=place):
-                guess_ref[place] = arrived[k][pl.ds(rank * scen, scen), :]
-                slope_ref[place] = arrived[k][pl.ds((CAP + rank) * scen, scen), :]
-
-    for k, out in enumerate(outs):
-        want = joined(told(k, 0), told(k, 1))
-        for slot in range(out.shape[0]):
-            out[slot] = guess_ref[lowest(want)]
-            want = want & (want - 1)
+    for at in range(slope_ref.shape[0]):
+        slope_ref[at] = old_slope[at]
+    settle(arrived, CAP, slope_ref)
 
 
 def where_kernel(rounds, span, rcap, last, partner_ref, _, index_ref, late_ref, reads, mine, starts, sem):
@@ -377,7 +383,7 @@
         ],
         [HBM] * 4,
         [VMEM] * (n + 1),
-        [pltpu.VMEM((1, blocks), I32)] * 2 + [pltpu.SemaphoreType.DMA((7,))],
+        [pltpu.VMEM((1, blocks), I32)] * 2 + [pltpu.SemaphoreType.DMA((11,))],
     )
     arrived = [swap(x, "die", n, k) for x, k in zip(leaving, rounds)]
     inverses = [rows] + [swap(rows, "blk", nblk, k) for k in range(1, nblk)]
@@ -389,14 +395,21 @@
         [VMEM, VMEM],
         [scalars(blocks), pltpu.SemaphoreType.DMA],
     )
-    guess, slopes, whole, *served = call(
-        functools.partial(serve_kernel, n, nblk),
-        [block, block, square] + [tiles(rcap)] * (n - 1),
-        [*arrived, *inverses, old_guess, old_slope],
-        [VMEM] * (n - 1 + nblk + 2),
-        [VMEM] * (n + 2),
+    guess, *served = call(
+        functools.partial(serve_kernel, n),
+        [block] + [tiles(rcap)] * (n - 1),
+        [*arrived, old_guess],
+        [VMEM] * n,
+        [VMEM] * n,
     )
     others = [swap(x, "die", n, k) for x, k in zip(served, rounds)]
+    slopes, whole = call(
+        functools.partial(merge_kernel, n, nblk),
+        [block, square],
+        [*arrived, *inverses, old_slope, guess],
+        [VMEM] * (n + nblk) + [ANY],
+        [VMEM] * 2,
+    )
     last = n - 2
     index, late = call(
         functools.partial(where_kernel, rounds, span, rcap, last),

time: 43.2 us -> 43.3 us (level)
    pallas_call x8 -> x9, Pallas kernels: 6.66 us -> 7.07 us  [call(): pl.pallas_call(body, out_shape=outs, in_specs=in_specs, out_specs=out_spe...]
  transfers between devices with their start and end apart: 10 -> 10, of which waited for: 6 -> 6; matrix products, arithmetic and copies ran while one was open for 0% -> 0% of each run, Pallas kernels for 20% -> 21%
where the time goes in v12:
time: 43.3 us; the launch traced here: 43.1 us
  waiting for transfers between devices  19 us (44%)
  Pallas kernels  12.3 us (28%)
  starting transfers between devices  11.1 us (26%)
  between operations  0.72 us (2%)
    ppermute x10, waiting for transfers between devices, swap(): return lax.ppermute(x, axes, [(d, d ^ k) for d in range(n)])  19 us
    ppermute x10, starting transfers between devices, swap(): return lax.ppermute(x, axes, [(d, d ^ k) for d in range(n)])  11.1 us
    pallas_call x9, Pallas kernels, call(): pl.pallas_call(body, out_shape=outs, in_specs=in_specs, out_specs=out_spe...  7.07 us
    pallas_call x1, Pallas kernels, shards(): pl.pallas_call(local_kernel, grid=(blocks // step,), out_shape=[block, bl...  5.19 us
  transfers between devices with their start and end apart: 10, of which 6 were waited for; matrix products, arithmetic and copies ran while one was open for 0% of the time, Pallas kernels for 21%

profile of v12, /device:TPU:9, one launch (start us, length us, event | category | flops | bytes accessed | tf_op | source)
XLA Modules:
  0.0 43.1 jit_solution(11410556651716254815)
XLA Ops:
  0.6 1.8 %shard_map.113 = (f32[32,3,32,128]{3,2,1,0:T(8,128)S(1)}, f32[64,128]{1,0:T(8,128)S(1)}, f32[136,128]{1,0:T(8,128)S(1)}, f32[136,128]{1,0:T(8,128)S(1)}, f32[136,128]{1,0:T(8,128)S(1)}) custom-call(s32[1,32]{1,0:T(1,128)} %bitcast.4, s32[1,32]{1,0:T(1,128)} %bitcast.5, f32[32,3,32,128]{3,2,1,0:T(8,128)} %history_ref.1, f32[64,128]{1,0:T(8,128)} %bitcast.3), custom_call_target="tpu_custom_call" | custom-call | tf_op jit(solution)/shard_map/pallas_call | solution.py:321
  2.4 2.4 %collective-permute-start = (f32[136,128]{1,0:T(8,128)S(1)}, f32[136,128]{1,0:T(8,128)S(1)}, u32[]{:S(2)}, u32[]{:S(2)}) collective-permute-start(f32[136,128]{1,0:T(8,128)S(1)} %get-tuple-element.25), channel_id=1, source_target_pairs={{0,8},{4,12},{8,0},{12,4},{1,9},{5,13},{9,1},{13,5},{2,10},{6,14},... | collective-permute-start | bytes 208904 | tf_op jit(solution)/shard_map/ppermute | solution.py:337
  4.8 0.0 collective-permute-start.1
  4.8 1.3 %collective-permute-start.2 = (f32[136,128]{1,0:T(8,128)S(1)}, f32[136,128]{1,0:T(8,128)S(1)}, u32[]{:S(2)}, u32[]{:S(2)}) collective-permute-start(f32[136,128]{1,0:T(8,128)S(1)} %get-tuple-element.27), channel_id=1, source_target_pairs={{0,4},{4,0},{8,12},{12,8},{1,5},{5,1},{9,13},{13,9},{2,6},{6,2},{1... | collective-permute-start | bytes 208904 | tf_op jit(solution)/shard_map/ppermute | solution.py:337
  6.0 1.1 %shard_map.114 = (f32[32,32,128]{2,1,0:T(8,128)S(1)}, f32[32,32,128]{2,1,0:T(8,128)S(1)}) custom-call(s32[32]{0:T(128)} %new_slot_ref.1, f32[32,3,32,128]{3,2,1,0:T(8,128)S(1)} %get-tuple-element.28.raw_ref), custom_call_target="tpu_custom_call" | custom-call | tf_op jit(solution)/shard_map/pallas_call | solution.py:321
  7.1 1.7 %collective-permute-done.rest_0_ = f32[136,128]{1,0:T(8,128)S(1)} collective-permute-done((f32[136,128]{1,0:T(8,128)S(1)}, f32[136,128]{1,0:T(8,128)S(1)}, u32[]{:S(2)}, u32[]{:S(2)}) %collective-permute-start) | collective-permute-done | bytes 69664 | tf_op jit(solution)/shard_map/ppermute | solution.py:337
  8.8 2.1 %collective-permute-done.1.rest_1_ = f32[136,128]{1,0:T(8,128)S(1)} collective-permute-done((f32[136,128]{1,0:T(8,128)S(1)}, f32[136,128]{1,0:T(8,128)S(1)}, u32[]{:S(2)}, u32[]{:S(2)}) %collective-permute-start.1) | collective-permute-done | bytes 69664 | tf_op jit(solution)/shard_map/ppermute | solution.py:337
  10.9 0.0 collective-permute-done.2.rest_2_
  10.9 0.5 %shard_map.115 = (f32[32,32,128]{2,1,0:T(8,128)S(1)}, f32[16,32,128]{2,1,0:T(8,128)S(1)}, f32[16,32,128]{2,1,0:T(8,128)S(1)}, f32[16,32,128]{2,1,0:T(8,128)S(1)}) custom-call(f32[136,128]{1,0:T(8,128)S(1)} %collective-permute-done.rest_0_, f32[136,128]{1,0:T(8,128)S(1)} %collective-permute-done.1.rest_1_, f32[136,128]{1,0:T(8,128)S(1)} %collective-permute-done.2.rest_2_, ...), custom_call_target="tpu_custom_call" | custom-call | tf_op jit(solution)/shard_map/pallas_call | solution.py:321
  11.3 1.9 %collective-permute-start.4 = (f32[16,32,128]{2,1,0:T(8,128)S(1)}, f32[16,32,128]{2,1,0:T(8,128)S(1)}, u32[]{:S(2)}, u32[]{:S(2)}) collective-permute-start(f32[16,32,128]{2,1,0:T(8,128)S(1)} %get-tuple-element.39), channel_id=1, source_target_pairs={{0,8},{4,12},{8,0},{12,4},{1,9},{5,13},{9,1},{13,5},{2,10},{6,14},... | collective-permute-start | bytes 786440 | tf_op jit(solution)/shard_map/ppermute | solution.py:337
  13.2 0.4 %collective-permute-start.5 = (f32[16,32,128]{2,1,0:T(8,128)S(1)}, f32[16,32,128]{2,1,0:T(8,128)S(1)}, u32[]{:S(2)}, u32[]{:S(2)}) collective-permute-start(f32[16,32,128]{2,1,0:T(8,128)S(1)} %get-tuple-element.40), channel_id=1, source_target_pairs={{0,12},{4,8},{8,4},{12,0},{1,13},{5,9},{9,5},{13,1},{2,14},{6,10},... | collective-permute-start | bytes 786440 | tf_op jit(solution)/shard_map/ppermute | solution.py:337
  13.6 1.3 %collective-permute-start.6 = (f32[16,32,128]{2,1,0:T(8,128)S(1)}, f32[16,32,128]{2,1,0:T(8,128)S(1)}, u32[]{:S(2)}, u32[]{:S(2)}) collective-permute-start(f32[16,32,128]{2,1,0:T(8,128)S(1)} %get-tuple-element.42), channel_id=1, source_target_pairs={{0,4},{4,0},{8,12},{12,8},{1,5},{5,1},{9,13},{13,9},{2,6},{6,2},{1... | collective-permute-start | bytes 786440 | tf_op jit(solution)/shard_map/ppermute | solution.py:337
  14.9 1.5 %collective-permute-start.3 = (f32[64,128]{1,0:T(8,128)S(1)}, f32[64,128]{1,0:T(8,128)S(1)}, u32[]{:S(2)}, u32[]{:S(2)}) collective-permute-start(f32[64,128]{1,0:T(8,128)S(1)} %get-tuple-element.33.rest_3_), channel_id=1, source_target_pairs={{0,1},{1,0},{2,3},{3,2},{4,5},{5,4},{6,7},{7,6},{8,9},{9,8},{10,11... | collective-permute-start | bytes 98312 | tf_op jit(solution)/shard_map/ppermute | solution.py:337
  16.5 1.4 %shard_map.116 = (s32[32]{0:T(128)S(4)}, s32[33]{0:T(128)S(4)}) custom-call(s32[32]{0:T(128)} %partner_ref.1, f32[32,32,128]{2,1,0:T(8,128)S(1)} %get-tuple-element.30._.rest_6_.guess_ref), custom_call_target="tpu_custom_call" | custom-call | tf_op jit(solution)/shard_map/pallas_call | solution.py:321
  17.9 0.0 collective-permute-done.3.rest_4_
  17.9 0.3 shard_map.117
  18.2 5.2 %shard_map.118 = (f32[32,32,128]{2,1,0:T(8,128)S(1)}, f32[32,32,128]{2,1,0:T(8,128)S(1)}, f32[32,32,128]{2,1,0:T(8,128)S(1)}, f32[32,128]{1,0:T(8,128)S(1)}) custom-call(f32[32,32,128]{2,1,0:T(8,128)S(1)} %get-tuple-element.30._.rest_6_.guess_ref, f32[32,32,128]{2,1,0:T(8,128)S(1)} %get-tuple-element.35.slope_ref, f32[32,128,128]{2,1,0:T(8,128)} %coupling_ref.1, ...), custom_call_target="tpu_custom_call" | custom-call | tf_op jit(solution)/shard_map/pallas_call | solution.py:425
  23.4 5.8 %collective-permute-done.4.rest_0_ = f32[16,32,128]{2,1,0:T(8,128)S(1)} collective-permute-done((f32[16,32,128]{2,1,0:T(8,128)S(1)}, f32[16,32,128]{2,1,0:T(8,128)S(1)}, u32[]{:S(2)}, u32[]{:S(2)}) %collective-permute-start.4) | collective-permute-done | bytes 262176 | tf_op jit(solution)/shard_map/ppermute | solution.py:337
  29.2 7.8 %collective-permute-done.5.rest_1_ = f32[16,32,128]{2,1,0:T(8,128)S(1)} collective-permute-done((f32[16,32,128]{2,1,0:T(8,128)S(1)}, f32[16,32,128]{2,1,0:T(8,128)S(1)}, u32[]{:S(2)}, u32[]{:S(2)}) %collective-permute-start.5) | collective-permute-done | bytes 262176 | tf_op jit(solution)/shard_map/ppermute | solution.py:337
  37.0 0.2 shard_map.119
  37.2 0.0 collective-permute-done.6.block_ref
  37.2 0.1 shard_map.120.rest_0_
  37.3 1.9 %collective-permute-start.9 = (f32[32,128]{1,0:T(8,128)S(1)}, f32[32,128]{1,0:T(8,128)S(1)}, u32[]{:S(2)}, u32[]{:S(2)}) collective-permute-start(f32[32,128]{1,0:T(8,128)S(1)} %shard_map.120.rest_0_), channel_id=1, source_target_pairs={{0,3},{1,2},{2,1},{3,0},{4,7},{5,6},{6,5},{7,4},{8,11},{9,10},{10,... | collective-permute-start | bytes 49160 | tf_op jit(solution)/shard_map/ppermute | solution.py:337
  39.2 0.3 collective-permute-start.8
  39.4 0.2 collective-permute-start.7
  39.6 0.9 %shard_map.121 = (f32[32,32,128]{2,1,0:T(8,128)S(1)}, f32[32,32,128]{2,1,0:T(8,128)}) custom-call(s32[32]{0:T(128)S(4)} %get-tuple-element.31.index_ref, f32[32,32,128]{2,1,0:T(8,128)S(1)} %get-tuple-element.44.near_ref, f32[16,32,128]{2,1,0:T(8,128)S(1)} %collective-permute-done.6.block_ref, f32[32,32,128]{2,1,0:T(8,128)S(1)} %get-tuple-element.38.base_ref, ...), custom_call_target="tpu_custom_call" | custom-call | tf_op jit(solution)/shard_map/pallas_call | solution.py:321
  40.5 0.4 %collective-permute-done.9.rest_3_ = f32[32,128]{1,0:T(8,128)S(1)} collective-permute-done((f32[32,128]{1,0:T(8,128)S(1)}, f32[32,128]{1,0:T(8,128)S(1)}, u32[]{:S(2)}, u32[]{:S(2)}) %collective-permute-start.9) | collective-permute-done | bytes 16416 | tf_op jit(solution)/shard_map/ppermute | solution.py:337
  41.0 1.1 %collective-permute-done.8.rest_2_ = f32[32,128]{1,0:T(8,128)S(1)} collective-permute-done((f32[32,128]{1,0:T(8,128)S(1)}, f32[32,128]{1,0:T(8,128)S(1)}, u32[]{:S(2)}, u32[]{:S(2)}) %collective-permute-start.8) | collective-permute-done | bytes 16416 | tf_op jit(solution)/shard_map/ppermute | solution.py:337
  42.1 0.0 collective-permute-done.7.rest_1_
  42.1 1.0 %shard_map.122 = f32[32,32,128]{2,1,0:T(8,128)} custom-call(f32[32,128]{1,0:T(8,128)S(1)} %shard_map.120.rest_0_, f32[32,128]{1,0:T(8,128)S(1)} %collective-permute-done.7.rest_1_, f32[32,128]{1,0:T(8,128)S(1)} %collective-permute-done.8.rest_2_, f32[32,128]{1,0:T(8,128)S(1)} %collective-permute-done.9.rest_3_, f32[128,128]{1,0:T(8,128)S(1)} %get-tuple-element.43.rest_4_, ...), custom_call_target="tpu_custom_call" | custom-call | tf_op jit(solution)/shard_map/pallas_call | solution.py:321
Async XLA Ops:
  2.4 6.4 %collective-permute-start = (f32[136,128]{1,0:T(8,128)S(1)}, f32[136,128]{1,0:T(8,128)S(1)}, u32[]{:S(2)}, u32[]{:S(2)}) collective-permute-start(f32[136,128]{1,0:T(8,128)S(1)} %get-tuple-element.25), channel_id=1, source_target_pairs={{0,8},{4,12},{8,0},{12,4},{1,9},{5,13},{9,1},{13,5},{2,10},{6,14},... | collective-permute-start | bytes 208904 | tf_op jit(solution)/shard_map/ppermute | solution.py:337
  4.8 6.1 %collective-permute-start.1 = (f32[136,128]{1,0:T(8,128)S(1)}, f32[136,128]{1,0:T(8,128)S(1)}, u32[]{:S(2)}, u32[]{:S(2)}) collective-permute-start(f32[136,128]{1,0:T(8,128)S(1)} %get-tuple-element.26), channel_id=1, source_target_pairs={{0,12},{4,8},{8,4},{12,0},{1,13},{5,9},{9,5},{13,1},{2,14},{6,10},... | collective-permute-start | bytes 208904 | tf_op jit(solution)/shard_map/ppermute | solution.py:337
  4.8 6.1 %collective-permute-start.2 = (f32[136,128]{1,0:T(8,128)S(1)}, f32[136,128]{1,0:T(8,128)S(1)}, u32[]{:S(2)}, u32[]{:S(2)}) collective-permute-start(f32[136,128]{1,0:T(8,128)S(1)} %get-tuple-element.27), channel_id=1, source_target_pairs={{0,4},{4,0},{8,12},{12,8},{1,5},{5,1},{9,13},{13,9},{2,6},{6,2},{1... | collective-permute-start | bytes 208904 | tf_op jit(solution)/shard_map/ppermute | solution.py:337
  11.3 17.9 %collective-permute-start.4 = (f32[16,32,128]{2,1,0:T(8,128)S(1)}, f32[16,32,128]{2,1,0:T(8,128)S(1)}, u32[]{:S(2)}, u32[]{:S(2)}) collective-permute-start(f32[16,32,128]{2,1,0:T(8,128)S(1)} %get-tuple-element.39), channel_id=1, source_target_pairs={{0,8},{4,12},{8,0},{12,4},{1,9},{5,13},{9,1},{13,5},{2,10},{6,14},... | collective-permute-start | bytes 786440 | tf_op jit(solution)/shard_map/ppermute | solution.py:337
  13.2 23.8 %collective-permute-start.5 = (f32[16,32,128]{2,1,0:T(8,128)S(1)}, f32[16,32,128]{2,1,0:T(8,128)S(1)}, u32[]{:S(2)}, u32[]{:S(2)}) collective-permute-start(f32[16,32,128]{2,1,0:T(8,128)S(1)} %get-tuple-element.40), channel_id=1, source_target_pairs={{0,12},{4,8},{8,4},{12,0},{1,13},{5,9},{9,5},{13,1},{2,14},{6,10},... | collective-permute-start | bytes 786440 | tf_op jit(solution)/shard_map/ppermute | solution.py:337
  13.6 23.6 %collective-permute-start.6 = (f32[16,32,128]{2,1,0:T(8,128)S(1)}, f32[16,32,128]{2,1,0:T(8,128)S(1)}, u32[]{:S(2)}, u32[]{:S(2)}) collective-permute-start(f32[16,32,128]{2,1,0:T(8,128)S(1)} %get-tuple-element.42), channel_id=1, source_target_pairs={{0,4},{4,0},{8,12},{12,8},{1,5},{5,1},{9,13},{13,9},{2,6},{6,2},{1... | collective-permute-start | bytes 786440 | tf_op jit(solution)/shard_map/ppermute | solution.py:337
  14.9 2.9 %collective-permute-start.3 = (f32[64,128]{1,0:T(8,128)S(1)}, f32[64,128]{1,0:T(8,128)S(1)}, u32[]{:S(2)}, u32[]{:S(2)}) collective-permute-start(f32[64,128]{1,0:T(8,128)S(1)} %get-tuple-element.33.rest_3_), channel_id=1, source_target_pairs={{0,1},{1,0},{2,3},{3,2},{4,5},{5,4},{6,7},{7,6},{8,9},{9,8},{10,11... | collective-permute-start | bytes 98312 | tf_op jit(solution)/shard_map/ppermute | solution.py:337
  37.3 3.6 %collective-permute-start.9 = (f32[32,128]{1,0:T(8,128)S(1)}, f32[32,128]{1,0:T(8,128)S(1)}, u32[]{:S(2)}, u32[]{:S(2)}) collective-permute-start(f32[32,128]{1,0:T(8,128)S(1)} %shard_map.120.rest_0_), channel_id=1, source_target_pairs={{0,3},{1,2},{2,1},{3,0},{4,7},{5,6},{6,5},{7,4},{8,11},{9,10},{10,... | collective-permute-start | bytes 49160 | tf_op jit(solution)/shard_map/ppermute | solution.py:337
  39.2 2.9 %collective-permute-start.8 = (f32[32,128]{1,0:T(8,128)S(1)}, f32[32,128]{1,0:T(8,128)S(1)}, u32[]{:S(2)}, u32[]{:S(2)}) collective-permute-start(f32[32,128]{1,0:T(8,128)S(1)} %shard_map.120.rest_0_), channel_id=1, source_target_pairs={{0,2},{1,3},{2,0},{3,1},{4,6},{5,7},{6,4},{7,5},{8,10},{9,11},{10,... | collective-permute-start | bytes 49160 | tf_op jit(solution)/shard_map/ppermute | solution.py:337
  39.4 2.6 %collective-permute-start.7 = (f32[32,128]{1,0:T(8,128)S(1)}, f32[32,128]{1,0:T(8,128)S(1)}, u32[]{:S(2)}, u32[]{:S(2)}) collective-permute-start(f32[32,128]{1,0:T(8,128)S(1)} %shard_map.120.rest_0_), channel_id=1, source_target_pairs={{0,1},{1,0},{2,3},{3,2},{4,5},{5,4},{6,7},{7,6},{8,9},{9,8},{10,11... | collective-permute-start | bytes 49160 | tf_op jit(solution)/shard_map/ppermute | solution.py:337

commit v13 on v12

--- a/solution.py
+++ b/solution.py
@@ -78,7 +78,7 @@
     n = len(rounds) + 1
     outs, (slots, reads, sems) = rest[: n - 1], rest[n - 1 :]
     blocks, _, scen, nodes = history_ref.shape
-    pieces = 8 if blocks % 8 == 0 else 1
+    pieces = 2 if blocks % 2 == 0 else 1
     piece = blocks // pieces
     die = lax.axis_index("die")
     copies = [
@@ -91,8 +91,8 @@
         copies.append(
             pltpu.make_async_copy(history_ref.at[some], raw_ref.at[some], sems.at[3 + at])
         )
-    for at, copy in enumerate(copies):
-        copy.start(priority=at % 2)
+    for copy in copies:
+        copy.start()
     height = max(8, n)
     turn = lax.broadcasted_iota(I32, (height, blocks), 0)
     lane = lax.broadcasted_iota(I32, (height, blocks), 1)
@@ -292,7 +292,7 @@
             partial_ref[at] = guess_ref[at] - residual * inv_ref[at]
         some = pl.ds(part * step, step)
         copies.append(pltpu.make_async_copy(held.at[some], out_ref.at[some], sems.at[part]))
-        copies[-1].start(priority=part % 2)
+        copies[-1].start()
     for copy in copies:
         copy.wait()
 
@@ -312,7 +312,7 @@
             held[at] = partial_ref[at] + scale_ref[at] * region
         span = pl.ds(part * step, step)
         copies.append(pltpu.make_async_copy(held.at[span], updated_ref.at[span], sems.at[part]))
-        copies[-1].start(priority=part % 2)
+        copies[-1].start()
     for copy in copies:
         copy.wait()
 
@@ -383,7 +383,7 @@
         ],
         [HBM] * 4,
         [VMEM] * (n + 1),
-        [pltpu.VMEM((1, blocks), I32)] * 2 + [pltpu.SemaphoreType.DMA((11,))],
+        [pltpu.VMEM((1, blocks), I32)] * 2 + [pltpu.SemaphoreType.DMA((5,))],
     )
     arrived = [swap(x, "die", n, k) for x, k in zip(leaving, rounds)]
     inverses = [rows] + [swap(rows, "blk", nblk, k) for k in range(1, nblk)]
@@ -468,7 +468,7 @@
         [SMEM] * 2 + [VMEM] * 4,
         [VMEM],
     )
-    parts = 8 if blocks % 8 == 0 else 1
+    parts = 4 if blocks % 4 == 0 else 1
     partial, residual = call(
         functools.partial(residual_kernel, rcap, last, parts),
         [block, block],

time: 43.3 us -> 43.1 us (level)
  no operation moved by 1% of the time
where the time goes in v13:
time: 43.1 us; the launch traced here: 42.5 us
  waiting for transfers between devices  18.7 us (43%)
  Pallas kernels  12 us (28%)
  starting transfers between devices  11.1 us (26%)
  between operations  0.72 us (2%)
    ppermute x10, waiting for transfers between devices, swap(): return lax.ppermute(x, axes, [(d, d ^ k) for d in range(n)])  18.7 us
    ppermute x10, starting transfers between devices, swap(): return lax.ppermute(x, axes, [(d, d ^ k) for d in range(n)])  11.1 us
    pallas_call x9, Pallas kernels, call(): pl.pallas_call(body, out_shape=outs, in_specs=in_specs, out_specs=out_spe...  6.8 us
    pallas_call x1, Pallas kernels, shards(): pl.pallas_call(local_kernel, grid=(blocks // step,), out_shape=[block, bl...  5.19 us
  transfers between devices with their start and end apart: 10, of which 6 were waited for; matrix products, arithmetic and copies ran while one was open for 0% of the time, Pallas kernels for 21%

profile of v13, /device:TPU:9, one launch (start us, length us, event | category | flops | bytes accessed | tf_op | source)
XLA Modules:
  0.0 42.5 jit_solution(268158636948276507)
XLA Ops:
  0.6 1.5 %shard_map.113 = (f32[32,3,32,128]{3,2,1,0:T(8,128)S(1)}, f32[64,128]{1,0:T(8,128)S(1)}, f32[136,128]{1,0:T(8,128)S(1)}, f32[136,128]{1,0:T(8,128)S(1)}, f32[136,128]{1,0:T(8,128)S(1)}) custom-call(s32[1,32]{1,0:T(1,128)} %bitcast.4, s32[1,32]{1,0:T(1,128)} %bitcast.5, f32[32,3,32,128]{3,2,1,0:T(8,128)} %history_ref.1, f32[64,128]{1,0:T(8,128)} %bitcast.3), custom_call_target="tpu_custom_call" | custom-call | tf_op jit(solution)/shard_map/pallas_call | solution.py:321
  2.2 2.4 %collective-permute-start = (f32[136,128]{1,0:T(8,128)S(1)}, f32[136,128]{1,0:T(8,128)S(1)}, u32[]{:S(2)}, u32[]{:S(2)}) collective-permute-start(f32[136,128]{1,0:T(8,128)S(1)} %get-tuple-element.25), channel_id=1, source_target_pairs={{0,8},{4,12},{8,0},{12,4},{1,9},{5,13},{9,1},{13,5},{2,10},{6,14},... | collective-permute-start | bytes 208904 | tf_op jit(solution)/shard_map/ppermute | solution.py:337
  4.5 0.0 collective-permute-start.1
  4.5 1.3 %collective-permute-start.2 = (f32[136,128]{1,0:T(8,128)S(1)}, f32[136,128]{1,0:T(8,128)S(1)}, u32[]{:S(2)}, u32[]{:S(2)}) collective-permute-start(f32[136,128]{1,0:T(8,128)S(1)} %get-tuple-element.27), channel_id=1, source_target_pairs={{0,4},{4,0},{8,12},{12,8},{1,5},{5,1},{9,13},{13,9},{2,6},{6,2},{1... | collective-permute-start | bytes 208904 | tf_op jit(solution)/shard_map/ppermute | solution.py:337
  5.8 1.1 %shard_map.114 = (f32[32,32,128]{2,1,0:T(8,128)S(1)}, f32[32,32,128]{2,1,0:T(8,128)S(1)}) custom-call(s32[32]{0:T(128)} %new_slot_ref.1, f32[32,3,32,128]{3,2,1,0:T(8,128)S(1)} %get-tuple-element.28.raw_ref), custom_call_target="tpu_custom_call" | custom-call | tf_op jit(solution)/shard_map/pallas_call | solution.py:321
  6.9 1.7 %collective-permute-done.rest_0_ = f32[136,128]{1,0:T(8,128)S(1)} collective-permute-done((f32[136,128]{1,0:T(8,128)S(1)}, f32[136,128]{1,0:T(8,128)S(1)}, u32[]{:S(2)}, u32[]{:S(2)}) %collective-permute-start) | collective-permute-done | bytes 69664 | tf_op jit(solution)/shard_map/ppermute | solution.py:337
  8.6 2.1 %collective-permute-done.1.rest_1_ = f32[136,128]{1,0:T(8,128)S(1)} collective-permute-done((f32[136,128]{1,0:T(8,128)S(1)}, f32[136,128]{1,0:T(8,128)S(1)}, u32[]{:S(2)}, u32[]{:S(2)}) %collective-permute-start.1) | collective-permute-done | bytes 69664 | tf_op jit(solution)/shard_map/ppermute | solution.py:337
  10.6 0.0 collective-permute-done.2.rest_2_
  10.6 0.5 %shard_map.115 = (f32[32,32,128]{2,1,0:T(8,128)S(1)}, f32[16,32,128]{2,1,0:T(8,128)S(1)}, f32[16,32,128]{2,1,0:T(8,128)S(1)}, f32[16,32,128]{2,1,0:T(8,128)S(1)}) custom-call(f32[136,128]{1,0:T(8,128)S(1)} %collective-permute-done.rest_0_, f32[136,128]{1,0:T(8,128)S(1)} %collective-permute-done.1.rest_1_, f32[136,128]{1,0:T(8,128)S(1)} %collective-permute-done.2.rest_2_, ...), custom_call_target="tpu_custom_call" | custom-call | tf_op jit(solution)/shard_map/pallas_call | solution.py:321
  11.1 1.9 %collective-permute-start.4 = (f32[16,32,128]{2,1,0:T(8,128)S(1)}, f32[16,32,128]{2,1,0:T(8,128)S(1)}, u32[]{:S(2)}, u32[]{:S(2)}) collective-permute-start(f32[16,32,128]{2,1,0:T(8,128)S(1)} %get-tuple-element.39), channel_id=1, source_target_pairs={{0,8},{4,12},{8,0},{12,4},{1,9},{5,13},{9,1},{13,5},{2,10},{6,14},... | collective-permute-start | bytes 786440 | tf_op jit(solution)/shard_map/ppermute | solution.py:337
  13.0 0.4 %collective-permute-start.5 = (f32[16,32,128]{2,1,0:T(8,128)S(1)}, f32[16,32,128]{2,1,0:T(8,128)S(1)}, u32[]{:S(2)}, u32[]{:S(2)}) collective-permute-start(f32[16,32,128]{2,1,0:T(8,128)S(1)} %get-tuple-element.40), channel_id=1, source_target_pairs={{0,12},{4,8},{8,4},{12,0},{1,13},{5,9},{9,5},{13,1},{2,14},{6,10},... | collective-permute-start | bytes 786440 | tf_op jit(solution)/shard_map/ppermute | solution.py:337
  13.4 1.3 %collective-permute-start.6 = (f32[16,32,128]{2,1,0:T(8,128)S(1)}, f32[16,32,128]{2,1,0:T(8,128)S(1)}, u32[]{:S(2)}, u32[]{:S(2)}) collective-permute-start(f32[16,32,128]{2,1,0:T(8,128)S(1)} %get-tuple-element.42), channel_id=1, source_target_pairs={{0,4},{4,0},{8,12},{12,8},{1,5},{5,1},{9,13},{13,9},{2,6},{6,2},{1... | collective-permute-start | bytes 786440 | tf_op jit(solution)/shard_map/ppermute | solution.py:337
  14.7 1.5 %collective-permute-start.3 = (f32[64,128]{1,0:T(8,128)S(1)}, f32[64,128]{1,0:T(8,128)S(1)}, u32[]{:S(2)}, u32[]{:S(2)}) collective-permute-start(f32[64,128]{1,0:T(8,128)S(1)} %get-tuple-element.33.rest_3_), channel_id=1, source_target_pairs={{0,1},{1,0},{2,3},{3,2},{4,5},{5,4},{6,7},{7,6},{8,9},{9,8},{10,11... | collective-permute-start | bytes 98312 | tf_op jit(solution)/shard_map/ppermute | solution.py:337
  16.3 1.4 %shard_map.116 = (s32[32]{0:T(128)S(4)}, s32[33]{0:T(128)S(4)}) custom-call(s32[32]{0:T(128)} %partner_ref.1, f32[32,32,128]{2,1,0:T(8,128)S(1)} %get-tuple-element.30._.rest_6_.guess_ref), custom_call_target="tpu_custom_call" | custom-call | tf_op jit(solution)/shard_map/pallas_call | solution.py:321
  17.6 0.0 collective-permute-done.3.rest_4_
  17.7 0.3 shard_map.117
  18.0 5.2 %shard_map.118 = (f32[32,32,128]{2,1,0:T(8,128)S(1)}, f32[32,32,128]{2,1,0:T(8,128)S(1)}, f32[32,32,128]{2,1,0:T(8,128)S(1)}, f32[32,128]{1,0:T(8,128)S(1)}) custom-call(f32[32,32,128]{2,1,0:T(8,128)S(1)} %get-tuple-element.30._.rest_6_.guess_ref, f32[32,32,128]{2,1,0:T(8,128)S(1)} %get-tuple-element.35.slope_ref, f32[32,128,128]{2,1,0:T(8,128)} %coupling_ref.1, ...), custom_call_target="tpu_custom_call" | custom-call | tf_op jit(solution)/shard_map/pallas_call | solution.py:425
  23.1 5.8 %collective-permute-done.4.rest_0_ = f32[16,32,128]{2,1,0:T(8,128)S(1)} collective-permute-done((f32[16,32,128]{2,1,0:T(8,128)S(1)}, f32[16,32,128]{2,1,0:T(8,128)S(1)}, u32[]{:S(2)}, u32[]{:S(2)}) %collective-permute-start.4) | collective-permute-done | bytes 262176 | tf_op jit(solution)/shard_map/ppermute | solution.py:337
  29.0 7.8 %collective-permute-done.5.rest_1_ = f32[16,32,128]{2,1,0:T(8,128)S(1)} collective-permute-done((f32[16,32,128]{2,1,0:T(8,128)S(1)}, f32[16,32,128]{2,1,0:T(8,128)S(1)}, u32[]{:S(2)}, u32[]{:S(2)}) %collective-permute-start.5) | collective-permute-done | bytes 262176 | tf_op jit(solution)/shard_map/ppermute | solution.py:337
  36.8 0.2 shard_map.119
  37.0 0.0 collective-permute-done.6.block_ref
  37.0 0.1 shard_map.120.rest_0_
  37.1 1.9 %collective-permute-start.9 = (f32[32,128]{1,0:T(8,128)S(1)}, f32[32,128]{1,0:T(8,128)S(1)}, u32[]{:S(2)}, u32[]{:S(2)}) collective-permute-start(f32[32,128]{1,0:T(8,128)S(1)} %shard_map.120.rest_0_), channel_id=1, source_target_pairs={{0,3},{1,2},{2,1},{3,0},{4,7},{5,6},{6,5},{7,4},{8,11},{9,10},{10,... | collective-permute-start | bytes 49160 | tf_op jit(solution)/shard_map/ppermute | solution.py:337
  38.9 0.3 collective-permute-start.8
  39.2 0.2 collective-permute-start.7
  39.4 0.8 %shard_map.121 = (f32[32,32,128]{2,1,0:T(8,128)S(1)}, f32[32,32,128]{2,1,0:T(8,128)}) custom-call(s32[32]{0:T(128)S(4)} %get-tuple-element.31.index_ref, f32[32,32,128]{2,1,0:T(8,128)S(1)} %get-tuple-element.44.near_ref, f32[16,32,128]{2,1,0:T(8,128)S(1)} %collective-permute-done.6.block_ref, f32[32,32,128]{2,1,0:T(8,128)S(1)} %get-tuple-element.38.base_ref, ...), custom_call_target="tpu_custom_call" | custom-call | tf_op jit(solution)/shard_map/pallas_call | solution.py:321
  40.3 0.5 %collective-permute-done.9.rest_3_ = f32[32,128]{1,0:T(8,128)S(1)} collective-permute-done((f32[32,128]{1,0:T(8,128)S(1)}, f32[32,128]{1,0:T(8,128)S(1)}, u32[]{:S(2)}, u32[]{:S(2)}) %collective-permute-start.9) | collective-permute-done | bytes 16416 | tf_op jit(solution)/shard_map/ppermute | solution.py:337
  40.7 0.8 %collective-permute-done.8.rest_2_ = f32[32,128]{1,0:T(8,128)S(1)} collective-permute-done((f32[32,128]{1,0:T(8,128)S(1)}, f32[32,128]{1,0:T(8,128)S(1)}, u32[]{:S(2)}, u32[]{:S(2)}) %collective-permute-start.8) | collective-permute-done | bytes 16416 | tf_op jit(solution)/shard_map/ppermute | solution.py:337
  41.5 0.0 collective-permute-done.7.rest_1_
  41.5 1.0 %shard_map.122 = f32[32,32,128]{2,1,0:T(8,128)} custom-call(f32[32,128]{1,0:T(8,128)S(1)} %shard_map.120.rest_0_, f32[32,128]{1,0:T(8,128)S(1)} %collective-permute-done.7.rest_1_, f32[32,128]{1,0:T(8,128)S(1)} %collective-permute-done.8.rest_2_, f32[32,128]{1,0:T(8,128)S(1)} %collective-permute-done.9.rest_3_, f32[128,128]{1,0:T(8,128)S(1)} %get-tuple-element.43.rest_4_, ...), custom_call_target="tpu_custom_call" | custom-call | tf_op jit(solution)/shard_map/pallas_call | solution.py:321
Async XLA Ops:
  2.2 6.4 %collective-permute-start = (f32[136,128]{1,0:T(8,128)S(1)}, f32[136,128]{1,0:T(8,128)S(1)}, u32[]{:S(2)}, u32[]{:S(2)}) collective-permute-start(f32[136,128]{1,0:T(8,128)S(1)} %get-tuple-element.25), channel_id=1, source_target_pairs={{0,8},{4,12},{8,0},{12,4},{1,9},{5,13},{9,1},{13,5},{2,10},{6,14},... | collective-permute-start | bytes 208904 | tf_op jit(solution)/shard_map/ppermute | solution.py:337
  4.5 6.1 %collective-permute-start.1 = (f32[136,128]{1,0:T(8,128)S(1)}, f32[136,128]{1,0:T(8,128)S(1)}, u32[]{:S(2)}, u32[]{:S(2)}) collective-permute-start(f32[136,128]{1,0:T(8,128)S(1)} %get-tuple-element.26), channel_id=1, source_target_pairs={{0,12},{4,8},{8,4},{12,0},{1,13},{5,9},{9,5},{13,1},{2,14},{6,10},... | collective-permute-start | bytes 208904 | tf_op jit(solution)/shard_map/ppermute | solution.py:337
  4.5 6.1 %collective-permute-start.2 = (f32[136,128]{1,0:T(8,128)S(1)}, f32[136,128]{1,0:T(8,128)S(1)}, u32[]{:S(2)}, u32[]{:S(2)}) collective-permute-start(f32[136,128]{1,0:T(8,128)S(1)} %get-tuple-element.27), channel_id=1, source_target_pairs={{0,4},{4,0},{8,12},{12,8},{1,5},{5,1},{9,13},{13,9},{2,6},{6,2},{1... | collective-permute-start | bytes 208904 | tf_op jit(solution)/shard_map/ppermute | solution.py:337
  11.1 17.9 %collective-permute-start.4 = (f32[16,32,128]{2,1,0:T(8,128)S(1)}, f32[16,32,128]{2,1,0:T(8,128)S(1)}, u32[]{:S(2)}, u32[]{:S(2)}) collective-permute-start(f32[16,32,128]{2,1,0:T(8,128)S(1)} %get-tuple-element.39), channel_id=1, source_target_pairs={{0,8},{4,12},{8,0},{12,4},{1,9},{5,13},{9,1},{13,5},{2,10},{6,14},... | collective-permute-start | bytes 786440 | tf_op jit(solution)/shard_map/ppermute | solution.py:337
  13.0 23.8 %collective-permute-start.5 = (f32[16,32,128]{2,1,0:T(8,128)S(1)}, f32[16,32,128]{2,1,0:T(8,128)S(1)}, u32[]{:S(2)}, u32[]{:S(2)}) collective-permute-start(f32[16,32,128]{2,1,0:T(8,128)S(1)} %get-tuple-element.40), channel_id=1, source_target_pairs={{0,12},{4,8},{8,4},{12,0},{1,13},{5,9},{9,5},{13,1},{2,14},{6,10},... | collective-permute-start | bytes 786440 | tf_op jit(solution)/shard_map/ppermute | solution.py:337
  13.4 23.6 %collective-permute-start.6 = (f32[16,32,128]{2,1,0:T(8,128)S(1)}, f32[16,32,128]{2,1,0:T(8,128)S(1)}, u32[]{:S(2)}, u32[]{:S(2)}) collective-permute-start(f32[16,32,128]{2,1,0:T(8,128)S(1)} %get-tuple-element.42), channel_id=1, source_target_pairs={{0,4},{4,0},{8,12},{12,8},{1,5},{5,1},{9,13},{13,9},{2,6},{6,2},{1... | collective-permute-start | bytes 786440 | tf_op jit(solution)/shard_map/ppermute | solution.py:337
  14.7 2.9 %collective-permute-start.3 = (f32[64,128]{1,0:T(8,128)S(1)}, f32[64,128]{1,0:T(8,128)S(1)}, u32[]{:S(2)}, u32[]{:S(2)}) collective-permute-start(f32[64,128]{1,0:T(8,128)S(1)} %get-tuple-element.33.rest_3_), channel_id=1, source_target_pairs={{0,1},{1,0},{2,3},{3,2},{4,5},{5,4},{6,7},{7,6},{8,9},{9,8},{10,11... | collective-permute-start | bytes 98312 | tf_op jit(solution)/shard_map/ppermute | solution.py:337
  37.1 3.6 %collective-permute-start.9 = (f32[32,128]{1,0:T(8,128)S(1)}, f32[32,128]{1,0:T(8,128)S(1)}, u32[]{:S(2)}, u32[]{:S(2)}) collective-permute-start(f32[32,128]{1,0:T(8,128)S(1)} %shard_map.120.rest_0_), channel_id=1, source_target_pairs={{0,3},{1,2},{2,1},{3,0},{4,7},{5,6},{6,5},{7,4},{8,11},{9,10},{10,... | collective-permute-start | bytes 49160 | tf_op jit(solution)/shard_map/ppermute | solution.py:337
  38.9 2.6 %collective-permute-start.8 = (f32[32,128]{1,0:T(8,128)S(1)}, f32[32,128]{1,0:T(8,128)S(1)}, u32[]{:S(2)}, u32[]{:S(2)}) collective-permute-start(f32[32,128]{1,0:T(8,128)S(1)} %shard_map.120.rest_0_), channel_id=1, source_target_pairs={{0,2},{1,3},{2,0},{3,1},{4,6},{5,7},{6,4},{7,5},{8,10},{9,11},{10,... | collective-permute-start | bytes 49160 | tf_op jit(solution)/shard_map/ppermute | solution.py:337
  39.2 2.3 %collective-permute-start.7 = (f32[32,128]{1,0:T(8,128)S(1)}, f32[32,128]{1,0:T(8,128)S(1)}, u32[]{:S(2)}, u32[]{:S(2)}) collective-permute-start(f32[32,128]{1,0:T(8,128)S(1)} %shard_map.120.rest_0_), channel_id=1, source_target_pairs={{0,1},{1,0},{2,3},{3,2},{4,5},{5,4},{6,7},{7,6},{8,9},{9,8},{10,11... | collective-permute-start | bytes 49160 | tf_op jit(solution)/shard_map/ppermute | solution.py:337

commit v14 on v13

--- a/solution.py
+++ b/solution.py
@@ -477,12 +477,17 @@
         [VMEM, HBM],
         [pltpu.VMEM((blocks, scen, nodes), F32), pltpu.SemaphoreType.DMA((parts,))],
     )
-    shares = [share] + [swap(share, ("sub", "blk"), ncol, k) for k in range(1, ncol)]
+    column = ("sub", "blk")
+    shares = [share] + [swap(share, column, ncol, k) for k in range(1, nblk)]
+    for up in (True, False):
+        for k in range(nblk, ncol):
+            pairs = [(d, d ^ k) for d in range(ncol) if (d < d ^ k) == up]
+            shares.append(lax.ppermute(share, column, pairs))
     (updated,) = call(
-        functools.partial(update_kernel, ncol, parts),
+        functools.partial(update_kernel, len(shares), parts),
         [block],
         [*shares, whole, partial, scale],
-        [VMEM] * (ncol + 3),
+        [VMEM] * (len(shares) + 3),
         [HBM],
         [pltpu.VMEM((blocks, scen, nodes), F32), pltpu.SemaphoreType.DMA((parts,))],
     )

time: 43.1 us -> 49.1 us (1.14)
  starting transfers between devices: 11.1 us -> 18 us
  waiting for transfers between devices: 18.7 us -> 17.5 us
    ppermute x0 -> x4, starting transfers between devices: none -> 8.71 us  [shards(): shares.append(lax.ppermute(share, column, pairs))]
    ppermute x10 -> x8, starting transfers between devices: 11.1 us -> 9.26 us  [swap(): return lax.ppermute(x, axes, [(d, d ^ k) for d in range(n)])]
    ppermute x10 -> x8, waiting for transfers between devices: 18.7 us -> 17.4 us  [swap(): return lax.ppermute(x, axes, [(d, d ^ k) for d in range(n)])]
  transfers between devices with their start and end apart: 10 -> 12, of which waited for: 6 -> 4; matrix products, arithmetic and copies ran while one was open for 0% -> 0% of each run, Pallas kernels for 21% -> 19%
where the time goes in v14:
time: 49.1 us; the launch traced here: 48.2 us
  starting transfers between devices  18 us (37%)
  waiting for transfers between devices  17.5 us (36%)
  Pallas kernels  12 us (24%)
  between operations  0.79 us (2%)
    ppermute x8, waiting for transfers between devices, swap(): return lax.ppermute(x, axes, [(d, d ^ k) for d in range(n)])  17.4 us
    ppermute x8, starting transfers between devices, swap(): return lax.ppermute(x, axes, [(d, d ^ k) for d in range(n)])  9.26 us
    ppermute x4, starting transfers between devices, shards(): shares.append(lax.ppermute(share, column, pairs))  8.71 us
    pallas_call x9, Pallas kernels, call(): pl.pallas_call(body, out_shape=outs, in_specs=in_specs, out_specs=out_spe...  6.8 us
    pallas_call x1, Pallas kernels, shards(): pl.pallas_call(local_kernel, grid=(blocks // step,), out_shape=[block, bl...  5.19 us
  transfers between devices with their start and end apart: 12, of which 4 were waited for; matrix products, arithmetic and copies ran while one was open for 0% of the time, Pallas kernels for 19%

profile of v14, /device:TPU:9, one launch (start us, length us, event | category | flops | bytes accessed | tf_op | source)
XLA Modules:
  0.0 48.2 jit_solution(14989892930934202961)
XLA Ops:
  0.6 1.5 %shard_map.113 = (f32[32,3,32,128]{3,2,1,0:T(8,128)S(1)}, f32[64,128]{1,0:T(8,128)S(1)}, f32[136,128]{1,0:T(8,128)S(1)}, f32[136,128]{1,0:T(8,128)S(1)}, f32[136,128]{1,0:T(8,128)S(1)}) custom-call(s32[1,32]{1,0:T(1,128)} %bitcast.4, s32[1,32]{1,0:T(1,128)} %bitcast.5, f32[32,3,32,128]{3,2,1,0:T(8,128)} %history_ref.1, f32[64,128]{1,0:T(8,128)} %bitcast.3), custom_call_target="tpu_custom_call" | custom-call | tf_op jit(solution)/shard_map/pallas_call | solution.py:321
  2.2 2.4 %collective-permute-start = (f32[136,128]{1,0:T(8,128)S(1)}, f32[136,128]{1,0:T(8,128)S(1)}, u32[]{:S(2)}, u32[]{:S(2)}) collective-permute-start(f32[136,128]{1,0:T(8,128)S(1)} %get-tuple-element.25), channel_id=1, source_target_pairs={{0,8},{4,12},{8,0},{12,4},{1,9},{5,13},{9,1},{13,5},{2,10},{6,14},... | collective-permute-start | bytes 208904 | tf_op jit(solution)/shard_map/ppermute | solution.py:337
  4.5 0.0 collective-permute-start.1
  4.5 1.3 %collective-permute-start.2 = (f32[136,128]{1,0:T(8,128)S(1)}, f32[136,128]{1,0:T(8,128)S(1)}, u32[]{:S(2)}, u32[]{:S(2)}) collective-permute-start(f32[136,128]{1,0:T(8,128)S(1)} %get-tuple-element.27), channel_id=1, source_target_pairs={{0,4},{4,0},{8,12},{12,8},{1,5},{5,1},{9,13},{13,9},{2,6},{6,2},{1... | collective-permute-start | bytes 208904 | tf_op jit(solution)/shard_map/ppermute | solution.py:337
  5.8 1.1 %shard_map.114 = (f32[32,32,128]{2,1,0:T(8,128)S(1)}, f32[32,32,128]{2,1,0:T(8,128)S(1)}) custom-call(s32[32]{0:T(128)} %new_slot_ref.1, f32[32,3,32,128]{3,2,1,0:T(8,128)S(1)} %get-tuple-element.28.raw_ref), custom_call_target="tpu_custom_call" | custom-call | tf_op jit(solution)/shard_map/pallas_call | solution.py:321
  6.9 1.7 %collective-permute-done.rest_0_ = f32[136,128]{1,0:T(8,128)S(1)} collective-permute-done((f32[136,128]{1,0:T(8,128)S(1)}, f32[136,128]{1,0:T(8,128)S(1)}, u32[]{:S(2)}, u32[]{:S(2)}) %collective-permute-start) | collective-permute-done | bytes 69664 | tf_op jit(solution)/shard_map/ppermute | solution.py:337
  8.6 2.1 %collective-permute-done.1.rest_1_ = f32[136,128]{1,0:T(8,128)S(1)} collective-permute-done((f32[136,128]{1,0:T(8,128)S(1)}, f32[136,128]{1,0:T(8,128)S(1)}, u32[]{:S(2)}, u32[]{:S(2)}) %collective-permute-start.1) | collective-permute-done | bytes 69664 | tf_op jit(solution)/shard_map/ppermute | solution.py:337
  10.6 0.0 collective-permute-done.2.rest_2_
  10.6 0.5 shard_map.115
  11.1 1.9 %collective-permute-start.4 = (f32[16,32,128]{2,1,0:T(8,128)S(1)}, f32[16,32,128]{2,1,0:T(8,128)S(1)}, u32[]{:S(2)}, u32[]{:S(2)}) collective-permute-start(f32[16,32,128]{2,1,0:T(8,128)S(1)} %get-tuple-element.39), channel_id=1, source_target_pairs={{0,8},{4,12},{8,0},{12,4},{1,9},{5,13},{9,1},{13,5},{2,10},{6,14},... | collective-permute-start | bytes 786440 | tf_op jit(solution)/shard_map/ppermute | solution.py:337
  13.0 0.4 collective-permute-start.5
  13.4 1.3 %collective-permute-start.6 = (f32[16,32,128]{2,1,0:T(8,128)S(1)}, f32[16,32,128]{2,1,0:T(8,128)S(1)}, u32[]{:S(2)}, u32[]{:S(2)}) collective-permute-start(f32[16,32,128]{2,1,0:T(8,128)S(1)} %get-tuple-element.42), channel_id=1, source_target_pairs={{0,4},{4,0},{8,12},{12,8},{1,5},{5,1},{9,13},{13,9},{2,6},{6,2},{1... | collective-permute-start | bytes 786440 | tf_op jit(solution)/shard_map/ppermute | solution.py:337
  14.7 1.6 %collective-permute-start.3 = (f32[64,128]{1,0:T(8,128)S(1)}, f32[64,128]{1,0:T(8,128)S(1)}, u32[]{:S(2)}, u32[]{:S(2)}) collective-permute-start(f32[64,128]{1,0:T(8,128)S(1)} %get-tuple-element.33.rest_3_), channel_id=1, source_target_pairs={{0,1},{1,0},{2,3},{3,2},{4,5},{5,4},{6,7},{7,6},{8,9},{9,8},{10,11... | collective-permute-start | bytes 98312 | tf_op jit(solution)/shard_map/ppermute | solution.py:337
  16.3 1.4 %shard_map.116 = (s32[32]{0:T(128)S(4)}, s32[33]{0:T(128)S(4)}) custom-call(s32[32]{0:T(128)} %partner_ref.1, f32[32,32,128]{2,1,0:T(8,128)S(1)} %get-tuple-element.30._.rest_6_.guess_ref), custom_call_target="tpu_custom_call" | custom-call | tf_op jit(solution)/shard_map/pallas_call | solution.py:321
  17.6 0.0 collective-permute-done.3.rest_4_
  17.7 0.3 shard_map.117
  18.0 5.2 %shard_map.118 = (f32[32,32,128]{2,1,0:T(8,128)S(1)}, f32[32,32,128]{2,1,0:T(8,128)S(1)}, f32[32,32,128]{2,1,0:T(8,128)S(1)}, f32[32,128]{1,0:T(8,128)S(1)}) custom-call(f32[32,32,128]{2,1,0:T(8,128)S(1)} %get-tuple-element.30._.rest_6_.guess_ref, f32[32,32,128]{2,1,0:T(8,128)S(1)} %get-tuple-element.35.slope_ref, f32[32,128,128]{2,1,0:T(8,128)} %coupling_ref.1, ...), custom_call_target="tpu_custom_call" | custom-call | tf_op jit(solution)/shard_map/pallas_call | solution.py:425
  23.1 5.8 %collective-permute-done.4.rest_0_ = f32[16,32,128]{2,1,0:T(8,128)S(1)} collective-permute-done((f32[16,32,128]{2,1,0:T(8,128)S(1)}, f32[16,32,128]{2,1,0:T(8,128)S(1)}, u32[]{:S(2)}, u32[]{:S(2)}) %collective-permute-start.4) | collective-permute-done | bytes 262176 | tf_op jit(solution)/shard_map/ppermute | solution.py:337
  29.0 7.8 %collective-permute-done.5.rest_1_ = f32[16,32,128]{2,1,0:T(8,128)S(1)} collective-permute-done((f32[16,32,128]{2,1,0:T(8,128)S(1)}, f32[16,32,128]{2,1,0:T(8,128)S(1)}, u32[]{:S(2)}, u32[]{:S(2)}) %collective-permute-start.5) | collective-permute-done | bytes 262176 | tf_op jit(solution)/shard_map/ppermute | solution.py:337
  36.8 0.2 shard_map.119
  37.0 0.0 collective-permute-done.6.block_ref
  37.0 0.1 shard_map.120.rest_0_
  37.1 1.3 %collective-permute-start.11 = (f32[32,128]{1,0:T(8,128)S(1)}, f32[32,128]{1,0:T(8,128)S(1)}, u32[]{:S(2)}, u32[]{:S(2)}) collective-permute-start(f32[32,128]{1,0:T(8,128)S(1)} %shard_map.120.rest_0_), channel_id=1, source_target_pairs={{2,1},{3,0},{6,5},{7,4},{10,9},{11,8},{14,13},{15,12},{18,17},{19,... | collective-permute-start | bytes 49160 | tf_op jit(solution)/shard_map/ppermute | solution.py:485
  38.4 1.3 %collective-permute-start.10 = (f32[32,128]{1,0:T(8,128)S(1)}, f32[32,128]{1,0:T(8,128)S(1)}, u32[]{:S(2)}, u32[]{:S(2)}) collective-permute-start(f32[32,128]{1,0:T(8,128)S(1)} %shard_map.120.rest_0_), channel_id=1, source_target_pairs={{2,0},{3,1},{6,4},{7,5},{10,8},{11,9},{14,12},{15,13},{18,16},{19,... | collective-permute-start | bytes 49160 | tf_op jit(solution)/shard_map/ppermute | solution.py:485
  39.7 4.8 %collective-permute-start.9 = (f32[32,128]{1,0:T(8,128)S(1)}, f32[32,128]{1,0:T(8,128)S(1)}, u32[]{:S(2)}, u32[]{:S(2)}) collective-permute-start(f32[32,128]{1,0:T(8,128)S(1)} %shard_map.120.rest_0_), channel_id=1, source_target_pairs={{0,3},{1,2},{4,7},{5,6},{8,11},{9,10},{12,15},{13,14},{16,19},{17,... | collective-permute-start | bytes 49160 | tf_op jit(solution)/shard_map/ppermute | solution.py:485
  44.5 1.3 %collective-permute-start.8 = (f32[32,128]{1,0:T(8,128)S(1)}, f32[32,128]{1,0:T(8,128)S(1)}, u32[]{:S(2)}, u32[]{:S(2)}) collective-permute-start(f32[32,128]{1,0:T(8,128)S(1)} %shard_map.120.rest_0_), channel_id=1, source_target_pairs={{0,2},{1,3},{4,6},{5,7},{8,10},{9,11},{12,14},{13,15},{16,18},{17,... | collective-permute-start | bytes 49160 | tf_op jit(solution)/shard_map/ppermute | solution.py:485
  45.8 0.5 collective-permute-start.7
  46.3 0.8 %shard_map.121 = (f32[32,32,128]{2,1,0:T(8,128)S(1)}, f32[32,32,128]{2,1,0:T(8,128)}) custom-call(s32[32]{0:T(128)S(4)} %get-tuple-element.31.index_ref, f32[32,32,128]{2,1,0:T(8,128)S(1)} %get-tuple-element.44.near_ref, f32[16,32,128]{2,1,0:T(8,128)S(1)} %collective-permute-done.6.block_ref, f32[32,32,128]{2,1,0:T(8,128)S(1)} %get-tuple-element.38.base_ref, ...), custom_call_target="tpu_custom_call" | custom-call | tf_op jit(solution)/shard_map/pallas_call | solution.py:321
  47.1 0.0 collective-permute-done.11.rest_5_
  47.2 0.0 collective-permute-done.10.rest_4_
  47.2 0.0 collective-permute-done.9.rest_3_
  47.2 0.0 collective-permute-done.8.rest_2_
  47.2 0.0 collective-permute-done.7.rest_1_
  47.2 1.0 %shard_map.122 = f32[32,32,128]{2,1,0:T(8,128)} custom-call(f32[32,128]{1,0:T(8,128)S(1)} %shard_map.120.rest_0_, f32[32,128]{1,0:T(8,128)S(1)} %collective-permute-done.7.rest_1_, f32[32,128]{1,0:T(8,128)S(1)} %collective-permute-done.8.rest_2_, f32[32,128]{1,0:T(8,128)S(1)} %collective-permute-done.9.rest_3_, ...), custom_call_target="tpu_custom_call" | custom-call | tf_op jit(solution)/shard_map/pallas_call | solution.py:321
Async XLA Ops:
  2.2 6.4 %collective-permute-start = (f32[136,128]{1,0:T(8,128)S(1)}, f32[136,128]{1,0:T(8,128)S(1)}, u32[]{:S(2)}, u32[]{:S(2)}) collective-permute-start(f32[136,128]{1,0:T(8,128)S(1)} %get-tuple-element.25), channel_id=1, source_target_pairs={{0,8},{4,12},{8,0},{12,4},{1,9},{5,13},{9,1},{13,5},{2,10},{6,14},... | collective-permute-start | bytes 208904 | tf_op jit(solution)/shard_map/ppermute | solution.py:337
  4.5 6.1 %collective-permute-start.1 = (f32[136,128]{1,0:T(8,128)S(1)}, f32[136,128]{1,0:T(8,128)S(1)}, u32[]{:S(2)}, u32[]{:S(2)}) collective-permute-start(f32[136,128]{1,0:T(8,128)S(1)} %get-tuple-element.26), channel_id=1, source_target_pairs={{0,12},{4,8},{8,4},{12,0},{1,13},{5,9},{9,5},{13,1},{2,14},{6,10},... | collective-permute-start | bytes 208904 | tf_op jit(solution)/shard_map/ppermute | solution.py:337
  4.5 6.1 %collective-permute-start.2 = (f32[136,128]{1,0:T(8,128)S(1)}, f32[136,128]{1,0:T(8,128)S(1)}, u32[]{:S(2)}, u32[]{:S(2)}) collective-permute-start(f32[136,128]{1,0:T(8,128)S(1)} %get-tuple-element.27), channel_id=1, source_target_pairs={{0,4},{4,0},{8,12},{12,8},{1,5},{5,1},{9,13},{13,9},{2,6},{6,2},{1... | collective-permute-start | bytes 208904 | tf_op jit(solution)/shard_map/ppermute | solution.py:337
  11.1 17.9 %collective-permute-start.4 = (f32[16,32,128]{2,1,0:T(8,128)S(1)}, f32[16,32,128]{2,1,0:T(8,128)S(1)}, u32[]{:S(2)}, u32[]{:S(2)}) collective-permute-start(f32[16,32,128]{2,1,0:T(8,128)S(1)} %get-tuple-element.39), channel_id=1, source_target_pairs={{0,8},{4,12},{8,0},{12,4},{1,9},{5,13},{9,1},{13,5},{2,10},{6,14},... | collective-permute-start | bytes 786440 | tf_op jit(solution)/shard_map/ppermute | solution.py:337
  13.0 23.8 %collective-permute-start.5 = (f32[16,32,128]{2,1,0:T(8,128)S(1)}, f32[16,32,128]{2,1,0:T(8,128)S(1)}, u32[]{:S(2)}, u32[]{:S(2)}) collective-permute-start(f32[16,32,128]{2,1,0:T(8,128)S(1)} %get-tuple-element.40), channel_id=1, source_target_pairs={{0,12},{4,8},{8,4},{12,0},{1,13},{5,9},{9,5},{13,1},{2,14},{6,10},... | collective-permute-start | bytes 786440 | tf_op jit(solution)/shard_map/ppermute | solution.py:337
  13.4 23.6 %collective-permute-start.6 = (f32[16,32,128]{2,1,0:T(8,128)S(1)}, f32[16,32,128]{2,1,0:T(8,128)S(1)}, u32[]{:S(2)}, u32[]{:S(2)}) collective-permute-start(f32[16,32,128]{2,1,0:T(8,128)S(1)} %get-tuple-element.42), channel_id=1, source_target_pairs={{0,4},{4,0},{8,12},{12,8},{1,5},{5,1},{9,13},{13,9},{2,6},{6,2},{1... | collective-permute-start | bytes 786440 | tf_op jit(solution)/shard_map/ppermute | solution.py:337
  14.7 2.9 %collective-permute-start.3 = (f32[64,128]{1,0:T(8,128)S(1)}, f32[64,128]{1,0:T(8,128)S(1)}, u32[]{:S(2)}, u32[]{:S(2)}) collective-permute-start(f32[64,128]{1,0:T(8,128)S(1)} %get-tuple-element.33.rest_3_), channel_id=1, source_target_pairs={{0,1},{1,0},{2,3},{3,2},{4,5},{5,4},{6,7},{7,6},{8,9},{9,8},{10,11... | collective-permute-start | bytes 98312 | tf_op jit(solution)/shard_map/ppermute | solution.py:337
  37.1 10.1 %collective-permute-start.11 = (f32[32,128]{1,0:T(8,128)S(1)}, f32[32,128]{1,0:T(8,128)S(1)}, u32[]{:S(2)}, u32[]{:S(2)}) collective-permute-start(f32[32,128]{1,0:T(8,128)S(1)} %shard_map.120.rest_0_), channel_id=1, source_target_pairs={{2,1},{3,0},{6,5},{7,4},{10,9},{11,8},{14,13},{15,12},{18,17},{19,... | collective-permute-start | bytes 49160 | tf_op jit(solution)/shard_map/ppermute | solution.py:485
  38.4 8.8 %collective-permute-start.10 = (f32[32,128]{1,0:T(8,128)S(1)}, f32[32,128]{1,0:T(8,128)S(1)}, u32[]{:S(2)}, u32[]{:S(2)}) collective-permute-start(f32[32,128]{1,0:T(8,128)S(1)} %shard_map.120.rest_0_), channel_id=1, source_target_pairs={{2,0},{3,1},{6,4},{7,5},{10,8},{11,9},{14,12},{15,13},{18,16},{19,... | collective-permute-start | bytes 49160 | tf_op jit(solution)/shard_map/ppermute | solution.py:485
  39.7 7.5 %collective-permute-start.9 = (f32[32,128]{1,0:T(8,128)S(1)}, f32[32,128]{1,0:T(8,128)S(1)}, u32[]{:S(2)}, u32[]{:S(2)}) collective-permute-start(f32[32,128]{1,0:T(8,128)S(1)} %shard_map.120.rest_0_), channel_id=1, source_target_pairs={{0,3},{1,2},{4,7},{5,6},{8,11},{9,10},{12,15},{13,14},{16,19},{17,... | collective-permute-start | bytes 49160 | tf_op jit(solution)/shard_map/ppermute | solution.py:485
  44.5 2.6 %collective-permute-start.8 = (f32[32,128]{1,0:T(8,128)S(1)}, f32[32,128]{1,0:T(8,128)S(1)}, u32[]{:S(2)}, u32[]{:S(2)}) collective-permute-start(f32[32,128]{1,0:T(8,128)S(1)} %shard_map.120.rest_0_), channel_id=1, source_target_pairs={{0,2},{1,3},{4,6},{5,7},{8,10},{9,11},{12,14},{13,15},{16,18},{17,... | collective-permute-start | bytes 49160 | tf_op jit(solution)/shard_map/ppermute | solution.py:485
  45.8 1.4 %collective-permute-start.7 = (f32[32,128]{1,0:T(8,128)S(1)}, f32[32,128]{1,0:T(8,128)S(1)}, u32[]{:S(2)}, u32[]{:S(2)}) collective-permute-start(f32[32,128]{1,0:T(8,128)S(1)} %shard_map.120.rest_0_), channel_id=1, source_target_pairs={{0,1},{1,0},{2,3},{3,2},{4,5},{5,4},{6,7},{7,6},{8,9},{9,8},{10,11... | collective-permute-start | bytes 49160 | tf_op jit(solution)/shard_map/ppermute | solution.py:337

commit v15 on v9

--- a/solution.py
+++ b/solution.py
@@ -149,37 +149,43 @@
             slope_ref[local] = slope(raw, guess)
 
 
-def serve_kernel(n, nblk, *rest):
+def told(message, j):
+    return message[message.shape[0] - 8 + j, 0].astype(I32)
+
+
+def settle(arrived, first, out):
+    scen = out.shape[1]
+    for message in arrived:
+        for rank in range(CAP):
+            place = told(message, 2 + rank)
+
+            @pl.when(place >= 0)
+            def _(message=message, rank=rank, place=place):
+                out[place] = message[pl.ds((first + rank) * scen, scen), :]
+
+
+def serve_kernel(n, *rest):
+    arrived, (old_guess, guess_ref, *outs) = rest[: n - 1], rest[n - 1 :]
+    for at in range(guess_ref.shape[0]):
+        guess_ref[at] = old_guess[at]
+    settle(arrived, 0, guess_ref)
+    for message, out in zip(arrived, outs):
+        want = joined(told(message, 0), told(message, 1))
+        for slot in range(out.shape[0]):
+            out[slot] = guess_ref[lowest(want)]
+            want = want & (want - 1)
+
+
+def merge_kernel(n, nblk, *rest):
     arrived, rest = rest[: n - 1], rest[n - 1 :]
-    inverses, rest = rest[:nblk], rest[nblk:]
-    old_guess, old_slope, guess_ref, slope_ref, whole_ref, *rest = rest
-    outs = rest
-    blocks, scen, nodes = guess_ref.shape
-
-    def told(k, j):
-        return arrived[k][2 * CAP * scen + j, 0].astype(I32)
-
-    for at in range(blocks):
-        guess_ref[at] = old_guess[at]
-        slope_ref[at] = old_slope[at]
+    inverses, (old_slope, _, slope_ref, whole_ref) = rest[:nblk], rest[nblk:]
     height = inverses[0].shape[0]
     for k in range(nblk):
         at = pl.multiple_of((lax.axis_index("blk") ^ k) * height, height)
         whole_ref[pl.ds(at, height), :] = inverses[k][...]
-    for k in range(n - 1):
-        for rank in range(CAP):
-            place = told(k, 2 + rank)
-
-            @pl.when(place >= 0)
-            def _(k=k, rank=rank, place=place):
-                guess_ref[place] = arrived[k][pl.ds(rank * scen, scen), :]
-                slope_ref[place] = arrived[k][pl.ds((CAP + rank) * scen, scen), :]
-
-    for k, out in enumerate(outs):
-        want = joined(told(k, 0), told(k, 1))
-        for slot in range(out.shape[0]):
-            out[slot] = guess_ref[lowest(want)]
-            want = want & (want - 1)
+    for at in range(slope_ref.shape[0]):
+        slope_ref[at] = old_slope[at]
+    settle(arrived, CAP, slope_ref)
 
 
 def where_kernel(rounds, span, rcap, last, partner_ref, _, index_ref, late_ref, reads, mine, starts, sem):
@@ -284,7 +290,7 @@
             partial_ref[at] = guess_ref[at] - residual * inv_ref[at]
         some = pl.ds(part * step, step)
         copies.append(pltpu.make_async_copy(held.at[some], out_ref.at[some], sems.at[part]))
-        copies[-1].start(priority=part % 2)
+        copies[-1].start()
     for copy in copies:
         copy.wait()
 
@@ -304,7 +310,7 @@
             held[at] = partial_ref[at] + scale_ref[at] * region
         span = pl.ds(part * step, step)
         copies.append(pltpu.make_async_copy(held.at[span], updated_ref.at[span], sems.at[part]))
-        copies[-1].start(priority=part % 2)
+        copies[-1].start()
     for copy in copies:
         copy.wait()
 
@@ -347,7 +353,7 @@
     ncol = lax.axis_size("sub") * nblk
     for size in (n, nblk, ncol):
         assert size & (size - 1) == 0
-    assert blocks <= 32
+    assert CAP == 2 and blocks <= 32 and blocks & (blocks - 1) == 0
     rcap = 2 * max(1, blocks // n)
     span = ncol * blocks
 
@@ -386,14 +392,21 @@
         [VMEM, VMEM],
         [scalars(blocks), pltpu.SemaphoreType.DMA],
     )
-    guess, slopes, whole, *served = call(
-        functools.partial(serve_kernel, n, nblk),
-        [block, block, square] + [tiles(rcap)] * (n - 1),
-        [*arrived, *inverses, old_guess, old_slope],
-        [VMEM] * (n - 1 + nblk + 2),
-        [VMEM] * (n + 2),
+    guess, *served = call(
+        functools.partial(serve_kernel, n),
+        [block] + [tiles(rcap)] * (n - 1),
+        [*arrived, old_guess],
+        [VMEM] * n,
+        [VMEM] * n,
     )
     others = [swap(x, "die", n, k) for x, k in zip(served, rounds)]
+    slopes, whole = call(
+        functools.partial(merge_kernel, n, nblk),
+        [block, square],
+        [*arrived, *inverses, old_slope, guess],
+        [VMEM] * (n + nblk) + [ANY],
+        [VMEM] * 2,
+    )
     last = n - 2
     index, late = call(
         functools.partial(where_kernel, rounds, span, rcap, last),
@@ -452,7 +465,7 @@
         [SMEM] * 2 + [VMEM] * 4,
         [VMEM],
     )
-    parts = 8 if blocks % 8 == 0 else 1
+    parts = 4 if blocks % 4 == 0 else 1
     partial, residual = call(
         functools.partial(residual_kernel, rcap, last, parts),
         [block, block],

time: 43.1 us -> 43 us (level)
    pallas_call x8 -> x9, Pallas kernels: 6.61 us -> 6.74 us  [call(): pl.pallas_call(body, out_shape=outs, in_specs=in_specs, out_specs=out_spe...]
  transfers between devices with their start and end apart: 10 -> 10, of which waited for: 6 -> 6; matrix products, arithmetic and copies ran while one was open for 0% -> 0% of each run, Pallas kernels for 20% -> 21%
where the time goes in v15:
time: 43 us; the launch traced here: 42.8 us
  waiting for transfers between devices  19 us (44%)
  Pallas kernels  11.9 us (28%)
  starting transfers between devices  11.1 us (26%)
  between operations  0.72 us (2%)
    ppermute x10, waiting for transfers between devices, swap(): return lax.ppermute(x, axes, [(d, d ^ k) for d in range(n)])  19 us
    ppermute x10, starting transfers between devices, swap(): return lax.ppermute(x, axes, [(d, d ^ k) for d in range(n)])  11.1 us
    pallas_call x9, Pallas kernels, call(): pl.pallas_call(body, out_shape=outs, in_specs=in_specs, out_specs=out_spe...  6.74 us
    pallas_call x1, Pallas kernels, shards(): pl.pallas_call(local_kernel, grid=(blocks // step,), out_shape=[block, bl...  5.19 us
  transfers between devices with their start and end apart: 10, of which 6 were waited for; matrix products, arithmetic and copies ran while one was open for 0% of the time, Pallas kernels for 21%

profile of v15, /device:TPU:9, one launch (start us, length us, event | category | flops | bytes accessed | tf_op | source)
XLA Modules:
  0.0 42.8 jit_solution(10830461347374897127)
XLA Ops:
  0.6 1.5 %shard_map.113 = (f32[32,3,32,128]{3,2,1,0:T(8,128)S(1)}, f32[64,128]{1,0:T(8,128)S(1)}, f32[136,128]{1,0:T(8,128)S(1)}, f32[136,128]{1,0:T(8,128)S(1)}, f32[136,128]{1,0:T(8,128)S(1)}) custom-call(s32[32]{0:T(128)} %new_slot_ref.3, s32[32]{0:T(128)} %partner_ref.3, f32[32,3,32,128]{3,2,1,0:T(8,128)} %history_ref.1, f32[64,128]{1,0:T(8,128)} %bitcast.1), custom_call_target="tpu_custom_call" | custom-call | tf_op jit(solution)/shard_map/pallas_call | solution.py:319
  2.1 2.4 %collective-permute-start = (f32[136,128]{1,0:T(8,128)S(1)}, f32[136,128]{1,0:T(8,128)S(1)}, u32[]{:S(2)}, u32[]{:S(2)}) collective-permute-start(f32[136,128]{1,0:T(8,128)S(1)} %get-tuple-element.25), channel_id=1, source_target_pairs={{0,8},{4,12},{8,0},{12,4},{1,9},{5,13},{9,1},{13,5},{2,10},{6,14},... | collective-permute-start | bytes 208904 | tf_op jit(solution)/shard_map/ppermute | solution.py:335
  4.5 0.0 collective-permute-start.1
  4.5 1.3 %collective-permute-start.2 = (f32[136,128]{1,0:T(8,128)S(1)}, f32[136,128]{1,0:T(8,128)S(1)}, u32[]{:S(2)}, u32[]{:S(2)}) collective-permute-start(f32[136,128]{1,0:T(8,128)S(1)} %get-tuple-element.27), channel_id=1, source_target_pairs={{0,4},{4,0},{8,12},{12,8},{1,5},{5,1},{9,13},{13,9},{2,6},{6,2},{1... | collective-permute-start | bytes 208904 | tf_op jit(solution)/shard_map/ppermute | solution.py:335
  5.7 1.1 %shard_map.114 = (f32[32,32,128]{2,1,0:T(8,128)S(1)}, f32[32,32,128]{2,1,0:T(8,128)S(1)}) custom-call(s32[32]{0:T(128)} %new_slot_ref.3, f32[32,3,32,128]{3,2,1,0:T(8,128)S(1)} %get-tuple-element.28.raw_ref), custom_call_target="tpu_custom_call" | custom-call | tf_op jit(solution)/shard_map/pallas_call | solution.py:319
  6.8 1.7 %collective-permute-done.rest_0_ = f32[136,128]{1,0:T(8,128)S(1)} collective-permute-done((f32[136,128]{1,0:T(8,128)S(1)}, f32[136,128]{1,0:T(8,128)S(1)}, u32[]{:S(2)}, u32[]{:S(2)}) %collective-permute-start) | collective-permute-done | bytes 69664 | tf_op jit(solution)/shard_map/ppermute | solution.py:335
  8.5 2.1 %collective-permute-done.1.rest_1_ = f32[136,128]{1,0:T(8,128)S(1)} collective-permute-done((f32[136,128]{1,0:T(8,128)S(1)}, f32[136,128]{1,0:T(8,128)S(1)}, u32[]{:S(2)}, u32[]{:S(2)}) %collective-permute-start.1) | collective-permute-done | bytes 69664 | tf_op jit(solution)/shard_map/ppermute | solution.py:335
  10.6 0.0 collective-permute-done.2.rest_2_
  10.6 0.5 %shard_map.115 = (f32[32,32,128]{2,1,0:T(8,128)S(1)}, f32[16,32,128]{2,1,0:T(8,128)S(1)}, f32[16,32,128]{2,1,0:T(8,128)S(1)}, f32[16,32,128]{2,1,0:T(8,128)S(1)}) custom-call(f32[136,128]{1,0:T(8,128)S(1)} %collective-permute-done.rest_0_, f32[136,128]{1,0:T(8,128)S(1)} %collective-permute-done.1.rest_1_, f32[136,128]{1,0:T(8,128)S(1)} %collective-permute-done.2.rest_2_, ...), custom_call_target="tpu_custom_call" | custom-call | tf_op jit(solution)/shard_map/pallas_call | solution.py:319
  11.0 1.9 %collective-permute-start.4 = (f32[16,32,128]{2,1,0:T(8,128)S(1)}, f32[16,32,128]{2,1,0:T(8,128)S(1)}, u32[]{:S(2)}, u32[]{:S(2)}) collective-permute-start(f32[16,32,128]{2,1,0:T(8,128)S(1)} %get-tuple-element.39), channel_id=1, source_target_pairs={{0,8},{4,12},{8,0},{12,4},{1,9},{5,13},{9,1},{13,5},{2,10},{6,14},... | collective-permute-start | bytes 786440 | tf_op jit(solution)/shard_map/ppermute | solution.py:335
  12.9 0.4 %collective-permute-start.5 = (f32[16,32,128]{2,1,0:T(8,128)S(1)}, f32[16,32,128]{2,1,0:T(8,128)S(1)}, u32[]{:S(2)}, u32[]{:S(2)}) collective-permute-start(f32[16,32,128]{2,1,0:T(8,128)S(1)} %get-tuple-element.40), channel_id=1, source_target_pairs={{0,12},{4,8},{8,4},{12,0},{1,13},{5,9},{9,5},{13,1},{2,14},{6,10},... | collective-permute-start | bytes 786440 | tf_op jit(solution)/shard_map/ppermute | solution.py:335
  13.4 1.3 %collective-permute-start.6 = (f32[16,32,128]{2,1,0:T(8,128)S(1)}, f32[16,32,128]{2,1,0:T(8,128)S(1)}, u32[]{:S(2)}, u32[]{:S(2)}) collective-permute-start(f32[16,32,128]{2,1,0:T(8,128)S(1)} %get-tuple-element.42), channel_id=1, source_target_pairs={{0,4},{4,0},{8,12},{12,8},{1,5},{5,1},{9,13},{13,9},{2,6},{6,2},{1... | collective-permute-start | bytes 786440 | tf_op jit(solution)/shard_map/ppermute | solution.py:335
  14.7 1.5 %collective-permute-start.3 = (f32[64,128]{1,0:T(8,128)S(1)}, f32[64,128]{1,0:T(8,128)S(1)}, u32[]{:S(2)}, u32[]{:S(2)}) collective-permute-start(f32[64,128]{1,0:T(8,128)S(1)} %get-tuple-element.33.rest_3_), channel_id=1, source_target_pairs={{0,1},{1,0},{2,3},{3,2},{4,5},{5,4},{6,7},{7,6},{8,9},{9,8},{10,11... | collective-permute-start | bytes 98312 | tf_op jit(solution)/shard_map/ppermute | solution.py:335
  16.2 1.4 %shard_map.116 = (s32[32]{0:T(128)S(4)}, s32[33]{0:T(128)S(4)}) custom-call(s32[32]{0:T(128)} %partner_ref.3, f32[32,32,128]{2,1,0:T(8,128)S(1)} %get-tuple-element.30._.rest_6_.guess_ref), custom_call_target="tpu_custom_call" | custom-call | tf_op jit(solution)/shard_map/pallas_call | solution.py:319
  17.6 0.0 collective-permute-done.3.rest_4_
  17.6 0.3 shard_map.117
  17.9 5.2 %shard_map.118 = (f32[32,32,128]{2,1,0:T(8,128)S(1)}, f32[32,32,128]{2,1,0:T(8,128)S(1)}, f32[32,32,128]{2,1,0:T(8,128)S(1)}, f32[32,128]{1,0:T(8,128)S(1)}) custom-call(f32[32,32,128]{2,1,0:T(8,128)S(1)} %get-tuple-element.30._.rest_6_.guess_ref, f32[32,32,128]{2,1,0:T(8,128)S(1)} %get-tuple-element.35.slope_ref, f32[32,128,128]{2,1,0:T(8,128)} %coupling_ref.1, ...), custom_call_target="tpu_custom_call" | custom-call | tf_op jit(solution)/shard_map/pallas_call | solution.py:422
  23.1 5.8 %collective-permute-done.4.rest_0_ = f32[16,32,128]{2,1,0:T(8,128)S(1)} collective-permute-done((f32[16,32,128]{2,1,0:T(8,128)S(1)}, f32[16,32,128]{2,1,0:T(8,128)S(1)}, u32[]{:S(2)}, u32[]{:S(2)}) %collective-permute-start.4) | collective-permute-done | bytes 262176 | tf_op jit(solution)/shard_map/ppermute | solution.py:335
  28.9 7.9 %collective-permute-done.5.rest_1_ = f32[16,32,128]{2,1,0:T(8,128)S(1)} collective-permute-done((f32[16,32,128]{2,1,0:T(8,128)S(1)}, f32[16,32,128]{2,1,0:T(8,128)S(1)}, u32[]{:S(2)}, u32[]{:S(2)}) %collective-permute-start.5) | collective-permute-done | bytes 262176 | tf_op jit(solution)/shard_map/ppermute | solution.py:335
  36.8 0.2 shard_map.119
  36.9 0.0 collective-permute-done.6.block_ref
  37.0 0.1 shard_map.120.rest_0_
  37.0 1.8 %collective-permute-start.9 = (f32[32,128]{1,0:T(8,128)S(1)}, f32[32,128]{1,0:T(8,128)S(1)}, u32[]{:S(2)}, u32[]{:S(2)}) collective-permute-start(f32[32,128]{1,0:T(8,128)S(1)} %shard_map.120.rest_0_), channel_id=1, source_target_pairs={{0,3},{1,2},{2,1},{3,0},{4,7},{5,6},{6,5},{7,4},{8,11},{9,10},{10,... | collective-permute-start | bytes 49160 | tf_op jit(solution)/shard_map/ppermute | solution.py:335
  38.9 0.3 collective-permute-start.8
  39.1 0.2 collective-permute-start.7
  39.4 0.8 %shard_map.121 = (f32[32,32,128]{2,1,0:T(8,128)S(1)}, f32[32,32,128]{2,1,0:T(8,128)}) custom-call(s32[32]{0:T(128)S(4)} %get-tuple-element.31.index_ref, f32[32,32,128]{2,1,0:T(8,128)S(1)} %get-tuple-element.44.near_ref, f32[16,32,128]{2,1,0:T(8,128)S(1)} %collective-permute-done.6.block_ref, f32[32,32,128]{2,1,0:T(8,128)S(1)} %get-tuple-element.38.base_ref, ...), custom_call_target="tpu_custom_call" | custom-call | tf_op jit(solution)/shard_map/pallas_call | solution.py:319
  40.2 0.5 %collective-permute-done.9.rest_3_ = f32[32,128]{1,0:T(8,128)S(1)} collective-permute-done((f32[32,128]{1,0:T(8,128)S(1)}, f32[32,128]{1,0:T(8,128)S(1)}, u32[]{:S(2)}, u32[]{:S(2)}) %collective-permute-start.9) | collective-permute-done | bytes 16416 | tf_op jit(solution)/shard_map/ppermute | solution.py:335
  40.7 1.1 %collective-permute-done.8.rest_2_ = f32[32,128]{1,0:T(8,128)S(1)} collective-permute-done((f32[32,128]{1,0:T(8,128)S(1)}, f32[32,128]{1,0:T(8,128)S(1)}, u32[]{:S(2)}, u32[]{:S(2)}) %collective-permute-start.8) | collective-permute-done | bytes 16416 | tf_op jit(solution)/shard_map/ppermute | solution.py:335
  41.8 0.0 collective-permute-done.7.rest_1_
  41.8 1.0 %shard_map.122 = f32[32,32,128]{2,1,0:T(8,128)} custom-call(f32[32,128]{1,0:T(8,128)S(1)} %shard_map.120.rest_0_, f32[32,128]{1,0:T(8,128)S(1)} %collective-permute-done.7.rest_1_, f32[32,128]{1,0:T(8,128)S(1)} %collective-permute-done.8.rest_2_, f32[32,128]{1,0:T(8,128)S(1)} %collective-permute-done.9.rest_3_, f32[128,128]{1,0:T(8,128)S(1)} %get-tuple-element.43.rest_4_, ...), custom_call_target="tpu_custom_call" | custom-call | tf_op jit(solution)/shard_map/pallas_call | solution.py:319
Async XLA Ops:
  2.1 6.4 %collective-permute-start = (f32[136,128]{1,0:T(8,128)S(1)}, f32[136,128]{1,0:T(8,128)S(1)}, u32[]{:S(2)}, u32[]{:S(2)}) collective-permute-start(f32[136,128]{1,0:T(8,128)S(1)} %get-tuple-element.25), channel_id=1, source_target_pairs={{0,8},{4,12},{8,0},{12,4},{1,9},{5,13},{9,1},{13,5},{2,10},{6,14},... | collective-permute-start | bytes 208904 | tf_op jit(solution)/shard_map/ppermute | solution.py:335
  4.5 6.1 %collective-permute-start.1 = (f32[136,128]{1,0:T(8,128)S(1)}, f32[136,128]{1,0:T(8,128)S(1)}, u32[]{:S(2)}, u32[]{:S(2)}) collective-permute-start(f32[136,128]{1,0:T(8,128)S(1)} %get-tuple-element.26), channel_id=1, source_target_pairs={{0,12},{4,8},{8,4},{12,0},{1,13},{5,9},{9,5},{13,1},{2,14},{6,10},... | collective-permute-start | bytes 208904 | tf_op jit(solution)/shard_map/ppermute | solution.py:335
  4.5 6.1 %collective-permute-start.2 = (f32[136,128]{1,0:T(8,128)S(1)}, f32[136,128]{1,0:T(8,128)S(1)}, u32[]{:S(2)}, u32[]{:S(2)}) collective-permute-start(f32[136,128]{1,0:T(8,128)S(1)} %get-tuple-element.27), channel_id=1, source_target_pairs={{0,4},{4,0},{8,12},{12,8},{1,5},{5,1},{9,13},{13,9},{2,6},{6,2},{1... | collective-permute-start | bytes 208904 | tf_op jit(solution)/shard_map/ppermute | solution.py:335
  11.0 17.9 %collective-permute-start.4 = (f32[16,32,128]{2,1,0:T(8,128)S(1)}, f32[16,32,128]{2,1,0:T(8,128)S(1)}, u32[]{:S(2)}, u32[]{:S(2)}) collective-permute-start(f32[16,32,128]{2,1,0:T(8,128)S(1)} %get-tuple-element.39), channel_id=1, source_target_pairs={{0,8},{4,12},{8,0},{12,4},{1,9},{5,13},{9,1},{13,5},{2,10},{6,14},... | collective-permute-start | bytes 786440 | tf_op jit(solution)/shard_map/ppermute | solution.py:335
  12.9 23.8 %collective-permute-start.5 = (f32[16,32,128]{2,1,0:T(8,128)S(1)}, f32[16,32,128]{2,1,0:T(8,128)S(1)}, u32[]{:S(2)}, u32[]{:S(2)}) collective-permute-start(f32[16,32,128]{2,1,0:T(8,128)S(1)} %get-tuple-element.40), channel_id=1, source_target_pairs={{0,12},{4,8},{8,4},{12,0},{1,13},{5,9},{9,5},{13,1},{2,14},{6,10},... | collective-permute-start | bytes 786440 | tf_op jit(solution)/shard_map/ppermute | solution.py:335
  13.4 23.6 %collective-permute-start.6 = (f32[16,32,128]{2,1,0:T(8,128)S(1)}, f32[16,32,128]{2,1,0:T(8,128)S(1)}, u32[]{:S(2)}, u32[]{:S(2)}) collective-permute-start(f32[16,32,128]{2,1,0:T(8,128)S(1)} %get-tuple-element.42), channel_id=1, source_target_pairs={{0,4},{4,0},{8,12},{12,8},{1,5},{5,1},{9,13},{13,9},{2,6},{6,2},{1... | collective-permute-start | bytes 786440 | tf_op jit(solution)/shard_map/ppermute | solution.py:335
  14.7 2.9 %collective-permute-start.3 = (f32[64,128]{1,0:T(8,128)S(1)}, f32[64,128]{1,0:T(8,128)S(1)}, u32[]{:S(2)}, u32[]{:S(2)}) collective-permute-start(f32[64,128]{1,0:T(8,128)S(1)} %get-tuple-element.33.rest_3_), channel_id=1, source_target_pairs={{0,1},{1,0},{2,3},{3,2},{4,5},{5,4},{6,7},{7,6},{8,9},{9,8},{10,11... | collective-permute-start | bytes 98312 | tf_op jit(solution)/shard_map/ppermute | solution.py:335
  37.0 3.6 %collective-permute-start.9 = (f32[32,128]{1,0:T(8,128)S(1)}, f32[32,128]{1,0:T(8,128)S(1)}, u32[]{:S(2)}, u32[]{:S(2)}) collective-permute-start(f32[32,128]{1,0:T(8,128)S(1)} %shard_map.120.rest_0_), channel_id=1, source_target_pairs={{0,3},{1,2},{2,1},{3,0},{4,7},{5,6},{6,5},{7,4},{8,11},{9,10},{10,... | collective-permute-start | bytes 49160 | tf_op jit(solution)/shard_map/ppermute | solution.py:335
  38.9 2.9 %collective-permute-start.8 = (f32[32,128]{1,0:T(8,128)S(1)}, f32[32,128]{1,0:T(8,128)S(1)}, u32[]{:S(2)}, u32[]{:S(2)}) collective-permute-start(f32[32,128]{1,0:T(8,128)S(1)} %shard_map.120.rest_0_), channel_id=1, source_target_pairs={{0,2},{1,3},{2,0},{3,1},{4,6},{5,7},{6,4},{7,5},{8,10},{9,11},{10,... | collective-permute-start | bytes 49160 | tf_op jit(solution)/shard_map/ppermute | solution.py:335
  39.1 2.6 %collective-permute-start.7 = (f32[32,128]{1,0:T(8,128)S(1)}, f32[32,128]{1,0:T(8,128)S(1)}, u32[]{:S(2)}, u32[]{:S(2)}) collective-permute-start(f32[32,128]{1,0:T(8,128)S(1)} %shard_map.120.rest_0_), channel_id=1, source_target_pairs={{0,1},{1,0},{2,3},{3,2},{4,5},{5,4},{6,7},{7,6},{8,9},{9,8},{10,11... | collective-permute-start | bytes 49160 | tf_op jit(solution)/shard_map/ppermute | solution.py:335

commit v16 on v15

--- a/solution.py
+++ b/solution.py
@@ -474,7 +474,8 @@
         [VMEM, HBM],
         [pltpu.VMEM((blocks, scen, nodes), F32), pltpu.SemaphoreType.DMA((parts,))],
     )
-    shares = [share] + [swap(share, ("sub", "blk"), ncol, k) for k in range(1, ncol)]
+    turns = [*range(1, nblk), *range(ncol - 1, nblk - 1, -1)]
+    shares = [share] + [swap(share, ("sub", "blk"), ncol, k) for k in turns]
     (updated,) = call(
         functools.partial(update_kernel, ncol, parts),
         [block],

time: 43 us -> 43 us (level)
  waiting for transfers between devices: 19 us -> 18.5 us
    ppermute x10, waiting for transfers between devices: 19 us -> 18.5 us  [swap(): return lax.ppermute(x, axes, [(d, d ^ k) for d in range(n)])]
  transfers between devices with their start and end apart: 10 -> 10, of which waited for: 6 -> 5; matrix products, arithmetic and copies ran while one was open for 0% -> 0% of each run, Pallas kernels for 21% -> 21%
where the time goes in v16:
time: 43 us; the launch traced here: 42.4 us
  waiting for transfers between devices  18.5 us (43%)
  Pallas kernels  11.9 us (28%)
  starting transfers between devices  11.2 us (26%)
  between operations  0.73 us (2%)
    ppermute x10, waiting for transfers between devices, swap(): return lax.ppermute(x, axes, [(d, d ^ k) for d in range(n)])  18.5 us
    ppermute x10, starting transfers between devices, swap(): return lax.ppermute(x, axes, [(d, d ^ k) for d in range(n)])  11.2 us
    pallas_call x9, Pallas kernels, call(): pl.pallas_call(body, out_shape=outs, in_specs=in_specs, out_specs=out_spe...  6.76 us
    pallas_call x1, Pallas kernels, shards(): pl.pallas_call(local_kernel, grid=(blocks // step,), out_shape=[block, bl...  5.19 us
  transfers between devices with their start and end apart: 10, of which 5 were waited for; matrix products, arithmetic and copies ran while one was open for 0% of the time, Pallas kernels for 21%

profile of v16, /device:TPU:9, one launch (start us, length us, event | category | flops | bytes accessed | tf_op | source)
XLA Modules:
  0.0 42.4 jit_solution(8202964363195068215)
XLA Ops:
  0.6 1.5 %shard_map.113 = (f32[32,3,32,128]{3,2,1,0:T(8,128)S(1)}, f32[64,128]{1,0:T(8,128)S(1)}, f32[136,128]{1,0:T(8,128)S(1)}, f32[136,128]{1,0:T(8,128)S(1)}, f32[136,128]{1,0:T(8,128)S(1)}) custom-call(s32[32]{0:T(128)} %new_slot_ref.3, s32[32]{0:T(128)} %partner_ref.3, f32[32,3,32,128]{3,2,1,0:T(8,128)} %history_ref.1, f32[64,128]{1,0:T(8,128)} %bitcast.1), custom_call_target="tpu_custom_call" | custom-call | tf_op jit(solution)/shard_map/pallas_call | solution.py:319
  2.1 2.4 %collective-permute-start = (f32[136,128]{1,0:T(8,128)S(1)}, f32[136,128]{1,0:T(8,128)S(1)}, u32[]{:S(2)}, u32[]{:S(2)}) collective-permute-start(f32[136,128]{1,0:T(8,128)S(1)} %get-tuple-element.25), channel_id=1, source_target_pairs={{0,8},{4,12},{8,0},{12,4},{1,9},{5,13},{9,1},{13,5},{2,10},{6,14},... | collective-permute-start | bytes 208904 | tf_op jit(solution)/shard_map/ppermute | solution.py:335
  4.5 0.0 collective-permute-start.1
  4.5 1.3 %collective-permute-start.2 = (f32[136,128]{1,0:T(8,128)S(1)}, f32[136,128]{1,0:T(8,128)S(1)}, u32[]{:S(2)}, u32[]{:S(2)}) collective-permute-start(f32[136,128]{1,0:T(8,128)S(1)} %get-tuple-element.27), channel_id=1, source_target_pairs={{0,4},{4,0},{8,12},{12,8},{1,5},{5,1},{9,13},{13,9},{2,6},{6,2},{1... | collective-permute-start | bytes 208904 | tf_op jit(solution)/shard_map/ppermute | solution.py:335
  5.7 1.1 %shard_map.114 = (f32[32,32,128]{2,1,0:T(8,128)S(1)}, f32[32,32,128]{2,1,0:T(8,128)S(1)}) custom-call(s32[32]{0:T(128)} %new_slot_ref.3, f32[32,3,32,128]{3,2,1,0:T(8,128)S(1)} %get-tuple-element.28.raw_ref), custom_call_target="tpu_custom_call" | custom-call | tf_op jit(solution)/shard_map/pallas_call | solution.py:319
  6.8 1.7 %collective-permute-done.rest_0_ = f32[136,128]{1,0:T(8,128)S(1)} collective-permute-done((f32[136,128]{1,0:T(8,128)S(1)}, f32[136,128]{1,0:T(8,128)S(1)}, u32[]{:S(2)}, u32[]{:S(2)}) %collective-permute-start) | collective-permute-done | bytes 69664 | tf_op jit(solution)/shard_map/ppermute | solution.py:335
  8.5 2.1 %collective-permute-done.1.rest_1_ = f32[136,128]{1,0:T(8,128)S(1)} collective-permute-done((f32[136,128]{1,0:T(8,128)S(1)}, f32[136,128]{1,0:T(8,128)S(1)}, u32[]{:S(2)}, u32[]{:S(2)}) %collective-permute-start.1) | collective-permute-done | bytes 69664 | tf_op jit(solution)/shard_map/ppermute | solution.py:335
  10.6 0.0 collective-permute-done.2.rest_2_
  10.6 0.5 %shard_map.115 = (f32[32,32,128]{2,1,0:T(8,128)S(1)}, f32[16,32,128]{2,1,0:T(8,128)S(1)}, f32[16,32,128]{2,1,0:T(8,128)S(1)}, f32[16,32,128]{2,1,0:T(8,128)S(1)}) custom-call(f32[136,128]{1,0:T(8,128)S(1)} %collective-permute-done.rest_0_, f32[136,128]{1,0:T(8,128)S(1)} %collective-permute-done.1.rest_1_, f32[136,128]{1,0:T(8,128)S(1)} %collective-permute-done.2.rest_2_, ...), custom_call_target="tpu_custom_call" | custom-call | tf_op jit(solution)/shard_map/pallas_call | solution.py:319
  11.0 1.9 %collective-permute-start.4 = (f32[16,32,128]{2,1,0:T(8,128)S(1)}, f32[16,32,128]{2,1,0:T(8,128)S(1)}, u32[]{:S(2)}, u32[]{:S(2)}) collective-permute-start(f32[16,32,128]{2,1,0:T(8,128)S(1)} %get-tuple-element.39), channel_id=1, source_target_pairs={{0,8},{4,12},{8,0},{12,4},{1,9},{5,13},{9,1},{13,5},{2,10},{6,14},... | collective-permute-start | bytes 786440 | tf_op jit(solution)/shard_map/ppermute | solution.py:335
  12.9 0.4 %collective-permute-start.5 = (f32[16,32,128]{2,1,0:T(8,128)S(1)}, f32[16,32,128]{2,1,0:T(8,128)S(1)}, u32[]{:S(2)}, u32[]{:S(2)}) collective-permute-start(f32[16,32,128]{2,1,0:T(8,128)S(1)} %get-tuple-element.40), channel_id=1, source_target_pairs={{0,12},{4,8},{8,4},{12,0},{1,13},{5,9},{9,5},{13,1},{2,14},{6,10},... | collective-permute-start | bytes 786440 | tf_op jit(solution)/shard_map/ppermute | solution.py:335
  13.4 1.3 %collective-permute-start.6 = (f32[16,32,128]{2,1,0:T(8,128)S(1)}, f32[16,32,128]{2,1,0:T(8,128)S(1)}, u32[]{:S(2)}, u32[]{:S(2)}) collective-permute-start(f32[16,32,128]{2,1,0:T(8,128)S(1)} %get-tuple-element.42), channel_id=1, source_target_pairs={{0,4},{4,0},{8,12},{12,8},{1,5},{5,1},{9,13},{13,9},{2,6},{6,2},{1... | collective-permute-start | bytes 786440 | tf_op jit(solution)/shard_map/ppermute | solution.py:335
  14.7 1.5 %collective-permute-start.3 = (f32[64,128]{1,0:T(8,128)S(1)}, f32[64,128]{1,0:T(8,128)S(1)}, u32[]{:S(2)}, u32[]{:S(2)}) collective-permute-start(f32[64,128]{1,0:T(8,128)S(1)} %get-tuple-element.33.rest_3_), channel_id=1, source_target_pairs={{0,1},{1,0},{2,3},{3,2},{4,5},{5,4},{6,7},{7,6},{8,9},{9,8},{10,11... | collective-permute-start | bytes 98312 | tf_op jit(solution)/shard_map/ppermute | solution.py:335
  16.2 1.4 %shard_map.116 = (s32[32]{0:T(128)S(4)}, s32[33]{0:T(128)S(4)}) custom-call(s32[32]{0:T(128)} %partner_ref.3, f32[32,32,128]{2,1,0:T(8,128)S(1)} %get-tuple-element.30._.rest_6_.guess_ref), custom_call_target="tpu_custom_call" | custom-call | tf_op jit(solution)/shard_map/pallas_call | solution.py:319
  17.6 0.0 collective-permute-done.3.rest_4_
  17.6 0.3 shard_map.117
  17.9 5.2 %shard_map.118 = (f32[32,32,128]{2,1,0:T(8,128)S(1)}, f32[32,32,128]{2,1,0:T(8,128)S(1)}, f32[32,32,128]{2,1,0:T(8,128)S(1)}, f32[32,128]{1,0:T(8,128)S(1)}) custom-call(f32[32,32,128]{2,1,0:T(8,128)S(1)} %get-tuple-element.30._.rest_6_.guess_ref, f32[32,32,128]{2,1,0:T(8,128)S(1)} %get-tuple-element.35.slope_ref, f32[32,128,128]{2,1,0:T(8,128)} %coupling_ref.1, ...), custom_call_target="tpu_custom_call" | custom-call | tf_op jit(solution)/shard_map/pallas_call | solution.py:422
  23.1 5.8 %collective-permute-done.4.rest_0_ = f32[16,32,128]{2,1,0:T(8,128)S(1)} collective-permute-done((f32[16,32,128]{2,1,0:T(8,128)S(1)}, f32[16,32,128]{2,1,0:T(8,128)S(1)}, u32[]{:S(2)}, u32[]{:S(2)}) %collective-permute-start.4) | collective-permute-done | bytes 262176 | tf_op jit(solution)/shard_map/ppermute | solution.py:335
  28.9 7.8 %collective-permute-done.5.rest_1_ = f32[16,32,128]{2,1,0:T(8,128)S(1)} collective-permute-done((f32[16,32,128]{2,1,0:T(8,128)S(1)}, f32[16,32,128]{2,1,0:T(8,128)S(1)}, u32[]{:S(2)}, u32[]{:S(2)}) %collective-permute-start.5) | collective-permute-done | bytes 262176 | tf_op jit(solution)/shard_map/ppermute | solution.py:335
  36.8 0.2 shard_map.119
  36.9 0.0 collective-permute-done.6.block_ref
  37.0 0.1 shard_map.120.rest_0_
  37.0 1.2 %collective-permute-start.9 = (f32[32,128]{1,0:T(8,128)S(1)}, f32[32,128]{1,0:T(8,128)S(1)}, u32[]{:S(2)}, u32[]{:S(2)}) collective-permute-start(f32[32,128]{1,0:T(8,128)S(1)} %shard_map.120.rest_0_), channel_id=1, source_target_pairs={{0,2},{1,3},{2,0},{3,1},{4,6},{5,7},{6,4},{7,5},{8,10},{9,11},{10,... | collective-permute-start | bytes 49160 | tf_op jit(solution)/shard_map/ppermute | solution.py:335
  38.2 1.2 %collective-permute-start.8 = (f32[32,128]{1,0:T(8,128)S(1)}, f32[32,128]{1,0:T(8,128)S(1)}, u32[]{:S(2)}, u32[]{:S(2)}) collective-permute-start(f32[32,128]{1,0:T(8,128)S(1)} %shard_map.120.rest_0_), channel_id=1, source_target_pairs={{0,3},{1,2},{2,1},{3,0},{4,7},{5,6},{6,5},{7,4},{8,11},{9,10},{10,... | collective-permute-start | bytes 49160 | tf_op jit(solution)/shard_map/ppermute | solution.py:335
  39.4 0.0 collective-permute-start.7
  39.4 0.8 %shard_map.121 = (f32[32,32,128]{2,1,0:T(8,128)S(1)}, f32[32,32,128]{2,1,0:T(8,128)}) custom-call(s32[32]{0:T(128)S(4)} %get-tuple-element.31.index_ref, f32[32,32,128]{2,1,0:T(8,128)S(1)} %get-tuple-element.44.near_ref, f32[16,32,128]{2,1,0:T(8,128)S(1)} %collective-permute-done.6.block_ref, f32[32,32,128]{2,1,0:T(8,128)S(1)} %get-tuple-element.38.base_ref, ...), custom_call_target="tpu_custom_call" | custom-call | tf_op jit(solution)/shard_map/pallas_call | solution.py:319
  40.3 0.0 collective-permute-done.9.rest_3_
  40.3 1.1 %collective-permute-done.8.rest_2_ = f32[32,128]{1,0:T(8,128)S(1)} collective-permute-done((f32[32,128]{1,0:T(8,128)S(1)}, f32[32,128]{1,0:T(8,128)S(1)}, u32[]{:S(2)}, u32[]{:S(2)}) %collective-permute-start.8) | collective-permute-done | bytes 16416 | tf_op jit(solution)/shard_map/ppermute | solution.py:335
  41.4 0.0 collective-permute-done.7.rest_1_
  41.4 1.0 %shard_map.122 = f32[32,32,128]{2,1,0:T(8,128)} custom-call(f32[32,128]{1,0:T(8,128)S(1)} %shard_map.120.rest_0_, f32[32,128]{1,0:T(8,128)S(1)} %collective-permute-done.7.rest_1_, f32[32,128]{1,0:T(8,128)S(1)} %collective-permute-done.8.rest_2_, f32[32,128]{1,0:T(8,128)S(1)} %collective-permute-done.9.rest_3_, f32[128,128]{1,0:T(8,128)S(1)} %get-tuple-element.43.rest_4_, ...), custom_call_target="tpu_custom_call" | custom-call | tf_op jit(solution)/shard_map/pallas_call | solution.py:319
Async XLA Ops:
  2.1 6.4 %collective-permute-start = (f32[136,128]{1,0:T(8,128)S(1)}, f32[136,128]{1,0:T(8,128)S(1)}, u32[]{:S(2)}, u32[]{:S(2)}) collective-permute-start(f32[136,128]{1,0:T(8,128)S(1)} %get-tuple-element.25), channel_id=1, source_target_pairs={{0,8},{4,12},{8,0},{12,4},{1,9},{5,13},{9,1},{13,5},{2,10},{6,14},... | collective-permute-start | bytes 208904 | tf_op jit(solution)/shard_map/ppermute | solution.py:335
  4.5 6.1 %collective-permute-start.1 = (f32[136,128]{1,0:T(8,128)S(1)}, f32[136,128]{1,0:T(8,128)S(1)}, u32[]{:S(2)}, u32[]{:S(2)}) collective-permute-start(f32[136,128]{1,0:T(8,128)S(1)} %get-tuple-element.26), channel_id=1, source_target_pairs={{0,12},{4,8},{8,4},{12,0},{1,13},{5,9},{9,5},{13,1},{2,14},{6,10},... | collective-permute-start | bytes 208904 | tf_op jit(solution)/shard_map/ppermute | solution.py:335
  4.5 6.1 %collective-permute-start.2 = (f32[136,128]{1,0:T(8,128)S(1)}, f32[136,128]{1,0:T(8,128)S(1)}, u32[]{:S(2)}, u32[]{:S(2)}) collective-permute-start(f32[136,128]{1,0:T(8,128)S(1)} %get-tuple-element.27), channel_id=1, source_target_pairs={{0,4},{4,0},{8,12},{12,8},{1,5},{5,1},{9,13},{13,9},{2,6},{6,2},{1... | collective-permute-start | bytes 208904 | tf_op jit(solution)/shard_map/ppermute | solution.py:335
  11.0 17.9 %collective-permute-start.4 = (f32[16,32,128]{2,1,0:T(8,128)S(1)}, f32[16,32,128]{2,1,0:T(8,128)S(1)}, u32[]{:S(2)}, u32[]{:S(2)}) collective-permute-start(f32[16,32,128]{2,1,0:T(8,128)S(1)} %get-tuple-element.39), channel_id=1, source_target_pairs={{0,8},{4,12},{8,0},{12,4},{1,9},{5,13},{9,1},{13,5},{2,10},{6,14},... | collective-permute-start | bytes 786440 | tf_op jit(solution)/shard_map/ppermute | solution.py:335
  12.9 23.8 %collective-permute-start.5 = (f32[16,32,128]{2,1,0:T(8,128)S(1)}, f32[16,32,128]{2,1,0:T(8,128)S(1)}, u32[]{:S(2)}, u32[]{:S(2)}) collective-permute-start(f32[16,32,128]{2,1,0:T(8,128)S(1)} %get-tuple-element.40), channel_id=1, source_target_pairs={{0,12},{4,8},{8,4},{12,0},{1,13},{5,9},{9,5},{13,1},{2,14},{6,10},... | collective-permute-start | bytes 786440 | tf_op jit(solution)/shard_map/ppermute | solution.py:335
  13.4 23.6 %collective-permute-start.6 = (f32[16,32,128]{2,1,0:T(8,128)S(1)}, f32[16,32,128]{2,1,0:T(8,128)S(1)}, u32[]{:S(2)}, u32[]{:S(2)}) collective-permute-start(f32[16,32,128]{2,1,0:T(8,128)S(1)} %get-tuple-element.42), channel_id=1, source_target_pairs={{0,4},{4,0},{8,12},{12,8},{1,5},{5,1},{9,13},{13,9},{2,6},{6,2},{1... | collective-permute-start | bytes 786440 | tf_op jit(solution)/shard_map/ppermute | solution.py:335
  14.7 2.9 %collective-permute-start.3 = (f32[64,128]{1,0:T(8,128)S(1)}, f32[64,128]{1,0:T(8,128)S(1)}, u32[]{:S(2)}, u32[]{:S(2)}) collective-permute-start(f32[64,128]{1,0:T(8,128)S(1)} %get-tuple-element.33.rest_3_), channel_id=1, source_target_pairs={{0,1},{1,0},{2,3},{3,2},{4,5},{5,4},{6,7},{7,6},{8,9},{9,8},{10,11... | collective-permute-start | bytes 98312 | tf_op jit(solution)/shard_map/ppermute | solution.py:335
  37.0 3.2 %collective-permute-start.9 = (f32[32,128]{1,0:T(8,128)S(1)}, f32[32,128]{1,0:T(8,128)S(1)}, u32[]{:S(2)}, u32[]{:S(2)}) collective-permute-start(f32[32,128]{1,0:T(8,128)S(1)} %shard_map.120.rest_0_), channel_id=1, source_target_pairs={{0,2},{1,3},{2,0},{3,1},{4,6},{5,7},{6,4},{7,5},{8,10},{9,11},{10,... | collective-permute-start | bytes 49160 | tf_op jit(solution)/shard_map/ppermute | solution.py:335
  38.2 3.2 %collective-permute-start.8 = (f32[32,128]{1,0:T(8,128)S(1)}, f32[32,128]{1,0:T(8,128)S(1)}, u32[]{:S(2)}, u32[]{:S(2)}) collective-permute-start(f32[32,128]{1,0:T(8,128)S(1)} %shard_map.120.rest_0_), channel_id=1, source_target_pairs={{0,3},{1,2},{2,1},{3,0},{4,7},{5,6},{6,5},{7,4},{8,11},{9,10},{10,... | collective-permute-start | bytes 49160 | tf_op jit(solution)/shard_map/ppermute | solution.py:335
  39.4 2.0 %collective-permute-start.7 = (f32[32,128]{1,0:T(8,128)S(1)}, f32[32,128]{1,0:T(8,128)S(1)}, u32[]{:S(2)}, u32[]{:S(2)}) collective-permute-start(f32[32,128]{1,0:T(8,128)S(1)} %shard_map.120.rest_0_), channel_id=1, source_target_pairs={{0,1},{1,0},{2,3},{3,2},{4,5},{5,4},{6,7},{7,6},{8,9},{9,8},{10,11... | collective-permute-start | bytes 49160 | tf_op jit(solution)/shard_map/ppermute | solution.py:335
